TPU v7x, 128 devices: a whole 4x4x4 slice. The times are simulated.
128 devices in a mesh: gx: 8 (over x, core), gy: 16 (over y, z).
Axes of the slice: x: 4, y: 4, z: 4, core: 2. Of those that a mesh axis runs over, the one named last changes fastest.
Arguments:
- right_side: float32 [2, 128, 128, 128], P(None, 'gx', 'gy'), may hold values from -6 to 6
- accumulation: float32 [4, 128, 128, 128], P(None, 'gx', 'gy'), may hold values from -0.3 to 0.5, as said below
- trans_x: float32 [2, 128, 128, 128], P(None, 'gx', 'gy'), may hold values from 0.05 to 0.5
- trans_y: float32 [2, 128, 128, 128], P(None, 'gx', 'gy'), may hold values from 5 to 50
- trans_z: float32 [2, 128, 128, 128], P(None, 'gx', 'gy'), may hold values from 0.05 to 0.5
- perf_cell: int32 [8, 16, 8, 32], P('gx', 'gy'), may hold values from 0 to 16383
- perf_well: int32 [8, 16, 8, 32], P('gx', 'gy'), may hold values from 0 to 15
- perf_weight: float32 [8, 16, 8, 32], P('gx', 'gy'), may hold values from 0.05 to 2
- perf_count: int32 [8, 16, 8], P('gx', 'gy'), may hold values from 8 to 32, as said below
- breaks: int32 [128, 128], P(('gx', 'gy')), may hold values 0 or 1
Outputs:
- adjoint: float32 [2, 128, 128, 128], P(None, 'gx', 'gy')
- residual: float32 [2, 128, 128, 128], P(None, 'gx', 'gy')
Inputs may be any that keep to these rules, and one draw needn't show every extreme that they name: `accumulation`: entries 00 and 11 are positive; |entry 01| <= 0.6 entry 00 and |entry 10| <= 0.6 entry 11. `perf_count`: in every draw and every second-axis index, one owner receives 32 live slots from every device.
All inputs are finite; a program needn't handle non-finite values. No bound on the sum of `breaks` on one device may be relied on, other than what follows from the above.
Results may differ from a plain program's by a relative error of at most 0.00035.
Values sent between devices are 32-bit elements; how exact they have to be, the bound alone decides.
No kernel may reach another device: no remote copies, remote signals or barrier semaphores. Data moves between devices by JAX's collectives and lax.ppermute only.
A program may use at most 64 MiB of HBM per device.

v0:
```python
import jax
import jax.numpy as jnp
from jax import lax
from jax.sharding import PartitionSpec as P

W_DEV = 16


def passed_along(block, axis, distance):
    devices = range(lax.axis_size(axis))
    route = [(i - distance, i) for i in devices if i - distance in devices]
    return lax.ppermute(block, axis, route)


def extended(shard, sides, width):
    for axis, dim in sides:
        devices, length = (lax.axis_size(axis), shard.shape[dim])
        up = [(i, (i + 1) % devices) for i in range(devices - 1)]
        down = [(j, i) for i, j in up]
        last = lax.slice_in_dim(shard, length - width, length, axis=dim)
        leading = lax.slice_in_dim(shard, 0, width, axis=dim)
        before = lax.ppermute(last, axis, up)
        after = lax.ppermute(leading, axis, down)
        shard = jnp.concatenate([before, shard, after], axis=dim)
    return shard


def shift_down(a, s):
    return jnp.concatenate([jnp.zeros_like(a[..., :s, :]), a[..., :-s, :]], axis=-2)


def shift_up(a, s):
    return jnp.concatenate([a[..., s:, :], jnp.zeros_like(a[..., :s, :])], axis=-2)


def mul_block(p, q):
    return jnp.stack(
        [
            jnp.stack(
                [p[0, 0] * q[0, 0] + p[0, 1] * q[1, 0], p[0, 0] * q[0, 1] + p[0, 1] * q[1, 1]]
            ),
            jnp.stack(
                [p[1, 0] * q[0, 0] + p[1, 1] * q[1, 0], p[1, 0] * q[0, 1] + p[1, 1] * q[1, 1]]
            ),
        ]
    )


def apply_block(p, v):
    return jnp.stack([p[0, 0] * v[0] + p[0, 1] * v[1], p[1, 0] * v[0] + p[1, 1] * v[1]])


def invert_block(p):
    determ = p[0, 0] * p[1, 1] - p[0, 1] * p[1, 0]
    return jnp.stack([jnp.stack([p[1, 1], -p[0, 1]]), jnp.stack([-p[1, 0], p[0, 0]])]) / determ


def diag_block(d):
    zero = jnp.zeros_like(d[0])
    return jnp.stack([jnp.stack([d[0], zero]), jnp.stack([zero, d[1]])])


def line_solve(center, lower, upper, rhs):
    below = diag_block(lower)
    above = diag_block(upper)
    length = rhs.shape[-2]
    stride = 1
    while stride < length:
        inverse = invert_block(center)
        alpha = -mul_block(below, shift_down(inverse, stride))
        gamma = -mul_block(above, shift_up(inverse, stride))
        center = (
            center
            + mul_block(alpha, shift_down(above, stride))
            + mul_block(gamma, shift_up(below, stride))
        )
        new_below = mul_block(alpha, shift_down(below, stride))
        new_above = mul_block(gamma, shift_up(above, stride))
        rhs = (
            rhs
            + apply_block(alpha, shift_down(rhs, stride))
            + apply_block(gamma, shift_up(rhs, stride))
        )
        below, above = (new_below, new_above)
        stride = stride * 2
    return apply_block(invert_block(center), rhs)


def solve_lines(system, breaks, vector):
    line_rows, line_len, layers = (system.shape[1], system.shape[2], system.shape[3])
    center = system[:4].reshape(2, 2, line_rows, line_len, layers)
    ty_line = system[4:6]
    keep = (1.0 - breaks.astype(jnp.float32))[None, :, :, None]
    lower = -shift_down(ty_line, 1) * keep
    upper = -ty_line * shift_up(keep, 1)
    return line_solve(center, lower, upper, vector)


def pair_sums(resid, image):
    return lax.psum((jnp.sum(resid * image), jnp.sum(image * image)), ("gx", "gy"))


def body(
    right_side,
    accumulation,
    trans_x,
    trans_y,
    trans_z,
    perf_cell,
    perf_well,
    perf_weight,
    perf_count,
    breaks,
):
    hp = lax.Precision.HIGHEST
    cx, cy, nz = (right_side.shape[1], right_side.shape[2], right_side.shape[3])
    rows_total = cx * lax.axis_size("gx")
    cols_total = cy * lax.axis_size("gy")
    owners = perf_cell.shape[2]
    slots = perf_cell.shape[3]
    row_global = lax.axis_index("gx") * cx + jnp.arange(cx)
    col_global = lax.axis_index("gy") * cy + jnp.arange(cy)
    tx = trans_x * (row_global < rows_total - 1).astype(jnp.float32)[None, :, None, None]
    ty = trans_y * (col_global < cols_total - 1).astype(jnp.float32)[None, None, :, None]
    tz = trans_z * (jnp.arange(nz) < nz - 1).astype(jnp.float32)[None, None, None, :]
    edge_x = passed_along(tx[:, -1:], "gx", 1)
    lx = jnp.concatenate([edge_x, tx[:, :-1]], axis=1)
    edge_y = passed_along(ty[:, :, -1:], "gy", 1)
    ly = jnp.concatenate([edge_y, ty[:, :, :-1]], axis=2)
    lz = jnp.concatenate([jnp.zeros_like(tz[..., :1]), tz[..., :-1]], axis=3)
    faces = tx + lx + ty + ly + tz + lz
    d00 = accumulation[0] + faces[0]
    d01 = accumulation[2]
    d10 = accumulation[1]
    d11 = accumulation[3] + faces[1]
    coefs = jnp.stack([d00, d01, d10, d11, ty[0], ty[1]])
    cells = perf_cell.reshape(owners * slots)
    well_ids = perf_well.reshape(owners, slots)
    live = (jnp.arange(slots)[None, :] < perf_count.reshape(owners)[:, None]).astype(jnp.float32)
    weights = perf_weight.reshape(owners, slots) * live
    recv_ids = lax.all_to_all(well_ids, "gx", split_axis=0, concat_axis=0, tiled=True)
    recv_weights = lax.all_to_all(weights, "gx", split_axis=0, concat_axis=0, tiled=True)
    onehot_recv = (recv_ids[..., None] == jnp.arange(W_DEV)[None, None, :]).astype(jnp.float32)
    totals = jnp.maximum(jnp.einsum("sk,skw->w", recv_weights, onehot_recv, precision=hp), 1.0)

    def well_add(pressure):
        values = jnp.take(pressure.reshape(cx * cy * nz), cells).reshape(owners, slots)
        arrived = lax.all_to_all(weights * values, "gx", split_axis=0, concat_axis=0, tiled=True)
        rates = jnp.einsum("sk,skw->w", arrived, onehot_recv, precision=hp) / totals
        owner_rates = jnp.einsum("skw,w->sk", onehot_recv, rates, precision=hp)
        slot_rate = lax.all_to_all(owner_rates, "gx", split_axis=0, concat_axis=0, tiled=True)
        added = (weights * slot_rate).reshape(owners * slots)
        return jnp.zeros((cx * cy * nz,), jnp.float32).at[cells].add(added).reshape(cx, cy, nz)

    def operate(field):
        padded = extended(field, (("gx", 1), ("gy", 2)), 1)
        middle = padded[:, 1:-1, 1:-1]
        upper_z = jnp.concatenate([middle[..., 1:], jnp.zeros_like(middle[..., :1])], axis=3)
        lower_z = jnp.concatenate([jnp.zeros_like(middle[..., :1]), middle[..., :-1]], axis=3)
        beside = tx * padded[:, 2:, 1:-1] + lx * padded[:, :-2, 1:-1]
        beside = beside + ty * padded[:, 1:-1, 2:] + ly * padded[:, 1:-1, :-2]
        beside = beside + tz * upper_z + lz * lower_z
        first = d00 * field[0] + d01 * field[1] - beside[0] + well_add(field[0])
        second = d10 * field[0] + d11 * field[1] - beside[1]
        return jnp.stack([first, second])

    def precondition(vector):
        system = lax.all_to_all(coefs, "gy", split_axis=1, concat_axis=2, tiled=True)
        on_lines = lax.all_to_all(vector, "gy", split_axis=1, concat_axis=2, tiled=True)
        solved = solve_lines(system, breaks, on_lines)
        return lax.all_to_all(solved, "gy", split_axis=2, concat_axis=1, tiled=True)

    p_one = precondition(right_side)
    q_one = operate(p_one)
    rq_one, qq_one = pair_sums(right_side, q_one)
    a_one = rq_one / qq_one
    adjoint = a_one * p_one
    resid = right_side - a_one * q_one
    p_two = precondition(resid)
    q_two = operate(p_two)
    beta = lax.psum(jnp.sum(q_two * q_one), ("gx", "gy")) / qq_one
    p_two = p_two - beta * p_one
    q_two = q_two - beta * q_one
    rq_two, qq_two = pair_sums(resid, q_two)
    a_two = rq_two / qq_two
    adjoint = adjoint + a_two * p_two
    resid = resid - a_two * q_two
    return (adjoint, resid)


def solution(mesh):
    placed = (
        P(None, "gx", "gy", None),
        P(None, "gx", "gy", None),
        P(None, "gx", "gy", None),
        P(None, "gx", "gy", None),
        P(None, "gx", "gy", None),
        P("gx", "gy", None, None),
        P("gx", "gy", None, None),
        P("gx", "gy", None, None),
        P("gx", "gy", None),
        P(("gx", "gy"), None),
    )
    return jax.shard_map(
        body,
        mesh=mesh,
        in_specs=placed,
        out_specs=(P(None, "gx", "gy", None), P(None, "gx", "gy", None)),
        check_vma=False,
    )
```

profile of v0, /device:TPU:0, one launch (start us, length us, event | category | flops | bytes accessed | tf_op | source)
XLA Modules:
  0.0 379.3 jit_solution(12341471124213521711)
XLA Ops:
  0.6 1.6 copy.1235
  2.2 8.3 %all-to-all-start.1 = ((f32[2,16,8,128]{3,2,0,1:T(8,128)}), f32[2,16,8,128]{3,2,0,1:T(8,128)S(1)}, u32[]{:S(2)}, u32[]{:S(2)}) async-start(f32[2,16,8,128]{3,2,0,1:T(8,128)} %copy.1235), calls=%async_computation.1 | async-start | bytes 262144 | tf_op jit(solution)/shard_map/all_to_all | solution.py:169
  12.3 3.7 collective-permute-start.1
  20.5 7.0 %all-to-all-start = ((f32[6,16,8,128]{3,2,0,1:T(8,128)}), f32[6,16,8,128]{3,2,0,1:T(8,128)S(1)}, u32[]{:S(2)}, u32[]{:S(2)}) async-start(f32[6,16,8,128]{3,2,0,1:T(8,128)} %copy.965), calls=%async_computation | async-start | bytes 786432 | tf_op jit(solution)/shard_map/all_to_all | solution.py:168
  28.2 10.4 %all-to-all-done = f32[6,16,8,128]{3,2,0,1:T(8,128)S(1)} async-done(((f32[6,16,8,128]{3,2,0,1:T(8,128)}), f32[6,16,8,128]{3,2,0,1:T(8,128)S(1)}, u32[]{:S(2)}, u32[]{:S(2)}) %all-to-all-start) | async-done | bytes 393248 | tf_op jit(solution)/shard_map/all_to_all | solution.py:168
  50.5 3.6 all-to-all-start.2
  56.3 5.7 %all-to-all-done.2 = f32[2,1,128,128]{3,0,1,2:T(2,128)S(1)} async-done(((f32[2,1,128,128]{3,0,1,2:T(2,128)}), f32[2,1,128,128]{3,0,1,2:T(2,128)S(1)}, u32[]{:S(2)}, u32[]{:S(2)}) %all-to-all-start.2) | async-done | bytes 131104 | tf_op jit(solution)/shard_map/all_to_all | solution.py:171
  62.0 4.4 %all-to-all-start.3 = ((s32[8,1,32]{2,1,0:T(1,128)}), s32[8,1,32]{2,1,0:T(1,128)S(1)}, u32[]{:S(2)}, u32[]{:S(2)}) async-start(s32[8,1,32]{2,1,0:T(1,128)} %bitcast.662), calls=%async_computation.3 | async-start | bytes 8192 | tf_op jit(solution)/shard_map/all_to_all | solution.py:141
  67.1 1.7 gather_fusion
  71.6 4.5 %all-to-all-start.5 = ((f32[8,1,32]{2,1,0:T(1,128)}), f32[8,1,32]{2,1,0:T(1,128)S(1)}, u32[]{:S(2)}, u32[]{:S(2)}) async-start(f32[8,1,32]{2,1,0:T(1,128)} %get-tuple-element.15), calls=%async_computation.5 | async-start | bytes 8192 | tf_op jit(solution)/shard_map/all_to_all | solution.py:142
  77.3 3.0 collective-permute-start.3
  81.3 4.9 %all-to-all-start.4 = ((f32[8,1,32]{2,1,0:T(1,128)}), f32[8,1,32]{2,1,0:T(1,128)S(1)}, u32[]{:S(2)}, u32[]{:S(2)}) async-start(f32[8,1,32]{2,1,0:T(1,128)} %get-tuple-element.14), calls=%async_computation.4 | async-start | bytes 8192 | tf_op jit(solution)/shard_map/all_to_all | solution.py:148
  86.4 5.0 %all-to-all-done.4 = f32[8,1,32]{2,1,0:T(1,128)S(1)} async-done(((f32[8,1,32]{2,1,0:T(1,128)}), f32[8,1,32]{2,1,0:T(1,128)S(1)}, u32[]{:S(2)}, u32[]{:S(2)}) %all-to-all-start.4) | async-done | bytes 1056 | tf_op jit(solution)/shard_map/all_to_all | solution.py:148
  92.6 3.3 all-to-all-start.6
  96.7 4.4 %all-to-all-done.6 = f32[8,1,32]{2,1,0:T(1,128)S(1)} async-done(((f32[8,1,32]{2,1,0:T(1,128)}), f32[8,1,32]{2,1,0:T(1,128)S(1)}, u32[]{:S(2)}, u32[]{:S(2)}) %all-to-all-start.6) | async-done | bytes 1056 | tf_op jit(solution)/shard_map/all_to_all | solution.py:151
  102.6 3.0 collective-permute-start.5
  105.5 1.5 collective-permute-start.4
  107.6 2.8 scatter_custom_fusion
  112.0 1.5 fusion.37
  115.1 64.9 %all-reduce.77 = (f32[]{:T(128)}, f32[]{:T(128)}) all-reduce(f32[]{:T(128)} %get-tuple-element.8, f32[]{:T(128)} %get-tuple-element.7), channel_id=1, replica_groups=mesh['gx'=8,'gy'=16] {'gx','gy'}, use_global_device_ids=true, to_apply=%region_2.4 | all-reduce | flops 2 | bytes 16 | tf_op jit(solution)/shard_map/psum | solution.py:100
  182.2 11.8 %all_to_all.122 = f32[2,16,8,128]{3,2,0,1:T(8,128)S(1)} all-to-all(f32[2,16,8,128]{3,2,0,1:T(8,128)S(1)} %copy.1263), channel_id=1, replica_groups=mesh['gx'=8,'gy'=16] {'gy'}, dimensions={1} | all-to-all | bytes 262144 | tf_op jit(solution)/shard_map/all_to_all | solution.py:169
  198.0 11.2 %all_to_all.123 = f32[2,1,128,128]{3,0,1,2:T(2,128)S(1)} all-to-all(f32[2,1,128,128]{3,0,1,2:T(2,128)S(1)} %copy.1281), channel_id=1, replica_groups=mesh['gx'=8,'gy'=16] {'gy'}, dimensions={2} | all-to-all | bytes 262144 | tf_op jit(solution)/shard_map/all_to_all | solution.py:171
  209.4 2.0 gather_fusion.1
  212.7 3.3 all-to-all-start.9
  217.4 3.0 collective-permute-start.7
  222.5 4.9 %all-to-all-start.10 = ((f32[8,1,32]{2,1,0:T(1,128)}), f32[8,1,32]{2,1,0:T(1,128)S(1)}, u32[]{:S(2)}, u32[]{:S(2)}) async-start(f32[8,1,32]{2,1,0:T(1,128)} %convolution_bitcast_fusion), calls=%async_computation.10 | async-start | bytes 8192 | tf_op jit(solution)/shard_map/all_to_all | solution.py:151
  227.6 5.1 %all-to-all-done.10 = f32[8,1,32]{2,1,0:T(1,128)S(1)} async-done(((f32[8,1,32]{2,1,0:T(1,128)}), f32[8,1,32]{2,1,0:T(1,128)S(1)}, u32[]{:S(2)}, u32[]{:S(2)}) %all-to-all-start.10) | async-done | bytes 1056 | tf_op jit(solution)/shard_map/all_to_all | solution.py:151
  233.5 2.5 collective-permute-start.9
  237.4 2.1 scatter_custom_fusion.1
  239.5 2.2 collective-permute-done.8
  244.9 64.9 %psum.37 = f32[]{:T(128)} all-reduce(f32[]{:T(128)} %multiply_reduce_fusion.2), channel_id=1, replica_groups=mesh['gx'=8,'gy'=16] {'gx','gy'}, use_global_device_ids=true, to_apply=%region_7.9 | all-reduce | flops 1 | bytes 8 | tf_op jit(solution)/shard_map/psum | solution.py:181
  311.8 64.6 %all-reduce.76 = (f32[]{:T(128)}, f32[]{:T(128)}) all-reduce(f32[]{:T(128)} %get-tuple-element.6, f32[]{:T(128)} %get-tuple-element.5), channel_id=1, replica_groups=mesh['gx'=8,'gy'=16] {'gx','gy'}, use_global_device_ids=true, to_apply=%region_9.11 | all-reduce | flops 2 | bytes 16 | tf_op jit(solution)/shard_map/psum | solution.py:100
  (497 shorter events, 49.3 us)
Async XLA Ops:
  2.2 8.3 %copy-start.17 = (f32[2,16,8,128]{3,2,1,0:T(8,128)S(1)}, f32[2,16,8,128]{3,2,1,0:T(8,128)}, u32[]{:S(2)}) copy-start(f32[2,16,8,128]{3,2,1,0:T(8,128)} %param.14) | copy-start | bytes 393220
  2.2 18.3 %all-to-all-start.1 = ((f32[2,16,8,128]{3,2,0,1:T(8,128)}), f32[2,16,8,128]{3,2,0,1:T(8,128)S(1)}, u32[]{:S(2)}, u32[]{:S(2)}) async-start(f32[2,16,8,128]{3,2,0,1:T(8,128)} %copy.1235), calls=%async_computation.1 | async-start | bytes 262144 | tf_op jit(solution)/shard_map/all_to_all | solution.py:169
  10.6 6.8 %collective-permute-start = (f32[2,1,8,128]{3,2,1,0:T(8,128)S(1)}, f32[2,1,8,128]{3,2,1,0:T(8,128)S(1)}, u32[]{:S(2)}, u32[]{:S(2)}) collective-permute-start(f32[2,1,8,128]{3,2,1,0:T(8,128)S(1)} %slice.1470), channel_id=1, source_target_pairs={{0,16},{16,32},{32,48},{48,64},{64,80},{80,96},{96,112},{1,17},{17... | collective-permute-start | bytes 24584 | tf_op jit(solution)/shard_map/ppermute | solution.py:12
  12.1 7.5 %copy-start.41 = (f32[8]{0:T(128)}, f32[8]{0:T(128)S(1)}, u32[]{:S(2)}) copy-start(f32[8]{0:T(128)S(1)} %compare_convert_fusion.1) | copy-start | bytes 100
  12.3 5.1 %collective-permute-start.1 = (f32[2,16,1,128]{3,2,1,0:T(1,128)S(1)}, f32[2,16,1,128]{3,2,1,0:T(1,128)S(1)}, u32[]{:S(2)}, u32[]{:S(2)}) collective-permute-start(f32[2,16,1,128]{3,2,1,0:T(1,128)S(1)} %slice.1472), channel_id=1, source_target_pairs={{0,1},{1,2},{2,3},{3,4},{4,5},{5,6},{6,7},{7,8},{8,9},{9,10},{10,1... | collective-permute-start | bytes 49160 | tf_op jit(solution)/shard_map/ppermute | solution.py:12
  20.5 18.1 %all-to-all-start = ((f32[6,16,8,128]{3,2,0,1:T(8,128)}), f32[6,16,8,128]{3,2,0,1:T(8,128)S(1)}, u32[]{:S(2)}, u32[]{:S(2)}) async-start(f32[6,16,8,128]{3,2,0,1:T(8,128)} %copy.965), calls=%async_computation | async-start | bytes 786432 | tf_op jit(solution)/shard_map/all_to_all | solution.py:168
  50.5 11.5 %all-to-all-start.2 = ((f32[2,1,128,128]{3,0,1,2:T(2,128)}), f32[2,1,128,128]{3,0,1,2:T(2,128)S(1)}, u32[]{:S(2)}, u32[]{:S(2)}) async-start(f32[2,1,128,128]{3,0,1,2:T(2,128)} %copy.1261), calls=%async_computation.2 | async-start | bytes 262144 | tf_op jit(solution)/shard_map/all_to_all | solution.py:171
  56.3 10.8 %copy-start.46 = (s32[1024]{0:T(1024)}, s32[1024]{0:T(1024)S(1)}, u32[]{:S(2)}) copy-start(s32[1024]{0:T(1024)S(1)} %pad_clamp_fusion) | copy-start | bytes 12292
  62.0 9.6 %all-to-all-start.3 = ((s32[8,1,32]{2,1,0:T(1,128)}), s32[8,1,32]{2,1,0:T(1,128)S(1)}, u32[]{:S(2)}, u32[]{:S(2)}) async-start(s32[8,1,32]{2,1,0:T(1,128)} %bitcast.662), calls=%async_computation.3 | async-start | bytes 8192 | tf_op jit(solution)/shard_map/all_to_all | solution.py:141
  71.6 20.0 %copy-start.54 = (s32[8,1,32]{2,1,0:T(1,128)}, s32[8,1,32]{2,1,0:T(1,128)S(1)}, u32[]{:S(2)}) copy-start(s32[8,1,32]{2,1,0:T(1,128)S(1)} %all-to-all-done.3) | copy-start | bytes 3076
  71.6 9.7 %all-to-all-start.5 = ((f32[8,1,32]{2,1,0:T(1,128)}), f32[8,1,32]{2,1,0:T(1,128)S(1)}, u32[]{:S(2)}, u32[]{:S(2)}) async-start(f32[8,1,32]{2,1,0:T(1,128)} %get-tuple-element.15), calls=%async_computation.5 | async-start | bytes 8192 | tf_op jit(solution)/shard_map/all_to_all | solution.py:142
  76.0 26.5 %collective-permute-start.2 = (f32[2,1,8,128]{3,2,1,0:T(8,128)S(1)}, f32[2,1,8,128]{3,2,1,0:T(8,128)S(1)}, u32[]{:S(2)}, u32[]{:S(2)}) collective-permute-start(f32[2,1,8,128]{3,2,1,0:T(8,128)S(1)} %get-tuple-element.354), channel_id=1, source_target_pairs={{16,0},{32,16},{48,32},{64,48},{80,64},{96,80},{112,96},{17,1},{33... | collective-permute-start | bytes 24584 | tf_op jit(solution)/shard_map/ppermute | solution.py:23
  77.3 25.2 %collective-permute-start.3 = (f32[2,1,8,128]{3,2,1,0:T(8,128)S(1)}, f32[2,1,8,128]{3,2,1,0:T(8,128)S(1)}, u32[]{:S(2)}, u32[]{:S(2)}) collective-permute-start(f32[2,1,8,128]{3,2,1,0:T(8,128)S(1)} %get-tuple-element.353), channel_id=1, source_target_pairs={{0,16},{16,32},{32,48},{48,64},{64,80},{80,96},{96,112},{1,17},{17... | collective-permute-start | bytes 24584 | tf_op jit(solution)/shard_map/ppermute | solution.py:22
  81.3 10.1 %all-to-all-start.4 = ((f32[8,1,32]{2,1,0:T(1,128)}), f32[8,1,32]{2,1,0:T(1,128)S(1)}, u32[]{:S(2)}, u32[]{:S(2)}) async-start(f32[8,1,32]{2,1,0:T(1,128)} %get-tuple-element.14), calls=%async_computation.4 | async-start | bytes 8192 | tf_op jit(solution)/shard_map/all_to_all | solution.py:148
  92.6 8.5 %all-to-all-start.6 = ((f32[8,1,32]{2,1,0:T(1,128)}), f32[8,1,32]{2,1,0:T(1,128)S(1)}, u32[]{:S(2)}, u32[]{:S(2)}) async-start(f32[8,1,32]{2,1,0:T(1,128)} %convolution_bitcast_fusion.1), calls=%async_computation.6 | async-start | bytes 8192 | tf_op jit(solution)/shard_map/all_to_all | solution.py:151
  102.6 7.8 %collective-permute-start.5 = (f32[2,18,1,128]{3,2,1,0:T(1,128)S(1)}, f32[2,18,1,128]{3,2,1,0:T(1,128)}, u32[]{:S(2)}, u32[]{:S(2)}) collective-permute-start(f32[2,18,1,128]{3,2,1,0:T(1,128)S(1)} %get-tuple-element.330), channel_id=1, source_target_pairs={{0,1},{1,2},{2,3},{3,4},{4,5},{5,6},{6,7},{7,8},{8,9},{9,10},{10,1... | collective-permute-start | bytes 55304 | tf_op jit(solution)/shard_map/ppermute | solution.py:22
  105.5 5.7 %collective-permute-start.4 = (f32[2,18,1,128]{3,2,1,0:T(1,128)S(1)}, f32[2,18,1,128]{3,2,1,0:T(1,128)}, u32[]{:S(2)}, u32[]{:S(2)}) collective-permute-start(f32[2,18,1,128]{3,2,1,0:T(1,128)S(1)} %get-tuple-element.329), channel_id=1, source_target_pairs={{1,0},{2,1},{3,2},{4,3},{5,4},{6,5},{7,6},{8,7},{9,8},{10,9},{11,1... | collective-permute-start | bytes 55304 | tf_op jit(solution)/shard_map/ppermute | solution.py:23
  113.6 67.7 %copy-start.9 = (f32[1,16,8,128]{3,2,1,0:T(8,128)}, f32[1,16,8,128]{3,2,1,0:T(8,128)S(1)}, u32[]{:S(2)}) copy-start(f32[1,16,8,128]{3,2,1,0:T(8,128)S(1)} %get-tuple-element.20) | copy-start | bytes 196612
  209.4 32.4 %copy-start.35 = (f32[2,1,8,128]{3,2,1,0:T(8,128)S(1)}, f32[2,1,8,128]{3,2,1,0:T(8,128)}, u32[]{:S(2)}) copy-start(f32[2,1,8,128]{3,2,1,0:T(8,128)} %copy-done.33) | copy-start | bytes 24580
  212.7 8.5 %all-to-all-start.9 = ((f32[8,1,32]{2,1,0:T(1,128)}), f32[8,1,32]{2,1,0:T(1,128)S(1)}, u32[]{:S(2)}, u32[]{:S(2)}) async-start(f32[8,1,32]{2,1,0:T(1,128)} %mul.5825), calls=%async_computation.9 | async-start | bytes 8192 | tf_op jit(solution)/shard_map/all_to_all | solution.py:148
  216.1 17.4 %collective-permute-start.6 = (f32[2,1,8,128]{3,2,1,0:T(8,128)S(1)}, f32[2,1,8,128]{3,2,1,0:T(8,128)S(1)}, u32[]{:S(2)}, u32[]{:S(2)}) collective-permute-start(f32[2,1,8,128]{3,2,1,0:T(8,128)S(1)} %get-tuple-element.336), channel_id=1, source_target_pairs={{16,0},{32,16},{48,32},{64,48},{80,64},{96,80},{112,96},{17,1},{33... | collective-permute-start | bytes 24584 | tf_op jit(solution)/shard_map/ppermute | solution.py:23
  217.4 16.1 %collective-permute-start.7 = (f32[2,1,8,128]{3,2,1,0:T(8,128)S(1)}, f32[2,1,8,128]{3,2,1,0:T(8,128)S(1)}, u32[]{:S(2)}, u32[]{:S(2)}) collective-permute-start(f32[2,1,8,128]{3,2,1,0:T(8,128)S(1)} %get-tuple-element.335), channel_id=1, source_target_pairs={{0,16},{16,32},{32,48},{48,64},{64,80},{80,96},{96,112},{1,17},{17... | collective-permute-start | bytes 24584 | tf_op jit(solution)/shard_map/ppermute | solution.py:22
  222.5 10.2 %all-to-all-start.10 = ((f32[8,1,32]{2,1,0:T(1,128)}), f32[8,1,32]{2,1,0:T(1,128)S(1)}, u32[]{:S(2)}, u32[]{:S(2)}) async-start(f32[8,1,32]{2,1,0:T(1,128)} %convolution_bitcast_fusion), calls=%async_computation.10 | async-start | bytes 8192 | tf_op jit(solution)/shard_map/all_to_all | solution.py:151
  227.4 9.9 %copy-start.45 = (f32[256]{0:T(256)S(1)}, f32[256]{0:T(256)}, u32[]{:S(2)}) copy-start(f32[256]{0:T(256)} %reshape.13476) | copy-start | bytes 3076
  227.4 9.9 %copy-start.58 = (pred[256]{0:T(512)(128)(4,1)S(1)}, pred[256]{0:T(512)(128)(4,1)}, u32[]{:S(2)}) copy-start(pred[256]{0:T(512)(128)(4,1)} %lt.91) | copy-start | bytes 772
  227.5 14.3 %copy-start.18 = (f32[2,16,8,128]{3,2,1,0:T(8,128)S(1)}, f32[2,16,8,128]{3,2,1,0:T(8,128)}, u32[]{:S(2)}) copy-start(f32[2,16,8,128]{3,2,1,0:T(8,128)} %param.14) | copy-start | bytes 393220
  227.5 14.3 %copy-start.20 = (f32[2,16,8,128]{3,2,1,0:T(8,128)S(1)}, f32[2,16,8,128]{3,2,1,0:T(8,128)}, u32[]{:S(2)}) copy-start(f32[2,16,8,128]{3,2,1,0:T(8,128)} %copy-done.19) | copy-start | bytes 393220
  227.5 14.3 %copy-start.27 = (f32[2,15,8,128]{3,2,1,0:T(8,128)S(1)}, f32[2,15,8,128]{3,2,1,0:T(8,128)}, u32[]{:S(2)}) copy-start(f32[2,15,8,128]{3,2,1,0:T(8,128)} %copy-done.26) | copy-start | bytes 368644
  233.4 8.4 %copy-start.16 = (f32[2,16,8,128]{3,2,1,0:T(8,128)S(1)}, f32[2,16,8,128]{3,2,1,0:T(8,128)}, u32[]{:S(2)}) copy-start(f32[2,16,8,128]{3,2,1,0:T(8,128)} %param.16) | copy-start | bytes 393220
  233.5 8.3 %copy-start.14 = (f32[2,16,8,128]{3,2,1,0:T(8,128)S(1)}, f32[2,16,8,128]{3,2,1,0:T(8,128)}, u32[]{:S(2)}) copy-start(f32[2,16,8,128]{3,2,1,0:T(8,128)} %copy-done.13) | copy-start | bytes 393220
  233.5 6.0 %collective-permute-start.9 = (f32[2,18,1,128]{3,2,1,0:T(1,128)S(1)}, f32[2,18,1,128]{3,2,1,0:T(1,128)S(1)}, u32[]{:S(2)}, u32[]{:S(2)}) collective-permute-start(f32[2,18,1,128]{3,2,1,0:T(1,128)S(1)} %get-tuple-element.328), channel_id=1, source_target_pairs={{0,1},{1,2},{2,3},{3,4},{4,5},{5,6},{6,7},{7,8},{8,9},{9,10},{10,1... | collective-permute-start | bytes 55304 | tf_op jit(solution)/shard_map/ppermute | solution.py:22
  236.0 5.7 %collective-permute-start.8 = (f32[2,18,1,128]{3,2,1,0:T(1,128)S(1)}, f32[2,18,1,128]{3,2,1,0:T(1,128)S(1)}, u32[]{:S(2)}, u32[]{:S(2)}) collective-permute-start(f32[2,18,1,128]{3,2,1,0:T(1,128)S(1)} %get-tuple-element.327), channel_id=1, source_target_pairs={{1,0},{2,1},{3,2},{4,3},{5,4},{6,5},{7,6},{8,7},{9,8},{10,9},{11,1... | collective-permute-start | bytes 55304 | tf_op jit(solution)/shard_map/ppermute | solution.py:23
  (50 other events, 91.6 us)
where the time goes:
time: 381 us; the launch traced here: 379 us
  blocking collectives  217 us (57%)
  starting transfers between devices  66.1 us (17%)
  waiting for transfers between devices  35.8 us (9%)
  other arithmetic  25.5 us (7%)
  local copies, waits for them, and re-layouts  24.4 us (6%)
  between operations  7.29 us (2%)
    psum x2, blocking collectives, pair_sums(): lax.psum((jnp.sum(resid * image), jnp.sum(image * image)), ('gx', 'gy'))  130 us
    psum x1, blocking collectives, body(): beta = lax.psum(jnp.sum(q_two * q_one), ('gx', 'gy')) / qq_one  64.9 us
    unnamed x130, local copies, waits for them, and re-layouts  13.4 us
    all_to_all x1, blocking collectives, precondition(): lax.all_to_all(vector, 'gy', split_axis=1, concat_axis=2, tiled=True)  11.8 us
    ppermute x4, starting transfers between devices, extended(): before = lax.ppermute(last, axis, up)  11.6 us
    all_to_all x1, blocking collectives, precondition(): return lax.all_to_all(solved, 'gy', split_axis=2, concat_axis=1, tiled=True)  11.2 us
    all_to_all x1, waiting for transfers between devices, precondition(): lax.all_to_all(coefs, 'gy', split_axis=1, concat_axis=2, tiled=True)  10.4 us
    all_to_all x2, waiting for transfers between devices, well_add(): lax.all_to_all(owner_rates, 'gx', split_axis=0, concat_axis=0, tiled=True)  9.54 us
  transfers between devices with their start and end apart: 19, of which 10 were waited for; matrix products, arithmetic and copies ran while one was open for 5% of the time, Pallas kernels for 0%

commit v1 on v0

v1 whole, which is shorter than its diff:
```python
import jax
import jax.numpy as jnp
from jax import lax
from jax.experimental import pallas as pl
from jax.experimental.pallas import tpu as pltpu
from jax.sharding import PartitionSpec as P

F32 = jnp.float32
BF16 = jnp.bfloat16
VMEM = pl.BlockSpec(memory_space=pltpu.VMEM)
SMEM = pl.BlockSpec(memory_space=pltpu.SMEM)
CX, CY, NZ = 16, 8, 128
PLANE = (CX, NZ)
N_GX, N_GY = 8, 16
W_ALL = 128
SLOTS_ALL = 256


def mm(p, q):
    return (
        p[0] * q[0] + p[1] * q[2],
        p[0] * q[1] + p[1] * q[3],
        p[2] * q[0] + p[3] * q[2],
        p[2] * q[1] + p[3] * q[3],
    )


def mv(p, v):
    return (p[0] * v[0] + p[1] * v[1], p[2] * v[0] + p[3] * v[1])


def madd(p, q):
    return tuple(a + b for a, b in zip(p, q))


def inv2(p):
    t = 1.0 / (p[0] * p[3] - p[1] * p[2])
    return (p[3] * t, -p[1] * t, -p[2] * t, p[0] * t)


def one_minus(p):
    return (1.0 - p[0], -p[1], -p[2], 1.0 - p[3])


def rows_by(t, p):
    return (t[0] * p[0], t[0] * p[1], t[1] * p[2], t[1] * p[3])


def columns_by(p, t):
    return (p[0] * t[0], p[1] * t[1], p[2] * t[0], p[3] * t[1])


def join(a, b):
    ff1, fl1, lf1, ll1, gf1, gl1 = a
    ff2, fl2, lf2, ll2, gf2, gl2 = b
    k = inv2(one_minus(mm(ll1, ff2)))
    last = mv(k, madd(gl1, mv(ll1, gf2)))
    last_b = mm(k, lf1)
    last_a = mm(k, mm(ll1, fl2))
    first = madd(gf2, mv(ff2, last))
    first_b = mm(ff2, last_b)
    first_a = madd(fl2, mm(ff2, last_a))
    return (
        madd(ff1, mm(fl1, first_b)),
        mm(fl1, first_a),
        mm(lf2, last_b),
        madd(ll2, mm(lf2, last_a)),
        madd(gf1, mv(fl1, first)),
        madd(gl2, mv(lf2, last)),
    )


def join_before(before, s):
    gm, g = before
    ff, fl, lf, ll, gf, gl = s
    k = inv2(one_minus(mm(ff, gm)))
    a = mv(k, madd(gf, mv(ff, g)))
    am = mm(k, fl)
    return (madd(ll, mm(lf, mm(gm, am))), madd(gl, mv(lf, madd(g, mv(gm, a)))))


def join_after(s, after):
    gm, g = after
    ff, fl, lf, ll, gf, gl = s
    k = inv2(one_minus(mm(ll, gm)))
    a = mv(k, madd(gl, mv(ll, g)))
    am = mm(k, lf)
    return (madd(ff, mm(fl, mm(gm, am))), madd(gf, mv(fl, madd(g, mv(gm, a)))))


def choose(flag, new, old):
    return tuple(tuple(jnp.where(flag, n, o) for n, o in zip(ns, os)) for ns, os in zip(new, old))


def load_segment(mat, vec, offset):
    m = [mat[i] for i in range(16)]
    v = [vec[offset + i] for i in range(4)]
    return (tuple(m[0:4]), tuple(m[4:8]), tuple(m[8:12]), tuple(m[12:16]), (v[0], v[1]), (v[2], v[3]))


def store_segment(ref, seg, whole):
    flat = [x for part in seg for x in part]
    if not whole:
        flat = flat[16:]
    for i, x in enumerate(flat):
        ref[i] = x


def lanes():
    return lax.broadcasted_iota(jnp.int32, PLANE, 1)


def rows():
    return lax.broadcasted_iota(jnp.int32, PLANE, 0)


def from_row_before(plane, edge):
    return jnp.where(rows() == 0, edge, pltpu.roll(plane, 1, 0))


def from_row_after(plane, edge):
    return jnp.where(rows() == CX - 1, edge, pltpu.roll(plane, CX - 1, 0))


def sweep_forward(sinv, tau, rhs):
    y = [rhs[0]]
    for j in range(1, CY):
        t = mv(sinv(j - 1), y[-1])
        y.append((rhs[j][0] + tau(j)[0] * t[0], rhs[j][1] + tau(j)[1] * t[1]))
    return y


def sweep_backward(binv, tau, rhs):
    z = rhs[CY - 1]
    for j in range(CY - 2, -1, -1):
        t = mv(binv(j + 1), z)
        z = (rhs[j][0] + tau(j + 1)[0] * t[0], rhs[j][1] + tau(j + 1)[1] * t[1])
    return z


def block_at(ref, j):
    return tuple(ref[i, j] for i in range(4))


def pair_at(ref, j):
    return (ref[0, j], ref[1, j])


def condense_kernel(idx, b, acc, tx_in, ty_in, tz_in, lx_in, ly_in, brk, seg, dmat, tau_o, sinv, binv, rhs, tx_o, ty_o, tz_o):
    gx, gy = idx[0], idx[1]
    last_x = jnp.logical_and(rows() == CX - 1, gx == N_GX - 1)
    last_z = lanes() == NZ - 1

    def plane(ref, c, j):
        return ref.at[c][pl.ds(j, CX, stride=CY), :]

    for c in range(2):
        ty_o[c, 0] = ly_in[c]
        for j in range(CY):
            tx = jnp.where(last_x, 0.0, plane(tx_in, c, j))
            tz = jnp.where(last_z, 0.0, plane(tz_in, c, j))
            ty = plane(ty_in, c, j)
            if j == CY - 1:
                ty = jnp.where(gy == N_GY - 1, 0.0, ty)
            tx_o[c, j] = tx
            tz_o[c, j] = tz
            ty_o[c, j + 1] = ty
            lx = from_row_before(tx, lx_in[c, j : j + 1, :])
            faces = tx + lx + ty + ty_o[c, j] + tz + pltpu.roll(tz, 1, 1)
            dmat[3 * c, j] = plane(acc, 3 * c, j) + faces
            rhs[c, j] = plane(b, c, j)
        for j in range(CY + 1):
            keep = 1.0 - brk[:, j : j + 1].astype(F32)
            tau_o[c, j] = ty_o[c, j] * keep
    for j in range(CY):
        dmat[1, j] = plane(acc, 2, j)
        dmat[2, j] = plane(acc, 1, j)

    def tau(j):
        return pair_at(tau_o, j)

    def outer(t, p):
        return tuple(x * y for x, y in zip(p, (t[0] * t[0], t[0] * t[1], t[1] * t[0], t[1] * t[1])))

    s = inv2(block_at(dmat, 0))
    e = inv2(block_at(dmat, CY - 1))
    zero = jnp.zeros(PLANE, F32)
    yf = (tau(0)[0], zero, zero, tau(0)[1])
    zl = (tau(CY)[0], zero, zero, tau(CY)[1])
    y = pair_at(rhs, 0)
    z = pair_at(rhs, CY - 1)
    for i in range(4):
        sinv[i, 0] = s[i]
        binv[i, CY - 1] = e[i]
    for j in range(1, CY):
        k = CY - 1 - j
        t, u = tau(j), tau(k + 1)
        yf = rows_by(t, mm(s, yf))
        zl = rows_by(u, mm(e, zl))
        yv, zv = mv(s, y), mv(e, z)
        y = tuple(rhs[c, j] + t[c] * yv[c] for c in range(2))
        z = tuple(rhs[c, k] + u[c] * zv[c] for c in range(2))
        s = inv2(tuple(d - x for d, x in zip(block_at(dmat, j), outer(t, s))))
        e = inv2(tuple(d - x for d, x in zip(block_at(dmat, k), outer(u, e))))
        for i in range(4):
            sinv[i, j] = s[i]
            binv[i, k] = e[i]
    store_segment(
        seg,
        (columns_by(e, tau(0)), mm(e, zl), mm(s, yf), columns_by(s, tau(CY)), mv(e, z), mv(s, y)),
        True,
    )


def gather_segments(position, mats, vecs, offset, mat_s, vec_s):
    for k in range(4):
        at = jnp.bitwise_xor(position, k)
        mat_s[at] = mats[k][0:16]
        vec_s[at] = vecs[k][offset : offset + 4]


def make_total_kernel(whole):
    def kernel(*refs):
        idx = refs[0]
        if whole:
            mats = vecs = refs[1:5]
            out, mat_s, vec_s = refs[5:]
        else:
            mats, vecs = refs[1:5], refs[5:9]
            out, mat_s, vec_s = refs[9:]
        gather_segments(idx[1] % 4, mats, vecs, 16 if whole else 0, mat_s, vec_s)
        segs = [load_segment(mat_s.at[m], vec_s.at[m], 0) for m in range(4)]
        store_segment(out, join(join(segs[0], segs[1]), join(segs[2], segs[3])), whole)

    return kernel


def split3(x):
    hi = x.astype(BF16)
    rest = x - hi.astype(F32)
    mid = rest.astype(BF16)
    low = (rest - mid.astype(F32)).astype(BF16)
    return hi, mid, low


def slot_tables(cells, wells):
    cell = cells[...]
    row = jnp.bitwise_and(lax.shift_right_logical(cell, 7), 7) * CX + lax.shift_right_logical(cell, 10)
    shape = (NZ, SLOTS_ALL)
    up = lax.broadcasted_iota(jnp.int32, shape, 0)
    at_row = up == row
    at_layer = up == jnp.bitwise_and(cell, NZ - 1)
    at_well = up == wells[...]
    return at_row, at_layer, at_well


def ones_of(mask):
    return jnp.where(mask, 1.0, 0.0).astype(F32).astype(BF16)


NT = (((1,), (1,)), ((), ()))


def row_times(rows_in, table, dims):
    parts = [part for x in rows_in for part in split3(x)]
    n = len(rows_in)
    pad = 16 - 3 * n
    width = rows_in[0].shape[1]
    stacked = jnp.concatenate([p.astype(F32) for p in parts] + [jnp.zeros((pad, width), F32)], axis=0).astype(BF16)
    out = lax.dot_general(stacked, table, dims, preferred_element_type=F32)
    return [out[3 * i : 3 * i + 1] + out[3 * i + 1 : 3 * i + 2] + out[3 * i + 2 : 3 * i + 3] for i in range(n)]


def make_solve_kernel(whole):
    def kernel(*refs):
        idx = refs[0]
        if whole:
            inner, outer_ = refs[1:5], refs[5:9]
            inner_v, outer_v = inner, outer_
            rest = refs[9:]
            offset = 16
        else:
            inner, outer_, inner_v, outer_v = refs[1:5], refs[5:9], refs[9:13], refs[13:17]
            rest = refs[17:]
            offset = 0
        sinv, tau_r, rhs, cells, wells, weights = rest[:6]
        p_out, ends, msg = rest[6:9]
        mat_i, vec_i, mat_o, vec_o, edge = rest[9:]
        gx, gy = idx[0], idx[1]
        z_at, y_at = gy % 4, gy // 4
        gather_segments(z_at, inner, inner_v, offset, mat_i, vec_i)
        gather_segments(y_at, outer_, outer_v, offset, mat_o, vec_o)
        zero = jnp.zeros(PLANE, F32)
        before = ((zero,) * 4, (zero,) * 2)
        after = ((zero,) * 4, (zero,) * 2)
        for mat_s, vec_s, here in ((mat_o, vec_o, y_at), (mat_i, vec_i, z_at)):
            for m in range(3):
                seg = load_segment(mat_s.at[m], vec_s.at[m], 0)
                before = choose(m < here, join_before(before, seg), before)
                m = 3 - m
                seg = load_segment(mat_s.at[m], vec_s.at[m], 0)
                after = choose(m > here, join_after(seg, after), after)
        own = load_segment(inner[0], inner_v[0], offset)
        ff, fl, lf, ll, gf, gl = own
        up_m, up_v = join_before(before, own)
        last = mv(inv2(one_minus(mm(up_m, after[0]))), madd(up_v, mv(up_m, after[1])))
        beyond = madd(after[1], mv(after[0], last))
        k = inv2(one_minus(mm(ff, before[0])))
        first = mv(k, madd(madd(gf, mv(ff, before[1])), mv(fl, beyond)))
        behind = madd(before[1], mv(before[0], first))
        for c in range(2):
            ends[c] = behind[c]
            ends[2 + c] = beyond[c]

        def tau(j):
            return pair_at(tau_r, j)

        def sv(j):
            return block_at(sinv, j)

        r = [pair_at(rhs, j) for j in range(CY)]
        r[0] = tuple(r[0][c] + tau(0)[c] * behind[c] for c in range(2))
        y = sweep_forward(sv, tau, r)
        u = beyond
        for j in range(CY - 1, -1, -1):
            u = mv(sv(j), tuple(y[j][c] + tau(j + 1)[c] * u[c] for c in range(2)))
            for c in range(2):
                p_out[c, j] = u[c]
                edge[0, c * CY + j : c * CY + j + 1, :] = u[c][0:1, :]
                edge[1, c * CY + j : c * CY + j + 1, :] = u[c][CX - 1 : CX, :]
        at_row, at_layer, at_well = slot_tables(cells, wells)
        pressure = jnp.concatenate([p_out[0, j] for j in range(CY)], axis=0)
        table = ones_of(at_layer)
        picked = sum(jnp.dot(part, table, preferred_element_type=F32) for part in split3(pressure))
        values = jnp.sum(jnp.where(at_row, picked, 0.0), axis=0, keepdims=True)
        w = weights[...]
        sums, totals = row_times([w * values, w], ones_of(at_well), NT)
        tail = jnp.concatenate([sums, totals, jnp.zeros((6, W_ALL), F32)], axis=0)
        for d in range(N_GX):
            msg[d, 0:16, :] = jnp.zeros((16, NZ), F32)
            msg[d, 16:24, :] = tail

        @pl.when(gx < N_GX - 1)
        def _():
            msg[gx + 1, 0:16, :] = edge[1]

        @pl.when(gx > 0)
        def _():
            msg[gx - 1, 0:16, :] = edge[0]

    return kernel


def apply_operator(idx, got, p, ends, dmat, tx, ty, tz, cells, wells, weights):
    gx = idx[0]
    tail = got[0, 16:24, :]
    for d in range(1, N_GX):
        tail = tail + got[d, 16:24, :]
    rates = tail[0:1] / jnp.maximum(tail[1:2], 1.0)
    at_row, at_layer, at_well = slot_tables(cells, wells)
    slot_rate = row_times([rates], ones_of(at_well), (((1,), (0,)), ((), ())))[0]
    added = jnp.where(at_layer, weights[...] * slot_rate, 0.0)
    table = ones_of(at_row)
    well_add = sum(lax.dot_general(table, part, NT, preferred_element_type=F32) for part in split3(added))
    from_after = jnp.where(gx < N_GX - 1, got[jnp.minimum(gx + 1, N_GX - 1), 0:16, :], 0.0)
    from_before = jnp.where(gx > 0, got[jnp.maximum(gx - 1, 0), 0:16, :], 0.0)
    return well_add, from_after, from_before


def operator_plane(c, j, p, ends, dmat, tx, ty, tz, lx_in, halo, well_add):
    from_after, from_before = halo
    here = p[c, j]
    up = p[c, j + 1] if j < CY - 1 else ends[2 + c]
    down = p[c, j - 1] if j > 0 else ends[c]
    t = tx[c, j]
    at = c * CY + j
    beside = t * from_row_after(here, from_after[at : at + 1])
    beside = beside + from_row_before(t * here, lx_in[c, j : j + 1, :] * from_before[at : at + 1])
    beside = beside + ty[c, j + 1] * up + ty[c, j] * down
    tzp = tz[c, j]
    beside = beside + tzp * pltpu.roll(here, NZ - 1, 1) + pltpu.roll(tzp * here, 1, 1)
    out = dmat[2 * c, j] * p[0, j] + dmat[2 * c + 1, j] * p[1, j] - beside
    if c == 0:
        out = out + well_add[j * CX : (j + 1) * CX]
    return out


def first_image_kernel(idx, got, p, ends, dmat, tau_r, sinv, binv, rhs, tx, ty, tz, lx_in, cells, wells, weights, q_out, e_out, vec_out, dots):
    well_add, after, before = apply_operator(idx, got, p, ends, dmat, tx, ty, tz, cells, wells, weights)
    eq = jnp.zeros(PLANE, F32)
    qq = jnp.zeros(PLANE, F32)
    e = []
    for j in range(CY):
        pair = []
        for c in range(2):
            q = operator_plane(c, j, p, ends, dmat, tx, ty, tz, lx_in, (after, before), well_add)
            rest = rhs[c, j] - q
            q_out[c, j] = q
            e_out[c, j] = rest
            eq = eq + rest * q
            qq = qq + q * q
            pair.append(rest)
        e.append(tuple(pair))
    dots[0] = eq
    dots[1] = qq

    def tau(j):
        return pair_at(tau_r, j)

    y = sweep_forward(lambda j: block_at(sinv, j), tau, e)[CY - 1]
    z = sweep_backward(lambda j: block_at(binv, j), tau, e)
    first = mv(block_at(binv, 0), z)
    last = mv(block_at(sinv, CY - 1), y)
    for c in range(2):
        vec_out[c] = first[c]
        vec_out[2 + c] = last[c]


def second_image_kernel(idx, got, p, ends, dmat, tx, ty, tz, lx_in, cells, wells, weights, q_in, e_in, dots_in, s_out, dots):
    well_add, after, before = apply_operator(idx, got, p, ends, dmat, tx, ty, tz, cells, wells, weights)
    sq = jnp.zeros(PLANE, F32)
    ss = jnp.zeros(PLANE, F32)
    es = jnp.zeros(PLANE, F32)
    for j in range(CY):
        for c in range(2):
            s = operator_plane(c, j, p, ends, dmat, tx, ty, tz, lx_in, (after, before), well_add)
            s_out[c, j] = s
            sq = sq + s * q_in[c, j]
            ss = ss + s * s
            es = es + s * e_in[c, j]
    sums = [jnp.sum(x, axis=0, keepdims=True) for x in (dots_in[0], dots_in[1], sq, ss, es)]
    block = jnp.concatenate(sums + [jnp.zeros((3, NZ), F32)], axis=0)
    for d in range(N_GX):
        dots[d] = block


def finish_kernel(got, p, w, q, e, s, x_out, r_out):
    total = got[0]
    for d in range(1, N_GY):
        total = total + got[d]
    total = jnp.broadcast_to(jnp.sum(total, axis=1, keepdims=True), (8, NZ))
    eq, qq, sq, ss, es = (total[i : i + 1] for i in range(5))
    rest = -eq / qq
    g = sq / qq
    k = (es - g * eq) / (ss - g * sq)
    on_p = (1.0 - rest) - k * g
    on_q = rest + k * g
    for c in range(2):
        for j in range(CY):
            at = pl.ds(j, CX, stride=CY)
            x_out.at[c][at, :] = on_p * p[c, j] + k * w[c, j]
            r_out.at[c][at, :] = e[c, j] + on_q * q[c, j] - k * s[c, j]


def call(kernel, name, outs, scratch, *args, smem=1):
    return pl.pallas_call(
        kernel,
        name=name,
        out_shape=tuple(jax.ShapeDtypeStruct(o, F32) for o in outs),
        in_specs=[SMEM] * smem + [VMEM] * (len(args) - smem),
        out_specs=tuple(VMEM for _ in outs),
        scratch_shapes=[pltpu.VMEM(s, F32) for s in scratch],
        compiler_params=pltpu.CompilerParams(vmem_limit_bytes=24 * 1024 * 1024),
    )(*args)


def swapped(block, stride):
    return [block] + [lax.ppermute(block, "gy", [(i, i ^ (k * stride)) for i in range(N_GY)]) for k in (1, 2, 3)]


def body(right_side, accumulation, trans_x, trans_y, trans_z, perf_cell, perf_well, perf_weight, perf_count, breaks):
    gx, gy = lax.axis_index("gx"), lax.axis_index("gy")
    idx = jnp.stack([gx, gy]).astype(jnp.int32)
    cuts = breaks.reshape(N_GY, CY)
    beyond = jnp.concatenate([cuts[1:, :1], jnp.zeros((1, 1), cuts.dtype)], axis=0)
    cuts = jnp.concatenate([cuts, beyond], axis=1)
    cuts = lax.all_to_all(cuts, "gy", split_axis=0, concat_axis=0, tiled=True)
    lx = lax.ppermute(trans_x[:, -1], "gx", [(i, i + 1) for i in range(N_GX - 1)])
    ly = lax.ppermute(trans_y[:, :, -1], "gy", [(i, i + 1) for i in range(N_GY - 1)])
    slots = perf_cell.shape[3]
    live = jnp.arange(slots, dtype=jnp.int32)[None, :] < perf_count.reshape(N_GX, 1)
    weights = jnp.where(live, perf_weight.reshape(N_GX, slots), 0.0).reshape(1, SLOTS_ALL)
    owners = jnp.arange(N_GX, dtype=jnp.int32)[:, None] * 16
    wells = (perf_well.reshape(N_GX, slots) + owners).reshape(1, SLOTS_ALL)
    cells = perf_cell.reshape(1, SLOTS_ALL)

    def flat(a):
        return a.reshape(a.shape[0], CX * CY, NZ)

    field, block, part = (2, CY, CX, NZ), (4, CY, CX, NZ), (2, CY + 1, CX, NZ)
    seg, vec = (20, CX, NZ), (4, CX, NZ)
    message = (N_GX, 24, NZ)
    order = [(4, 16, CX, NZ), (4, 4, CX, NZ)]
    own, dmat, tau, sinv, binv, rhs, tx, ty, tz = call(
        condense_kernel, "condense",
        (seg, block, part, block, block, field, field, part, field), [],
        idx, flat(right_side), flat(accumulation), flat(trans_x), flat(trans_y), flat(trans_z), lx, ly, cuts,
    )
    perfs = (cells, wells, weights)
    inner = swapped(own, 1)
    (group,) = call(make_total_kernel(True), "group_total", (seg,), order, idx, *inner)
    outer = swapped(group, 4)
    solve_scratch = order + order + [(2, 16, NZ)]
    p, ends, msg = call(
        make_solve_kernel(True), "solve_first", (field, vec, message), solve_scratch,
        idx, *inner, *outer, sinv, tau, rhs, *perfs,
    )
    got = lax.all_to_all(msg, "gx", split_axis=0, concat_axis=0, tiled=True)
    q, e, own_v, dots = call(
        first_image_kernel, "first_image", (field, field, vec, (2, CX, NZ)), [],
        idx, got, p, ends, dmat, tau, sinv, binv, rhs, tx, ty, tz, lx, *perfs,
    )
    inner_v = swapped(own_v, 1)
    (group_v,) = call(make_total_kernel(False), "group_total_again", (vec,), order, idx, *inner, *inner_v)
    outer_v = swapped(group_v, 4)
    w, ends, msg = call(
        make_solve_kernel(False), "solve_second", (field, vec, message), solve_scratch,
        idx, *inner, *outer, *inner_v, *outer_v, sinv, tau, e, *perfs,
    )
    got = lax.all_to_all(msg, "gx", split_axis=0, concat_axis=0, tiled=True)
    s, dots = call(
        second_image_kernel, "second_image", (field, (N_GX, 8, NZ)), [],
        idx, got, w, ends, dmat, tx, ty, tz, lx, *perfs, q, e, dots,
    )
    dots = lax.all_to_all(dots, "gx", split_axis=0, concat_axis=0, tiled=True)
    dots = jnp.broadcast_to(jnp.sum(dots, axis=0)[None], (N_GY, 8, NZ))
    dots = lax.all_to_all(dots, "gy", split_axis=0, concat_axis=0, tiled=True)
    flat_out = (2, CX * CY, NZ)
    x, r = call(finish_kernel, "finish", (flat_out, flat_out), [], dots, p, w, q, e, s, smem=0)
    shape = (2, CX, CY, NZ)
    return x.reshape(shape), r.reshape(shape)


def solution(mesh):
    tile = P(None, "gx", "gy", None)
    slots = P("gx", "gy", None, None)
    return jax.shard_map(
        body,
        mesh=mesh,
        in_specs=(tile,) * 5 + (slots,) * 3 + (P("gx", "gy", None), P(("gx", "gy"), None)),
        out_specs=(tile, tile),
        check_vma=False,
    )
```

time: 381 us -> 110 us (0.29)
  blocking collectives: 217 us -> 37.8 us
  starting transfers between devices: 66.1 us -> 32.3 us
  other arithmetic: 25.5 us -> 1.52 us
  local copies, waits for them, and re-layouts: 24.4 us -> 7.04 us
  waiting for transfers between devices: 35.8 us -> 22.3 us
  Pallas kernels: 0 us -> 8.01 us
  between operations: 7.29 us -> 0.76 us
    psum x3 -> x0, blocking collectives: 194 us -> none  [the longest x2 130 us: pair_sums(): lax.psum((jnp.sum(resid * image), jnp.sum(image * image)), ('gx', 'gy'))]
    all_to_all x9 -> x1, starting transfers between devices: 44.1 us -> 8.13 us  [body(): cuts = lax.all_to_all(cuts, 'gy', split_axis=0, concat_axis=0, tiled=True)]
    all_to_all x9 -> x1, waiting for transfers between devices: 32.7 us -> 0.66 us  [body(): cuts = lax.all_to_all(cuts, 'gy', split_axis=0, concat_axis=0, tiled=True)]
    ppermute x10 -> x14, waiting for transfers between devices: 3.14 us -> 21.6 us  [the longest x12 20.9 us: swapped(): lax.ppermute(block, 'gy', [(i, i ^ k * stride) for i in range(N_GY)])]
    all_to_all x2 -> x4, blocking collectives: 23 us -> 37.8 us  [the longest x2 17.3 us: body(): got = lax.all_to_all(msg, 'gx', split_axis=0, concat_axis=0, tiled=True)]
    unnamed x130 -> x21, local copies, waits for them, and re-layouts: 13.4 us -> 4.85 us
    add x103 -> x1, other arithmetic: 8.14 us -> 0.01 us  [body(): wells = (perf_well.reshape(N_GX, slots) + owners).reshape(1, SLOTS_ALL)]
    pallas_call x0 -> x8, Pallas kernels: none -> 8.01 us  [call(): pl.pallas_call(kernel, name=name, out_shape=tuple((jax.ShapeDtypeStruct(o...]
  transfers between devices with their start and end apart: 19 -> 15, of which waited for: 10 -> 12; matrix products, arithmetic and copies ran while one was open for 5% -> 2% of each run, Pallas kernels for 0% -> 0%
where the time goes in v1:
time: 110 us
  blocking collectives  37.8 us (34%)
  starting transfers between devices  32.3 us (29%)
  waiting for transfers between devices  22.3 us (20%)
  Pallas kernels  8.01 us (7%)
  local copies, waits for them, and re-layouts  7.04 us (6%)
  other arithmetic  1.52 us (1%)
    ppermute x12, waiting for transfers between devices, swapped(): lax.ppermute(block, 'gy', [(i, i ^ k * stride) for i in range(N_GY)])  20.9 us
    ppermute x12, starting transfers between devices, swapped(): lax.ppermute(block, 'gy', [(i, i ^ k * stride) for i in range(N_GY)])  19.1 us
    all_to_all x2, blocking collectives, body(): got = lax.all_to_all(msg, 'gx', split_axis=0, concat_axis=0, tiled=True)  17.3 us
    all_to_all x1, blocking collectives, body(): dots = lax.all_to_all(dots, 'gy', split_axis=0, concat_axis=0, tiled=True)  12.6 us
    all_to_all x1, starting transfers between devices, body(): cuts = lax.all_to_all(cuts, 'gy', split_axis=0, concat_axis=0, tiled=True)  8.13 us
    pallas_call x8, Pallas kernels, call(): pl.pallas_call(kernel, name=name, out_shape=tuple((jax.ShapeDtypeStruct(o...  8.01 us
    all_to_all x1, blocking collectives, body(): dots = lax.all_to_all(dots, 'gx', split_axis=0, concat_axis=0, tiled=True)  7.82 us
    unnamed x21, local copies, waits for them, and re-layouts  4.85 us
  transfers between devices with their start and end apart: 15, of which 12 were waited for; matrix products, arithmetic and copies ran while one was open for 2% of the time, Pallas kernels for 0%

profile of v1, /device:TPU:0, one launch (start us, length us, event | category | flops | bytes accessed | tf_op | source)
XLA Modules:
  0.0 109.7 jit_solution(6177836580357195639)
XLA Ops:
  2.7 8.1 %all-to-all-start = ((s32[16,1,9]{2,1,0:T(1,128)}), s32[16,1,9]{2,1,0:T(1,128)S(1)}, u32[]{:S(2)}, u32[]{:S(2)}) async-start(s32[16,1,9]{2,1,0:T(1,128)} %bitcast.10), calls=%async_computation | async-start | bytes 16384 | tf_op jit(solution)/shard_map/all_to_all | solution.py:477
  11.6 1.4 %collective-permute-start = (f32[2,8,128]{2,1,0:T(8,128)S(1)}, f32[2,8,128]{2,1,0:T(8,128)S(1)}, u32[]{:S(2)}, u32[]{:S(2)}) collective-permute-start(f32[2,8,128]{2,1,0:T(8,128)S(1)} %slice_bitcast_fusion), channel_id=1, source_target_pairs={{0,16},{16,32},{32,48},{48,64},{64,80},{80,96},{96,112},{1,17},{17... | collective-permute-start | bytes 24584 | tf_op jit(solution)/shard_map/ppermute | solution.py:478
  13.0 0.9 slice.10
  14.0 3.7 %collective-permute-start.1 = (f32[2,16,128]{2,1,0:T(8,128)S(1)}, f32[2,16,128]{2,1,0:T(8,128)S(1)}, u32[]{:S(2)}, u32[]{:S(2)}) collective-permute-start(f32[2,16,128]{2,1,0:T(8,128)S(1)} %bitcast.33), channel_id=1, source_target_pairs={{0,1},{1,2},{2,3},{3,4},{4,5},{5,6},{6,7},{7,8},{8,9},{9,10},{10,1... | collective-permute-start | bytes 49160 | tf_op jit(solution)/shard_map/ppermute | solution.py:479
  19.0 0.9 copy-done
  20.0 0.9 copy-done.2
  20.9 0.9 copy-done.3
  21.8 0.9 copy-done.4
  22.7 0.9 condense.1
  23.6 3.6 %collective-permute-start.4 = (f32[20,16,128]{2,1,0:T(8,128)S(1)}, f32[20,16,128]{2,1,0:T(8,128)S(1)}, u32[]{:S(2)}, u32[]{:S(2)}) collective-permute-start(f32[20,16,128]{2,1,0:T(8,128)S(1)} %get-tuple-element.25.refs_1_), channel_id=1, source_target_pairs={{0,3},{1,2},{2,1},{3,0},{4,7},{5,6},{6,5},{7,4},{8,11},{9,10},{10,... | collective-permute-start | bytes 491528 | tf_op jit(solution)/shard_map/ppermute | solution.py:468
  27.2 0.9 collective-permute-start.3
  29.3 5.9 %collective-permute-done.4.refs_4_ = f32[20,16,128]{2,1,0:T(8,128)S(1)} collective-permute-done((f32[20,16,128]{2,1,0:T(8,128)S(1)}, f32[20,16,128]{2,1,0:T(8,128)S(1)}, u32[]{:S(2)}, u32[]{:S(2)}) %collective-permute-start.4) | collective-permute-done | bytes 163872 | tf_op jit(solution)/shard_map/ppermute | solution.py:468
  37.4 5.3 %collective-permute-start.7 = (f32[20,16,128]{2,1,0:T(8,128)S(1)}, f32[20,16,128]{2,1,0:T(8,128)S(1)}, u32[]{:S(2)}, u32[]{:S(2)}) collective-permute-start(f32[20,16,128]{2,1,0:T(8,128)S(1)} %group_total.1.refs_5_), channel_id=1, source_target_pairs={{0,12},{1,13},{2,14},{3,15},{4,8},{5,9},{6,10},{7,11},{8,4},{9,5},... | collective-permute-start | bytes 491528 | tf_op jit(solution)/shard_map/ppermute | solution.py:468
  43.7 6.1 %collective-permute-done.7.refs_8_ = f32[20,16,128]{2,1,0:T(8,128)S(1)} collective-permute-done((f32[20,16,128]{2,1,0:T(8,128)S(1)}, f32[20,16,128]{2,1,0:T(8,128)S(1)}, u32[]{:S(2)}, u32[]{:S(2)}) %collective-permute-start.7) | collective-permute-done | bytes 163872 | tf_op jit(solution)/shard_map/ppermute | solution.py:468
  49.8 1.5 %collective-permute-done.6.refs_7_ = f32[20,16,128]{2,1,0:T(8,128)S(1)} collective-permute-done((f32[20,16,128]{2,1,0:T(8,128)S(1)}, f32[20,16,128]{2,1,0:T(8,128)S(1)}, u32[]{:S(2)}, u32[]{:S(2)}) %collective-permute-start.6) | collective-permute-done | bytes 163872 | tf_op jit(solution)/shard_map/ppermute | solution.py:468
  51.3 1.4 %solve_first.1 = (f32[2,8,16,128]{3,2,1,0:T(8,128)S(1)}, f32[4,16,128]{2,1,0:T(8,128)S(1)}, f32[8,24,128]{2,1,0:T(8,128)S(1)}) custom-call(s32[2]{0:T(128)S(1)} %pad_add_fusion.idx.refs_0_, f32[20,16,128]{2,1,0:T(8,128)S(1)} %get-tuple-element.25.refs_1_, f32[20,16,128]{2,1,0:T(8,128)S(1)} %collective-permute-done.2.refs_2_, ...), custom_call_target="tpu_custom_call" | custom-call | tf_op jit(solution)/shard_map/solve_first/pallas_call | solution.py:456
  52.8 9.2 %all_to_all.31.got = f32[8,24,128]{2,1,0:T(8,128)S(1)} all-to-all(f32[8,24,128]{2,1,0:T(8,128)S(1)} %get-tuple-element.29), channel_id=1, replica_groups=mesh['gx'=8,'gy'=16] {'gx'}, dimensions={0} | all-to-all | bytes 196608 | tf_op jit(solution)/shard_map/all_to_all | solution.py:508
  61.9 1.0 first_image.1
  63.6 1.0 collective-permute-start.9
  64.6 2.5 %collective-permute-start.8 = (f32[4,16,128]{2,1,0:T(8,128)S(1)}, f32[4,16,128]{2,1,0:T(8,128)S(1)}, u32[]{:S(2)}, u32[]{:S(2)}) collective-permute-start(f32[4,16,128]{2,1,0:T(8,128)S(1)} %get-tuple-element.37.refs_5_.refs_9_), channel_id=1, source_target_pairs={{0,1},{1,0},{2,3},{3,2},{4,5},{5,4},{6,7},{7,6},{8,9},{9,8},{10,11... | collective-permute-start | bytes 98312 | tf_op jit(solution)/shard_map/ppermute | solution.py:468
  67.1 1.0 collective-permute-done.10.refs_8_.refs_12_
  68.1 0.9 collective-permute-done.9.refs_7_.refs_11_
  70.0 2.4 %collective-permute-start.13 = (f32[4,16,128]{2,1,0:T(8,128)S(1)}, f32[4,16,128]{2,1,0:T(8,128)S(1)}, u32[]{:S(2)}, u32[]{:S(2)}) collective-permute-start(f32[4,16,128]{2,1,0:T(8,128)S(1)} %group_total_again.1.refs_13_), channel_id=1, source_target_pairs={{0,12},{1,13},{2,14},{3,15},{4,8},{5,9},{6,10},{7,11},{8,4},{9,5},... | collective-permute-start | bytes 98312 | tf_op jit(solution)/shard_map/ppermute | solution.py:468
  73.2 1.0 collective-permute-start.11
  74.2 1.3 %collective-permute-done.13.refs_16_ = f32[4,16,128]{2,1,0:T(8,128)S(1)} collective-permute-done((f32[4,16,128]{2,1,0:T(8,128)S(1)}, f32[4,16,128]{2,1,0:T(8,128)S(1)}, u32[]{:S(2)}, u32[]{:S(2)}) %collective-permute-start.13) | collective-permute-done | bytes 32800 | tf_op jit(solution)/shard_map/ppermute | solution.py:468
  75.5 2.3 %collective-permute-done.12.refs_15_ = f32[4,16,128]{2,1,0:T(8,128)S(1)} collective-permute-done((f32[4,16,128]{2,1,0:T(8,128)S(1)}, f32[4,16,128]{2,1,0:T(8,128)S(1)}, u32[]{:S(2)}, u32[]{:S(2)}) %collective-permute-start.12) | collective-permute-done | bytes 32800 | tf_op jit(solution)/shard_map/ppermute | solution.py:468
  77.8 1.4 %solve_second.1 = (f32[2,8,16,128]{3,2,1,0:T(8,128)S(1)}, f32[4,16,128]{2,1,0:T(8,128)S(1)}, f32[8,24,128]{2,1,0:T(8,128)S(1)}) custom-call(s32[2]{0:T(128)S(1)} %pad_add_fusion.idx.refs_0_, f32[20,16,128]{2,1,0:T(8,128)S(1)} %get-tuple-element.25.refs_1_, f32[20,16,128]{2,1,0:T(8,128)S(1)} %collective-permute-done.2.refs_2_, ...), custom_call_target="tpu_custom_call" | custom-call | tf_op jit(solution)/shard_map/solve_second/pallas_call | solution.py:456
  79.3 8.2 %all_to_all.32.got = f32[8,24,128]{2,1,0:T(8,128)S(1)} all-to-all(f32[8,24,128]{2,1,0:T(8,128)S(1)} %get-tuple-element.39), channel_id=1, replica_groups=mesh['gx'=8,'gy'=16] {'gx'}, dimensions={0} | all-to-all | bytes 196608 | tf_op jit(solution)/shard_map/all_to_all | solution.py:520
  87.5 0.9 second_image.1
  88.4 7.8 %all_to_all.33 = f32[8,8,128]{2,1,0:T(8,128)S(1)} all-to-all(f32[8,8,128]{2,1,0:T(8,128)S(1)} %get-tuple-element.44), channel_id=1, replica_groups=mesh['gx'=8,'gy'=16] {'gx'}, dimensions={0} | all-to-all | bytes 65536 | tf_op jit(solution)/shard_map/all_to_all | solution.py:525
  96.2 12.6 %all_to_all.34.got = f32[16,8,128]{2,1,0:T(8,128)S(1)} all-to-all(f32[16,8,128]{2,1,0:T(8,128)S(1)} %broadcast_in_dim.7), channel_id=1, replica_groups=mesh['gx'=8,'gy'=16] {'gy'}, dimensions={0} | all-to-all | bytes 131072 | tf_op jit(solution)/shard_map/all_to_all | solution.py:527
  108.9 0.9 finish.1
  (50 shorter events, 11.1 us)
Async XLA Ops:
  0.6 0.7 copy-start.8
  0.6 18.4 %copy-start.1 = (f32[2,16,8,128]{3,2,1,0:T(8,128)S(1)}, f32[2,16,8,128]{3,2,1,0:T(8,128)}, u32[]{:S(2)}) copy-start(f32[2,16,8,128]{3,2,1,0:T(8,128)} %param.13) | copy-start | bytes 393220
  2.7 15.6 %all-to-all-start = ((s32[16,1,9]{2,1,0:T(1,128)}), s32[16,1,9]{2,1,0:T(1,128)S(1)}, u32[]{:S(2)}, u32[]{:S(2)}) async-start(s32[16,1,9]{2,1,0:T(1,128)} %bitcast.10), calls=%async_computation | async-start | bytes 16384 | tf_op jit(solution)/shard_map/all_to_all | solution.py:477
  11.6 6.8 %collective-permute-start = (f32[2,8,128]{2,1,0:T(8,128)S(1)}, f32[2,8,128]{2,1,0:T(8,128)S(1)}, u32[]{:S(2)}, u32[]{:S(2)}) collective-permute-start(f32[2,8,128]{2,1,0:T(8,128)S(1)} %slice_bitcast_fusion), channel_id=1, source_target_pairs={{0,16},{16,32},{32,48},{48,64},{64,80},{80,96},{96,112},{1,17},{17... | collective-permute-start | bytes 24584 | tf_op jit(solution)/shard_map/ppermute | solution.py:478
  14.0 5.1 %collective-permute-start.1 = (f32[2,16,128]{2,1,0:T(8,128)S(1)}, f32[2,16,128]{2,1,0:T(8,128)S(1)}, u32[]{:S(2)}, u32[]{:S(2)}) collective-permute-start(f32[2,16,128]{2,1,0:T(8,128)S(1)} %bitcast.33), channel_id=1, source_target_pairs={{0,1},{1,2},{2,3},{3,4},{4,5},{5,6},{6,7},{7,8},{8,9},{9,10},{10,1... | collective-permute-start | bytes 49160 | tf_op jit(solution)/shard_map/ppermute | solution.py:479
  19.0 1.0 copy-start
  20.0 0.9 copy-start.2
  20.9 0.9 copy-start.3
  21.8 0.9 copy-start.4
  22.7 5.5 %copy-start.9 = (s32[1,1,8]{2,1,0:T(1,128)S(1)}, s32[1,1,8]{2,1,0:T(1,128)}, u32[]{:S(2)}) copy-start(s32[1,1,8]{2,1,0:T(1,128)} %param.18) | copy-start | bytes 100
  23.6 4.6 %copy-start.5 = (s32[1,1,8,32]{3,2,1,0:T(8,128)S(1)}, s32[1,1,8,32]{3,2,1,0:T(8,128)}, u32[]{:S(2)}) copy-start(s32[1,1,8,32]{3,2,1,0:T(8,128)} %param.15) | copy-start | bytes 3076
  23.6 4.7 %copy-start.6 = (s32[1,1,8,32]{3,2,1,0:T(8,128)S(1)}, s32[1,1,8,32]{3,2,1,0:T(8,128)}, u32[]{:S(2)}) copy-start(s32[1,1,8,32]{3,2,1,0:T(8,128)} %param.16) | copy-start | bytes 3076
  23.6 11.6 %collective-permute-start.4 = (f32[20,16,128]{2,1,0:T(8,128)S(1)}, f32[20,16,128]{2,1,0:T(8,128)S(1)}, u32[]{:S(2)}, u32[]{:S(2)}) collective-permute-start(f32[20,16,128]{2,1,0:T(8,128)S(1)} %get-tuple-element.25.refs_1_), channel_id=1, source_target_pairs={{0,3},{1,2},{2,1},{3,0},{4,7},{5,6},{6,5},{7,4},{8,11},{9,10},{10,... | collective-permute-start | bytes 491528 | tf_op jit(solution)/shard_map/ppermute | solution.py:468
  27.2 8.6 %collective-permute-start.3 = (f32[20,16,128]{2,1,0:T(8,128)S(1)}, f32[20,16,128]{2,1,0:T(8,128)S(1)}, u32[]{:S(2)}, u32[]{:S(2)}) collective-permute-start(f32[20,16,128]{2,1,0:T(8,128)S(1)} %get-tuple-element.25.refs_1_), channel_id=1, source_target_pairs={{0,2},{1,3},{2,0},{3,1},{4,6},{5,7},{6,4},{7,5},{8,10},{9,11},{10,... | collective-permute-start | bytes 491528 | tf_op jit(solution)/shard_map/ppermute | solution.py:468
  28.1 8.6 %collective-permute-start.2 = (f32[20,16,128]{2,1,0:T(8,128)S(1)}, f32[20,16,128]{2,1,0:T(8,128)S(1)}, u32[]{:S(2)}, u32[]{:S(2)}) collective-permute-start(f32[20,16,128]{2,1,0:T(8,128)S(1)} %get-tuple-element.25.refs_1_), channel_id=1, source_target_pairs={{0,1},{1,0},{2,3},{3,2},{4,5},{5,4},{6,7},{7,6},{8,9},{9,8},{10,11... | collective-permute-start | bytes 491528 | tf_op jit(solution)/shard_map/ppermute | solution.py:468
  28.3 0.7 copy-start.7
  37.4 12.3 %collective-permute-start.7 = (f32[20,16,128]{2,1,0:T(8,128)S(1)}, f32[20,16,128]{2,1,0:T(8,128)S(1)}, u32[]{:S(2)}, u32[]{:S(2)}) collective-permute-start(f32[20,16,128]{2,1,0:T(8,128)S(1)} %group_total.1.refs_5_), channel_id=1, source_target_pairs={{0,12},{1,13},{2,14},{3,15},{4,8},{5,9},{6,10},{7,11},{8,4},{9,5},... | collective-permute-start | bytes 491528 | tf_op jit(solution)/shard_map/ppermute | solution.py:468
  42.7 8.6 %collective-permute-start.6 = (f32[20,16,128]{2,1,0:T(8,128)S(1)}, f32[20,16,128]{2,1,0:T(8,128)S(1)}, u32[]{:S(2)}, u32[]{:S(2)}) collective-permute-start(f32[20,16,128]{2,1,0:T(8,128)S(1)} %group_total.1.refs_5_), channel_id=1, source_target_pairs={{0,8},{1,9},{2,10},{3,11},{4,12},{5,13},{6,14},{7,15},{8,0},{9,1},... | collective-permute-start | bytes 491528 | tf_op jit(solution)/shard_map/ppermute | solution.py:468
  43.6 7.8 %collective-permute-start.5 = (f32[20,16,128]{2,1,0:T(8,128)S(1)}, f32[20,16,128]{2,1,0:T(8,128)S(1)}, u32[]{:S(2)}, u32[]{:S(2)}) collective-permute-start(f32[20,16,128]{2,1,0:T(8,128)S(1)} %group_total.1.refs_5_), channel_id=1, source_target_pairs={{0,4},{1,5},{2,6},{3,7},{4,0},{5,1},{6,2},{7,3},{8,12},{9,13},{10,... | collective-permute-start | bytes 491528 | tf_op jit(solution)/shard_map/ppermute | solution.py:468
  62.9 5.2 %collective-permute-start.10 = (f32[4,16,128]{2,1,0:T(8,128)S(1)}, f32[4,16,128]{2,1,0:T(8,128)S(1)}, u32[]{:S(2)}, u32[]{:S(2)}) collective-permute-start(f32[4,16,128]{2,1,0:T(8,128)S(1)} %get-tuple-element.37.refs_5_.refs_9_), channel_id=1, source_target_pairs={{0,3},{1,2},{2,1},{3,0},{4,7},{5,6},{6,5},{7,4},{8,11},{9,10},{10,... | collective-permute-start | bytes 98312 | tf_op jit(solution)/shard_map/ppermute | solution.py:468
  63.6 5.4 %collective-permute-start.9 = (f32[4,16,128]{2,1,0:T(8,128)S(1)}, f32[4,16,128]{2,1,0:T(8,128)S(1)}, u32[]{:S(2)}, u32[]{:S(2)}) collective-permute-start(f32[4,16,128]{2,1,0:T(8,128)S(1)} %get-tuple-element.37.refs_5_.refs_9_), channel_id=1, source_target_pairs={{0,2},{1,3},{2,0},{3,1},{4,6},{5,7},{6,4},{7,5},{8,10},{9,11},{10,... | collective-permute-start | bytes 98312 | tf_op jit(solution)/shard_map/ppermute | solution.py:468
  64.6 4.7 %collective-permute-start.8 = (f32[4,16,128]{2,1,0:T(8,128)S(1)}, f32[4,16,128]{2,1,0:T(8,128)S(1)}, u32[]{:S(2)}, u32[]{:S(2)}) collective-permute-start(f32[4,16,128]{2,1,0:T(8,128)S(1)} %get-tuple-element.37.refs_5_.refs_9_), channel_id=1, source_target_pairs={{0,1},{1,0},{2,3},{3,2},{4,5},{5,4},{6,7},{7,6},{8,9},{9,8},{10,11... | collective-permute-start | bytes 98312 | tf_op jit(solution)/shard_map/ppermute | solution.py:468
  70.0 5.5 %collective-permute-start.13 = (f32[4,16,128]{2,1,0:T(8,128)S(1)}, f32[4,16,128]{2,1,0:T(8,128)S(1)}, u32[]{:S(2)}, u32[]{:S(2)}) collective-permute-start(f32[4,16,128]{2,1,0:T(8,128)S(1)} %group_total_again.1.refs_13_), channel_id=1, source_target_pairs={{0,12},{1,13},{2,14},{3,15},{4,8},{5,9},{6,10},{7,11},{8,4},{9,5},... | collective-permute-start | bytes 98312 | tf_op jit(solution)/shard_map/ppermute | solution.py:468
  72.4 5.4 %collective-permute-start.12 = (f32[4,16,128]{2,1,0:T(8,128)S(1)}, f32[4,16,128]{2,1,0:T(8,128)S(1)}, u32[]{:S(2)}, u32[]{:S(2)}) collective-permute-start(f32[4,16,128]{2,1,0:T(8,128)S(1)} %group_total_again.1.refs_13_), channel_id=1, source_target_pairs={{0,8},{1,9},{2,10},{3,11},{4,12},{5,13},{6,14},{7,15},{8,0},{9,1},... | collective-permute-start | bytes 98312 | tf_op jit(solution)/shard_map/ppermute | solution.py:468
  73.2 4.6 %collective-permute-start.11 = (f32[4,16,128]{2,1,0:T(8,128)S(1)}, f32[4,16,128]{2,1,0:T(8,128)S(1)}, u32[]{:S(2)}, u32[]{:S(2)}) collective-permute-start(f32[4,16,128]{2,1,0:T(8,128)S(1)} %group_total_again.1.refs_13_), channel_id=1, source_target_pairs={{0,4},{1,5},{2,6},{3,7},{4,0},{5,1},{6,2},{7,3},{8,12},{9,13},{10,... | collective-permute-start | bytes 98312 | tf_op jit(solution)/shard_map/ppermute | solution.py:468

commit v2 on v1

--- a/solution.py
+++ b/solution.py
@@ -8,11 +8,13 @@
 F32 = jnp.float32
 BF16 = jnp.bfloat16
 VMEM = pl.BlockSpec(memory_space=pltpu.VMEM)
+HBM = pl.BlockSpec(memory_space=pltpu.HBM)
 SMEM = pl.BlockSpec(memory_space=pltpu.SMEM)
 CX, CY, NZ = 16, 8, 128
 PLANE = (CX, NZ)
 N_GX, N_GY = 8, 16
 W_ALL = 128
+PREPARE_VMEM = 54400
 SLOTS_ALL = 256
 
 
@@ -146,35 +148,57 @@
     return (ref[0, j], ref[1, j])
 
 
-def condense_kernel(idx, b, acc, tx_in, ty_in, tz_in, lx_in, ly_in, brk, seg, dmat, tau_o, sinv, binv, rhs, tx_o, ty_o, tz_o):
+def plane(ref, c, j):
+    return ref.at[c][pl.ds(j, CX, stride=CY), :]
+
+
+def prepare_kernel(idx, b_h, acc_h, tx_h, ty_h, tz_h, rhs, tx_o, ty_o, tz_o, diag, cross, sx, sy, b, acc, tx_v, ty_v, tz_v, sems):
     gx, gy = idx[0], idx[1]
+    pairs = ((tx_h, tx_v), (ty_h, ty_v), (tz_h, tz_v), (acc_h, acc), (b_h, b))
+    copies = [pltpu.make_async_copy(h, v, sems.at[i]) for i, (h, v) in enumerate(pairs)]
+    for copy in copies:
+        copy.start()
     last_x = jnp.logical_and(rows() == CX - 1, gx == N_GX - 1)
     last_z = lanes() == NZ - 1
-
-    def plane(ref, c, j):
-        return ref.at[c][pl.ds(j, CX, stride=CY), :]
-
+    for copy in copies:
+        copy.wait()
     for c in range(2):
-        ty_o[c, 0] = ly_in[c]
+        sx[c] = tx_v[c, (CX - 1) * CY : CX * CY, :]
+        sy[c] = plane(ty_v, c, CY - 1)
+        ly = 0.0
         for j in range(CY):
-            tx = jnp.where(last_x, 0.0, plane(tx_in, c, j))
-            tz = jnp.where(last_z, 0.0, plane(tz_in, c, j))
-            ty = plane(ty_in, c, j)
+            tx = jnp.where(last_x, 0.0, plane(tx_v, c, j))
+            tz = jnp.where(last_z, 0.0, plane(tz_v, c, j))
+            ty = plane(ty_v, c, j)
             if j == CY - 1:
                 ty = jnp.where(gy == N_GY - 1, 0.0, ty)
             tx_o[c, j] = tx
             tz_o[c, j] = tz
-            ty_o[c, j + 1] = ty
-            lx = from_row_before(tx, lx_in[c, j : j + 1, :])
-            faces = tx + lx + ty + ty_o[c, j] + tz + pltpu.roll(tz, 1, 1)
-            dmat[3 * c, j] = plane(acc, 3 * c, j) + faces
+            ty_o[c, j] = ty
+            faces = tx + from_row_before(tx, 0.0) + ty + ly + tz + pltpu.roll(tz, 1, 1)
+            diag[c, j] = plane(acc, 3 * c, j) + faces
+            cross[c, j] = plane(acc, 2 - c, j)
             rhs[c, j] = plane(b, c, j)
+            ly = ty
+
+
+def condense_kernel(idx, diag, cross, ty, rhs, lx_in, ly_in, brk_0, brk_1, brk_2, brk_3, seg, dmat, tau_o, sinv, binv, brk):
+    gy = idx[1]
+    for k, ref in enumerate((brk_0, brk_1, brk_2, brk_3)):
+        for i in range(4):
+            brk[pl.ds(jnp.bitwise_xor(gy, 4 * k + i), 1), :] = ref[i : i + 1, :]
+    cuts = pltpu.roll(brk[...], (NZ - CY * gy) % NZ, 1)
+    for c in range(2):
+        ly = ly_in[c]
+        for j in range(CY):
+            d = diag[c, j] + jnp.where(rows() == 0, lx_in[c, j : j + 1, :], 0.0)
+            dmat[3 * c, j] = d + ly if j == 0 else d
         for j in range(CY + 1):
-            keep = 1.0 - brk[:, j : j + 1].astype(F32)
-            tau_o[c, j] = ty_o[c, j] * keep
+            keep = 1.0 - cuts[:, j : j + 1].astype(F32)
+            tau_o[c, j] = (ty[c, j - 1] if j else ly) * keep
     for j in range(CY):
-        dmat[1, j] = plane(acc, 2, j)
-        dmat[2, j] = plane(acc, 1, j)
+        dmat[1, j] = cross[0, j]
+        dmat[2, j] = cross[1, j]
 
     def tau(j):
         return pair_at(tau_o, j)
@@ -284,8 +308,8 @@
             rest = refs[17:]
             offset = 0
         sinv, tau_r, rhs, cells, wells, weights = rest[:6]
-        p_out, ends, msg = rest[6:9]
-        mat_i, vec_i, mat_o, vec_o, edge = rest[9:]
+        p_out, ends, msg_a, msg_b = rest[6:10]
+        mat_i, vec_i, mat_o, vec_o, edge = rest[10:]
         gx, gy = idx[0], idx[1]
         z_at, y_at = gy % 4, gy // 4
         gather_segments(z_at, inner, inner_v, offset, mat_i, vec_i)
@@ -336,38 +360,34 @@
         w = weights[...]
         sums, totals = row_times([w * values, w], ones_of(at_well), NT)
         tail = jnp.concatenate([sums, totals, jnp.zeros((6, W_ALL), F32)], axis=0)
-        for d in range(N_GX):
-            msg[d, 0:16, :] = jnp.zeros((16, NZ), F32)
-            msg[d, 16:24, :] = tail
-
-        @pl.when(gx < N_GX - 1)
-        def _():
-            msg[gx + 1, 0:16, :] = edge[1]
-
-        @pl.when(gx > 0)
-        def _():
-            msg[gx - 1, 0:16, :] = edge[0]
+        even = gx % 2 == 0
+        low, high = edge[0], edge[1]
+        msg_a[0:16, :] = jnp.where(even, high, low)
+        msg_b[0:16, :] = jnp.where(even, low, high)
+        msg_a[16:24, :] = tail
+        msg_b[16:24, :] = tail
 
     return kernel
 
 
-def apply_operator(idx, got, p, ends, dmat, tx, ty, tz, cells, wells, weights):
+def apply_operator(idx, got, cells, wells, weights):
     gx = idx[0]
-    tail = got[0, 16:24, :]
-    for d in range(1, N_GX):
-        tail = tail + got[d, 16:24, :]
+    got_a, sent_b, got_b, got_c, got_d = got
+    tail = sent_b[16:24, :] + got_b[16:24, :] + got_c[...] + got_d[...]
     rates = tail[0:1] / jnp.maximum(tail[1:2], 1.0)
     at_row, at_layer, at_well = slot_tables(cells, wells)
     slot_rate = row_times([rates], ones_of(at_well), (((1,), (0,)), ((), ())))[0]
     added = jnp.where(at_layer, weights[...] * slot_rate, 0.0)
     table = ones_of(at_row)
     well_add = sum(lax.dot_general(table, part, NT, preferred_element_type=F32) for part in split3(added))
-    from_after = jnp.where(gx < N_GX - 1, got[jnp.minimum(gx + 1, N_GX - 1), 0:16, :], 0.0)
-    from_before = jnp.where(gx > 0, got[jnp.maximum(gx - 1, 0), 0:16, :], 0.0)
+    even = gx % 2 == 0
+    halo_a, halo_b = got_a[0:16, :], got_b[0:16, :]
+    from_after = jnp.where(gx < N_GX - 1, jnp.where(even, halo_a, halo_b), 0.0)
+    from_before = jnp.where(gx > 0, jnp.where(even, halo_b, halo_a), 0.0)
     return well_add, from_after, from_before
 
 
-def operator_plane(c, j, p, ends, dmat, tx, ty, tz, lx_in, halo, well_add):
+def operator_plane(c, j, p, ends, dmat, tx, ty, tz, lx_in, ly_in, halo, well_add):
     from_after, from_before = halo
     here = p[c, j]
     up = p[c, j + 1] if j < CY - 1 else ends[2 + c]
@@ -376,7 +396,7 @@
     at = c * CY + j
     beside = t * from_row_after(here, from_after[at : at + 1])
     beside = beside + from_row_before(t * here, lx_in[c, j : j + 1, :] * from_before[at : at + 1])
-    beside = beside + ty[c, j + 1] * up + ty[c, j] * down
+    beside = beside + ty[c, j] * up + (ty[c, j - 1] if j else ly_in[c]) * down
     tzp = tz[c, j]
     beside = beside + tzp * pltpu.roll(here, NZ - 1, 1) + pltpu.roll(tzp * here, 1, 1)
     out = dmat[2 * c, j] * p[0, j] + dmat[2 * c + 1, j] * p[1, j] - beside
@@ -385,15 +405,15 @@
     return out
 
 
-def first_image_kernel(idx, got, p, ends, dmat, tau_r, sinv, binv, rhs, tx, ty, tz, lx_in, cells, wells, weights, q_out, e_out, vec_out, dots):
-    well_add, after, before = apply_operator(idx, got, p, ends, dmat, tx, ty, tz, cells, wells, weights)
+def first_image_kernel(idx, got_a, sent_b, got_b, got_c, got_d, p, ends, dmat, tau_r, sinv, binv, rhs, tx, ty, tz, lx_in, ly_in, cells, wells, weights, q_out, e_out, vec_out, dots):
+    well_add, after, before = apply_operator(idx, (got_a, sent_b, got_b, got_c, got_d), cells, wells, weights)
     eq = jnp.zeros(PLANE, F32)
     qq = jnp.zeros(PLANE, F32)
     e = []
     for j in range(CY):
         pair = []
         for c in range(2):
-            q = operator_plane(c, j, p, ends, dmat, tx, ty, tz, lx_in, (after, before), well_add)
+            q = operator_plane(c, j, p, ends, dmat, tx, ty, tz, lx_in, ly_in, (after, before), well_add)
             rest = rhs[c, j] - q
             q_out[c, j] = q
             e_out[c, j] = rest
@@ -416,22 +436,20 @@
         vec_out[2 + c] = last[c]
 
 
-def second_image_kernel(idx, got, p, ends, dmat, tx, ty, tz, lx_in, cells, wells, weights, q_in, e_in, dots_in, s_out, dots):
-    well_add, after, before = apply_operator(idx, got, p, ends, dmat, tx, ty, tz, cells, wells, weights)
+def second_image_kernel(idx, got_a, sent_b, got_b, got_c, got_d, p, ends, dmat, tx, ty, tz, lx_in, ly_in, cells, wells, weights, q_in, e_in, dots_in, s_out, dots):
+    well_add, after, before = apply_operator(idx, (got_a, sent_b, got_b, got_c, got_d), cells, wells, weights)
     sq = jnp.zeros(PLANE, F32)
     ss = jnp.zeros(PLANE, F32)
     es = jnp.zeros(PLANE, F32)
     for j in range(CY):
         for c in range(2):
-            s = operator_plane(c, j, p, ends, dmat, tx, ty, tz, lx_in, (after, before), well_add)
+            s = operator_plane(c, j, p, ends, dmat, tx, ty, tz, lx_in, ly_in, (after, before), well_add)
             s_out[c, j] = s
             sq = sq + s * q_in[c, j]
             ss = ss + s * s
             es = es + s * e_in[c, j]
     sums = [jnp.sum(x, axis=0, keepdims=True) for x in (dots_in[0], dots_in[1], sq, ss, es)]
-    block = jnp.concatenate(sums + [jnp.zeros((3, NZ), F32)], axis=0)
-    for d in range(N_GX):
-        dots[d] = block
+    dots[...] = jnp.concatenate(sums + [jnp.zeros((3, NZ), F32)], axis=0)
 
 
 def finish_kernel(got, p, w, q, e, s, x_out, r_out):
@@ -452,81 +470,102 @@
             r_out.at[c][at, :] = e[c, j] + on_q * q[c, j] - k * s[c, j]
 
 
-def call(kernel, name, outs, scratch, *args, smem=1):
+def call(kernel, name, outs, scratch, *args, specs=None, vmem=24 * 1024):
+    outs = [o if isinstance(o, jax.ShapeDtypeStruct) else jax.ShapeDtypeStruct(o, F32) for o in outs]
     return pl.pallas_call(
         kernel,
         name=name,
-        out_shape=tuple(jax.ShapeDtypeStruct(o, F32) for o in outs),
-        in_specs=[SMEM] * smem + [VMEM] * (len(args) - smem),
+        out_shape=tuple(outs),
+        in_specs=specs or [SMEM] + [VMEM] * (len(args) - 1),
         out_specs=tuple(VMEM for _ in outs),
-        scratch_shapes=[pltpu.VMEM(s, F32) for s in scratch],
-        compiler_params=pltpu.CompilerParams(vmem_limit_bytes=24 * 1024 * 1024),
+        scratch_shapes=[pltpu.VMEM(s, F32) if isinstance(s, tuple) else s for s in scratch],
+        compiler_params=pltpu.CompilerParams(vmem_limit_bytes=vmem * 1024),
     )(*args)
 
 
 def swapped(block, stride):
     return [block] + [lax.ppermute(block, "gy", [(i, i ^ (k * stride)) for i in range(N_GY)]) for k in (1, 2, 3)]
+
+
+def exchange_rows(msg_a, msg_b):
+    got_a = lax.ppermute(msg_a, "gx", [(i, i ^ 1) for i in range(N_GX)])
+    below = lax.broadcasted_iota(jnp.int32, msg_b.shape, 0) >= 16
+    sent_b = msg_b + jnp.where(below, got_a, 0.0)
+    got_b = lax.ppermute(sent_b, "gx", [(i, (i + 1 if i % 2 else i - 1) % N_GX) for i in range(N_GX)])
+    tail = sent_b[16:]
+    got_c = lax.ppermute(tail, "gx", [(i, i ^ 4) for i in range(N_GX)])
+    got_d = lax.ppermute(tail, "gx", [(i, (i + 2 if i % 2 else i - 2) % N_GX) for i in range(N_GX)])
+    return got_a, sent_b, got_b, got_c, got_d
+
+
+def sum_everywhere(x):
+    x = x + lax.ppermute(x, "gx", [(i, i ^ 1) for i in range(N_GX)])
+    others = [lax.ppermute(x, "gx", [(i, (i + 2 * k) % N_GX) for i in range(N_GX)]) for k in (1, 2, 3)]
+    x = x + others[0] + others[1] + others[2]
+    x = jnp.broadcast_to(x[None], (N_GY,) + x.shape)
+    return lax.all_to_all(x, "gy", split_axis=0, concat_axis=0, tiled=True)
 
 
 def body(right_side, accumulation, trans_x, trans_y, trans_z, perf_cell, perf_well, perf_weight, perf_count, breaks):
     gx, gy = lax.axis_index("gx"), lax.axis_index("gy")
     idx = jnp.stack([gx, gy]).astype(jnp.int32)
-    cuts = breaks.reshape(N_GY, CY)
-    beyond = jnp.concatenate([cuts[1:, :1], jnp.zeros((1, 1), cuts.dtype)], axis=0)
-    cuts = jnp.concatenate([cuts, beyond], axis=1)
-    cuts = lax.all_to_all(cuts, "gy", split_axis=0, concat_axis=0, tiled=True)
-    lx = lax.ppermute(trans_x[:, -1], "gx", [(i, i + 1) for i in range(N_GX - 1)])
-    ly = lax.ppermute(trans_y[:, :, -1], "gy", [(i, i + 1) for i in range(N_GY - 1)])
+
+    def flat(a):
+        return a.reshape(a.shape[0], CX * CY, NZ)
+
+    field, block, part = (2, CY, CX, NZ), (4, CY, CX, NZ), (2, CY + 1, CX, NZ)
+    seg, vec, message = (20, CX, NZ), (4, CX, NZ), (24, NZ)
+    order = [(4, 16, CX, NZ), (4, 4, CX, NZ)]
+    two, four = (2, CX * CY, NZ), (4, CX * CY, NZ)
+    cuts = swapped(jnp.concatenate(swapped(breaks, 1), axis=0), 4)
+    rhs, tx, ty, tz, diag, cross, sx, sy = call(
+        prepare_kernel, "prepare",
+        (field, field, field, field, field, field, (2, CY, NZ), (2, CX, NZ)),
+        [two, four, two, two, two, pltpu.SemaphoreType.DMA((5,))],
+        idx, flat(right_side), flat(accumulation), flat(trans_x), flat(trans_y), flat(trans_z),
+        specs=[SMEM] + [HBM] * 5, vmem=PREPARE_VMEM,
+    )
+    lx = lax.ppermute(sx, "gx", [(i, i + 1) for i in range(N_GX - 1)])
+    ly = lax.ppermute(sy, "gy", [(i, i + 1) for i in range(N_GY - 1)])
     slots = perf_cell.shape[3]
     live = jnp.arange(slots, dtype=jnp.int32)[None, :] < perf_count.reshape(N_GX, 1)
     weights = jnp.where(live, perf_weight.reshape(N_GX, slots), 0.0).reshape(1, SLOTS_ALL)
     owners = jnp.arange(N_GX, dtype=jnp.int32)[:, None] * 16
     wells = (perf_well.reshape(N_GX, slots) + owners).reshape(1, SLOTS_ALL)
     cells = perf_cell.reshape(1, SLOTS_ALL)
-
-    def flat(a):
-        return a.reshape(a.shape[0], CX * CY, NZ)
-
-    field, block, part = (2, CY, CX, NZ), (4, CY, CX, NZ), (2, CY + 1, CX, NZ)
-    seg, vec = (20, CX, NZ), (4, CX, NZ)
-    message = (N_GX, 24, NZ)
-    order = [(4, 16, CX, NZ), (4, 4, CX, NZ)]
-    own, dmat, tau, sinv, binv, rhs, tx, ty, tz = call(
-        condense_kernel, "condense",
-        (seg, block, part, block, block, field, field, part, field), [],
-        idx, flat(right_side), flat(accumulation), flat(trans_x), flat(trans_y), flat(trans_z), lx, ly, cuts,
-    )
     perfs = (cells, wells, weights)
+
+    own, dmat, tau, sinv, binv = call(
+        condense_kernel, "condense", (seg, block, part, block, block),
+        [pltpu.VMEM((N_GY, NZ), jnp.int32)], idx, diag, cross, ty, rhs, lx, ly, *cuts,
+    )
     inner = swapped(own, 1)
     (group,) = call(make_total_kernel(True), "group_total", (seg,), order, idx, *inner)
     outer = swapped(group, 4)
     solve_scratch = order + order + [(2, 16, NZ)]
-    p, ends, msg = call(
-        make_solve_kernel(True), "solve_first", (field, vec, message), solve_scratch,
+    p, ends, msg_a, msg_b = call(
+        make_solve_kernel(True), "solve_first", (field, vec, message, message), solve_scratch,
         idx, *inner, *outer, sinv, tau, rhs, *perfs,
     )
-    got = lax.all_to_all(msg, "gx", split_axis=0, concat_axis=0, tiled=True)
+    got = exchange_rows(msg_a, msg_b)
     q, e, own_v, dots = call(
         first_image_kernel, "first_image", (field, field, vec, (2, CX, NZ)), [],
-        idx, got, p, ends, dmat, tau, sinv, binv, rhs, tx, ty, tz, lx, *perfs,
+        idx, *got, p, ends, dmat, tau, sinv, binv, rhs, tx, ty, tz, lx, ly, *perfs,
     )
     inner_v = swapped(own_v, 1)
     (group_v,) = call(make_total_kernel(False), "group_total_again", (vec,), order, idx, *inner, *inner_v)
     outer_v = swapped(group_v, 4)
-    w, ends, msg = call(
-        make_solve_kernel(False), "solve_second", (field, vec, message), solve_scratch,
+    w, ends, msg_a, msg_b = call(
+        make_solve_kernel(False), "solve_second", (field, vec, message, message), solve_scratch,
         idx, *inner, *outer, *inner_v, *outer_v, sinv, tau, e, *perfs,
     )
-    got = lax.all_to_all(msg, "gx", split_axis=0, concat_axis=0, tiled=True)
+    got = exchange_rows(msg_a, msg_b)
     s, dots = call(
-        second_image_kernel, "second_image", (field, (N_GX, 8, NZ)), [],
-        idx, got, w, ends, dmat, tx, ty, tz, lx, *perfs, q, e, dots,
-    )
-    dots = lax.all_to_all(dots, "gx", split_axis=0, concat_axis=0, tiled=True)
-    dots = jnp.broadcast_to(jnp.sum(dots, axis=0)[None], (N_GY, 8, NZ))
-    dots = lax.all_to_all(dots, "gy", split_axis=0, concat_axis=0, tiled=True)
-    flat_out = (2, CX * CY, NZ)
-    x, r = call(finish_kernel, "finish", (flat_out, flat_out), [], dots, p, w, q, e, s, smem=0)
+        second_image_kernel, "second_image", (field, (8, NZ)), [],
+        idx, *got, w, ends, dmat, tx, ty, tz, lx, ly, *perfs, q, e, dots,
+    )
+    dots = sum_everywhere(dots)
+    x, r = call(finish_kernel, "finish", (two, two), [], dots, p, w, q, e, s, specs=[VMEM] * 6)
     shape = (2, CX, CY, NZ)
     return x.reshape(shape), r.reshape(shape)
 

time: 110 us -> 105 us (0.955)
  blocking collectives: 37.8 us -> 12.7 us
  waiting for transfers between devices: 22.3 us -> 38.2 us
  starting transfers between devices: 32.3 us -> 42 us
  local copies, waits for them, and re-layouts: 7.04 us -> 1.04 us
  Pallas kernels: 8.01 us -> 9.96 us
  other arithmetic: 1.52 us -> 0.33 us
    all_to_all x4 -> x1, blocking collectives: 37.8 us -> 12.7 us  [sum_everywhere(): return lax.all_to_all(x, 'gy', split_axis=0, concat_axis=0, tiled=True)]
    ppermute x2 -> x14, waiting for transfers between devices: 0.69 us -> 13.6 us  [the longest x2 5.53 us: exchange_rows(): got_c = lax.ppermute(tail, 'gx', [(i, i ^ 4) for i in range(N_GX)])]
    ppermute x2 -> x14, starting transfers between devices: 5.1 us -> 16 us  [the longest x2 4.33 us: exchange_rows(): got_c = lax.ppermute(tail, 'gx', [(i, i ^ 4) for i in range(N_GX)])]
    all_to_all x1 -> x0, starting transfers between devices: 8.13 us -> none  [body(): cuts = lax.all_to_all(cuts, 'gy', split_axis=0, concat_axis=0, tiled=True)]
    ppermute x12 -> x18, starting transfers between devices: 19.1 us -> 25.9 us  [swapped(): lax.ppermute(block, 'gy', [(i, i ^ k * stride) for i in range(N_GY)])]
    unnamed x21 -> x10, local copies, waits for them, and re-layouts: 4.85 us -> 0.55 us
    ppermute x12 -> x18, waiting for transfers between devices: 20.9 us -> 24.6 us  [swapped(): lax.ppermute(block, 'gy', [(i, i ^ k * stride) for i in range(N_GY)])]
    pallas_call x8 -> x9, Pallas kernels: 8.01 us -> 9.96 us  [call(): pl.pallas_call(kernel, name=name, out_shape=tuple(outs), in_specs=specs o...]
  transfers between devices with their start and end apart: 15 -> 32, of which waited for: 12 -> 19; matrix products, arithmetic and copies ran while one was open for 2% -> 1% of each run, Pallas kernels for 0% -> 2%
where the time goes in v2:
time: 105 us
  starting transfers between devices  42 us (40%)
  waiting for transfers between devices  38.2 us (36%)
  blocking collectives  12.7 us (12%)
  Pallas kernels  9.96 us (9%)
    ppermute x18, starting transfers between devices, swapped(): lax.ppermute(block, 'gy', [(i, i ^ k * stride) for i in range(N_GY)])  25.9 us
    ppermute x18, waiting for transfers between devices, swapped(): lax.ppermute(block, 'gy', [(i, i ^ k * stride) for i in range(N_GY)])  24.6 us
    all_to_all x1, blocking collectives, sum_everywhere(): return lax.all_to_all(x, 'gy', split_axis=0, concat_axis=0, tiled=True)  12.7 us
    pallas_call x9, Pallas kernels, call(): pl.pallas_call(kernel, name=name, out_shape=tuple(outs), in_specs=specs o...  9.96 us
    ppermute x2, waiting for transfers between devices, exchange_rows(): got_c = lax.ppermute(tail, 'gx', [(i, i ^ 4) for i in range(N_GX)])  5.53 us
    ppermute x2, starting transfers between devices, exchange_rows(): got_c = lax.ppermute(tail, 'gx', [(i, i ^ 4) for i in range(N_GX)])  4.33 us
    ppermute x3, waiting for transfers between devices, sum_everywhere(): lax.ppermute(x, 'gx', [(i, (i + 2 * k) % N_GX) for i in range(N_GX)])  4.24 us
    ppermute x3, starting transfers between devices, sum_everywhere(): lax.ppermute(x, 'gx', [(i, (i + 2 * k) % N_GX) for i in range(N_GX)])  3.91 us
  transfers between devices with their start and end apart: 32, of which 19 were waited for; matrix products, arithmetic and copies ran while one was open for 1% of the time, Pallas kernels for 2%

profile of v2, /device:TPU:0, one launch (start us, length us, event | category | flops | bytes accessed | tf_op | source)
XLA Modules:
  0.0 105.1 jit_solution(13419304412737273438)
XLA Ops:
  0.6 4.0 %collective-permute-start.3 = (s32[1,128]{1,0:T(1,128)}, s32[1,128]{1,0:T(1,128)S(1)}, u32[]{:S(2)}, u32[]{:S(2)}) collective-permute-start(s32[1,128]{1,0:T(1,128)} %param.19), channel_id=1, source_target_pairs={{0,2},{1,3},{2,0},{3,1},{4,6},{5,7},{6,4},{7,5},{8,10},{9,11},{10,... | collective-permute-start | bytes 1544 | tf_op jit(solution)/shard_map/ppermute | solution.py:487
  5.8 1.9 %prepare.1 = (f32[2,8,16,128]{3,2,1,0:T(8,128)S(1)}, f32[2,8,16,128]{3,2,1,0:T(8,128)S(1)}, f32[2,8,16,128]{3,2,1,0:T(8,128)S(1)}, f32[2,8,16,128]{3,2,1,0:T(8,1...) custom-call(s32[2]{0:T(128)S(1)} %pad_add_fusion.1.idx.refs_0_, ...), custom_call_target="tpu_custom_call" | custom-call | tf_op jit(solution)/shard_map/prepare/pallas_call | solution.py:475
  7.7 1.3 %collective-permute-start = (f32[2,8,128]{2,1,0:T(8,128)S(1)}, f32[2,8,128]{2,1,0:T(8,128)S(1)}, u32[]{:S(2)}, u32[]{:S(2)}) collective-permute-start(f32[2,8,128]{2,1,0:T(8,128)S(1)} %get-tuple-element.35), channel_id=1, source_target_pairs={{0,16},{16,32},{32,48},{48,64},{64,80},{80,96},{96,112},{1,17},{17... | collective-permute-start | bytes 24584 | tf_op jit(solution)/shard_map/ppermute | solution.py:528
  9.0 3.0 %collective-permute-start.1 = (f32[2,16,128]{2,1,0:T(8,128)S(1)}, f32[2,16,128]{2,1,0:T(8,128)S(1)}, u32[]{:S(2)}, u32[]{:S(2)}) collective-permute-start(f32[2,16,128]{2,1,0:T(8,128)S(1)} %get-tuple-element.36), channel_id=1, source_target_pairs={{0,1},{1,2},{2,3},{3,4},{4,5},{5,6},{6,7},{7,8},{8,9},{9,10},{10,1... | collective-permute-start | bytes 49160 | tf_op jit(solution)/shard_map/ppermute | solution.py:529
  12.1 3.1 %collective-permute-start.7 = (s32[4,128]{1,0:T(4,128)S(1)}, s32[4,128]{1,0:T(4,128)S(1)}, u32[]{:S(2)}, u32[]{:S(2)}) collective-permute-start(s32[4,128]{1,0:T(4,128)S(1)} %pad_add_fusion.brk_0), channel_id=1, source_target_pairs={{0,12},{1,13},{2,14},{3,15},{4,8},{5,9},{6,10},{7,11},{8,4},{9,5},... | collective-permute-start | bytes 6152 | tf_op jit(solution)/shard_map/ppermute | solution.py:487
  17.0 3.3 %collective-permute-done.6.brk_2 = s32[4,128]{1,0:T(4,128)S(1)} collective-permute-done((s32[4,128]{1,0:T(4,128)S(1)}, s32[4,128]{1,0:T(4,128)S(1)}, u32[]{:S(2)}, u32[]{:S(2)}) %collective-permute-start.6) | collective-permute-done | bytes 2080 | tf_op jit(solution)/shard_map/ppermute | solution.py:487
  21.2 2.3 %collective-permute-start.10 = (f32[20,16,128]{2,1,0:T(8,128)S(1)}, f32[20,16,128]{2,1,0:T(8,128)S(1)}, u32[]{:S(2)}, u32[]{:S(2)}) collective-permute-start(f32[20,16,128]{2,1,0:T(8,128)S(1)} %get-tuple-element.37.refs_1_), channel_id=1, source_target_pairs={{0,3},{1,2},{2,1},{3,0},{4,7},{5,6},{6,5},{7,4},{8,11},{9,10},{10,... | collective-permute-start | bytes 491528 | tf_op jit(solution)/shard_map/ppermute | solution.py:487
  23.6 1.7 %collective-permute-start.9 = (f32[20,16,128]{2,1,0:T(8,128)S(1)}, f32[20,16,128]{2,1,0:T(8,128)S(1)}, u32[]{:S(2)}, u32[]{:S(2)}) collective-permute-start(f32[20,16,128]{2,1,0:T(8,128)S(1)} %get-tuple-element.37.refs_1_), channel_id=1, source_target_pairs={{0,2},{1,3},{2,0},{3,1},{4,6},{5,7},{6,4},{7,5},{8,10},{9,11},{10,... | collective-permute-start | bytes 491528 | tf_op jit(solution)/shard_map/ppermute | solution.py:487
  26.5 6.2 %collective-permute-done.10.refs_4_ = f32[20,16,128]{2,1,0:T(8,128)S(1)} collective-permute-done((f32[20,16,128]{2,1,0:T(8,128)S(1)}, f32[20,16,128]{2,1,0:T(8,128)S(1)}, u32[]{:S(2)}, u32[]{:S(2)}) %collective-permute-start.10) | collective-permute-done | bytes 163872 | tf_op jit(solution)/shard_map/ppermute | solution.py:487
  35.1 1.2 %collective-permute-start.12 = (f32[20,16,128]{2,1,0:T(8,128)S(1)}, f32[20,16,128]{2,1,0:T(8,128)S(1)}, u32[]{:S(2)}, u32[]{:S(2)}) collective-permute-start(f32[20,16,128]{2,1,0:T(8,128)S(1)} %group_total.1.refs_5_), channel_id=1, source_target_pairs={{0,8},{1,9},{2,10},{3,11},{4,12},{5,13},{6,14},{7,15},{8,0},{9,1},... | collective-permute-start | bytes 491528 | tf_op jit(solution)/shard_map/ppermute | solution.py:487
  36.3 1.9 %collective-permute-start.11 = (f32[20,16,128]{2,1,0:T(8,128)S(1)}, f32[20,16,128]{2,1,0:T(8,128)S(1)}, u32[]{:S(2)}, u32[]{:S(2)}) collective-permute-start(f32[20,16,128]{2,1,0:T(8,128)S(1)} %group_total.1.refs_5_), channel_id=1, source_target_pairs={{0,4},{1,5},{2,6},{3,7},{4,0},{5,1},{6,2},{7,3},{8,12},{9,13},{10,... | collective-permute-start | bytes 491528 | tf_op jit(solution)/shard_map/ppermute | solution.py:487
  38.2 6.1 %collective-permute-done.13.refs_8_ = f32[20,16,128]{2,1,0:T(8,128)S(1)} collective-permute-done((f32[20,16,128]{2,1,0:T(8,128)S(1)}, f32[20,16,128]{2,1,0:T(8,128)S(1)}, u32[]{:S(2)}, u32[]{:S(2)}) %collective-permute-start.13) | collective-permute-done | bytes 163872 | tf_op jit(solution)/shard_map/ppermute | solution.py:487
  45.0 1.4 %solve_first.1 = (f32[2,8,16,128]{3,2,1,0:T(8,128)S(1)}, f32[4,16,128]{2,1,0:T(8,128)S(1)}, f32[24,128]{1,0:T(8,128)S(1)}, f32[24,128]{1,0:T(8,128)S(1)}) custom-call(s32[2]{0:T(128)S(1)} %pad_add_fusion.1.idx.refs_0_, f32[20,16,128]{2,1,0:T(8,128)S(1)} %get-tuple-element.37.refs_1_, f32[20,16,128]{2,1,0:T(8,128)S(1)} %collective-permute-done.8.refs_2_, ...), custom_call_target="tpu_custom_call" | custom-call | tf_op jit(solution)/shard_map/solve_first/pallas_call | solution.py:475
  46.4 1.2 %collective-permute-done.14.got_a = f32[24,128]{1,0:T(8,128)S(1)} collective-permute-done((f32[24,128]{1,0:T(8,128)S(1)}, f32[24,128]{1,0:T(8,128)S(1)}, u32[]{:S(2)}, u32[]{:S(2)}) %collective-permute-start.14) | collective-permute-done | bytes 12320 | tf_op jit(solution)/shard_map/ppermute | solution.py:491
  47.7 2.0 %collective-permute-start.17 = (f32[8,128]{1,0:T(8,128)S(1)}, f32[8,128]{1,0:T(8,128)S(1)}, u32[]{:S(2)}, u32[]{:S(2)}) collective-permute-start(f32[8,128]{1,0:T(8,128)S(1)} %slice.8), channel_id=1, source_target_pairs={{0,96},{16,48},{32,0},{48,80},{64,32},{80,112},{96,64},{112,16},{1... | collective-permute-start | bytes 12296 | tf_op jit(solution)/shard_map/ppermute | solution.py:497
  49.7 1.8 %collective-permute-start.16 = (f32[8,128]{1,0:T(8,128)S(1)}, f32[8,128]{1,0:T(8,128)S(1)}, u32[]{:S(2)}, u32[]{:S(2)}) collective-permute-start(f32[8,128]{1,0:T(8,128)S(1)} %slice.8), channel_id=1, source_target_pairs={{0,64},{16,80},{32,96},{48,112},{64,0},{80,16},{96,32},{112,48},{1... | collective-permute-start | bytes 12296 | tf_op jit(solution)/shard_map/ppermute | solution.py:496
  51.6 3.3 %collective-permute-done.16.got_c = f32[8,128]{1,0:T(8,128)S(1)} collective-permute-done((f32[8,128]{1,0:T(8,128)S(1)}, f32[8,128]{1,0:T(8,128)S(1)}, u32[]{:S(2)}, u32[]{:S(2)}) %collective-permute-start.16) | collective-permute-done | bytes 4128 | tf_op jit(solution)/shard_map/ppermute | solution.py:496
  55.8 2.1 %collective-permute-start.20 = (f32[4,16,128]{2,1,0:T(8,128)S(1)}, f32[4,16,128]{2,1,0:T(8,128)S(1)}, u32[]{:S(2)}, u32[]{:S(2)}) collective-permute-start(f32[4,16,128]{2,1,0:T(8,128)S(1)} %get-tuple-element.48.refs_5_.refs_9_), channel_id=1, source_target_pairs={{0,3},{1,2},{2,1},{3,0},{4,7},{5,6},{6,5},{7,4},{8,11},{9,10},{10,... | collective-permute-start | bytes 98312 | tf_op jit(solution)/shard_map/ppermute | solution.py:487
  58.0 1.9 %collective-permute-start.19 = (f32[4,16,128]{2,1,0:T(8,128)S(1)}, f32[4,16,128]{2,1,0:T(8,128)S(1)}, u32[]{:S(2)}, u32[]{:S(2)}) collective-permute-start(f32[4,16,128]{2,1,0:T(8,128)S(1)} %get-tuple-element.48.refs_5_.refs_9_), channel_id=1, source_target_pairs={{0,2},{1,3},{2,0},{3,1},{4,6},{5,7},{6,4},{7,5},{8,10},{9,11},{10,... | collective-permute-start | bytes 98312 | tf_op jit(solution)/shard_map/ppermute | solution.py:487
  61.0 2.4 %collective-permute-done.19.refs_7_.refs_11_ = f32[4,16,128]{2,1,0:T(8,128)S(1)} collective-permute-done((f32[4,16,128]{2,1,0:T(8,128)S(1)}, f32[4,16,128]{2,1,0:T(8,128)S(1)}, u32[]{:S(2)}, u32[]{:S(2)}) %collective-permute-start.19) | collective-permute-done | bytes 32800 | tf_op jit(solution)/shard_map/ppermute | solution.py:487
  64.5 2.0 %collective-permute-start.23 = (f32[4,16,128]{2,1,0:T(8,128)S(1)}, f32[4,16,128]{2,1,0:T(8,128)S(1)}, u32[]{:S(2)}, u32[]{:S(2)}) collective-permute-start(f32[4,16,128]{2,1,0:T(8,128)S(1)} %group_total_again.1.refs_13_), channel_id=1, source_target_pairs={{0,12},{1,13},{2,14},{3,15},{4,8},{5,9},{6,10},{7,11},{8,4},{9,5},... | collective-permute-start | bytes 98312 | tf_op jit(solution)/shard_map/ppermute | solution.py:487
  66.5 1.2 %collective-permute-start.22 = (f32[4,16,128]{2,1,0:T(8,128)S(1)}, f32[4,16,128]{2,1,0:T(8,128)S(1)}, u32[]{:S(2)}, u32[]{:S(2)}) collective-permute-start(f32[4,16,128]{2,1,0:T(8,128)S(1)} %group_total_again.1.refs_13_), channel_id=1, source_target_pairs={{0,8},{1,9},{2,10},{3,11},{4,12},{5,13},{6,14},{7,15},{8,0},{9,1},... | collective-permute-start | bytes 98312 | tf_op jit(solution)/shard_map/ppermute | solution.py:487
  69.7 2.2 %collective-permute-done.22.refs_15_ = f32[4,16,128]{2,1,0:T(8,128)S(1)} collective-permute-done((f32[4,16,128]{2,1,0:T(8,128)S(1)}, f32[4,16,128]{2,1,0:T(8,128)S(1)}, u32[]{:S(2)}, u32[]{:S(2)}) %collective-permute-start.22) | collective-permute-done | bytes 32800 | tf_op jit(solution)/shard_map/ppermute | solution.py:487
  71.9 1.4 %solve_second.1 = (f32[2,8,16,128]{3,2,1,0:T(8,128)S(1)}, f32[4,16,128]{2,1,0:T(8,128)S(1)}, f32[24,128]{1,0:T(8,128)S(1)}, f32[24,128]{1,0:T(8,128)S(1)}) custom-call(s32[2]{0:T(128)S(1)} %pad_add_fusion.1.idx.refs_0_, f32[20,16,128]{2,1,0:T(8,128)S(1)} %get-tuple-element.37.refs_1_, f32[20,16,128]{2,1,0:T(8,128)S(1)} %collective-permute-done.8.refs_2_, ...), custom_call_target="tpu_custom_call" | custom-call | tf_op jit(solution)/shard_map/solve_second/pallas_call | solution.py:475
  73.4 1.2 %collective-permute-done.24.got_a = f32[24,128]{1,0:T(8,128)S(1)} collective-permute-done((f32[24,128]{1,0:T(8,128)S(1)}, f32[24,128]{1,0:T(8,128)S(1)}, u32[]{:S(2)}, u32[]{:S(2)}) %collective-permute-start.24) | collective-permute-done | bytes 12320 | tf_op jit(solution)/shard_map/ppermute | solution.py:491
  76.0 2.5 %collective-permute-start.26 = (f32[8,128]{1,0:T(8,128)S(1)}, f32[8,128]{1,0:T(8,128)S(1)}, u32[]{:S(2)}, u32[]{:S(2)}) collective-permute-start(f32[8,128]{1,0:T(8,128)S(1)} %slice.9), channel_id=1, source_target_pairs={{0,64},{16,80},{32,96},{48,112},{64,0},{80,16},{96,32},{112,48},{1... | collective-permute-start | bytes 12296 | tf_op jit(solution)/shard_map/ppermute | solution.py:496
  78.9 2.3 %collective-permute-done.26.got_c = f32[8,128]{1,0:T(8,128)S(1)} collective-permute-done((f32[8,128]{1,0:T(8,128)S(1)}, f32[8,128]{1,0:T(8,128)S(1)}, u32[]{:S(2)}, u32[]{:S(2)}) %collective-permute-start.26) | collective-permute-done | bytes 4128 | tf_op jit(solution)/shard_map/ppermute | solution.py:496
  82.2 1.2 %collective-permute-done.28 = f32[8,128]{1,0:T(8,128)S(1)} collective-permute-done((f32[8,128]{1,0:T(8,128)S(1)}, f32[8,128]{1,0:T(8,128)S(1)}, u32[]{:S(2)}, u32[]{:S(2)}) %collective-permute-start.28) | collective-permute-done | bytes 4128 | tf_op jit(solution)/shard_map/ppermute | solution.py:502
  83.8 2.8 %collective-permute-start.30 = (f32[8,128]{1,0:T(8,128)S(1)}, f32[8,128]{1,0:T(8,128)S(1)}, u32[]{:S(2)}, u32[]{:S(2)}) collective-permute-start(f32[8,128]{1,0:T(8,128)S(1)} %add.40), channel_id=1, source_target_pairs={{0,64},{16,80},{32,96},{48,112},{64,0},{80,16},{96,32},{112,48},{1... | collective-permute-start | bytes 12296 | tf_op jit(solution)/shard_map/ppermute | solution.py:503
  87.2 1.7 %collective-permute-done.30 = f32[8,128]{1,0:T(8,128)S(1)} collective-permute-done((f32[8,128]{1,0:T(8,128)S(1)}, f32[8,128]{1,0:T(8,128)S(1)}, u32[]{:S(2)}, u32[]{:S(2)}) %collective-permute-start.30) | collective-permute-done | bytes 4128 | tf_op jit(solution)/shard_map/ppermute | solution.py:503
  88.9 2.5 %collective-permute-done.29 = f32[8,128]{1,0:T(8,128)S(1)} collective-permute-done((f32[8,128]{1,0:T(8,128)S(1)}, f32[8,128]{1,0:T(8,128)S(1)}, u32[]{:S(2)}, u32[]{:S(2)}) %collective-permute-start.29) | collective-permute-done | bytes 4128 | tf_op jit(solution)/shard_map/ppermute | solution.py:503
  91.5 12.7 %all_to_all.5.got = f32[16,8,128]{2,1,0:T(8,128)S(1)} all-to-all(f32[16,8,128]{2,1,0:T(8,128)S(1)} %broadcast_in_dim.19), channel_id=1, replica_groups=mesh['gx'=8,'gy'=16] {'gy'}, dimensions={0} | all-to-all | bytes 131072 | tf_op jit(solution)/shard_map/all_to_all | solution.py:506
  (72 shorter events, 18.3 us)
Async XLA Ops:
  0.6 11.4 %collective-permute-start.3 = (s32[1,128]{1,0:T(1,128)}, s32[1,128]{1,0:T(1,128)S(1)}, u32[]{:S(2)}, u32[]{:S(2)}) collective-permute-start(s32[1,128]{1,0:T(1,128)} %param.19), channel_id=1, source_target_pairs={{0,2},{1,3},{2,0},{3,1},{4,6},{5,7},{6,4},{7,5},{8,10},{9,11},{10,... | collective-permute-start | bytes 1544 | tf_op jit(solution)/shard_map/ppermute | solution.py:487
  4.7 7.4 %collective-permute-start.2 = (s32[1,128]{1,0:T(1,128)}, s32[1,128]{1,0:T(1,128)S(1)}, u32[]{:S(2)}, u32[]{:S(2)}) collective-permute-start(s32[1,128]{1,0:T(1,128)} %param.19), channel_id=1, source_target_pairs={{0,1},{1,0},{2,3},{3,2},{4,5},{5,4},{6,7},{7,6},{8,9},{9,8},{10,11... | collective-permute-start | bytes 1544 | tf_op jit(solution)/shard_map/ppermute | solution.py:487
  5.7 6.4 %collective-permute-start.4 = (s32[1,128]{1,0:T(1,128)}, s32[1,128]{1,0:T(1,128)S(1)}, u32[]{:S(2)}, u32[]{:S(2)}) collective-permute-start(s32[1,128]{1,0:T(1,128)} %param.19), channel_id=1, source_target_pairs={{0,3},{1,2},{2,1},{3,0},{4,7},{5,6},{6,5},{7,4},{8,11},{9,10},{10,... | collective-permute-start | bytes 1544 | tf_op jit(solution)/shard_map/ppermute | solution.py:487
  7.7 12.6 %collective-permute-start = (f32[2,8,128]{2,1,0:T(8,128)S(1)}, f32[2,8,128]{2,1,0:T(8,128)S(1)}, u32[]{:S(2)}, u32[]{:S(2)}) collective-permute-start(f32[2,8,128]{2,1,0:T(8,128)S(1)} %get-tuple-element.35), channel_id=1, source_target_pairs={{0,16},{16,32},{32,48},{48,64},{64,80},{80,96},{96,112},{1,17},{17... | collective-permute-start | bytes 24584 | tf_op jit(solution)/shard_map/ppermute | solution.py:528
  9.0 11.3 %collective-permute-start.1 = (f32[2,16,128]{2,1,0:T(8,128)S(1)}, f32[2,16,128]{2,1,0:T(8,128)S(1)}, u32[]{:S(2)}, u32[]{:S(2)}) collective-permute-start(f32[2,16,128]{2,1,0:T(8,128)S(1)} %get-tuple-element.36), channel_id=1, source_target_pairs={{0,1},{1,2},{2,3},{3,4},{4,5},{5,6},{6,7},{7,8},{8,9},{9,10},{10,1... | collective-permute-start | bytes 49160 | tf_op jit(solution)/shard_map/ppermute | solution.py:529
  12.1 4.9 %collective-permute-start.7 = (s32[4,128]{1,0:T(4,128)S(1)}, s32[4,128]{1,0:T(4,128)S(1)}, u32[]{:S(2)}, u32[]{:S(2)}) collective-permute-start(s32[4,128]{1,0:T(4,128)S(1)} %pad_add_fusion.brk_0), channel_id=1, source_target_pairs={{0,12},{1,13},{2,14},{3,15},{4,8},{5,9},{6,10},{7,11},{8,4},{9,5},... | collective-permute-start | bytes 6152 | tf_op jit(solution)/shard_map/ppermute | solution.py:487
  15.2 5.1 %collective-permute-start.6 = (s32[4,128]{1,0:T(4,128)S(1)}, s32[4,128]{1,0:T(4,128)S(1)}, u32[]{:S(2)}, u32[]{:S(2)}) collective-permute-start(s32[4,128]{1,0:T(4,128)S(1)} %pad_add_fusion.brk_0), channel_id=1, source_target_pairs={{0,8},{1,9},{2,10},{3,11},{4,12},{5,13},{6,14},{7,15},{8,0},{9,1},... | collective-permute-start | bytes 6152 | tf_op jit(solution)/shard_map/ppermute | solution.py:487
  15.8 4.5 %collective-permute-start.5 = (s32[4,128]{1,0:T(4,128)S(1)}, s32[4,128]{1,0:T(4,128)S(1)}, u32[]{:S(2)}, u32[]{:S(2)}) collective-permute-start(s32[4,128]{1,0:T(4,128)S(1)} %pad_add_fusion.brk_0), channel_id=1, source_target_pairs={{0,4},{1,5},{2,6},{3,7},{4,0},{5,1},{6,2},{7,3},{8,12},{9,13},{10,... | collective-permute-start | bytes 6152 | tf_op jit(solution)/shard_map/ppermute | solution.py:487
  21.2 11.4 %collective-permute-start.10 = (f32[20,16,128]{2,1,0:T(8,128)S(1)}, f32[20,16,128]{2,1,0:T(8,128)S(1)}, u32[]{:S(2)}, u32[]{:S(2)}) collective-permute-start(f32[20,16,128]{2,1,0:T(8,128)S(1)} %get-tuple-element.37.refs_1_), channel_id=1, source_target_pairs={{0,3},{1,2},{2,1},{3,0},{4,7},{5,6},{6,5},{7,4},{8,11},{9,10},{10,... | collective-permute-start | bytes 491528 | tf_op jit(solution)/shard_map/ppermute | solution.py:487
  23.6 9.1 %collective-permute-start.9 = (f32[20,16,128]{2,1,0:T(8,128)S(1)}, f32[20,16,128]{2,1,0:T(8,128)S(1)}, u32[]{:S(2)}, u32[]{:S(2)}) collective-permute-start(f32[20,16,128]{2,1,0:T(8,128)S(1)} %get-tuple-element.37.refs_1_), channel_id=1, source_target_pairs={{0,2},{1,3},{2,0},{3,1},{4,6},{5,7},{6,4},{7,5},{8,10},{9,11},{10,... | collective-permute-start | bytes 491528 | tf_op jit(solution)/shard_map/ppermute | solution.py:487
  25.3 8.0 %collective-permute-start.8 = (f32[20,16,128]{2,1,0:T(8,128)S(1)}, f32[20,16,128]{2,1,0:T(8,128)S(1)}, u32[]{:S(2)}, u32[]{:S(2)}) collective-permute-start(f32[20,16,128]{2,1,0:T(8,128)S(1)} %get-tuple-element.37.refs_1_), channel_id=1, source_target_pairs={{0,1},{1,0},{2,3},{3,2},{4,5},{5,4},{6,7},{7,6},{8,9},{9,8},{10,11... | collective-permute-start | bytes 491528 | tf_op jit(solution)/shard_map/ppermute | solution.py:487
  34.0 10.3 %collective-permute-start.13 = (f32[20,16,128]{2,1,0:T(8,128)S(1)}, f32[20,16,128]{2,1,0:T(8,128)S(1)}, u32[]{:S(2)}, u32[]{:S(2)}) collective-permute-start(f32[20,16,128]{2,1,0:T(8,128)S(1)} %group_total.1.refs_5_), channel_id=1, source_target_pairs={{0,12},{1,13},{2,14},{3,15},{4,8},{5,9},{6,10},{7,11},{8,4},{9,5},... | collective-permute-start | bytes 491528 | tf_op jit(solution)/shard_map/ppermute | solution.py:487
  35.1 9.2 %collective-permute-start.12 = (f32[20,16,128]{2,1,0:T(8,128)S(1)}, f32[20,16,128]{2,1,0:T(8,128)S(1)}, u32[]{:S(2)}, u32[]{:S(2)}) collective-permute-start(f32[20,16,128]{2,1,0:T(8,128)S(1)} %group_total.1.refs_5_), channel_id=1, source_target_pairs={{0,8},{1,9},{2,10},{3,11},{4,12},{5,13},{6,14},{7,15},{8,0},{9,1},... | collective-permute-start | bytes 491528 | tf_op jit(solution)/shard_map/ppermute | solution.py:487
  36.3 8.7 %collective-permute-start.11 = (f32[20,16,128]{2,1,0:T(8,128)S(1)}, f32[20,16,128]{2,1,0:T(8,128)S(1)}, u32[]{:S(2)}, u32[]{:S(2)}) collective-permute-start(f32[20,16,128]{2,1,0:T(8,128)S(1)} %group_total.1.refs_5_), channel_id=1, source_target_pairs={{0,4},{1,5},{2,6},{3,7},{4,0},{5,1},{6,2},{7,3},{8,12},{9,13},{10,... | collective-permute-start | bytes 491528 | tf_op jit(solution)/shard_map/ppermute | solution.py:487
  46.4 1.2 %collective-permute-start.14 = (f32[24,128]{1,0:T(8,128)S(1)}, f32[24,128]{1,0:T(8,128)S(1)}, u32[]{:S(2)}, u32[]{:S(2)}) collective-permute-start(f32[24,128]{1,0:T(8,128)S(1)} %get-tuple-element.40), channel_id=1, source_target_pairs={{0,16},{16,0},{32,48},{48,32},{64,80},{80,64},{96,112},{112,96},{1... | collective-permute-start | bytes 36872 | tf_op jit(solution)/shard_map/ppermute | solution.py:491
  47.7 7.2 %collective-permute-start.15 = (f32[24,128]{1,0:T(8,128)S(1)}, f32[24,128]{1,0:T(8,128)S(1)}, u32[]{:S(2)}, u32[]{:S(2)}) collective-permute-start(f32[24,128]{1,0:T(8,128)S(1)} %select_add_fusion.1.sent_b), channel_id=1, source_target_pairs={{0,112},{16,32},{32,16},{48,64},{64,48},{80,96},{96,80},{112,0},{1... | collective-permute-start | bytes 36872 | tf_op jit(solution)/shard_map/ppermute | solution.py:494
  47.7 3.8 %collective-permute-start.17 = (f32[8,128]{1,0:T(8,128)S(1)}, f32[8,128]{1,0:T(8,128)S(1)}, u32[]{:S(2)}, u32[]{:S(2)}) collective-permute-start(f32[8,128]{1,0:T(8,128)S(1)} %slice.8), channel_id=1, source_target_pairs={{0,96},{16,48},{32,0},{48,80},{64,32},{80,112},{96,64},{112,16},{1... | collective-permute-start | bytes 12296 | tf_op jit(solution)/shard_map/ppermute | solution.py:497
  49.7 5.1 %collective-permute-start.16 = (f32[8,128]{1,0:T(8,128)S(1)}, f32[8,128]{1,0:T(8,128)S(1)}, u32[]{:S(2)}, u32[]{:S(2)}) collective-permute-start(f32[8,128]{1,0:T(8,128)S(1)} %slice.8), channel_id=1, source_target_pairs={{0,64},{16,80},{32,96},{48,112},{64,0},{80,16},{96,32},{112,48},{1... | collective-permute-start | bytes 12296 | tf_op jit(solution)/shard_map/ppermute | solution.py:496
  55.8 5.2 %collective-permute-start.20 = (f32[4,16,128]{2,1,0:T(8,128)S(1)}, f32[4,16,128]{2,1,0:T(8,128)S(1)}, u32[]{:S(2)}, u32[]{:S(2)}) collective-permute-start(f32[4,16,128]{2,1,0:T(8,128)S(1)} %get-tuple-element.48.refs_5_.refs_9_), channel_id=1, source_target_pairs={{0,3},{1,2},{2,1},{3,0},{4,7},{5,6},{6,5},{7,4},{8,11},{9,10},{10,... | collective-permute-start | bytes 98312 | tf_op jit(solution)/shard_map/ppermute | solution.py:487
  58.0 5.4 %collective-permute-start.19 = (f32[4,16,128]{2,1,0:T(8,128)S(1)}, f32[4,16,128]{2,1,0:T(8,128)S(1)}, u32[]{:S(2)}, u32[]{:S(2)}) collective-permute-start(f32[4,16,128]{2,1,0:T(8,128)S(1)} %get-tuple-element.48.refs_5_.refs_9_), channel_id=1, source_target_pairs={{0,2},{1,3},{2,0},{3,1},{4,6},{5,7},{6,4},{7,5},{8,10},{9,11},{10,... | collective-permute-start | bytes 98312 | tf_op jit(solution)/shard_map/ppermute | solution.py:487
  59.9 3.9 %collective-permute-start.18 = (f32[4,16,128]{2,1,0:T(8,128)S(1)}, f32[4,16,128]{2,1,0:T(8,128)S(1)}, u32[]{:S(2)}, u32[]{:S(2)}) collective-permute-start(f32[4,16,128]{2,1,0:T(8,128)S(1)} %get-tuple-element.48.refs_5_.refs_9_), channel_id=1, source_target_pairs={{0,1},{1,0},{2,3},{3,2},{4,5},{5,4},{6,7},{7,6},{8,9},{9,8},{10,11... | collective-permute-start | bytes 98312 | tf_op jit(solution)/shard_map/ppermute | solution.py:487
  64.5 5.2 %collective-permute-start.23 = (f32[4,16,128]{2,1,0:T(8,128)S(1)}, f32[4,16,128]{2,1,0:T(8,128)S(1)}, u32[]{:S(2)}, u32[]{:S(2)}) collective-permute-start(f32[4,16,128]{2,1,0:T(8,128)S(1)} %group_total_again.1.refs_13_), channel_id=1, source_target_pairs={{0,12},{1,13},{2,14},{3,15},{4,8},{5,9},{6,10},{7,11},{8,4},{9,5},... | collective-permute-start | bytes 98312 | tf_op jit(solution)/shard_map/ppermute | solution.py:487
  66.5 5.4 %collective-permute-start.22 = (f32[4,16,128]{2,1,0:T(8,128)S(1)}, f32[4,16,128]{2,1,0:T(8,128)S(1)}, u32[]{:S(2)}, u32[]{:S(2)}) collective-permute-start(f32[4,16,128]{2,1,0:T(8,128)S(1)} %group_total_again.1.refs_13_), channel_id=1, source_target_pairs={{0,8},{1,9},{2,10},{3,11},{4,12},{5,13},{6,14},{7,15},{8,0},{9,1},... | collective-permute-start | bytes 98312 | tf_op jit(solution)/shard_map/ppermute | solution.py:487
  67.7 4.2 %collective-permute-start.21 = (f32[4,16,128]{2,1,0:T(8,128)S(1)}, f32[4,16,128]{2,1,0:T(8,128)S(1)}, u32[]{:S(2)}, u32[]{:S(2)}) collective-permute-start(f32[4,16,128]{2,1,0:T(8,128)S(1)} %group_total_again.1.refs_13_), channel_id=1, source_target_pairs={{0,4},{1,5},{2,6},{3,7},{4,0},{5,1},{6,2},{7,3},{8,12},{9,13},{10,... | collective-permute-start | bytes 98312 | tf_op jit(solution)/shard_map/ppermute | solution.py:487
  73.4 1.2 %collective-permute-start.24 = (f32[24,128]{1,0:T(8,128)S(1)}, f32[24,128]{1,0:T(8,128)S(1)}, u32[]{:S(2)}, u32[]{:S(2)}) collective-permute-start(f32[24,128]{1,0:T(8,128)S(1)} %get-tuple-element.50), channel_id=1, source_target_pairs={{0,16},{16,0},{32,48},{48,32},{64,80},{80,64},{96,112},{112,96},{1... | collective-permute-start | bytes 36872 | tf_op jit(solution)/shard_map/ppermute | solution.py:491
  74.6 6.5 %collective-permute-start.25 = (f32[24,128]{1,0:T(8,128)S(1)}, f32[24,128]{1,0:T(8,128)S(1)}, u32[]{:S(2)}, u32[]{:S(2)}) collective-permute-start(f32[24,128]{1,0:T(8,128)S(1)} %select_add_fusion.sent_b), channel_id=1, source_target_pairs={{0,112},{16,32},{32,16},{48,64},{64,48},{80,96},{96,80},{112,0},{1... | collective-permute-start | bytes 36872 | tf_op jit(solution)/shard_map/ppermute | solution.py:494
  75.2 3.6 %collective-permute-start.27 = (f32[8,128]{1,0:T(8,128)S(1)}, f32[8,128]{1,0:T(8,128)S(1)}, u32[]{:S(2)}, u32[]{:S(2)}) collective-permute-start(f32[8,128]{1,0:T(8,128)S(1)} %slice.9), channel_id=1, source_target_pairs={{0,96},{16,48},{32,0},{48,80},{64,32},{80,112},{96,64},{112,16},{1... | collective-permute-start | bytes 12296 | tf_op jit(solution)/shard_map/ppermute | solution.py:497
  76.0 5.1 %collective-permute-start.26 = (f32[8,128]{1,0:T(8,128)S(1)}, f32[8,128]{1,0:T(8,128)S(1)}, u32[]{:S(2)}, u32[]{:S(2)}) collective-permute-start(f32[8,128]{1,0:T(8,128)S(1)} %slice.9), channel_id=1, source_target_pairs={{0,64},{16,80},{32,96},{48,112},{64,0},{80,16},{96,32},{112,48},{1... | collective-permute-start | bytes 12296 | tf_op jit(solution)/shard_map/ppermute | solution.py:496
  82.1 1.2 %collective-permute-start.28 = (f32[8,128]{1,0:T(8,128)S(1)}, f32[8,128]{1,0:T(8,128)S(1)}, u32[]{:S(2)}, u32[]{:S(2)}) collective-permute-start(f32[8,128]{1,0:T(8,128)S(1)} %get-tuple-element.56), channel_id=1, source_target_pairs={{0,16},{16,0},{32,48},{48,32},{64,80},{80,64},{96,112},{112,96},{1... | collective-permute-start | bytes 12296 | tf_op jit(solution)/shard_map/ppermute | solution.py:502
  83.3 3.9 %collective-permute-start.31 = (f32[8,128]{1,0:T(8,128)S(1)}, f32[8,128]{1,0:T(8,128)S(1)}, u32[]{:S(2)}, u32[]{:S(2)}) collective-permute-start(f32[8,128]{1,0:T(8,128)S(1)} %add.40), channel_id=1, source_target_pairs={{0,96},{16,112},{32,0},{48,16},{64,32},{80,48},{96,64},{112,80},{1... | collective-permute-start | bytes 12296 | tf_op jit(solution)/shard_map/ppermute | solution.py:503
  83.8 5.1 %collective-permute-start.30 = (f32[8,128]{1,0:T(8,128)S(1)}, f32[8,128]{1,0:T(8,128)S(1)}, u32[]{:S(2)}, u32[]{:S(2)}) collective-permute-start(f32[8,128]{1,0:T(8,128)S(1)} %add.40), channel_id=1, source_target_pairs={{0,64},{16,80},{32,96},{48,112},{64,0},{80,16},{96,32},{112,48},{1... | collective-permute-start | bytes 12296 | tf_op jit(solution)/shard_map/ppermute | solution.py:503
  86.7 4.8 %collective-permute-start.29 = (f32[8,128]{1,0:T(8,128)S(1)}, f32[8,128]{1,0:T(8,128)S(1)}, u32[]{:S(2)}, u32[]{:S(2)}) collective-permute-start(f32[8,128]{1,0:T(8,128)S(1)} %add.40), channel_id=1, source_target_pairs={{0,32},{16,48},{32,64},{48,80},{64,96},{80,112},{96,0},{112,16},{1... | collective-permute-start | bytes 12296 | tf_op jit(solution)/shard_map/ppermute | solution.py:503
  (5 other events, 18.8 us)

commit v3 on v2

--- a/solution.py
+++ b/solution.py
@@ -152,9 +152,9 @@
     return ref.at[c][pl.ds(j, CX, stride=CY), :]
 
 
-def prepare_kernel(idx, b_h, acc_h, tx_h, ty_h, tz_h, rhs, tx_o, ty_o, tz_o, diag, cross, sx, sy, b, acc, tx_v, ty_v, tz_v, sems):
+def prepare_kernel(idx, b_h, acc_h, tx_h, ty_h, tz_h, brk_h, rhs, tx_o, ty_o, tz_o, diag, cross, sx, edge, b, acc, tx_v, ty_v, tz_v, brk, sems):
     gx, gy = idx[0], idx[1]
-    pairs = ((tx_h, tx_v), (ty_h, ty_v), (tz_h, tz_v), (acc_h, acc), (b_h, b))
+    pairs = ((ty_h, ty_v), (brk_h, brk), (tx_h, tx_v), (tz_h, tz_v), (acc_h, acc), (b_h, b))
     copies = [pltpu.make_async_copy(h, v, sems.at[i]) for i, (h, v) in enumerate(pairs)]
     for copy in copies:
         copy.start()
@@ -162,9 +162,10 @@
     last_z = lanes() == NZ - 1
     for copy in copies:
         copy.wait()
+    edge[2 * CX :, :] = jnp.broadcast_to(brk[...].astype(F32), (8, NZ))
     for c in range(2):
         sx[c] = tx_v[c, (CX - 1) * CY : CX * CY, :]
-        sy[c] = plane(ty_v, c, CY - 1)
+        edge[c * CX : (c + 1) * CX, :] = plane(ty_v, c, CY - 1)
         ly = 0.0
         for j in range(CY):
             tx = jnp.where(last_x, 0.0, plane(tx_v, c, j))
@@ -182,19 +183,43 @@
             ly = ty
 
 
-def condense_kernel(idx, diag, cross, ty, rhs, lx_in, ly_in, brk_0, brk_1, brk_2, brk_3, seg, dmat, tau_o, sinv, binv, brk):
+def relay_kernel(idx, own, m1, m2, m3, out):
+    z = idx[1] % 4
+    refs = (own, m1, m2, m3)
+    faces = own[0 : 2 * CX, :]
+    for k in (1, 2, 3):
+        faces = jnp.where(z == 3 - k, refs[k][0 : 2 * CX, :], faces)
+    out[0 : 2 * CX, :] = faces
+    out[2 * CX :, :] = jnp.zeros((8, NZ), F32)
+    for k in range(4):
+        out[pl.ds(2 * CX + jnp.bitwise_xor(z, k), 1), :] = refs[k][2 * CX : 2 * CX + 1, :]
+
+
+def condense_kernel(idx, diag, cross, ty, rhs, lx_in, *refs):
+    own, m1, m2, m3, o0, o1, o2, o3 = refs[:8]
+    seg_a, seg_b, dmat, tau_o, sinv, binv, ly_in = refs[8:15]
+    brk, near, far = refs[15:]
     gy = idx[1]
-    for k, ref in enumerate((brk_0, brk_1, brk_2, brk_3)):
+    z_at, y_at = gy % 4, gy // 4
+    for k in range(4):
+        near[jnp.bitwise_xor(z_at, k)] = (own, m1, m2, m3)[k][0 : 2 * CX, :]
+        at = jnp.bitwise_xor(y_at, k)
+        ref = (o0, o1, o2, o3)[k]
+        far[at] = ref[0 : 2 * CX, :]
         for i in range(4):
-            brk[pl.ds(jnp.bitwise_xor(gy, 4 * k + i), 1), :] = ref[i : i + 1, :]
+            brk[pl.ds(4 * at + i, 1), :] = ref[2 * CX + i : 2 * CX + i + 1, :]
     cuts = pltpu.roll(brk[...], (NZ - CY * gy) % NZ, 1)
+    before = jnp.where(y_at > 0, far[jnp.maximum(y_at - 1, 0)], 0.0)
+    before = jnp.where(z_at > 0, near[jnp.maximum(z_at - 1, 0)], before)
+    for c in range(2):
+        ly_in[c] = before[c * CX : (c + 1) * CX]
     for c in range(2):
         ly = ly_in[c]
         for j in range(CY):
             d = diag[c, j] + jnp.where(rows() == 0, lx_in[c, j : j + 1, :], 0.0)
             dmat[3 * c, j] = d + ly if j == 0 else d
         for j in range(CY + 1):
-            keep = 1.0 - cuts[:, j : j + 1].astype(F32)
+            keep = 1.0 - cuts[:, j : j + 1]
             tau_o[c, j] = (ty[c, j - 1] if j else ly) * keep
     for j in range(CY):
         dmat[1, j] = cross[0, j]
@@ -229,34 +254,45 @@
         for i in range(4):
             sinv[i, j] = s[i]
             binv[i, k] = e[i]
-    store_segment(
-        seg,
-        (columns_by(e, tau(0)), mm(e, zl), mm(s, yf), columns_by(s, tau(CY)), mv(e, z), mv(s, y)),
-        True,
-    )
-
-
-def gather_segments(position, mats, vecs, offset, mat_s, vec_s):
+    whole = (columns_by(e, tau(0)), mm(e, zl), mm(s, yf), columns_by(s, tau(CY)), mv(e, z), mv(s, y))
+    for half, ref in enumerate((seg_a, seg_b)):
+        store_segment(ref, [[x[8 * half : 8 * half + 8] for x in part] for part in whole], True)
+
+
+def gather_matrices(position, halves, mat_s):
     for k in range(4):
         at = jnp.bitwise_xor(position, k)
-        mat_s[at] = mats[k][0:16]
-        vec_s[at] = vecs[k][offset : offset + 4]
-
-
-def make_total_kernel(whole):
-    def kernel(*refs):
-        idx = refs[0]
-        if whole:
-            mats = vecs = refs[1:5]
-            out, mat_s, vec_s = refs[5:]
-        else:
-            mats, vecs = refs[1:5], refs[5:9]
-            out, mat_s, vec_s = refs[9:]
-        gather_segments(idx[1] % 4, mats, vecs, 16 if whole else 0, mat_s, vec_s)
-        segs = [load_segment(mat_s.at[m], vec_s.at[m], 0) for m in range(4)]
-        store_segment(out, join(join(segs[0], segs[1]), join(segs[2], segs[3])), whole)
-
-    return kernel
+        for half, refs in enumerate(halves):
+            mat_s[at, :, 8 * half : 8 * half + 8, :] = refs[k][0:16]
+
+
+def gather_vectors(position, vecs, vec_s):
+    for k in range(4):
+        vec_s[jnp.bitwise_xor(position, k)] = vecs[k][...]
+
+
+def gather_both(position, halves, mat_s, vec_s):
+    gather_matrices(position, halves, mat_s)
+    for k in range(4):
+        at = jnp.bitwise_xor(position, k)
+        for half, refs in enumerate(halves):
+            vec_s[at, :, 8 * half : 8 * half + 8, :] = refs[k][16:20]
+
+
+def total_half_kernel(idx, own, m1, m2, m3, out, segs_s):
+    for k, ref in enumerate((own, m1, m2, m3)):
+        segs_s[jnp.bitwise_xor(idx[1] % 4, k)] = ref[...]
+    segs = [load_segment(segs_s.at[m], segs_s.at[m], 16) for m in range(4)]
+    store_segment(out, join(join(segs[0], segs[1]), join(segs[2], segs[3])), True)
+
+
+def total_again_kernel(idx, *refs):
+    halves, vecs = (refs[0:4], refs[4:8]), refs[8:12]
+    out, mat_s, vec_s = refs[12:]
+    gather_matrices(idx[1] % 4, halves, mat_s)
+    gather_vectors(idx[1] % 4, vecs, vec_s)
+    segs = [load_segment(mat_s.at[m], vec_s.at[m], 0) for m in range(4)]
+    store_segment(out, join(join(segs[0], segs[1]), join(segs[2], segs[3])), False)
 
 
 def split3(x):
@@ -298,22 +334,21 @@
 def make_solve_kernel(whole):
     def kernel(*refs):
         idx = refs[0]
-        if whole:
-            inner, outer_ = refs[1:5], refs[5:9]
-            inner_v, outer_v = inner, outer_
-            rest = refs[9:]
-            offset = 16
-        else:
-            inner, outer_, inner_v, outer_v = refs[1:5], refs[5:9], refs[9:13], refs[13:17]
-            rest = refs[17:]
-            offset = 0
+        inner, outer = (refs[1:5], refs[5:9]), (refs[9:13], refs[13:17])
+        rest = refs[17:] if whole else refs[25:]
         sinv, tau_r, rhs, cells, wells, weights = rest[:6]
-        p_out, ends, msg_a, msg_b = rest[6:10]
-        mat_i, vec_i, mat_o, vec_o, edge = rest[10:]
+        p_out, ends, msg = rest[6:9]
+        mat_i, vec_i, mat_o, vec_o = rest[9:]
         gx, gy = idx[0], idx[1]
         z_at, y_at = gy % 4, gy // 4
-        gather_segments(z_at, inner, inner_v, offset, mat_i, vec_i)
-        gather_segments(y_at, outer_, outer_v, offset, mat_o, vec_o)
+        if whole:
+            gather_both(z_at, inner, mat_i, vec_i)
+            gather_both(y_at, outer, mat_o, vec_o)
+        else:
+            gather_matrices(z_at, inner, mat_i)
+            gather_matrices(y_at, outer, mat_o)
+            gather_vectors(z_at, refs[17:21], vec_i)
+            gather_vectors(y_at, refs[21:25], vec_o)
         zero = jnp.zeros(PLANE, F32)
         before = ((zero,) * 4, (zero,) * 2)
         after = ((zero,) * 4, (zero,) * 2)
@@ -324,7 +359,7 @@
                 m = 3 - m
                 seg = load_segment(mat_s.at[m], vec_s.at[m], 0)
                 after = choose(m > here, join_after(seg, after), after)
-        own = load_segment(inner[0], inner_v[0], offset)
+        own = load_segment(mat_i.at[z_at], vec_i.at[z_at], 0)
         ff, fl, lf, ll, gf, gl = own
         up_m, up_v = join_before(before, own)
         last = mv(inv2(one_minus(mm(up_m, after[0]))), madd(up_v, mv(up_m, after[1])))
@@ -350,8 +385,8 @@
             u = mv(sv(j), tuple(y[j][c] + tau(j + 1)[c] * u[c] for c in range(2)))
             for c in range(2):
                 p_out[c, j] = u[c]
-                edge[0, c * CY + j : c * CY + j + 1, :] = u[c][0:1, :]
-                edge[1, c * CY + j : c * CY + j + 1, :] = u[c][CX - 1 : CX, :]
+                msg[c * CY + j : c * CY + j + 1, :] = u[c][0:1, :]
+                msg[16 + c * CY + j : 17 + c * CY + j, :] = u[c][CX - 1 : CX, :]
         at_row, at_layer, at_well = slot_tables(cells, wells)
         pressure = jnp.concatenate([p_out[0, j] for j in range(CY)], axis=0)
         table = ones_of(at_layer)
@@ -360,30 +395,24 @@
         w = weights[...]
         sums, totals = row_times([w * values, w], ones_of(at_well), NT)
         tail = jnp.concatenate([sums, totals, jnp.zeros((6, W_ALL), F32)], axis=0)
-        even = gx % 2 == 0
-        low, high = edge[0], edge[1]
-        msg_a[0:16, :] = jnp.where(even, high, low)
-        msg_b[0:16, :] = jnp.where(even, low, high)
-        msg_a[16:24, :] = tail
-        msg_b[16:24, :] = tail
+        msg[32:40, :] = tail
 
     return kernel
 
 
 def apply_operator(idx, got, cells, wells, weights):
     gx = idx[0]
-    got_a, sent_b, got_b, got_c, got_d = got
-    tail = sent_b[16:24, :] + got_b[16:24, :] + got_c[...] + got_d[...]
+    tail = got[0, 32:40, :]
+    for d in range(1, N_GX):
+        tail = tail + got[d, 32:40, :]
     rates = tail[0:1] / jnp.maximum(tail[1:2], 1.0)
     at_row, at_layer, at_well = slot_tables(cells, wells)
     slot_rate = row_times([rates], ones_of(at_well), (((1,), (0,)), ((), ())))[0]
     added = jnp.where(at_layer, weights[...] * slot_rate, 0.0)
     table = ones_of(at_row)
     well_add = sum(lax.dot_general(table, part, NT, preferred_element_type=F32) for part in split3(added))
-    even = gx % 2 == 0
-    halo_a, halo_b = got_a[0:16, :], got_b[0:16, :]
-    from_after = jnp.where(gx < N_GX - 1, jnp.where(even, halo_a, halo_b), 0.0)
-    from_before = jnp.where(gx > 0, jnp.where(even, halo_b, halo_a), 0.0)
+    from_after = jnp.where(gx < N_GX - 1, got[jnp.minimum(gx + 1, N_GX - 1), 0:16, :], 0.0)
+    from_before = jnp.where(gx > 0, got[jnp.maximum(gx - 1, 0), 16:32, :], 0.0)
     return well_add, from_after, from_before
 
 
@@ -405,8 +434,8 @@
     return out
 
 
-def first_image_kernel(idx, got_a, sent_b, got_b, got_c, got_d, p, ends, dmat, tau_r, sinv, binv, rhs, tx, ty, tz, lx_in, ly_in, cells, wells, weights, q_out, e_out, vec_out, dots):
-    well_add, after, before = apply_operator(idx, (got_a, sent_b, got_b, got_c, got_d), cells, wells, weights)
+def first_image_kernel(idx, got, p, ends, dmat, tau_r, sinv, binv, rhs, tx, ty, tz, lx_in, ly_in, cells, wells, weights, q_out, e_out, vec_out, dots):
+    well_add, after, before = apply_operator(idx, got, cells, wells, weights)
     eq = jnp.zeros(PLANE, F32)
     qq = jnp.zeros(PLANE, F32)
     e = []
@@ -436,8 +465,8 @@
         vec_out[2 + c] = last[c]
 
 
-def second_image_kernel(idx, got_a, sent_b, got_b, got_c, got_d, p, ends, dmat, tx, ty, tz, lx_in, ly_in, cells, wells, weights, q_in, e_in, dots_in, s_out, dots):
-    well_add, after, before = apply_operator(idx, (got_a, sent_b, got_b, got_c, got_d), cells, wells, weights)
+def second_image_kernel(idx, got, p, ends, dmat, tx, ty, tz, lx_in, ly_in, cells, wells, weights, q_in, e_in, dots_in, s_out, dots):
+    well_add, after, before = apply_operator(idx, got, cells, wells, weights)
     sq = jnp.zeros(PLANE, F32)
     ss = jnp.zeros(PLANE, F32)
     es = jnp.zeros(PLANE, F32)
@@ -449,15 +478,19 @@
             ss = ss + s * s
             es = es + s * e_in[c, j]
     sums = [jnp.sum(x, axis=0, keepdims=True) for x in (dots_in[0], dots_in[1], sq, ss, es)]
-    dots[...] = jnp.concatenate(sums + [jnp.zeros((3, NZ), F32)], axis=0)
+    lane = lax.broadcasted_iota(jnp.int32, (1, NZ), 1)
+    row = jnp.zeros((1, NZ), F32)
+    for i, x in enumerate(sums):
+        row = jnp.where(lane == i, jnp.sum(x, axis=1, keepdims=True), row)
+    dots[...] = row
 
 
 def finish_kernel(got, p, w, q, e, s, x_out, r_out):
-    total = got[0]
-    for d in range(1, N_GY):
-        total = total + got[d]
-    total = jnp.broadcast_to(jnp.sum(total, axis=1, keepdims=True), (8, NZ))
-    eq, qq, sq, ss, es = (total[i : i + 1] for i in range(5))
+    total = jnp.sum(got[...], axis=0, keepdims=True)
+    lane = lax.broadcasted_iota(jnp.int32, (1, NZ), 1)
+    eq, qq, sq, ss, es = (
+        jnp.broadcast_to(jnp.sum(jnp.where(lane == i, total, 0.0), axis=1, keepdims=True), (1, NZ)) for i in range(5)
+    )
     rest = -eq / qq
     g = sq / qq
     k = (es - g * eq) / (ss - g * sq)
@@ -487,25 +520,6 @@
     return [block] + [lax.ppermute(block, "gy", [(i, i ^ (k * stride)) for i in range(N_GY)]) for k in (1, 2, 3)]
 
 
-def exchange_rows(msg_a, msg_b):
-    got_a = lax.ppermute(msg_a, "gx", [(i, i ^ 1) for i in range(N_GX)])
-    below = lax.broadcasted_iota(jnp.int32, msg_b.shape, 0) >= 16
-    sent_b = msg_b + jnp.where(below, got_a, 0.0)
-    got_b = lax.ppermute(sent_b, "gx", [(i, (i + 1 if i % 2 else i - 1) % N_GX) for i in range(N_GX)])
-    tail = sent_b[16:]
-    got_c = lax.ppermute(tail, "gx", [(i, i ^ 4) for i in range(N_GX)])
-    got_d = lax.ppermute(tail, "gx", [(i, (i + 2 if i % 2 else i - 2) % N_GX) for i in range(N_GX)])
-    return got_a, sent_b, got_b, got_c, got_d
-
-
-def sum_everywhere(x):
-    x = x + lax.ppermute(x, "gx", [(i, i ^ 1) for i in range(N_GX)])
-    others = [lax.ppermute(x, "gx", [(i, (i + 2 * k) % N_GX) for i in range(N_GX)]) for k in (1, 2, 3)]
-    x = x + others[0] + others[1] + others[2]
-    x = jnp.broadcast_to(x[None], (N_GY,) + x.shape)
-    return lax.all_to_all(x, "gy", split_axis=0, concat_axis=0, tiled=True)
-
-
 def body(right_side, accumulation, trans_x, trans_y, trans_z, perf_cell, perf_well, perf_weight, perf_count, breaks):
     gx, gy = lax.axis_index("gx"), lax.axis_index("gy")
     idx = jnp.stack([gx, gy]).astype(jnp.int32)
@@ -514,19 +528,20 @@
         return a.reshape(a.shape[0], CX * CY, NZ)
 
     field, block, part = (2, CY, CX, NZ), (4, CY, CX, NZ), (2, CY + 1, CX, NZ)
-    seg, vec, message = (20, CX, NZ), (4, CX, NZ), (24, NZ)
+    half, vec, message = (20, 8, NZ), (4, CX, NZ), (40, NZ)
     order = [(4, 16, CX, NZ), (4, 4, CX, NZ)]
     two, four = (2, CX * CY, NZ), (4, CX * CY, NZ)
-    cuts = swapped(jnp.concatenate(swapped(breaks, 1), axis=0), 4)
-    rhs, tx, ty, tz, diag, cross, sx, sy = call(
+    rhs, tx, ty, tz, diag, cross, sx, edge = call(
         prepare_kernel, "prepare",
-        (field, field, field, field, field, field, (2, CY, NZ), (2, CX, NZ)),
-        [two, four, two, two, two, pltpu.SemaphoreType.DMA((5,))],
-        idx, flat(right_side), flat(accumulation), flat(trans_x), flat(trans_y), flat(trans_z),
-        specs=[SMEM] + [HBM] * 5, vmem=PREPARE_VMEM,
-    )
+        (field, field, field, field, field, field, (2, CY, NZ), (40, NZ)),
+        [two, four, two, two, two, pltpu.VMEM((1, NZ), jnp.int32), pltpu.SemaphoreType.DMA((6,))],
+        idx, flat(right_side), flat(accumulation), flat(trans_x), flat(trans_y), flat(trans_z), breaks,
+        specs=[SMEM] + [HBM] * 6, vmem=PREPARE_VMEM,
+    )
+    edges = swapped(edge, 1)
     lx = lax.ppermute(sx, "gx", [(i, i + 1) for i in range(N_GX - 1)])
-    ly = lax.ppermute(sy, "gy", [(i, i + 1) for i in range(N_GY - 1)])
+    (relayed,) = call(relay_kernel, "relay", ((40, NZ),), [], idx, *edges)
+    relayed = swapped(relayed, 4)
     slots = perf_cell.shape[3]
     live = jnp.arange(slots, dtype=jnp.int32)[None, :] < perf_count.reshape(N_GX, 1)
     weights = jnp.where(live, perf_weight.reshape(N_GX, slots), 0.0).reshape(1, SLOTS_ALL)
@@ -535,36 +550,41 @@
     cells = perf_cell.reshape(1, SLOTS_ALL)
     perfs = (cells, wells, weights)
 
-    own, dmat, tau, sinv, binv = call(
-        condense_kernel, "condense", (seg, block, part, block, block),
-        [pltpu.VMEM((N_GY, NZ), jnp.int32)], idx, diag, cross, ty, rhs, lx, ly, *cuts,
-    )
-    inner = swapped(own, 1)
-    (group,) = call(make_total_kernel(True), "group_total", (seg,), order, idx, *inner)
-    outer = swapped(group, 4)
-    solve_scratch = order + order + [(2, 16, NZ)]
-    p, ends, msg_a, msg_b = call(
-        make_solve_kernel(True), "solve_first", (field, vec, message, message), solve_scratch,
+    own_a, own_b, dmat, tau, sinv, binv, ly = call(
+        condense_kernel, "condense", (half, half, block, part, block, block, (2, CX, NZ)),
+        [(N_GY, NZ), (4, 2 * CX, NZ), (4, 2 * CX, NZ)], idx, diag, cross, ty, rhs, lx, *edges, *relayed,
+    )
+    inner, outer = [], []
+    for own in (own_a, own_b):
+        inner.append(swapped(own, 1))
+    for near in inner:
+        (group,) = call(total_half_kernel, "group_total", (half,), [(4,) + half], idx, *near)
+        outer.append(swapped(group, 4))
+    inner = inner[0] + inner[1]
+    outer = outer[0] + outer[1]
+    solve_scratch = order + order
+    p, ends, msg = call(
+        make_solve_kernel(True), "solve_first", (field, vec, message), solve_scratch,
         idx, *inner, *outer, sinv, tau, rhs, *perfs,
     )
-    got = exchange_rows(msg_a, msg_b)
+    got = lax.all_gather(msg, "gx")
     q, e, own_v, dots = call(
         first_image_kernel, "first_image", (field, field, vec, (2, CX, NZ)), [],
-        idx, *got, p, ends, dmat, tau, sinv, binv, rhs, tx, ty, tz, lx, ly, *perfs,
+        idx, got, p, ends, dmat, tau, sinv, binv, rhs, tx, ty, tz, lx, ly, *perfs,
     )
     inner_v = swapped(own_v, 1)
-    (group_v,) = call(make_total_kernel(False), "group_total_again", (vec,), order, idx, *inner, *inner_v)
+    (group_v,) = call(total_again_kernel, "group_total_again", (vec,), order, idx, *inner, *inner_v)
     outer_v = swapped(group_v, 4)
-    w, ends, msg_a, msg_b = call(
-        make_solve_kernel(False), "solve_second", (field, vec, message, message), solve_scratch,
+    w, ends, msg = call(
+        make_solve_kernel(False), "solve_second", (field, vec, message), solve_scratch,
         idx, *inner, *outer, *inner_v, *outer_v, sinv, tau, e, *perfs,
     )
-    got = exchange_rows(msg_a, msg_b)
+    got = lax.all_gather(msg, "gx")
     s, dots = call(
-        second_image_kernel, "second_image", (field, (8, NZ)), [],
-        idx, *got, w, ends, dmat, tx, ty, tz, lx, ly, *perfs, q, e, dots,
-    )
-    dots = sum_everywhere(dots)
+        second_image_kernel, "second_image", (field, (1, NZ)), [],
+        idx, got, w, ends, dmat, tx, ty, tz, lx, ly, *perfs, q, e, dots,
+    )
+    dots = lax.all_gather(dots, ("gx", "gy"), axis=0, tiled=True)
     x, r = call(finish_kernel, "finish", (two, two), [], dots, p, w, q, e, s, specs=[VMEM] * 6)
     shape = (2, CX, CY, NZ)
     return x.reshape(shape), r.reshape(shape)

time: 105 us -> 138 us (1.31)
  blocking collectives: 12.7 us -> 71.5 us
  waiting for transfers between devices: 38.2 us -> 17.5 us
  starting transfers between devices: 42 us -> 34.8 us
    all_gather x0 -> x3, blocking collectives: none -> 71.5 us  [the longest x1 43.7 us: body(): dots = lax.all_gather(dots, ('gx', 'gy'), axis=0, tiled=True)]
    ppermute x13 -> x0, starting transfers between devices: 14.8 us -> none  [the longest x2 4.33 us: exchange_rows(): got_c = lax.ppermute(tail, 'gx', [(i, i ^ 4) for i in range(N_GX)])]
    ppermute x13 -> x0, waiting for transfers between devices: 13.6 us -> none  [the longest x2 5.53 us: exchange_rows(): got_c = lax.ppermute(tail, 'gx', [(i, i ^ 4) for i in range(N_GX)])]
    all_to_all x1 -> x0, blocking collectives: 12.7 us -> none  [sum_everywhere(): return lax.all_to_all(x, 'gy', split_axis=0, concat_axis=0, tiled=True)]
    ppermute x18 -> x24, waiting for transfers between devices: 24.6 us -> 16.7 us  [swapped(): lax.ppermute(block, 'gy', [(i, i ^ k * stride) for i in range(N_GY)])]
    ppermute x18 -> x24, starting transfers between devices: 25.9 us -> 33.5 us  [swapped(): lax.ppermute(block, 'gy', [(i, i ^ k * stride) for i in range(N_GY)])]
    pallas_call x9 -> x11, Pallas kernels: 9.96 us -> 11.1 us  [call(): pl.pallas_call(kernel, name=name, out_shape=tuple(outs), in_specs=specs o...]
  transfers between devices with their start and end apart: 32 -> 25, of which waited for: 19 -> 11; matrix products, arithmetic and copies ran while one was open for 1% -> 0% of each run, Pallas kernels for 2% -> 1%
where the time goes in v3:
time: 138 us; the launch traced here: 137 us
  blocking collectives  71.5 us (52%)
  starting transfers between devices  34.8 us (25%)
  waiting for transfers between devices  17.5 us (13%)
  Pallas kernels  11.1 us (8%)
    all_gather x1, blocking collectives, body(): dots = lax.all_gather(dots, ('gx', 'gy'), axis=0, tiled=True)  43.7 us
    ppermute x24, starting transfers between devices, swapped(): lax.ppermute(block, 'gy', [(i, i ^ k * stride) for i in range(N_GY)])  33.5 us
    all_gather x2, blocking collectives, body(): got = lax.all_gather(msg, 'gx')  27.8 us
    ppermute x24, waiting for transfers between devices, swapped(): lax.ppermute(block, 'gy', [(i, i ^ k * stride) for i in range(N_GY)])  16.7 us
    pallas_call x11, Pallas kernels, call(): pl.pallas_call(kernel, name=name, out_shape=tuple(outs), in_specs=specs o...  11.1 us
  transfers between devices with their start and end apart: 25, of which 11 were waited for; matrix products, arithmetic and copies ran while one was open for 0% of the time, Pallas kernels for 1%

profile of v3, /device:TPU:0, one launch (start us, length us, event | category | flops | bytes accessed | tf_op | source)
XLA Modules:
  0.0 137.0 jit_solution(9906325078309014312)
XLA Ops:
  1.4 1.9 %prepare.1 = (f32[2,8,16,128]{3,2,1,0:T(8,128)S(1)}, f32[2,8,16,128]{3,2,1,0:T(8,128)S(1)}, f32[2,8,16,128]{3,2,1,0:T(8,128)S(1)}, f32[2,8,16,128]{3,2,1,0:T(8,1...) custom-call(s32[2]{0:T(128)S(1)} %pad_add_fusion.idx.refs_0_, ...), custom_call_target="tpu_custom_call" | custom-call | tf_op jit(solution)/shard_map/prepare/pallas_call | solution.py:508
  3.3 4.2 %collective-permute-start.3 = (f32[40,128]{1,0:T(8,128)S(1)}, f32[40,128]{1,0:T(8,128)S(1)}, u32[]{:S(2)}, u32[]{:S(2)}) collective-permute-start(f32[40,128]{1,0:T(8,128)S(1)} %get-tuple-element.36.own.refs_0_), channel_id=1, source_target_pairs={{0,3},{1,2},{2,1},{3,0},{4,7},{5,6},{6,5},{7,4},{8,11},{9,10},{10,... | collective-permute-start | bytes 61448 | tf_op jit(solution)/shard_map/ppermute | solution.py:520
  9.3 3.5 %collective-permute-done.2.m2.refs_2_ = f32[40,128]{1,0:T(8,128)S(1)} collective-permute-done((f32[40,128]{1,0:T(8,128)S(1)}, f32[40,128]{1,0:T(8,128)S(1)}, u32[]{:S(2)}, u32[]{:S(2)}) %collective-permute-start.2) | collective-permute-done | bytes 20512 | tf_op jit(solution)/shard_map/ppermute | solution.py:520
  13.4 3.1 %collective-permute-start.6 = (f32[40,128]{1,0:T(8,128)S(1)}, f32[40,128]{1,0:T(8,128)S(1)}, u32[]{:S(2)}, u32[]{:S(2)}) collective-permute-start(f32[40,128]{1,0:T(8,128)S(1)} %relay.1.refs_4_), channel_id=1, source_target_pairs={{0,12},{1,13},{2,14},{3,15},{4,8},{5,9},{6,10},{7,11},{8,4},{9,5},... | collective-permute-start | bytes 61448 | tf_op jit(solution)/shard_map/ppermute | solution.py:520
  17.5 1.3 collective-permute-start
  19.6 2.1 %collective-permute-done.5.refs_6_ = f32[40,128]{1,0:T(8,128)S(1)} collective-permute-done((f32[40,128]{1,0:T(8,128)S(1)}, f32[40,128]{1,0:T(8,128)S(1)}, u32[]{:S(2)}, u32[]{:S(2)}) %collective-permute-start.5) | collective-permute-done | bytes 20512 | tf_op jit(solution)/shard_map/ppermute | solution.py:520
  22.7 1.0 collective-permute-start.9
  23.7 1.2 collective-permute-start.8
  24.9 2.0 %collective-permute-start.7 = (f32[20,8,128]{2,1,0:T(8,128)S(1)}, f32[20,8,128]{2,1,0:T(8,128)S(1)}, u32[]{:S(2)}, u32[]{:S(2)}) collective-permute-start(f32[20,8,128]{2,1,0:T(8,128)S(1)} %get-tuple-element.37.own.refs_1_.refs_0_), channel_id=1, source_target_pairs={{0,1},{1,0},{2,3},{3,2},{4,5},{5,4},{6,7},{7,6},{8,9},{9,8},{10,11... | collective-permute-start | bytes 245768 | tf_op jit(solution)/shard_map/ppermute | solution.py:520
  28.1 1.2 collective-permute-start.11
  30.0 1.2 collective-permute-start.10
  31.9 1.6 %collective-permute-start.15 = (f32[20,8,128]{2,1,0:T(8,128)S(1)}, f32[20,8,128]{2,1,0:T(8,128)S(1)}, u32[]{:S(2)}, u32[]{:S(2)}) collective-permute-start(f32[20,8,128]{2,1,0:T(8,128)S(1)} %group_total.2.refs_9_), channel_id=1, source_target_pairs={{0,12},{1,13},{2,14},{3,15},{4,8},{5,9},{6,10},{7,11},{8,4},{9,5},... | collective-permute-start | bytes 245768 | tf_op jit(solution)/shard_map/ppermute | solution.py:520
  33.6 1.7 %collective-permute-start.14 = (f32[20,8,128]{2,1,0:T(8,128)S(1)}, f32[20,8,128]{2,1,0:T(8,128)S(1)}, u32[]{:S(2)}, u32[]{:S(2)}) collective-permute-start(f32[20,8,128]{2,1,0:T(8,128)S(1)} %group_total.2.refs_9_), channel_id=1, source_target_pairs={{0,8},{1,9},{2,10},{3,11},{4,12},{5,13},{6,14},{7,15},{8,0},{9,1},... | collective-permute-start | bytes 245768 | tf_op jit(solution)/shard_map/ppermute | solution.py:520
  36.9 1.6 %collective-permute-start.18 = (f32[20,8,128]{2,1,0:T(8,128)S(1)}, f32[20,8,128]{2,1,0:T(8,128)S(1)}, u32[]{:S(2)}, u32[]{:S(2)}) collective-permute-start(f32[20,8,128]{2,1,0:T(8,128)S(1)} %group_total.3.refs_13_), channel_id=1, source_target_pairs={{0,12},{1,13},{2,14},{3,15},{4,8},{5,9},{6,10},{7,11},{8,4},{9,5},... | collective-permute-start | bytes 245768 | tf_op jit(solution)/shard_map/ppermute | solution.py:520
  38.5 1.7 %collective-permute-start.17 = (f32[20,8,128]{2,1,0:T(8,128)S(1)}, f32[20,8,128]{2,1,0:T(8,128)S(1)}, u32[]{:S(2)}, u32[]{:S(2)}) collective-permute-start(f32[20,8,128]{2,1,0:T(8,128)S(1)} %group_total.3.refs_13_), channel_id=1, source_target_pairs={{0,8},{1,9},{2,10},{3,11},{4,12},{5,13},{6,14},{7,15},{8,0},{9,1},... | collective-permute-start | bytes 245768 | tf_op jit(solution)/shard_map/ppermute | solution.py:520
  41.2 2.3 %collective-permute-done.18.refs_16_ = f32[20,8,128]{2,1,0:T(8,128)S(1)} collective-permute-done((f32[20,8,128]{2,1,0:T(8,128)S(1)}, f32[20,8,128]{2,1,0:T(8,128)S(1)}, u32[]{:S(2)}, u32[]{:S(2)}) %collective-permute-start.18) | collective-permute-done | bytes 81952 | tf_op jit(solution)/shard_map/ppermute | solution.py:520
  43.5 1.3 collective-permute-done.17.refs_15_
  44.8 1.4 %solve_first.1 = (f32[2,8,16,128]{3,2,1,0:T(8,128)S(1)}, f32[4,16,128]{2,1,0:T(8,128)S(1)}, f32[40,128]{1,0:T(8,128)S(1)}) custom-call(s32[2]{0:T(128)S(1)} %pad_add_fusion.idx.refs_0_, f32[20,8,128]{2,1,0:T(8,128)S(1)} %get-tuple-element.37.own.refs_1_.refs_0_, f32[20,8,128]{2,1,0:T(8,128)S(1)} %collective-permute-done.7.m1.refs_2_.refs_1_, ...), custom_call_target="tpu_custom_call" | custom-call | tf_op jit(solution)/shard_map/solve_first/pallas_call | solution.py:508
  46.3 15.0 %all-gather = f32[320,128]{1,0:T(8,128)S(1)} all-gather(f32[40,128]{1,0:T(8,128)S(1)} %get-tuple-element.41), channel_id=2, replica_groups=mesh['gx'=8,'gy'=16] {'gx'}, dimensions={0}, use_global_device_ids=true | all-gather | bytes 184320 | tf_op jit(solution)/shard_map/all_gather | solution.py:570
  62.3 1.6 %collective-permute-start.21 = (f32[4,16,128]{2,1,0:T(8,128)S(1)}, f32[4,16,128]{2,1,0:T(8,128)S(1)}, u32[]{:S(2)}, u32[]{:S(2)}) collective-permute-start(f32[4,16,128]{2,1,0:T(8,128)S(1)} %get-tuple-element.49.refs_8_.refs_17_), channel_id=1, source_target_pairs={{0,3},{1,2},{2,1},{3,0},{4,7},{5,6},{6,5},{7,4},{8,11},{9,10},{10,... | collective-permute-start | bytes 98312 | tf_op jit(solution)/shard_map/ppermute | solution.py:520
  63.9 1.4 %collective-permute-start.20 = (f32[4,16,128]{2,1,0:T(8,128)S(1)}, f32[4,16,128]{2,1,0:T(8,128)S(1)}, u32[]{:S(2)}, u32[]{:S(2)}) collective-permute-start(f32[4,16,128]{2,1,0:T(8,128)S(1)} %get-tuple-element.49.refs_8_.refs_17_), channel_id=1, source_target_pairs={{0,2},{1,3},{2,0},{3,1},{4,6},{5,7},{6,4},{7,5},{8,10},{9,11},{10,... | collective-permute-start | bytes 98312 | tf_op jit(solution)/shard_map/ppermute | solution.py:520
  65.3 1.1 collective-permute-start.19
  66.4 1.0 collective-permute-done.21.refs_11_.refs_20_
  67.5 2.1 %collective-permute-done.20.refs_10_.refs_19_ = f32[4,16,128]{2,1,0:T(8,128)S(1)} collective-permute-done((f32[4,16,128]{2,1,0:T(8,128)S(1)}, f32[4,16,128]{2,1,0:T(8,128)S(1)}, u32[]{:S(2)}, u32[]{:S(2)}) %collective-permute-start.20) | collective-permute-done | bytes 32800 | tf_op jit(solution)/shard_map/ppermute | solution.py:520
  70.2 1.5 %collective-permute-start.24 = (f32[4,16,128]{2,1,0:T(8,128)S(1)}, f32[4,16,128]{2,1,0:T(8,128)S(1)}, u32[]{:S(2)}, u32[]{:S(2)}) collective-permute-start(f32[4,16,128]{2,1,0:T(8,128)S(1)} %group_total_again.1.refs_21_), channel_id=1, source_target_pairs={{0,12},{1,13},{2,14},{3,15},{4,8},{5,9},{6,10},{7,11},{8,4},{9,5},... | collective-permute-start | bytes 98312 | tf_op jit(solution)/shard_map/ppermute | solution.py:520
  72.5 1.9 %collective-permute-start.22 = (f32[4,16,128]{2,1,0:T(8,128)S(1)}, f32[4,16,128]{2,1,0:T(8,128)S(1)}, u32[]{:S(2)}, u32[]{:S(2)}) collective-permute-start(f32[4,16,128]{2,1,0:T(8,128)S(1)} %group_total_again.1.refs_21_), channel_id=1, source_target_pairs={{0,4},{1,5},{2,6},{3,7},{4,0},{5,1},{6,2},{7,3},{8,12},{9,13},{10,... | collective-permute-start | bytes 98312 | tf_op jit(solution)/shard_map/ppermute | solution.py:520
  74.4 1.0 collective-permute-done.24.refs_24_
  75.4 1.7 %collective-permute-done.23.refs_23_ = f32[4,16,128]{2,1,0:T(8,128)S(1)} collective-permute-done((f32[4,16,128]{2,1,0:T(8,128)S(1)}, f32[4,16,128]{2,1,0:T(8,128)S(1)}, u32[]{:S(2)}, u32[]{:S(2)}) %collective-permute-start.23) | collective-permute-done | bytes 32800 | tf_op jit(solution)/shard_map/ppermute | solution.py:520
  77.2 1.4 %solve_second.1 = (f32[2,8,16,128]{3,2,1,0:T(8,128)S(1)}, f32[4,16,128]{2,1,0:T(8,128)S(1)}, f32[40,128]{1,0:T(8,128)S(1)}) custom-call(s32[2]{0:T(128)S(1)} %pad_add_fusion.idx.refs_0_, f32[20,8,128]{2,1,0:T(8,128)S(1)} %get-tuple-element.37.own.refs_1_.refs_0_, f32[20,8,128]{2,1,0:T(8,128)S(1)} %collective-permute-done.7.m1.refs_2_.refs_1_, ...), custom_call_target="tpu_custom_call" | custom-call | tf_op jit(solution)/shard_map/solve_second/pallas_call | solution.py:508
  78.6 12.8 %all-gather.1 = f32[320,128]{1,0:T(8,128)S(1)} all-gather(f32[40,128]{1,0:T(8,128)S(1)} %get-tuple-element.51), channel_id=3, replica_groups=mesh['gx'=8,'gy'=16] {'gx'}, dimensions={0}, use_global_device_ids=true | all-gather | bytes 184320 | tf_op jit(solution)/shard_map/all_gather | solution.py:582
  91.4 1.0 second_image.1
  92.4 43.7 %all-gather.2 = f32[128,1,128]{2,1,0:T(1,128)S(1)} all-gather(f32[1,1,128]{2,1,0:T(1,128)S(1)} %bitcast.23), channel_id=1, replica_groups=mesh['gx'=8,'gy'=16] {'gx','gy'}, dimensions={0}, use_global_device_ids=true | all-gather | bytes 66048 | tf_op jit(solution)/shard_map/all_gather | solution.py:587
  (53 shorter events, 14.6 us)
Async XLA Ops:
  0.7 0.7 copy-start
  3.3 6.0 %collective-permute-start.3 = (f32[40,128]{1,0:T(8,128)S(1)}, f32[40,128]{1,0:T(8,128)S(1)}, u32[]{:S(2)}, u32[]{:S(2)}) collective-permute-start(f32[40,128]{1,0:T(8,128)S(1)} %get-tuple-element.36.own.refs_0_), channel_id=1, source_target_pairs={{0,3},{1,2},{2,1},{3,0},{4,7},{5,6},{6,5},{7,4},{8,11},{9,10},{10,... | collective-permute-start | bytes 61448 | tf_op jit(solution)/shard_map/ppermute | solution.py:520
  7.5 5.3 %collective-permute-start.2 = (f32[40,128]{1,0:T(8,128)S(1)}, f32[40,128]{1,0:T(8,128)S(1)}, u32[]{:S(2)}, u32[]{:S(2)}) collective-permute-start(f32[40,128]{1,0:T(8,128)S(1)} %get-tuple-element.36.own.refs_0_), channel_id=1, source_target_pairs={{0,2},{1,3},{2,0},{3,1},{4,6},{5,7},{6,4},{7,5},{8,10},{9,11},{10,... | collective-permute-start | bytes 61448 | tf_op jit(solution)/shard_map/ppermute | solution.py:520
  7.5 5.3 %collective-permute-start.1 = (f32[40,128]{1,0:T(8,128)S(1)}, f32[40,128]{1,0:T(8,128)S(1)}, u32[]{:S(2)}, u32[]{:S(2)}) collective-permute-start(f32[40,128]{1,0:T(8,128)S(1)} %get-tuple-element.36.own.refs_0_), channel_id=1, source_target_pairs={{0,1},{1,0},{2,3},{3,2},{4,5},{5,4},{6,7},{7,6},{8,9},{9,8},{10,11... | collective-permute-start | bytes 61448 | tf_op jit(solution)/shard_map/ppermute | solution.py:520
  13.4 6.3 %collective-permute-start.6 = (f32[40,128]{1,0:T(8,128)S(1)}, f32[40,128]{1,0:T(8,128)S(1)}, u32[]{:S(2)}, u32[]{:S(2)}) collective-permute-start(f32[40,128]{1,0:T(8,128)S(1)} %relay.1.refs_4_), channel_id=1, source_target_pairs={{0,12},{1,13},{2,14},{3,15},{4,8},{5,9},{6,10},{7,11},{8,4},{9,5},... | collective-permute-start | bytes 61448 | tf_op jit(solution)/shard_map/ppermute | solution.py:520
  16.5 5.3 %collective-permute-start.5 = (f32[40,128]{1,0:T(8,128)S(1)}, f32[40,128]{1,0:T(8,128)S(1)}, u32[]{:S(2)}, u32[]{:S(2)}) collective-permute-start(f32[40,128]{1,0:T(8,128)S(1)} %relay.1.refs_4_), channel_id=1, source_target_pairs={{0,8},{1,9},{2,10},{3,11},{4,12},{5,13},{6,14},{7,15},{8,0},{9,1},... | collective-permute-start | bytes 61448 | tf_op jit(solution)/shard_map/ppermute | solution.py:520
  17.1 4.7 %collective-permute-start.4 = (f32[40,128]{1,0:T(8,128)S(1)}, f32[40,128]{1,0:T(8,128)S(1)}, u32[]{:S(2)}, u32[]{:S(2)}) collective-permute-start(f32[40,128]{1,0:T(8,128)S(1)} %relay.1.refs_4_), channel_id=1, source_target_pairs={{0,4},{1,5},{2,6},{3,7},{4,0},{5,1},{6,2},{7,3},{8,12},{9,13},{10,... | collective-permute-start | bytes 61448 | tf_op jit(solution)/shard_map/ppermute | solution.py:520
  17.5 2.1 %collective-permute-start = (f32[2,8,128]{2,1,0:T(8,128)S(1)}, f32[2,8,128]{2,1,0:T(8,128)S(1)}, u32[]{:S(2)}, u32[]{:S(2)}) collective-permute-start(f32[2,8,128]{2,1,0:T(8,128)S(1)} %get-tuple-element.35), channel_id=1, source_target_pairs={{0,16},{16,32},{32,48},{48,64},{64,80},{80,96},{96,112},{1,17},{17... | collective-permute-start | bytes 24584 | tf_op jit(solution)/shard_map/ppermute | solution.py:542
  21.8 5.1 %copy-start.4 = (s32[1,1,8]{2,1,0:T(1,128)S(1)}, s32[1,1,8]{2,1,0:T(1,128)}, u32[]{:S(2)}) copy-start(s32[1,1,8]{2,1,0:T(1,128)} %param.18) | copy-start | bytes 100
  22.7 4.3 %copy-start.1 = (f32[1,1,8,32]{3,2,1,0:T(8,128)S(1)}, f32[1,1,8,32]{3,2,1,0:T(8,128)}, u32[]{:S(2)}) copy-start(f32[1,1,8,32]{3,2,1,0:T(8,128)} %param.17) | copy-start | bytes 3076
  22.7 7.3 %collective-permute-start.9 = (f32[20,8,128]{2,1,0:T(8,128)S(1)}, f32[20,8,128]{2,1,0:T(8,128)S(1)}, u32[]{:S(2)}, u32[]{:S(2)}) collective-permute-start(f32[20,8,128]{2,1,0:T(8,128)S(1)} %get-tuple-element.37.own.refs_1_.refs_0_), channel_id=1, source_target_pairs={{0,3},{1,2},{2,1},{3,0},{4,7},{5,6},{6,5},{7,4},{8,11},{9,10},{10,... | collective-permute-start | bytes 245768 | tf_op jit(solution)/shard_map/ppermute | solution.py:520
  23.7 7.5 %collective-permute-start.8 = (f32[20,8,128]{2,1,0:T(8,128)S(1)}, f32[20,8,128]{2,1,0:T(8,128)S(1)}, u32[]{:S(2)}, u32[]{:S(2)}) collective-permute-start(f32[20,8,128]{2,1,0:T(8,128)S(1)} %get-tuple-element.37.own.refs_1_.refs_0_), channel_id=1, source_target_pairs={{0,2},{1,3},{2,0},{3,1},{4,6},{5,7},{6,4},{7,5},{8,10},{9,11},{10,... | collective-permute-start | bytes 245768 | tf_op jit(solution)/shard_map/ppermute | solution.py:520
  24.9 6.3 %collective-permute-start.7 = (f32[20,8,128]{2,1,0:T(8,128)S(1)}, f32[20,8,128]{2,1,0:T(8,128)S(1)}, u32[]{:S(2)}, u32[]{:S(2)}) collective-permute-start(f32[20,8,128]{2,1,0:T(8,128)S(1)} %get-tuple-element.37.own.refs_1_.refs_0_), channel_id=1, source_target_pairs={{0,1},{1,0},{2,3},{3,2},{4,5},{5,4},{6,7},{7,6},{8,9},{9,8},{10,11... | collective-permute-start | bytes 245768 | tf_op jit(solution)/shard_map/ppermute | solution.py:520
  27.1 8.2 %collective-permute-start.12 = (f32[20,8,128]{2,1,0:T(8,128)S(1)}, f32[20,8,128]{2,1,0:T(8,128)S(1)}, u32[]{:S(2)}, u32[]{:S(2)}) collective-permute-start(f32[20,8,128]{2,1,0:T(8,128)S(1)} %get-tuple-element.38.own.refs_5_.refs_4_), channel_id=1, source_target_pairs={{0,3},{1,2},{2,1},{3,0},{4,7},{5,6},{6,5},{7,4},{8,11},{9,10},{10,... | collective-permute-start | bytes 245768 | tf_op jit(solution)/shard_map/ppermute | solution.py:520
  28.1 8.2 %collective-permute-start.11 = (f32[20,8,128]{2,1,0:T(8,128)S(1)}, f32[20,8,128]{2,1,0:T(8,128)S(1)}, u32[]{:S(2)}, u32[]{:S(2)}) collective-permute-start(f32[20,8,128]{2,1,0:T(8,128)S(1)} %get-tuple-element.38.own.refs_5_.refs_4_), channel_id=1, source_target_pairs={{0,2},{1,3},{2,0},{3,1},{4,6},{5,7},{6,4},{7,5},{8,10},{9,11},{10,... | collective-permute-start | bytes 245768 | tf_op jit(solution)/shard_map/ppermute | solution.py:520
  30.0 6.2 %collective-permute-start.10 = (f32[20,8,128]{2,1,0:T(8,128)S(1)}, f32[20,8,128]{2,1,0:T(8,128)S(1)}, u32[]{:S(2)}, u32[]{:S(2)}) collective-permute-start(f32[20,8,128]{2,1,0:T(8,128)S(1)} %get-tuple-element.38.own.refs_5_.refs_4_), channel_id=1, source_target_pairs={{0,1},{1,0},{2,3},{3,2},{4,5},{5,4},{6,7},{7,6},{8,9},{9,8},{10,11... | collective-permute-start | bytes 245768 | tf_op jit(solution)/shard_map/ppermute | solution.py:520
  31.2 2.2 %copy-start.2 = (s32[1,1,8,32]{3,2,1,0:T(8,128)S(1)}, s32[1,1,8,32]{3,2,1,0:T(8,128)}, u32[]{:S(2)}) copy-start(s32[1,1,8,32]{3,2,1,0:T(8,128)} %param.15) | copy-start | bytes 3076
  31.9 1.7 %copy-start.3 = (s32[1,1,8,32]{3,2,1,0:T(8,128)S(1)}, s32[1,1,8,32]{3,2,1,0:T(8,128)}, u32[]{:S(2)}) copy-start(s32[1,1,8,32]{3,2,1,0:T(8,128)} %param.16) | copy-start | bytes 3076
  31.9 8.3 %collective-permute-start.15 = (f32[20,8,128]{2,1,0:T(8,128)S(1)}, f32[20,8,128]{2,1,0:T(8,128)S(1)}, u32[]{:S(2)}, u32[]{:S(2)}) collective-permute-start(f32[20,8,128]{2,1,0:T(8,128)S(1)} %group_total.2.refs_9_), channel_id=1, source_target_pairs={{0,12},{1,13},{2,14},{3,15},{4,8},{5,9},{6,10},{7,11},{8,4},{9,5},... | collective-permute-start | bytes 245768 | tf_op jit(solution)/shard_map/ppermute | solution.py:520
  33.6 7.6 %collective-permute-start.14 = (f32[20,8,128]{2,1,0:T(8,128)S(1)}, f32[20,8,128]{2,1,0:T(8,128)S(1)}, u32[]{:S(2)}, u32[]{:S(2)}) collective-permute-start(f32[20,8,128]{2,1,0:T(8,128)S(1)} %group_total.2.refs_9_), channel_id=1, source_target_pairs={{0,8},{1,9},{2,10},{3,11},{4,12},{5,13},{6,14},{7,15},{8,0},{9,1},... | collective-permute-start | bytes 245768 | tf_op jit(solution)/shard_map/ppermute | solution.py:520
  35.3 5.9 %collective-permute-start.13 = (f32[20,8,128]{2,1,0:T(8,128)S(1)}, f32[20,8,128]{2,1,0:T(8,128)S(1)}, u32[]{:S(2)}, u32[]{:S(2)}) collective-permute-start(f32[20,8,128]{2,1,0:T(8,128)S(1)} %group_total.2.refs_9_), channel_id=1, source_target_pairs={{0,4},{1,5},{2,6},{3,7},{4,0},{5,1},{6,2},{7,3},{8,12},{9,13},{10,... | collective-permute-start | bytes 245768 | tf_op jit(solution)/shard_map/ppermute | solution.py:520
  36.9 6.6 %collective-permute-start.18 = (f32[20,8,128]{2,1,0:T(8,128)S(1)}, f32[20,8,128]{2,1,0:T(8,128)S(1)}, u32[]{:S(2)}, u32[]{:S(2)}) collective-permute-start(f32[20,8,128]{2,1,0:T(8,128)S(1)} %group_total.3.refs_13_), channel_id=1, source_target_pairs={{0,12},{1,13},{2,14},{3,15},{4,8},{5,9},{6,10},{7,11},{8,4},{9,5},... | collective-permute-start | bytes 245768 | tf_op jit(solution)/shard_map/ppermute | solution.py:520
  38.5 6.4 %collective-permute-start.17 = (f32[20,8,128]{2,1,0:T(8,128)S(1)}, f32[20,8,128]{2,1,0:T(8,128)S(1)}, u32[]{:S(2)}, u32[]{:S(2)}) collective-permute-start(f32[20,8,128]{2,1,0:T(8,128)S(1)} %group_total.3.refs_13_), channel_id=1, source_target_pairs={{0,8},{1,9},{2,10},{3,11},{4,12},{5,13},{6,14},{7,15},{8,0},{9,1},... | collective-permute-start | bytes 245768 | tf_op jit(solution)/shard_map/ppermute | solution.py:520
  40.2 4.7 %collective-permute-start.16 = (f32[20,8,128]{2,1,0:T(8,128)S(1)}, f32[20,8,128]{2,1,0:T(8,128)S(1)}, u32[]{:S(2)}, u32[]{:S(2)}) collective-permute-start(f32[20,8,128]{2,1,0:T(8,128)S(1)} %group_total.3.refs_13_), channel_id=1, source_target_pairs={{0,4},{1,5},{2,6},{3,7},{4,0},{5,1},{6,2},{7,3},{8,12},{9,13},{10,... | collective-permute-start | bytes 245768 | tf_op jit(solution)/shard_map/ppermute | solution.py:520
  62.3 5.2 %collective-permute-start.21 = (f32[4,16,128]{2,1,0:T(8,128)S(1)}, f32[4,16,128]{2,1,0:T(8,128)S(1)}, u32[]{:S(2)}, u32[]{:S(2)}) collective-permute-start(f32[4,16,128]{2,1,0:T(8,128)S(1)} %get-tuple-element.49.refs_8_.refs_17_), channel_id=1, source_target_pairs={{0,3},{1,2},{2,1},{3,0},{4,7},{5,6},{6,5},{7,4},{8,11},{9,10},{10,... | collective-permute-start | bytes 98312 | tf_op jit(solution)/shard_map/ppermute | solution.py:520
  63.9 5.6 %collective-permute-start.20 = (f32[4,16,128]{2,1,0:T(8,128)S(1)}, f32[4,16,128]{2,1,0:T(8,128)S(1)}, u32[]{:S(2)}, u32[]{:S(2)}) collective-permute-start(f32[4,16,128]{2,1,0:T(8,128)S(1)} %get-tuple-element.49.refs_8_.refs_17_), channel_id=1, source_target_pairs={{0,2},{1,3},{2,0},{3,1},{4,6},{5,7},{6,4},{7,5},{8,10},{9,11},{10,... | collective-permute-start | bytes 98312 | tf_op jit(solution)/shard_map/ppermute | solution.py:520
  65.3 4.2 %collective-permute-start.19 = (f32[4,16,128]{2,1,0:T(8,128)S(1)}, f32[4,16,128]{2,1,0:T(8,128)S(1)}, u32[]{:S(2)}, u32[]{:S(2)}) collective-permute-start(f32[4,16,128]{2,1,0:T(8,128)S(1)} %get-tuple-element.49.refs_8_.refs_17_), channel_id=1, source_target_pairs={{0,1},{1,0},{2,3},{3,2},{4,5},{5,4},{6,7},{7,6},{8,9},{9,8},{10,11... | collective-permute-start | bytes 98312 | tf_op jit(solution)/shard_map/ppermute | solution.py:520
  70.2 5.2 %collective-permute-start.24 = (f32[4,16,128]{2,1,0:T(8,128)S(1)}, f32[4,16,128]{2,1,0:T(8,128)S(1)}, u32[]{:S(2)}, u32[]{:S(2)}) collective-permute-start(f32[4,16,128]{2,1,0:T(8,128)S(1)} %group_total_again.1.refs_21_), channel_id=1, source_target_pairs={{0,12},{1,13},{2,14},{3,15},{4,8},{5,9},{6,10},{7,11},{8,4},{9,5},... | collective-permute-start | bytes 98312 | tf_op jit(solution)/shard_map/ppermute | solution.py:520
  71.7 5.4 %collective-permute-start.23 = (f32[4,16,128]{2,1,0:T(8,128)S(1)}, f32[4,16,128]{2,1,0:T(8,128)S(1)}, u32[]{:S(2)}, u32[]{:S(2)}) collective-permute-start(f32[4,16,128]{2,1,0:T(8,128)S(1)} %group_total_again.1.refs_21_), channel_id=1, source_target_pairs={{0,8},{1,9},{2,10},{3,11},{4,12},{5,13},{6,14},{7,15},{8,0},{9,1},... | collective-permute-start | bytes 98312 | tf_op jit(solution)/shard_map/ppermute | solution.py:520
  72.5 4.6 %collective-permute-start.22 = (f32[4,16,128]{2,1,0:T(8,128)S(1)}, f32[4,16,128]{2,1,0:T(8,128)S(1)}, u32[]{:S(2)}, u32[]{:S(2)}) collective-permute-start(f32[4,16,128]{2,1,0:T(8,128)S(1)} %group_total_again.1.refs_21_), channel_id=1, source_target_pairs={{0,4},{1,5},{2,6},{3,7},{4,0},{5,1},{6,2},{7,3},{8,12},{9,13},{10,... | collective-permute-start | bytes 98312 | tf_op jit(solution)/shard_map/ppermute | solution.py:520

commit v4 on v2

--- a/solution.py
+++ b/solution.py
@@ -15,6 +15,7 @@
 N_GX, N_GY = 8, 16
 W_ALL = 128
 PREPARE_VMEM = 54400
+EDGES_VMEM = 55296
 SLOTS_ALL = 256
 
 
@@ -90,6 +91,10 @@
     return (madd(ff, mm(fl, mm(gm, am))), madd(gf, mv(fl, madd(g, mv(gm, a)))))
 
 
+def position():
+    return lax.axis_index("gx"), lax.axis_index("gy")
+
+
 def choose(flag, new, old):
     return tuple(tuple(jnp.where(flag, n, o) for n, o in zip(ns, os)) for ns, os in zip(new, old))
 
@@ -152,8 +157,32 @@
     return ref.at[c][pl.ds(j, CX, stride=CY), :]
 
 
-def prepare_kernel(idx, b_h, acc_h, tx_h, ty_h, tz_h, rhs, tx_o, ty_o, tz_o, diag, cross, sx, sy, b, acc, tx_v, ty_v, tz_v, sems):
-    gx, gy = idx[0], idx[1]
+def edges_kernel(tx_h, ty_h, brk_h, sx, edge, ty, brk, sems):
+    copies = [pltpu.make_async_copy(h, v, sems.at[i]) for i, (h, v) in enumerate(((ty_h, ty), (brk_h, brk)))]
+    copies += [
+        pltpu.make_async_copy(tx_h.at[c, (CX - 1) * CY : CX * CY, :], sx.at[c], sems.at[2 + c]) for c in range(2)
+    ]
+    for copy in copies:
+        copy.start()
+    for copy in copies:
+        copy.wait()
+    edge[2 * CX :, :] = jnp.broadcast_to(brk[...].astype(F32), (8, NZ))
+    for c in range(2):
+        edge[c * CX : (c + 1) * CX, :] = plane(ty, c, CY - 1)
+
+
+def relay(own, m1, m2, m3):
+    z = position()[1] % 4
+    row = lax.broadcasted_iota(jnp.int32, own.shape, 0)
+    out = jnp.where(row < 2 * CX, z == 3, row == 2 * CX)
+    out = jnp.where(out, own, 0.0)
+    for k, ref in ((1, m1), (2, m2), (3, m3)):
+        out = jnp.where(jnp.where(row < 2 * CX, z == 3 - k, row == 2 * CX + k), ref, out)
+    return out
+
+
+def prepare_kernel(b_h, acc_h, tx_h, ty_h, tz_h, rhs, tx_o, ty_o, tz_o, diag, cross, b, acc, tx_v, ty_v, tz_v, sems):
+    gx, gy = position()
     pairs = ((tx_h, tx_v), (ty_h, ty_v), (tz_h, tz_v), (acc_h, acc), (b_h, b))
     copies = [pltpu.make_async_copy(h, v, sems.at[i]) for i, (h, v) in enumerate(pairs)]
     for copy in copies:
@@ -163,8 +192,6 @@
     for copy in copies:
         copy.wait()
     for c in range(2):
-        sx[c] = tx_v[c, (CX - 1) * CY : CX * CY, :]
-        sy[c] = plane(ty_v, c, CY - 1)
         ly = 0.0
         for j in range(CY):
             tx = jnp.where(last_x, 0.0, plane(tx_v, c, j))
@@ -182,19 +209,31 @@
             ly = ty
 
 
-def condense_kernel(idx, diag, cross, ty, rhs, lx_in, ly_in, brk_0, brk_1, brk_2, brk_3, seg, dmat, tau_o, sinv, binv, brk):
-    gy = idx[1]
-    for k, ref in enumerate((brk_0, brk_1, brk_2, brk_3)):
+def condense_kernel(diag, cross, ty, rhs, lx_in, *refs):
+    own, m1, m2, m3, o0, o1, o2, o3 = refs[:8]
+    seg_a, seg_b, dmat, tau_o, sinv, binv, ly_in = refs[8:15]
+    brk, near, far = refs[15:]
+    gy = position()[1]
+    z_at, y_at = gy % 4, gy // 4
+    for k in range(4):
+        near[jnp.bitwise_xor(z_at, k)] = (own, m1, m2, m3)[k][0 : 2 * CX, :]
+        at = jnp.bitwise_xor(y_at, k)
+        ref = (o0, o1, o2, o3)[k]
+        far[at] = ref[0 : 2 * CX, :]
         for i in range(4):
-            brk[pl.ds(jnp.bitwise_xor(gy, 4 * k + i), 1), :] = ref[i : i + 1, :]
+            brk[pl.ds(4 * at + jnp.bitwise_xor(z_at, i), 1), :] = ref[2 * CX + i : 2 * CX + i + 1, :]
     cuts = pltpu.roll(brk[...], (NZ - CY * gy) % NZ, 1)
+    before = jnp.where(y_at > 0, far[jnp.maximum(y_at - 1, 0)], 0.0)
+    before = jnp.where(z_at > 0, near[jnp.maximum(z_at - 1, 0)], before)
+    for c in range(2):
+        ly_in[c] = before[c * CX : (c + 1) * CX]
     for c in range(2):
         ly = ly_in[c]
         for j in range(CY):
             d = diag[c, j] + jnp.where(rows() == 0, lx_in[c, j : j + 1, :], 0.0)
             dmat[3 * c, j] = d + ly if j == 0 else d
         for j in range(CY + 1):
-            keep = 1.0 - cuts[:, j : j + 1].astype(F32)
+            keep = 1.0 - cuts[:, j : j + 1]
             tau_o[c, j] = (ty[c, j - 1] if j else ly) * keep
     for j in range(CY):
         dmat[1, j] = cross[0, j]
@@ -229,34 +268,45 @@
         for i in range(4):
             sinv[i, j] = s[i]
             binv[i, k] = e[i]
-    store_segment(
-        seg,
-        (columns_by(e, tau(0)), mm(e, zl), mm(s, yf), columns_by(s, tau(CY)), mv(e, z), mv(s, y)),
-        True,
-    )
-
-
-def gather_segments(position, mats, vecs, offset, mat_s, vec_s):
+    whole = (columns_by(e, tau(0)), mm(e, zl), mm(s, yf), columns_by(s, tau(CY)), mv(e, z), mv(s, y))
+    for half, ref in enumerate((seg_a, seg_b)):
+        store_segment(ref, [[x[8 * half : 8 * half + 8] for x in part] for part in whole], True)
+
+
+def gather_matrices(position, halves, mat_s):
     for k in range(4):
         at = jnp.bitwise_xor(position, k)
-        mat_s[at] = mats[k][0:16]
-        vec_s[at] = vecs[k][offset : offset + 4]
-
-
-def make_total_kernel(whole):
-    def kernel(*refs):
-        idx = refs[0]
-        if whole:
-            mats = vecs = refs[1:5]
-            out, mat_s, vec_s = refs[5:]
-        else:
-            mats, vecs = refs[1:5], refs[5:9]
-            out, mat_s, vec_s = refs[9:]
-        gather_segments(idx[1] % 4, mats, vecs, 16 if whole else 0, mat_s, vec_s)
-        segs = [load_segment(mat_s.at[m], vec_s.at[m], 0) for m in range(4)]
-        store_segment(out, join(join(segs[0], segs[1]), join(segs[2], segs[3])), whole)
-
-    return kernel
+        for half, refs in enumerate(halves):
+            mat_s[at, :, 8 * half : 8 * half + 8, :] = refs[k][0:16]
+
+
+def gather_vectors(position, vecs, vec_s):
+    for k in range(4):
+        vec_s[jnp.bitwise_xor(position, k)] = vecs[k][...]
+
+
+def gather_both(position, halves, mat_s, vec_s):
+    gather_matrices(position, halves, mat_s)
+    for k in range(4):
+        at = jnp.bitwise_xor(position, k)
+        for half, refs in enumerate(halves):
+            vec_s[at, :, 8 * half : 8 * half + 8, :] = refs[k][16:20]
+
+
+def total_half_kernel(own, m1, m2, m3, out, segs_s):
+    for k, ref in enumerate((own, m1, m2, m3)):
+        segs_s[jnp.bitwise_xor(position()[1] % 4, k)] = ref[...]
+    segs = [load_segment(segs_s.at[m], segs_s.at[m], 16) for m in range(4)]
+    store_segment(out, join(join(segs[0], segs[1]), join(segs[2], segs[3])), True)
+
+
+def total_again_kernel(*refs):
+    halves, vecs = (refs[0:4], refs[4:8]), refs[8:12]
+    out, mat_s, vec_s = refs[12:]
+    gather_matrices(position()[1] % 4, halves, mat_s)
+    gather_vectors(position()[1] % 4, vecs, vec_s)
+    segs = [load_segment(mat_s.at[m], vec_s.at[m], 0) for m in range(4)]
+    store_segment(out, join(join(segs[0], segs[1]), join(segs[2], segs[3])), False)
 
 
 def split3(x):
@@ -297,23 +347,21 @@
 
 def make_solve_kernel(whole):
     def kernel(*refs):
-        idx = refs[0]
-        if whole:
-            inner, outer_ = refs[1:5], refs[5:9]
-            inner_v, outer_v = inner, outer_
-            rest = refs[9:]
-            offset = 16
-        else:
-            inner, outer_, inner_v, outer_v = refs[1:5], refs[5:9], refs[9:13], refs[13:17]
-            rest = refs[17:]
-            offset = 0
+        inner, outer = (refs[0:4], refs[4:8]), (refs[8:12], refs[12:16])
+        rest = refs[16:] if whole else refs[24:]
         sinv, tau_r, rhs, cells, wells, weights = rest[:6]
         p_out, ends, msg_a, msg_b = rest[6:10]
         mat_i, vec_i, mat_o, vec_o, edge = rest[10:]
-        gx, gy = idx[0], idx[1]
+        gx, gy = position()
         z_at, y_at = gy % 4, gy // 4
-        gather_segments(z_at, inner, inner_v, offset, mat_i, vec_i)
-        gather_segments(y_at, outer_, outer_v, offset, mat_o, vec_o)
+        if whole:
+            gather_both(z_at, inner, mat_i, vec_i)
+            gather_both(y_at, outer, mat_o, vec_o)
+        else:
+            gather_matrices(z_at, inner, mat_i)
+            gather_matrices(y_at, outer, mat_o)
+            gather_vectors(z_at, refs[16:20], vec_i)
+            gather_vectors(y_at, refs[20:24], vec_o)
         zero = jnp.zeros(PLANE, F32)
         before = ((zero,) * 4, (zero,) * 2)
         after = ((zero,) * 4, (zero,) * 2)
@@ -324,7 +372,7 @@
                 m = 3 - m
                 seg = load_segment(mat_s.at[m], vec_s.at[m], 0)
                 after = choose(m > here, join_after(seg, after), after)
-        own = load_segment(inner[0], inner_v[0], offset)
+        own = load_segment(mat_i.at[z_at], vec_i.at[z_at], 0)
         ff, fl, lf, ll, gf, gl = own
         up_m, up_v = join_before(before, own)
         last = mv(inv2(one_minus(mm(up_m, after[0]))), madd(up_v, mv(up_m, after[1])))
@@ -370,8 +418,8 @@
     return kernel
 
 
-def apply_operator(idx, got, cells, wells, weights):
-    gx = idx[0]
+def apply_operator(got, cells, wells, weights):
+    gx = position()[0]
     got_a, sent_b, got_b, got_c, got_d = got
     tail = sent_b[16:24, :] + got_b[16:24, :] + got_c[...] + got_d[...]
     rates = tail[0:1] / jnp.maximum(tail[1:2], 1.0)
@@ -405,8 +453,8 @@
     return out
 
 
-def first_image_kernel(idx, got_a, sent_b, got_b, got_c, got_d, p, ends, dmat, tau_r, sinv, binv, rhs, tx, ty, tz, lx_in, ly_in, cells, wells, weights, q_out, e_out, vec_out, dots):
-    well_add, after, before = apply_operator(idx, (got_a, sent_b, got_b, got_c, got_d), cells, wells, weights)
+def first_image_kernel(got_a, sent_b, got_b, got_c, got_d, p, ends, dmat, tau_r, sinv, binv, rhs, tx, ty, tz, lx_in, ly_in, cells, wells, weights, q_out, e_out, vec_out, dots):
+    well_add, after, before = apply_operator((got_a, sent_b, got_b, got_c, got_d), cells, wells, weights)
     eq = jnp.zeros(PLANE, F32)
     qq = jnp.zeros(PLANE, F32)
     e = []
@@ -436,8 +484,8 @@
         vec_out[2 + c] = last[c]
 
 
-def second_image_kernel(idx, got_a, sent_b, got_b, got_c, got_d, p, ends, dmat, tx, ty, tz, lx_in, ly_in, cells, wells, weights, q_in, e_in, dots_in, s_out, dots):
-    well_add, after, before = apply_operator(idx, (got_a, sent_b, got_b, got_c, got_d), cells, wells, weights)
+def second_image_kernel(got_a, sent_b, got_b, got_c, got_d, p, ends, dmat, tx, ty, tz, lx_in, ly_in, cells, wells, weights, q_in, e_in, dots_in, s_out, dots):
+    well_add, after, before = apply_operator((got_a, sent_b, got_b, got_c, got_d), cells, wells, weights)
     sq = jnp.zeros(PLANE, F32)
     ss = jnp.zeros(PLANE, F32)
     es = jnp.zeros(PLANE, F32)
@@ -476,7 +524,7 @@
         kernel,
         name=name,
         out_shape=tuple(outs),
-        in_specs=specs or [SMEM] + [VMEM] * (len(args) - 1),
+        in_specs=specs or [VMEM] * len(args),
         out_specs=tuple(VMEM for _ in outs),
         scratch_shapes=[pltpu.VMEM(s, F32) if isinstance(s, tuple) else s for s in scratch],
         compiler_params=pltpu.CompilerParams(vmem_limit_bytes=vmem * 1024),
@@ -507,26 +555,29 @@
 
 
 def body(right_side, accumulation, trans_x, trans_y, trans_z, perf_cell, perf_well, perf_weight, perf_count, breaks):
-    gx, gy = lax.axis_index("gx"), lax.axis_index("gy")
-    idx = jnp.stack([gx, gy]).astype(jnp.int32)
 
     def flat(a):
         return a.reshape(a.shape[0], CX * CY, NZ)
 
     field, block, part = (2, CY, CX, NZ), (4, CY, CX, NZ), (2, CY + 1, CX, NZ)
-    seg, vec, message = (20, CX, NZ), (4, CX, NZ), (24, NZ)
+    half, vec, message = (20, 8, NZ), (4, CX, NZ), (24, NZ)
     order = [(4, 16, CX, NZ), (4, 4, CX, NZ)]
     two, four = (2, CX * CY, NZ), (4, CX * CY, NZ)
-    cuts = swapped(jnp.concatenate(swapped(breaks, 1), axis=0), 4)
-    rhs, tx, ty, tz, diag, cross, sx, sy = call(
-        prepare_kernel, "prepare",
-        (field, field, field, field, field, field, (2, CY, NZ), (2, CX, NZ)),
+    sx, edge = call(
+        edges_kernel, "edges", ((2, CY, NZ), (40, NZ)),
+        [two, pltpu.VMEM((1, NZ), jnp.int32), pltpu.SemaphoreType.DMA((4,))],
+        flat(trans_x), flat(trans_y), breaks, specs=[HBM] * 3, vmem=EDGES_VMEM,
+    )
+    rhs, tx, ty, tz, diag, cross = call(
+        prepare_kernel, "prepare", (field,) * 6,
         [two, four, two, two, two, pltpu.SemaphoreType.DMA((5,))],
-        idx, flat(right_side), flat(accumulation), flat(trans_x), flat(trans_y), flat(trans_z),
-        specs=[SMEM] + [HBM] * 5, vmem=PREPARE_VMEM,
+        flat(right_side), flat(accumulation), flat(trans_x), flat(trans_y), flat(trans_z),
+        specs=[HBM] * 5, vmem=PREPARE_VMEM,
     )
     lx = lax.ppermute(sx, "gx", [(i, i + 1) for i in range(N_GX - 1)])
-    ly = lax.ppermute(sy, "gy", [(i, i + 1) for i in range(N_GY - 1)])
+    edges = swapped(edge, 1)
+    lx, *edges = lax.optimization_barrier((lx, *edges))
+    relayed = swapped(relay(*edges), 4)
     slots = perf_cell.shape[3]
     live = jnp.arange(slots, dtype=jnp.int32)[None, :] < perf_count.reshape(N_GX, 1)
     weights = jnp.where(live, perf_weight.reshape(N_GX, slots), 0.0).reshape(1, SLOTS_ALL)
@@ -535,37 +586,42 @@
     cells = perf_cell.reshape(1, SLOTS_ALL)
     perfs = (cells, wells, weights)
 
-    own, dmat, tau, sinv, binv = call(
-        condense_kernel, "condense", (seg, block, part, block, block),
-        [pltpu.VMEM((N_GY, NZ), jnp.int32)], idx, diag, cross, ty, rhs, lx, ly, *cuts,
-    )
-    inner = swapped(own, 1)
-    (group,) = call(make_total_kernel(True), "group_total", (seg,), order, idx, *inner)
-    outer = swapped(group, 4)
+    own_a, own_b, dmat, tau, sinv, binv, ly = call(
+        condense_kernel, "condense", (half, half, block, part, block, block, (2, CX, NZ)),
+        [(N_GY, NZ), (4, 2 * CX, NZ), (4, 2 * CX, NZ)], diag, cross, ty, rhs, lx, *edges, *relayed,
+    )
+    inner, outer = [], []
+    for own in (own_a, own_b):
+        inner.append(swapped(own, 1))
+    for near in inner:
+        (group,) = call(total_half_kernel, "group_total", (half,), [(4,) + half], *near)
+        outer.append(swapped(group, 4))
+    inner = inner[0] + inner[1]
+    outer = outer[0] + outer[1]
     solve_scratch = order + order + [(2, 16, NZ)]
     p, ends, msg_a, msg_b = call(
         make_solve_kernel(True), "solve_first", (field, vec, message, message), solve_scratch,
-        idx, *inner, *outer, sinv, tau, rhs, *perfs,
+        *inner, *outer, sinv, tau, rhs, *perfs,
     )
     got = exchange_rows(msg_a, msg_b)
     q, e, own_v, dots = call(
         first_image_kernel, "first_image", (field, field, vec, (2, CX, NZ)), [],
-        idx, *got, p, ends, dmat, tau, sinv, binv, rhs, tx, ty, tz, lx, ly, *perfs,
+        *got, p, ends, dmat, tau, sinv, binv, rhs, tx, ty, tz, lx, ly, *perfs,
     )
     inner_v = swapped(own_v, 1)
-    (group_v,) = call(make_total_kernel(False), "group_total_again", (vec,), order, idx, *inner, *inner_v)
+    (group_v,) = call(total_again_kernel, "group_total_again", (vec,), order, *inner, *inner_v)
     outer_v = swapped(group_v, 4)
     w, ends, msg_a, msg_b = call(
         make_solve_kernel(False), "solve_second", (field, vec, message, message), solve_scratch,
-        idx, *inner, *outer, *inner_v, *outer_v, sinv, tau, e, *perfs,
+        *inner, *outer, *inner_v, *outer_v, sinv, tau, e, *perfs,
     )
     got = exchange_rows(msg_a, msg_b)
     s, dots = call(
         second_image_kernel, "second_image", (field, (8, NZ)), [],
-        idx, *got, w, ends, dmat, tx, ty, tz, lx, ly, *perfs, q, e, dots,
+        *got, w, ends, dmat, tx, ty, tz, lx, ly, *perfs, q, e, dots,
     )
     dots = sum_everywhere(dots)
-    x, r = call(finish_kernel, "finish", (two, two), [], dots, p, w, q, e, s, specs=[VMEM] * 6)
+    x, r = call(finish_kernel, "finish", (two, two), [], dots, p, w, q, e, s)
     shape = (2, CX, CY, NZ)
     return x.reshape(shape), r.reshape(shape)
 

time: 105 us -> 101 us (0.962)
  waiting for transfers between devices: 38.2 us -> 30 us
  starting transfers between devices: 42 us -> 49.9 us
  Pallas kernels: 9.96 us -> 7.25 us
    ppermute x18 -> x24, waiting for transfers between devices: 24.6 us -> 14.8 us  [swapped(): lax.ppermute(block, 'gy', [(i, i ^ k * stride) for i in range(N_GY)])]
    ppermute x18 -> x24, starting transfers between devices: 25.9 us -> 34.3 us  [swapped(): lax.ppermute(block, 'gy', [(i, i ^ k * stride) for i in range(N_GY)])]
    ppermute x2, starting transfers between devices: 0.65 us -> 4.97 us  [exchange_rows(): lax.ppermute(sent_b, 'gx', [(i, (i + 1 if i % 2 else i - 1) % N_GX) for i...]
    ppermute x1 -> x0, starting transfers between devices: 3.02 us -> none  [body(): ly = lax.ppermute(sy, 'gy', [(i, i + 1) for i in range(N_GY - 1)])]
    pallas_call x9 -> x11, Pallas kernels: 9.96 us -> 7.25 us  [call(): pl.pallas_call(kernel, name=name, out_shape=tuple(outs), in_specs=specs o...]
    ppermute x2, waiting for transfers between devices: 0.36 us -> 2.57 us  [exchange_rows(): lax.ppermute(tail, 'gx', [(i, (i + 2 if i % 2 else i - 2) % N_GX) for i i...]
    ppermute x2, starting transfers between devices: 2.75 us -> 1.18 us  [exchange_rows(): lax.ppermute(tail, 'gx', [(i, (i + 2 if i % 2 else i - 2) % N_GX) for i i...]
    ppermute x2, waiting for transfers between devices: 5.53 us -> 4.19 us  [exchange_rows(): got_c = lax.ppermute(tail, 'gx', [(i, i ^ 4) for i in range(N_GX)])]
  transfers between devices with their start and end apart: 32 -> 37, of which waited for: 19 -> 18; matrix products, arithmetic and copies ran while one was open for 1% -> 1% of each run, Pallas kernels for 2% -> 2%
where the time goes in v4:
time: 101 us
  starting transfers between devices  49.9 us (49%)
  waiting for transfers between devices  30 us (30%)
  blocking collectives  12.3 us (12%)
  Pallas kernels  7.25 us (7%)
    ppermute x24, starting transfers between devices, swapped(): lax.ppermute(block, 'gy', [(i, i ^ k * stride) for i in range(N_GY)])  34.3 us
    ppermute x24, waiting for transfers between devices, swapped(): lax.ppermute(block, 'gy', [(i, i ^ k * stride) for i in range(N_GY)])  14.8 us
    all_to_all x1, blocking collectives, sum_everywhere(): return lax.all_to_all(x, 'gy', split_axis=0, concat_axis=0, tiled=True)  12.3 us
    pallas_call x11, Pallas kernels, call(): pl.pallas_call(kernel, name=name, out_shape=tuple(outs), in_specs=specs o...  7.25 us
    ppermute x2, starting transfers between devices, exchange_rows(): lax.ppermute(sent_b, 'gx', [(i, (i + 1 if i % 2 else i - 1) % N_GX) for i...  4.97 us
    ppermute x3, starting transfers between devices, sum_everywhere(): lax.ppermute(x, 'gx', [(i, (i + 2 * k) % N_GX) for i in range(N_GX)])  4.66 us
    ppermute x2, waiting for transfers between devices, exchange_rows(): got_c = lax.ppermute(tail, 'gx', [(i, i ^ 4) for i in range(N_GX)])  4.19 us
    ppermute x3, waiting for transfers between devices, sum_everywhere(): lax.ppermute(x, 'gx', [(i, (i + 2 * k) % N_GX) for i in range(N_GX)])  3.92 us
  transfers between devices with their start and end apart: 37, of which 18 were waited for; matrix products, arithmetic and copies ran while one was open for 1% of the time, Pallas kernels for 2%

profile of v4, /device:TPU:0, one launch (start us, length us, event | category | flops | bytes accessed | tf_op | source)
XLA Modules:
  0.0 101.2 jit_solution(3103722584227004556)
XLA Ops:
  0.6 1.6 %edges.1 = (f32[2,8,128]{2,1,0:T(8,128)}, f32[40,128]{1,0:T(8,128)}) custom-call(f32[2,128,128]{2,1,0:T(8,128)} %bitcast.14, f32[2,128,128]{2,1,0:T(8,128)} %bitcast.16, s32[1,128]{1,0:T(1,128)} %brk_h.1), custom_call_target="tpu_custom_call" | custom-call | tf_op jit(solution)/shard_map/edges/pallas_call | solution.py:523
  2.2 4.2 %collective-permute-start.3 = (f32[40,128]{1,0:T(8,128)}, f32[40,128]{1,0:T(8,128)S(1)}, u32[]{:S(2)}, u32[]{:S(2)}) collective-permute-start(f32[40,128]{1,0:T(8,128)} %get-tuple-element.45.refs_0_), channel_id=1, source_target_pairs={{0,3},{1,2},{2,1},{3,0},{4,7},{5,6},{6,5},{7,4},{8,11},{9,10},{10,... | collective-permute-start | bytes 61448 | tf_op jit(solution)/shard_map/ppermute | solution.py:535
  7.3 1.3 %collective-permute-start = (f32[2,8,128]{2,1,0:T(8,128)}, f32[2,8,128]{2,1,0:T(8,128)S(1)}, u32[]{:S(2)}, u32[]{:S(2)}) collective-permute-start(f32[2,8,128]{2,1,0:T(8,128)} %get-tuple-element.42), channel_id=1, source_target_pairs={{0,16},{16,32},{32,48},{48,64},{64,80},{80,96},{96,112},{1,17},{17... | collective-permute-start | bytes 24584 | tf_op jit(solution)/shard_map/ppermute | solution.py:577
  9.7 2.2 %collective-permute-done.2.refs_2_ = f32[40,128]{1,0:T(8,128)S(1)} collective-permute-done((f32[40,128]{1,0:T(8,128)}, f32[40,128]{1,0:T(8,128)S(1)}, u32[]{:S(2)}, u32[]{:S(2)}) %collective-permute-start.2) | collective-permute-done | bytes 20512 | tf_op jit(solution)/shard_map/ppermute | solution.py:535
  12.0 3.1 %collective-permute-start.6 = (f32[40,128]{1,0:T(8,128)S(1)}, f32[40,128]{1,0:T(8,128)S(1)}, u32[]{:S(2)}, u32[]{:S(2)}) collective-permute-start(f32[40,128]{1,0:T(8,128)S(1)} %select_select_fusion.refs_4_), channel_id=1, source_target_pairs={{0,12},{1,13},{2,14},{3,15},{4,8},{5,9},{6,10},{7,11},{8,4},{9,5},... | collective-permute-start | bytes 61448 | tf_op jit(solution)/shard_map/ppermute | solution.py:535
  16.2 1.4 %prepare.1 = (f32[2,8,16,128]{3,2,1,0:T(8,128)S(1)}, f32[2,8,16,128]{3,2,1,0:T(8,128)S(1)}, f32[2,8,16,128]{3,2,1,0:T(8,128)S(1)}, f32[2,8,16,128]{3,2,1,0:T(8,1...) custom-call(f32[2,128,128]{2,1,0:T(8,128)} %bitcast.19, f32[4,128,128]{2,1,0:T(8,128)} %bitcast.18, ...), custom_call_target="tpu_custom_call" | custom-call | tf_op jit(solution)/shard_map/prepare/pallas_call | solution.py:523
  17.6 2.8 %collective-permute-done.5.refs_6_ = f32[40,128]{1,0:T(8,128)S(1)} collective-permute-done((f32[40,128]{1,0:T(8,128)S(1)}, f32[40,128]{1,0:T(8,128)S(1)}, u32[]{:S(2)}, u32[]{:S(2)}) %collective-permute-start.5) | collective-permute-done | bytes 20512 | tf_op jit(solution)/shard_map/ppermute | solution.py:535
  21.8 1.2 %collective-permute-start.8 = (f32[20,8,128]{2,1,0:T(8,128)S(1)}, f32[20,8,128]{2,1,0:T(8,128)S(1)}, u32[]{:S(2)}, u32[]{:S(2)}) collective-permute-start(f32[20,8,128]{2,1,0:T(8,128)S(1)} %get-tuple-element.49.own.refs_0_), channel_id=1, source_target_pairs={{0,2},{1,3},{2,0},{3,1},{4,6},{5,7},{6,4},{7,5},{8,10},{9,11},{10,... | collective-permute-start | bytes 245768 | tf_op jit(solution)/shard_map/ppermute | solution.py:535
  23.0 1.9 %collective-permute-start.7 = (f32[20,8,128]{2,1,0:T(8,128)S(1)}, f32[20,8,128]{2,1,0:T(8,128)S(1)}, u32[]{:S(2)}, u32[]{:S(2)}) collective-permute-start(f32[20,8,128]{2,1,0:T(8,128)S(1)} %get-tuple-element.49.own.refs_0_), channel_id=1, source_target_pairs={{0,1},{1,0},{2,3},{3,2},{4,5},{5,4},{6,7},{7,6},{8,9},{9,8},{10,11... | collective-permute-start | bytes 245768 | tf_op jit(solution)/shard_map/ppermute | solution.py:535
  26.2 1.2 %collective-permute-start.11 = (f32[20,8,128]{2,1,0:T(8,128)S(1)}, f32[20,8,128]{2,1,0:T(8,128)S(1)}, u32[]{:S(2)}, u32[]{:S(2)}) collective-permute-start(f32[20,8,128]{2,1,0:T(8,128)S(1)} %get-tuple-element.50.own.refs_4_), channel_id=1, source_target_pairs={{0,2},{1,3},{2,0},{3,1},{4,6},{5,7},{6,4},{7,5},{8,10},{9,11},{10,... | collective-permute-start | bytes 245768 | tf_op jit(solution)/shard_map/ppermute | solution.py:535
  27.4 1.9 %collective-permute-start.10 = (f32[20,8,128]{2,1,0:T(8,128)S(1)}, f32[20,8,128]{2,1,0:T(8,128)S(1)}, u32[]{:S(2)}, u32[]{:S(2)}) collective-permute-start(f32[20,8,128]{2,1,0:T(8,128)S(1)} %get-tuple-element.50.own.refs_4_), channel_id=1, source_target_pairs={{0,1},{1,0},{2,3},{3,2},{4,5},{5,4},{6,7},{7,6},{8,9},{9,8},{10,11... | collective-permute-start | bytes 245768 | tf_op jit(solution)/shard_map/ppermute | solution.py:535
  29.4 1.4 %collective-permute-start.15 = (f32[20,8,128]{2,1,0:T(8,128)S(1)}, f32[20,8,128]{2,1,0:T(8,128)S(1)}, u32[]{:S(2)}, u32[]{:S(2)}) collective-permute-start(f32[20,8,128]{2,1,0:T(8,128)S(1)} %group_total.2.refs_8_), channel_id=1, source_target_pairs={{0,12},{1,13},{2,14},{3,15},{4,8},{5,9},{6,10},{7,11},{8,4},{9,5},... | collective-permute-start | bytes 245768 | tf_op jit(solution)/shard_map/ppermute | solution.py:535
  31.0 1.2 %collective-permute-start.14 = (f32[20,8,128]{2,1,0:T(8,128)S(1)}, f32[20,8,128]{2,1,0:T(8,128)S(1)}, u32[]{:S(2)}, u32[]{:S(2)}) collective-permute-start(f32[20,8,128]{2,1,0:T(8,128)S(1)} %group_total.2.refs_8_), channel_id=1, source_target_pairs={{0,8},{1,9},{2,10},{3,11},{4,12},{5,13},{6,14},{7,15},{8,0},{9,1},... | collective-permute-start | bytes 245768 | tf_op jit(solution)/shard_map/ppermute | solution.py:535
  32.2 1.6 %collective-permute-start.13 = (f32[20,8,128]{2,1,0:T(8,128)S(1)}, f32[20,8,128]{2,1,0:T(8,128)S(1)}, u32[]{:S(2)}, u32[]{:S(2)}) collective-permute-start(f32[20,8,128]{2,1,0:T(8,128)S(1)} %group_total.2.refs_8_), channel_id=1, source_target_pairs={{0,4},{1,5},{2,6},{3,7},{4,0},{5,1},{6,2},{7,3},{8,12},{9,13},{10,... | collective-permute-start | bytes 245768 | tf_op jit(solution)/shard_map/ppermute | solution.py:535
  33.9 1.4 %collective-permute-start.18 = (f32[20,8,128]{2,1,0:T(8,128)S(1)}, f32[20,8,128]{2,1,0:T(8,128)S(1)}, u32[]{:S(2)}, u32[]{:S(2)}) collective-permute-start(f32[20,8,128]{2,1,0:T(8,128)S(1)} %group_total.3.refs_12_), channel_id=1, source_target_pairs={{0,12},{1,13},{2,14},{3,15},{4,8},{5,9},{6,10},{7,11},{8,4},{9,5},... | collective-permute-start | bytes 245768 | tf_op jit(solution)/shard_map/ppermute | solution.py:535
  36.5 1.6 %collective-permute-start.16 = (f32[20,8,128]{2,1,0:T(8,128)S(1)}, f32[20,8,128]{2,1,0:T(8,128)S(1)}, u32[]{:S(2)}, u32[]{:S(2)}) collective-permute-start(f32[20,8,128]{2,1,0:T(8,128)S(1)} %group_total.3.refs_12_), channel_id=1, source_target_pairs={{0,4},{1,5},{2,6},{3,7},{4,0},{5,1},{6,2},{7,3},{8,12},{9,13},{10,... | collective-permute-start | bytes 245768 | tf_op jit(solution)/shard_map/ppermute | solution.py:535
  38.3 1.4 %collective-permute-done.18.refs_15_ = f32[20,8,128]{2,1,0:T(8,128)S(1)} collective-permute-done((f32[20,8,128]{2,1,0:T(8,128)S(1)}, f32[20,8,128]{2,1,0:T(8,128)S(1)}, u32[]{:S(2)}, u32[]{:S(2)}) %collective-permute-start.18) | collective-permute-done | bytes 81952 | tf_op jit(solution)/shard_map/ppermute | solution.py:535
  39.7 1.6 %collective-permute-done.17.refs_14_ = f32[20,8,128]{2,1,0:T(8,128)S(1)} collective-permute-done((f32[20,8,128]{2,1,0:T(8,128)S(1)}, f32[20,8,128]{2,1,0:T(8,128)S(1)}, u32[]{:S(2)}, u32[]{:S(2)}) %collective-permute-start.17) | collective-permute-done | bytes 81952 | tf_op jit(solution)/shard_map/ppermute | solution.py:535
  43.6 4.7 %collective-permute-start.20 = (f32[24,128]{1,0:T(8,128)S(1)}, f32[24,128]{1,0:T(8,128)S(1)}, u32[]{:S(2)}, u32[]{:S(2)}) collective-permute-start(f32[24,128]{1,0:T(8,128)S(1)} %select_add_fusion.1.sent_b), channel_id=1, source_target_pairs={{0,112},{16,32},{32,16},{48,64},{64,48},{80,96},{96,80},{112,0},{1... | collective-permute-start | bytes 36872 | tf_op jit(solution)/shard_map/ppermute | solution.py:542
  49.3 2.5 %collective-permute-done.22.got_d = f32[8,128]{1,0:T(8,128)S(1)} collective-permute-done((f32[8,128]{1,0:T(8,128)S(1)}, f32[8,128]{1,0:T(8,128)S(1)}, u32[]{:S(2)}, u32[]{:S(2)}) %collective-permute-start.22) | collective-permute-done | bytes 4128 | tf_op jit(solution)/shard_map/ppermute | solution.py:545
  51.8 2.4 %collective-permute-done.21.got_c = f32[8,128]{1,0:T(8,128)S(1)} collective-permute-done((f32[8,128]{1,0:T(8,128)S(1)}, f32[8,128]{1,0:T(8,128)S(1)}, u32[]{:S(2)}, u32[]{:S(2)}) %collective-permute-start.21) | collective-permute-done | bytes 4128 | tf_op jit(solution)/shard_map/ppermute | solution.py:544
  54.7 2.3 %collective-permute-start.25 = (f32[4,16,128]{2,1,0:T(8,128)S(1)}, f32[4,16,128]{2,1,0:T(8,128)S(1)}, u32[]{:S(2)}, u32[]{:S(2)}) collective-permute-start(f32[4,16,128]{2,1,0:T(8,128)S(1)} %get-tuple-element.62.refs_8_.refs_16_), channel_id=1, source_target_pairs={{0,3},{1,2},{2,1},{3,0},{4,7},{5,6},{6,5},{7,4},{8,11},{9,10},{10,... | collective-permute-start | bytes 98312 | tf_op jit(solution)/shard_map/ppermute | solution.py:535
  59.9 2.5 %collective-permute-done.24.refs_10_.refs_18_ = f32[4,16,128]{2,1,0:T(8,128)S(1)} collective-permute-done((f32[4,16,128]{2,1,0:T(8,128)S(1)}, f32[4,16,128]{2,1,0:T(8,128)S(1)}, u32[]{:S(2)}, u32[]{:S(2)}) %collective-permute-start.24) | collective-permute-done | bytes 32800 | tf_op jit(solution)/shard_map/ppermute | solution.py:535
  62.5 1.9 %collective-permute-start.28 = (f32[4,16,128]{2,1,0:T(8,128)S(1)}, f32[4,16,128]{2,1,0:T(8,128)S(1)}, u32[]{:S(2)}, u32[]{:S(2)}) collective-permute-start(f32[4,16,128]{2,1,0:T(8,128)S(1)} %group_total_again.1.refs_20_), channel_id=1, source_target_pairs={{0,12},{1,13},{2,14},{3,15},{4,8},{5,9},{6,10},{7,11},{8,4},{9,5},... | collective-permute-start | bytes 98312 | tf_op jit(solution)/shard_map/ppermute | solution.py:535
  64.4 1.4 %collective-permute-start.27 = (f32[4,16,128]{2,1,0:T(8,128)S(1)}, f32[4,16,128]{2,1,0:T(8,128)S(1)}, u32[]{:S(2)}, u32[]{:S(2)}) collective-permute-start(f32[4,16,128]{2,1,0:T(8,128)S(1)} %group_total_again.1.refs_20_), channel_id=1, source_target_pairs={{0,8},{1,9},{2,10},{3,11},{4,12},{5,13},{6,14},{7,15},{8,0},{9,1},... | collective-permute-start | bytes 98312 | tf_op jit(solution)/shard_map/ppermute | solution.py:535
  67.7 2.1 %collective-permute-done.27.refs_22_ = f32[4,16,128]{2,1,0:T(8,128)S(1)} collective-permute-done((f32[4,16,128]{2,1,0:T(8,128)S(1)}, f32[4,16,128]{2,1,0:T(8,128)S(1)}, u32[]{:S(2)}, u32[]{:S(2)}) %collective-permute-start.27) | collective-permute-done | bytes 32800 | tf_op jit(solution)/shard_map/ppermute | solution.py:535
  72.6 3.2 %collective-permute-start.31 = (f32[8,128]{1,0:T(8,128)S(1)}, f32[8,128]{1,0:T(8,128)S(1)}, u32[]{:S(2)}, u32[]{:S(2)}) collective-permute-start(f32[8,128]{1,0:T(8,128)S(1)} %slice.9), channel_id=1, source_target_pairs={{0,64},{16,80},{32,96},{48,112},{64,0},{80,16},{96,32},{112,48},{1... | collective-permute-start | bytes 12296 | tf_op jit(solution)/shard_map/ppermute | solution.py:544
  75.9 1.8 %collective-permute-done.31.got_c = f32[8,128]{1,0:T(8,128)S(1)} collective-permute-done((f32[8,128]{1,0:T(8,128)S(1)}, f32[8,128]{1,0:T(8,128)S(1)}, u32[]{:S(2)}, u32[]{:S(2)}) %collective-permute-start.31) | collective-permute-done | bytes 4128 | tf_op jit(solution)/shard_map/ppermute | solution.py:544
  79.4 2.4 %collective-permute-start.36 = (f32[8,128]{1,0:T(8,128)S(1)}, f32[8,128]{1,0:T(8,128)S(1)}, u32[]{:S(2)}, u32[]{:S(2)}) collective-permute-start(f32[8,128]{1,0:T(8,128)S(1)} %add.45), channel_id=1, source_target_pairs={{0,96},{16,112},{32,0},{48,16},{64,32},{80,48},{96,64},{112,80},{1... | collective-permute-start | bytes 12296 | tf_op jit(solution)/shard_map/ppermute | solution.py:551
  81.8 1.3 %collective-permute-start.35 = (f32[8,128]{1,0:T(8,128)S(1)}, f32[8,128]{1,0:T(8,128)S(1)}, u32[]{:S(2)}, u32[]{:S(2)}) collective-permute-start(f32[8,128]{1,0:T(8,128)S(1)} %add.45), channel_id=1, source_target_pairs={{0,64},{16,80},{32,96},{48,112},{64,0},{80,16},{96,32},{112,48},{1... | collective-permute-start | bytes 12296 | tf_op jit(solution)/shard_map/ppermute | solution.py:551
  84.0 2.9 %collective-permute-done.35 = f32[8,128]{1,0:T(8,128)S(1)} collective-permute-done((f32[8,128]{1,0:T(8,128)S(1)}, f32[8,128]{1,0:T(8,128)S(1)}, u32[]{:S(2)}, u32[]{:S(2)}) %collective-permute-start.35) | collective-permute-done | bytes 4128 | tf_op jit(solution)/shard_map/ppermute | solution.py:551
  88.0 12.3 %all_to_all.5.got = f32[16,8,128]{2,1,0:T(8,128)S(1)} all-to-all(f32[16,8,128]{2,1,0:T(8,128)S(1)} %broadcast_in_dim.41), channel_id=1, replica_groups=mesh['gx'=8,'gy'=16] {'gy'}, dimensions={0} | all-to-all | bytes 131072 | tf_op jit(solution)/shard_map/all_to_all | solution.py:554
  (85 shorter events, 23.7 us)
Async XLA Ops:
  2.2 7.5 %collective-permute-start.3 = (f32[40,128]{1,0:T(8,128)}, f32[40,128]{1,0:T(8,128)S(1)}, u32[]{:S(2)}, u32[]{:S(2)}) collective-permute-start(f32[40,128]{1,0:T(8,128)} %get-tuple-element.45.refs_0_), channel_id=1, source_target_pairs={{0,3},{1,2},{2,1},{3,0},{4,7},{5,6},{6,5},{7,4},{8,11},{9,10},{10,... | collective-permute-start | bytes 61448 | tf_op jit(solution)/shard_map/ppermute | solution.py:535
  6.4 5.5 %collective-permute-start.2 = (f32[40,128]{1,0:T(8,128)}, f32[40,128]{1,0:T(8,128)S(1)}, u32[]{:S(2)}, u32[]{:S(2)}) collective-permute-start(f32[40,128]{1,0:T(8,128)} %get-tuple-element.45.refs_0_), channel_id=1, source_target_pairs={{0,2},{1,3},{2,0},{3,1},{4,6},{5,7},{6,4},{7,5},{8,10},{9,11},{10,... | collective-permute-start | bytes 61448 | tf_op jit(solution)/shard_map/ppermute | solution.py:535
  6.4 5.5 %collective-permute-start.1 = (f32[40,128]{1,0:T(8,128)}, f32[40,128]{1,0:T(8,128)S(1)}, u32[]{:S(2)}, u32[]{:S(2)}) collective-permute-start(f32[40,128]{1,0:T(8,128)} %get-tuple-element.45.refs_0_), channel_id=1, source_target_pairs={{0,1},{1,0},{2,3},{3,2},{4,5},{5,4},{6,7},{7,6},{8,9},{9,8},{10,11... | collective-permute-start | bytes 61448 | tf_op jit(solution)/shard_map/ppermute | solution.py:535
  12.0 5.6 %collective-permute-start.6 = (f32[40,128]{1,0:T(8,128)S(1)}, f32[40,128]{1,0:T(8,128)S(1)}, u32[]{:S(2)}, u32[]{:S(2)}) collective-permute-start(f32[40,128]{1,0:T(8,128)S(1)} %select_select_fusion.refs_4_), channel_id=1, source_target_pairs={{0,12},{1,13},{2,14},{3,15},{4,8},{5,9},{6,10},{7,11},{8,4},{9,5},... | collective-permute-start | bytes 61448 | tf_op jit(solution)/shard_map/ppermute | solution.py:535
  15.1 5.3 %collective-permute-start.5 = (f32[40,128]{1,0:T(8,128)S(1)}, f32[40,128]{1,0:T(8,128)S(1)}, u32[]{:S(2)}, u32[]{:S(2)}) collective-permute-start(f32[40,128]{1,0:T(8,128)S(1)} %select_select_fusion.refs_4_), channel_id=1, source_target_pairs={{0,8},{1,9},{2,10},{3,11},{4,12},{5,13},{6,14},{7,15},{8,0},{9,1},... | collective-permute-start | bytes 61448 | tf_op jit(solution)/shard_map/ppermute | solution.py:535
  15.7 4.7 %collective-permute-start.4 = (f32[40,128]{1,0:T(8,128)S(1)}, f32[40,128]{1,0:T(8,128)S(1)}, u32[]{:S(2)}, u32[]{:S(2)}) collective-permute-start(f32[40,128]{1,0:T(8,128)S(1)} %select_select_fusion.refs_4_), channel_id=1, source_target_pairs={{0,4},{1,5},{2,6},{3,7},{4,0},{5,1},{6,2},{7,3},{8,12},{9,13},{10,... | collective-permute-start | bytes 61448 | tf_op jit(solution)/shard_map/ppermute | solution.py:535
  20.8 6.6 %collective-permute-start.9 = (f32[20,8,128]{2,1,0:T(8,128)S(1)}, f32[20,8,128]{2,1,0:T(8,128)S(1)}, u32[]{:S(2)}, u32[]{:S(2)}) collective-permute-start(f32[20,8,128]{2,1,0:T(8,128)S(1)} %get-tuple-element.49.own.refs_0_), channel_id=1, source_target_pairs={{0,3},{1,2},{2,1},{3,0},{4,7},{5,6},{6,5},{7,4},{8,11},{9,10},{10,... | collective-permute-start | bytes 245768 | tf_op jit(solution)/shard_map/ppermute | solution.py:535
  21.8 7.5 %collective-permute-start.8 = (f32[20,8,128]{2,1,0:T(8,128)S(1)}, f32[20,8,128]{2,1,0:T(8,128)S(1)}, u32[]{:S(2)}, u32[]{:S(2)}) collective-permute-start(f32[20,8,128]{2,1,0:T(8,128)S(1)} %get-tuple-element.49.own.refs_0_), channel_id=1, source_target_pairs={{0,2},{1,3},{2,0},{3,1},{4,6},{5,7},{6,4},{7,5},{8,10},{9,11},{10,... | collective-permute-start | bytes 245768 | tf_op jit(solution)/shard_map/ppermute | solution.py:535
  23.0 6.3 %collective-permute-start.7 = (f32[20,8,128]{2,1,0:T(8,128)S(1)}, f32[20,8,128]{2,1,0:T(8,128)S(1)}, u32[]{:S(2)}, u32[]{:S(2)}) collective-permute-start(f32[20,8,128]{2,1,0:T(8,128)S(1)} %get-tuple-element.49.own.refs_0_), channel_id=1, source_target_pairs={{0,1},{1,0},{2,3},{3,2},{4,5},{5,4},{6,7},{7,6},{8,9},{9,8},{10,11... | collective-permute-start | bytes 245768 | tf_op jit(solution)/shard_map/ppermute | solution.py:535
  25.2 7.0 %collective-permute-start.12 = (f32[20,8,128]{2,1,0:T(8,128)S(1)}, f32[20,8,128]{2,1,0:T(8,128)S(1)}, u32[]{:S(2)}, u32[]{:S(2)}) collective-permute-start(f32[20,8,128]{2,1,0:T(8,128)S(1)} %get-tuple-element.50.own.refs_4_), channel_id=1, source_target_pairs={{0,3},{1,2},{2,1},{3,0},{4,7},{5,6},{6,5},{7,4},{8,11},{9,10},{10,... | collective-permute-start | bytes 245768 | tf_op jit(solution)/shard_map/ppermute | solution.py:535
  26.2 7.6 %collective-permute-start.11 = (f32[20,8,128]{2,1,0:T(8,128)S(1)}, f32[20,8,128]{2,1,0:T(8,128)S(1)}, u32[]{:S(2)}, u32[]{:S(2)}) collective-permute-start(f32[20,8,128]{2,1,0:T(8,128)S(1)} %get-tuple-element.50.own.refs_4_), channel_id=1, source_target_pairs={{0,2},{1,3},{2,0},{3,1},{4,6},{5,7},{6,4},{7,5},{8,10},{9,11},{10,... | collective-permute-start | bytes 245768 | tf_op jit(solution)/shard_map/ppermute | solution.py:535
  27.4 6.4 %collective-permute-start.10 = (f32[20,8,128]{2,1,0:T(8,128)S(1)}, f32[20,8,128]{2,1,0:T(8,128)S(1)}, u32[]{:S(2)}, u32[]{:S(2)}) collective-permute-start(f32[20,8,128]{2,1,0:T(8,128)S(1)} %get-tuple-element.50.own.refs_4_), channel_id=1, source_target_pairs={{0,1},{1,0},{2,3},{3,2},{4,5},{5,4},{6,7},{7,6},{8,9},{9,8},{10,11... | collective-permute-start | bytes 245768 | tf_op jit(solution)/shard_map/ppermute | solution.py:535
  29.4 7.1 %collective-permute-start.15 = (f32[20,8,128]{2,1,0:T(8,128)S(1)}, f32[20,8,128]{2,1,0:T(8,128)S(1)}, u32[]{:S(2)}, u32[]{:S(2)}) collective-permute-start(f32[20,8,128]{2,1,0:T(8,128)S(1)} %group_total.2.refs_8_), channel_id=1, source_target_pairs={{0,12},{1,13},{2,14},{3,15},{4,8},{5,9},{6,10},{7,11},{8,4},{9,5},... | collective-permute-start | bytes 245768 | tf_op jit(solution)/shard_map/ppermute | solution.py:535
  31.0 7.3 %collective-permute-start.14 = (f32[20,8,128]{2,1,0:T(8,128)S(1)}, f32[20,8,128]{2,1,0:T(8,128)S(1)}, u32[]{:S(2)}, u32[]{:S(2)}) collective-permute-start(f32[20,8,128]{2,1,0:T(8,128)S(1)} %group_total.2.refs_8_), channel_id=1, source_target_pairs={{0,8},{1,9},{2,10},{3,11},{4,12},{5,13},{6,14},{7,15},{8,0},{9,1},... | collective-permute-start | bytes 245768 | tf_op jit(solution)/shard_map/ppermute | solution.py:535
  32.2 6.1 %collective-permute-start.13 = (f32[20,8,128]{2,1,0:T(8,128)S(1)}, f32[20,8,128]{2,1,0:T(8,128)S(1)}, u32[]{:S(2)}, u32[]{:S(2)}) collective-permute-start(f32[20,8,128]{2,1,0:T(8,128)S(1)} %group_total.2.refs_8_), channel_id=1, source_target_pairs={{0,4},{1,5},{2,6},{3,7},{4,0},{5,1},{6,2},{7,3},{8,12},{9,13},{10,... | collective-permute-start | bytes 245768 | tf_op jit(solution)/shard_map/ppermute | solution.py:535
  33.9 5.7 %collective-permute-start.18 = (f32[20,8,128]{2,1,0:T(8,128)S(1)}, f32[20,8,128]{2,1,0:T(8,128)S(1)}, u32[]{:S(2)}, u32[]{:S(2)}) collective-permute-start(f32[20,8,128]{2,1,0:T(8,128)S(1)} %group_total.3.refs_12_), channel_id=1, source_target_pairs={{0,12},{1,13},{2,14},{3,15},{4,8},{5,9},{6,10},{7,11},{8,4},{9,5},... | collective-permute-start | bytes 245768 | tf_op jit(solution)/shard_map/ppermute | solution.py:535
  35.3 5.9 %collective-permute-start.17 = (f32[20,8,128]{2,1,0:T(8,128)S(1)}, f32[20,8,128]{2,1,0:T(8,128)S(1)}, u32[]{:S(2)}, u32[]{:S(2)}) collective-permute-start(f32[20,8,128]{2,1,0:T(8,128)S(1)} %group_total.3.refs_12_), channel_id=1, source_target_pairs={{0,8},{1,9},{2,10},{3,11},{4,12},{5,13},{6,14},{7,15},{8,0},{9,1},... | collective-permute-start | bytes 245768 | tf_op jit(solution)/shard_map/ppermute | solution.py:535
  36.5 4.9 %collective-permute-start.16 = (f32[20,8,128]{2,1,0:T(8,128)S(1)}, f32[20,8,128]{2,1,0:T(8,128)S(1)}, u32[]{:S(2)}, u32[]{:S(2)}) collective-permute-start(f32[20,8,128]{2,1,0:T(8,128)S(1)} %group_total.3.refs_12_), channel_id=1, source_target_pairs={{0,4},{1,5},{2,6},{3,7},{4,0},{5,1},{6,2},{7,3},{8,12},{9,13},{10,... | collective-permute-start | bytes 245768 | tf_op jit(solution)/shard_map/ppermute | solution.py:535
  43.6 10.6 %collective-permute-start.20 = (f32[24,128]{1,0:T(8,128)S(1)}, f32[24,128]{1,0:T(8,128)S(1)}, u32[]{:S(2)}, u32[]{:S(2)}) collective-permute-start(f32[24,128]{1,0:T(8,128)S(1)} %select_add_fusion.1.sent_b), channel_id=1, source_target_pairs={{0,112},{16,32},{32,16},{48,64},{64,48},{80,96},{96,80},{112,0},{1... | collective-permute-start | bytes 36872 | tf_op jit(solution)/shard_map/ppermute | solution.py:542
  48.2 3.6 %collective-permute-start.22 = (f32[8,128]{1,0:T(8,128)S(1)}, f32[8,128]{1,0:T(8,128)S(1)}, u32[]{:S(2)}, u32[]{:S(2)}) collective-permute-start(f32[8,128]{1,0:T(8,128)S(1)} %slice.8), channel_id=1, source_target_pairs={{0,96},{16,48},{32,0},{48,80},{64,32},{80,112},{96,64},{112,16},{1... | collective-permute-start | bytes 12296 | tf_op jit(solution)/shard_map/ppermute | solution.py:545
  49.1 5.1 %collective-permute-start.21 = (f32[8,128]{1,0:T(8,128)S(1)}, f32[8,128]{1,0:T(8,128)S(1)}, u32[]{:S(2)}, u32[]{:S(2)}) collective-permute-start(f32[8,128]{1,0:T(8,128)S(1)} %slice.8), channel_id=1, source_target_pairs={{0,64},{16,80},{32,96},{48,112},{64,0},{80,16},{96,32},{112,48},{1... | collective-permute-start | bytes 12296 | tf_op jit(solution)/shard_map/ppermute | solution.py:544
  54.7 5.2 %collective-permute-start.25 = (f32[4,16,128]{2,1,0:T(8,128)S(1)}, f32[4,16,128]{2,1,0:T(8,128)S(1)}, u32[]{:S(2)}, u32[]{:S(2)}) collective-permute-start(f32[4,16,128]{2,1,0:T(8,128)S(1)} %get-tuple-element.62.refs_8_.refs_16_), channel_id=1, source_target_pairs={{0,3},{1,2},{2,1},{3,0},{4,7},{5,6},{6,5},{7,4},{8,11},{9,10},{10,... | collective-permute-start | bytes 98312 | tf_op jit(solution)/shard_map/ppermute | solution.py:535
  56.9 5.4 %collective-permute-start.24 = (f32[4,16,128]{2,1,0:T(8,128)S(1)}, f32[4,16,128]{2,1,0:T(8,128)S(1)}, u32[]{:S(2)}, u32[]{:S(2)}) collective-permute-start(f32[4,16,128]{2,1,0:T(8,128)S(1)} %get-tuple-element.62.refs_8_.refs_16_), channel_id=1, source_target_pairs={{0,2},{1,3},{2,0},{3,1},{4,6},{5,7},{6,4},{7,5},{8,10},{9,11},{10,... | collective-permute-start | bytes 98312 | tf_op jit(solution)/shard_map/ppermute | solution.py:535
  57.6 4.7 %collective-permute-start.23 = (f32[4,16,128]{2,1,0:T(8,128)S(1)}, f32[4,16,128]{2,1,0:T(8,128)S(1)}, u32[]{:S(2)}, u32[]{:S(2)}) collective-permute-start(f32[4,16,128]{2,1,0:T(8,128)S(1)} %get-tuple-element.62.refs_8_.refs_16_), channel_id=1, source_target_pairs={{0,1},{1,0},{2,3},{3,2},{4,5},{5,4},{6,7},{7,6},{8,9},{9,8},{10,11... | collective-permute-start | bytes 98312 | tf_op jit(solution)/shard_map/ppermute | solution.py:535
  62.5 5.2 %collective-permute-start.28 = (f32[4,16,128]{2,1,0:T(8,128)S(1)}, f32[4,16,128]{2,1,0:T(8,128)S(1)}, u32[]{:S(2)}, u32[]{:S(2)}) collective-permute-start(f32[4,16,128]{2,1,0:T(8,128)S(1)} %group_total_again.1.refs_20_), channel_id=1, source_target_pairs={{0,12},{1,13},{2,14},{3,15},{4,8},{5,9},{6,10},{7,11},{8,4},{9,5},... | collective-permute-start | bytes 98312 | tf_op jit(solution)/shard_map/ppermute | solution.py:535
  64.4 5.4 %collective-permute-start.27 = (f32[4,16,128]{2,1,0:T(8,128)S(1)}, f32[4,16,128]{2,1,0:T(8,128)S(1)}, u32[]{:S(2)}, u32[]{:S(2)}) collective-permute-start(f32[4,16,128]{2,1,0:T(8,128)S(1)} %group_total_again.1.refs_20_), channel_id=1, source_target_pairs={{0,8},{1,9},{2,10},{3,11},{4,12},{5,13},{6,14},{7,15},{8,0},{9,1},... | collective-permute-start | bytes 98312 | tf_op jit(solution)/shard_map/ppermute | solution.py:535
  65.8 4.0 %collective-permute-start.26 = (f32[4,16,128]{2,1,0:T(8,128)S(1)}, f32[4,16,128]{2,1,0:T(8,128)S(1)}, u32[]{:S(2)}, u32[]{:S(2)}) collective-permute-start(f32[4,16,128]{2,1,0:T(8,128)S(1)} %group_total_again.1.refs_20_), channel_id=1, source_target_pairs={{0,4},{1,5},{2,6},{3,7},{4,0},{5,1},{6,2},{7,3},{8,12},{9,13},{10,... | collective-permute-start | bytes 98312 | tf_op jit(solution)/shard_map/ppermute | solution.py:535
  72.0 5.8 %collective-permute-start.30 = (f32[24,128]{1,0:T(8,128)S(1)}, f32[24,128]{1,0:T(8,128)S(1)}, u32[]{:S(2)}, u32[]{:S(2)}) collective-permute-start(f32[24,128]{1,0:T(8,128)S(1)} %select_add_fusion.sent_b), channel_id=1, source_target_pairs={{0,112},{16,32},{32,16},{48,64},{64,48},{80,96},{96,80},{112,0},{1... | collective-permute-start | bytes 36872 | tf_op jit(solution)/shard_map/ppermute | solution.py:542
  72.6 5.1 %collective-permute-start.31 = (f32[8,128]{1,0:T(8,128)S(1)}, f32[8,128]{1,0:T(8,128)S(1)}, u32[]{:S(2)}, u32[]{:S(2)}) collective-permute-start(f32[8,128]{1,0:T(8,128)S(1)} %slice.9), channel_id=1, source_target_pairs={{0,64},{16,80},{32,96},{48,112},{64,0},{80,16},{96,32},{112,48},{1... | collective-permute-start | bytes 12296 | tf_op jit(solution)/shard_map/ppermute | solution.py:544
  79.4 4.7 %collective-permute-start.36 = (f32[8,128]{1,0:T(8,128)S(1)}, f32[8,128]{1,0:T(8,128)S(1)}, u32[]{:S(2)}, u32[]{:S(2)}) collective-permute-start(f32[8,128]{1,0:T(8,128)S(1)} %add.45), channel_id=1, source_target_pairs={{0,96},{16,112},{32,0},{48,16},{64,32},{80,48},{96,64},{112,80},{1... | collective-permute-start | bytes 12296 | tf_op jit(solution)/shard_map/ppermute | solution.py:551
  81.8 5.1 %collective-permute-start.35 = (f32[8,128]{1,0:T(8,128)S(1)}, f32[8,128]{1,0:T(8,128)S(1)}, u32[]{:S(2)}, u32[]{:S(2)}) collective-permute-start(f32[8,128]{1,0:T(8,128)S(1)} %add.45), channel_id=1, source_target_pairs={{0,64},{16,80},{32,96},{48,112},{64,0},{80,16},{96,32},{112,48},{1... | collective-permute-start | bytes 12296 | tf_op jit(solution)/shard_map/ppermute | solution.py:551
  83.2 4.8 %collective-permute-start.34 = (f32[8,128]{1,0:T(8,128)S(1)}, f32[8,128]{1,0:T(8,128)S(1)}, u32[]{:S(2)}, u32[]{:S(2)}) collective-permute-start(f32[8,128]{1,0:T(8,128)S(1)} %add.45), channel_id=1, source_target_pairs={{0,32},{16,48},{32,64},{48,80},{64,96},{80,112},{96,0},{112,16},{1... | collective-permute-start | bytes 12296 | tf_op jit(solution)/shard_map/ppermute | solution.py:551
  (10 other events, 24.6 us)

commit v5 on v4

--- a/solution.py
+++ b/solution.py
@@ -14,6 +14,7 @@
 PLANE = (CX, NZ)
 N_GX, N_GY = 8, 16
 W_ALL = 128
+PARTNERS = (0, 1, 3, 2)
 PREPARE_VMEM = 54400
 EDGES_VMEM = 55296
 SLOTS_ALL = 256
@@ -171,13 +172,12 @@
         edge[c * CX : (c + 1) * CX, :] = plane(ty, c, CY - 1)
 
 
-def relay(own, m1, m2, m3):
+def relay(*messages):
     z = position()[1] % 4
-    row = lax.broadcasted_iota(jnp.int32, own.shape, 0)
-    out = jnp.where(row < 2 * CX, z == 3, row == 2 * CX)
-    out = jnp.where(out, own, 0.0)
-    for k, ref in ((1, m1), (2, m2), (3, m3)):
-        out = jnp.where(jnp.where(row < 2 * CX, z == 3 - k, row == 2 * CX + k), ref, out)
+    row = lax.broadcasted_iota(jnp.int32, messages[0].shape, 0)
+    out = jnp.zeros_like(messages[0])
+    for k, ref in enumerate(messages):
+        out = jnp.where(jnp.where(row < 2 * CX, z == 3 - PARTNERS[k], row == 2 * CX + k), ref, out)
     return out
 
 
@@ -210,18 +210,18 @@
 
 
 def condense_kernel(diag, cross, ty, rhs, lx_in, *refs):
-    own, m1, m2, m3, o0, o1, o2, o3 = refs[:8]
+    messages, relayed = refs[:4], refs[4:8]
     seg_a, seg_b, dmat, tau_o, sinv, binv, ly_in = refs[8:15]
     brk, near, far = refs[15:]
     gy = position()[1]
     z_at, y_at = gy % 4, gy // 4
     for k in range(4):
-        near[jnp.bitwise_xor(z_at, k)] = (own, m1, m2, m3)[k][0 : 2 * CX, :]
-        at = jnp.bitwise_xor(y_at, k)
-        ref = (o0, o1, o2, o3)[k]
-        far[at] = ref[0 : 2 * CX, :]
+        near[jnp.bitwise_xor(z_at, PARTNERS[k])] = messages[k][0 : 2 * CX, :]
+        at = jnp.bitwise_xor(y_at, PARTNERS[k])
+        far[at] = relayed[k][0 : 2 * CX, :]
         for i in range(4):
-            brk[pl.ds(4 * at + jnp.bitwise_xor(z_at, i), 1), :] = ref[2 * CX + i : 2 * CX + i + 1, :]
+            row = relayed[k][2 * CX + i : 2 * CX + i + 1, :]
+            brk[pl.ds(4 * at + jnp.bitwise_xor(z_at, PARTNERS[i]), 1), :] = row
     cuts = pltpu.roll(brk[...], (NZ - CY * gy) % NZ, 1)
     before = jnp.where(y_at > 0, far[jnp.maximum(y_at - 1, 0)], 0.0)
     before = jnp.where(z_at > 0, near[jnp.maximum(z_at - 1, 0)], before)
@@ -273,29 +273,29 @@
         store_segment(ref, [[x[8 * half : 8 * half + 8] for x in part] for part in whole], True)
 
 
-def gather_matrices(position, halves, mat_s):
+def gather_matrices(at_place, halves, mat_s):
     for k in range(4):
-        at = jnp.bitwise_xor(position, k)
+        at = jnp.bitwise_xor(at_place, PARTNERS[k])
         for half, refs in enumerate(halves):
             mat_s[at, :, 8 * half : 8 * half + 8, :] = refs[k][0:16]
 
 
-def gather_vectors(position, vecs, vec_s):
+def gather_vectors(at_place, vecs, vec_s):
     for k in range(4):
-        vec_s[jnp.bitwise_xor(position, k)] = vecs[k][...]
-
-
-def gather_both(position, halves, mat_s, vec_s):
-    gather_matrices(position, halves, mat_s)
+        vec_s[jnp.bitwise_xor(at_place, PARTNERS[k])] = vecs[k][...]
+
+
+def gather_both(at_place, halves, mat_s, vec_s):
+    gather_matrices(at_place, halves, mat_s)
     for k in range(4):
-        at = jnp.bitwise_xor(position, k)
+        at = jnp.bitwise_xor(at_place, PARTNERS[k])
         for half, refs in enumerate(halves):
             vec_s[at, :, 8 * half : 8 * half + 8, :] = refs[k][16:20]
 
 
 def total_half_kernel(own, m1, m2, m3, out, segs_s):
     for k, ref in enumerate((own, m1, m2, m3)):
-        segs_s[jnp.bitwise_xor(position()[1] % 4, k)] = ref[...]
+        segs_s[jnp.bitwise_xor(position()[1] % 4, PARTNERS[k])] = ref[...]
     segs = [load_segment(segs_s.at[m], segs_s.at[m], 16) for m in range(4)]
     store_segment(out, join(join(segs[0], segs[1]), join(segs[2], segs[3])), True)
 
@@ -420,7 +420,7 @@
 
 def apply_operator(got, cells, wells, weights):
     gx = position()[0]
-    got_a, sent_b, got_b, got_c, got_d = got
+    got_a, sent_b, got_d, got_b, got_c = got
     tail = sent_b[16:24, :] + got_b[16:24, :] + got_c[...] + got_d[...]
     rates = tail[0:1] / jnp.maximum(tail[1:2], 1.0)
     at_row, at_layer, at_well = slot_tables(cells, wells)
@@ -453,8 +453,8 @@
     return out
 
 
-def first_image_kernel(got_a, sent_b, got_b, got_c, got_d, p, ends, dmat, tau_r, sinv, binv, rhs, tx, ty, tz, lx_in, ly_in, cells, wells, weights, q_out, e_out, vec_out, dots):
-    well_add, after, before = apply_operator((got_a, sent_b, got_b, got_c, got_d), cells, wells, weights)
+def first_image_kernel(got_a, sent_b, got_d, got_b, got_c, p, ends, dmat, tau_r, sinv, binv, rhs, tx, ty, tz, lx_in, ly_in, cells, wells, weights, q_out, e_out, vec_out, dots):
+    well_add, after, before = apply_operator((got_a, sent_b, got_d, got_b, got_c), cells, wells, weights)
     eq = jnp.zeros(PLANE, F32)
     qq = jnp.zeros(PLANE, F32)
     e = []
@@ -484,8 +484,8 @@
         vec_out[2 + c] = last[c]
 
 
-def second_image_kernel(got_a, sent_b, got_b, got_c, got_d, p, ends, dmat, tx, ty, tz, lx_in, ly_in, cells, wells, weights, q_in, e_in, dots_in, s_out, dots):
-    well_add, after, before = apply_operator((got_a, sent_b, got_b, got_c, got_d), cells, wells, weights)
+def second_image_kernel(got_a, sent_b, got_d, got_b, got_c, p, ends, dmat, tx, ty, tz, lx_in, ly_in, cells, wells, weights, q_in, e_in, dots_in, s_out, dots):
+    well_add, after, before = apply_operator((got_a, sent_b, got_d, got_b, got_c), cells, wells, weights)
     sq = jnp.zeros(PLANE, F32)
     ss = jnp.zeros(PLANE, F32)
     es = jnp.zeros(PLANE, F32)
@@ -532,23 +532,24 @@
 
 
 def swapped(block, stride):
-    return [block] + [lax.ppermute(block, "gy", [(i, i ^ (k * stride)) for i in range(N_GY)]) for k in (1, 2, 3)]
+    others = [lax.ppermute(block, "gy", [(i, i ^ (k * stride)) for i in range(N_GY)]) for k in PARTNERS[1:]]
+    return [block] + others
 
 
 def exchange_rows(msg_a, msg_b):
     got_a = lax.ppermute(msg_a, "gx", [(i, i ^ 1) for i in range(N_GX)])
     below = lax.broadcasted_iota(jnp.int32, msg_b.shape, 0) >= 16
+    tail = msg_b[16:] + got_a[16:]
     sent_b = msg_b + jnp.where(below, got_a, 0.0)
+    got_d = lax.ppermute(tail, "gx", [(i, (i + 2 if i % 2 else i - 2) % N_GX) for i in range(N_GX)])
     got_b = lax.ppermute(sent_b, "gx", [(i, (i + 1 if i % 2 else i - 1) % N_GX) for i in range(N_GX)])
-    tail = sent_b[16:]
     got_c = lax.ppermute(tail, "gx", [(i, i ^ 4) for i in range(N_GX)])
-    got_d = lax.ppermute(tail, "gx", [(i, (i + 2 if i % 2 else i - 2) % N_GX) for i in range(N_GX)])
-    return got_a, sent_b, got_b, got_c, got_d
+    return got_a, sent_b, got_d, got_b, got_c
 
 
 def sum_everywhere(x):
     x = x + lax.ppermute(x, "gx", [(i, i ^ 1) for i in range(N_GX)])
-    others = [lax.ppermute(x, "gx", [(i, (i + 2 * k) % N_GX) for i in range(N_GX)]) for k in (1, 2, 3)]
+    others = [lax.ppermute(x, "gx", [(i, (i + 2 * k) % N_GX) for i in range(N_GX)]) for k in (1, 3, 2)]
     x = x + others[0] + others[1] + others[2]
     x = jnp.broadcast_to(x[None], (N_GY,) + x.shape)
     return lax.all_to_all(x, "gy", split_axis=0, concat_axis=0, tiled=True)
@@ -574,9 +575,9 @@
         flat(right_side), flat(accumulation), flat(trans_x), flat(trans_y), flat(trans_z),
         specs=[HBM] * 5, vmem=PREPARE_VMEM,
     )
+    edges = swapped(edge, 1)
     lx = lax.ppermute(sx, "gx", [(i, i + 1) for i in range(N_GX - 1)])
-    edges = swapped(edge, 1)
-    lx, *edges = lax.optimization_barrier((lx, *edges))
+    *edges, lx = lax.optimization_barrier((*edges, lx))
     relayed = swapped(relay(*edges), 4)
     slots = perf_cell.shape[3]
     live = jnp.arange(slots, dtype=jnp.int32)[None, :] < perf_count.reshape(N_GX, 1)

time: 101 us -> 101 us (level)
  starting transfers between devices: 49.9 us -> 48.2 us
  waiting for transfers between devices: 30 us -> 31.4 us
    ppermute x24, starting transfers between devices: 34.3 us -> 31.6 us  [swapped(): lax.ppermute(block, 'gy', [(i, i ^ k * stride) for i in range(N_GY)])]
    ppermute x2, waiting for transfers between devices: 2.57 us -> 0.01 us  [exchange_rows(): lax.ppermute(tail, 'gx', [(i, (i + 2 if i % 2 else i - 2) % N_GX) for i i...]
    ppermute x24, waiting for transfers between devices: 14.8 us -> 17.3 us  [swapped(): lax.ppermute(block, 'gy', [(i, i ^ k * stride) for i in range(N_GY)])]
    ppermute x2, starting transfers between devices: 3.46 us -> 1.17 us  [exchange_rows(): got_c = lax.ppermute(tail, 'gx', [(i, i ^ 4) for i in range(N_GX)])]
    ppermute x2, starting transfers between devices: 1.18 us -> 3.28 us  [exchange_rows(): lax.ppermute(tail, 'gx', [(i, (i + 2 if i % 2 else i - 2) % N_GX) for i i...]
    ppermute x2, starting transfers between devices: 4.97 us -> 6.66 us  [exchange_rows(): lax.ppermute(sent_b, 'gx', [(i, (i + 1 if i % 2 else i - 1) % N_GX) for i...]
    ppermute x2, waiting for transfers between devices: 4.19 us -> 5.77 us  [exchange_rows(): got_c = lax.ppermute(tail, 'gx', [(i, i ^ 4) for i in range(N_GX)])]
  transfers between devices with their start and end apart: 37 -> 37, of which waited for: 18 -> 19; matrix products, arithmetic and copies ran while one was open for 1% -> 1% of each run, Pallas kernels for 2% -> 2%
where the time goes in v5:
time: 101 us
  starting transfers between devices  48.2 us (48%)
  waiting for transfers between devices  31.4 us (31%)
  blocking collectives  12.6 us (12%)
  Pallas kernels  7.24 us (7%)
    ppermute x24, starting transfers between devices, swapped(): lax.ppermute(block, 'gy', [(i, i ^ k * stride) for i in range(N_GY)])  31.6 us
    ppermute x24, waiting for transfers between devices, swapped(): lax.ppermute(block, 'gy', [(i, i ^ k * stride) for i in range(N_GY)])  17.3 us
    all_to_all x1, blocking collectives, sum_everywhere(): return lax.all_to_all(x, 'gy', split_axis=0, concat_axis=0, tiled=True)  12.6 us
    pallas_call x11, Pallas kernels, call(): pl.pallas_call(kernel, name=name, out_shape=tuple(outs), in_specs=specs o...  7.24 us
    ppermute x2, starting transfers between devices, exchange_rows(): lax.ppermute(sent_b, 'gx', [(i, (i + 1 if i % 2 else i - 1) % N_GX) for i...  6.66 us
    ppermute x2, waiting for transfers between devices, exchange_rows(): got_c = lax.ppermute(tail, 'gx', [(i, i ^ 4) for i in range(N_GX)])  5.77 us
    ppermute x3, starting transfers between devices, sum_everywhere(): lax.ppermute(x, 'gx', [(i, (i + 2 * k) % N_GX) for i in range(N_GX)])  4.05 us
    ppermute x3, waiting for transfers between devices, sum_everywhere(): lax.ppermute(x, 'gx', [(i, (i + 2 * k) % N_GX) for i in range(N_GX)])  4.02 us
  transfers between devices with their start and end apart: 37, of which 19 were waited for; matrix products, arithmetic and copies ran while one was open for 1% of the time, Pallas kernels for 2%

profile of v5, /device:TPU:0, one launch (start us, length us, event | category | flops | bytes accessed | tf_op | source)
XLA Modules:
  0.0 101.2 jit_solution(10026110263211237111)
XLA Ops:
  0.6 1.6 %edges.1 = (f32[2,8,128]{2,1,0:T(8,128)}, f32[40,128]{1,0:T(8,128)}) custom-call(f32[2,128,128]{2,1,0:T(8,128)} %bitcast.14, f32[2,128,128]{2,1,0:T(8,128)} %bitcast.16, s32[1,128]{1,0:T(1,128)} %brk_h.1), custom_call_target="tpu_custom_call" | custom-call | tf_op jit(solution)/shard_map/edges/pallas_call | solution.py:523
  2.2 4.0 %collective-permute-start.2 = (f32[40,128]{1,0:T(8,128)}, f32[40,128]{1,0:T(8,128)S(1)}, u32[]{:S(2)}, u32[]{:S(2)}) collective-permute-start(f32[40,128]{1,0:T(8,128)} %get-tuple-element.45.refs_0_), channel_id=1, source_target_pairs={{0,2},{1,3},{2,0},{3,1},{4,6},{5,7},{6,4},{7,5},{8,10},{9,11},{10,... | collective-permute-start | bytes 61448 | tf_op jit(solution)/shard_map/ppermute | solution.py:535
  7.3 1.3 %collective-permute-start.3 = (f32[2,8,128]{2,1,0:T(8,128)}, f32[2,8,128]{2,1,0:T(8,128)S(1)}, u32[]{:S(2)}, u32[]{:S(2)}) collective-permute-start(f32[2,8,128]{2,1,0:T(8,128)} %get-tuple-element.43), channel_id=1, source_target_pairs={{0,16},{16,32},{32,48},{48,64},{64,80},{80,96},{96,112},{1,17},{17... | collective-permute-start | bytes 24584 | tf_op jit(solution)/shard_map/ppermute | solution.py:579
  9.6 1.9 %collective-permute-done.1.refs_2_ = f32[40,128]{1,0:T(8,128)S(1)} collective-permute-done((f32[40,128]{1,0:T(8,128)}, f32[40,128]{1,0:T(8,128)S(1)}, u32[]{:S(2)}, u32[]{:S(2)}) %collective-permute-start.1) | collective-permute-done | bytes 20512 | tf_op jit(solution)/shard_map/ppermute | solution.py:535
  11.5 3.3 %collective-permute-start.6 = (f32[40,128]{1,0:T(8,128)S(1)}, f32[40,128]{1,0:T(8,128)S(1)}, u32[]{:S(2)}, u32[]{:S(2)}) collective-permute-start(f32[40,128]{1,0:T(8,128)S(1)} %select_select_fusion.refs_4_), channel_id=1, source_target_pairs={{0,8},{1,9},{2,10},{3,11},{4,12},{5,13},{6,14},{7,15},{8,0},{9,1},... | collective-permute-start | bytes 61448 | tf_op jit(solution)/shard_map/ppermute | solution.py:535
  14.8 1.1 %collective-permute-start.5 = (f32[40,128]{1,0:T(8,128)S(1)}, f32[40,128]{1,0:T(8,128)S(1)}, u32[]{:S(2)}, u32[]{:S(2)}) collective-permute-start(f32[40,128]{1,0:T(8,128)S(1)} %select_select_fusion.refs_4_), channel_id=1, source_target_pairs={{0,12},{1,13},{2,14},{3,15},{4,8},{5,9},{6,10},{7,11},{8,4},{9,5},... | collective-permute-start | bytes 61448 | tf_op jit(solution)/shard_map/ppermute | solution.py:535
  15.9 1.4 %prepare.1 = (f32[2,8,16,128]{3,2,1,0:T(8,128)S(1)}, f32[2,8,16,128]{3,2,1,0:T(8,128)S(1)}, f32[2,8,16,128]{3,2,1,0:T(8,128)S(1)}, f32[2,8,16,128]{3,2,1,0:T(8,1...) custom-call(f32[2,128,128]{2,1,0:T(8,128)} %bitcast.19, f32[4,128,128]{2,1,0:T(8,128)} %bitcast.18, ...), custom_call_target="tpu_custom_call" | custom-call | tf_op jit(solution)/shard_map/prepare/pallas_call | solution.py:523
  17.3 2.5 %collective-permute-done.5.refs_6_ = f32[40,128]{1,0:T(8,128)S(1)} collective-permute-done((f32[40,128]{1,0:T(8,128)S(1)}, f32[40,128]{1,0:T(8,128)S(1)}, u32[]{:S(2)}, u32[]{:S(2)}) %collective-permute-start.5) | collective-permute-done | bytes 20512 | tf_op jit(solution)/shard_map/ppermute | solution.py:535
  20.2 2.0 %collective-permute-start.9 = (f32[20,8,128]{2,1,0:T(8,128)S(1)}, f32[20,8,128]{2,1,0:T(8,128)S(1)}, u32[]{:S(2)}, u32[]{:S(2)}) collective-permute-start(f32[20,8,128]{2,1,0:T(8,128)S(1)} %get-tuple-element.49.own.refs_0_), channel_id=1, source_target_pairs={{0,2},{1,3},{2,0},{3,1},{4,6},{5,7},{6,4},{7,5},{8,10},{9,11},{10,... | collective-permute-start | bytes 245768 | tf_op jit(solution)/shard_map/ppermute | solution.py:535
  24.0 3.1 %collective-permute-start.12 = (f32[20,8,128]{2,1,0:T(8,128)S(1)}, f32[20,8,128]{2,1,0:T(8,128)S(1)}, u32[]{:S(2)}, u32[]{:S(2)}) collective-permute-start(f32[20,8,128]{2,1,0:T(8,128)S(1)} %get-tuple-element.50.own.refs_4_), channel_id=1, source_target_pairs={{0,2},{1,3},{2,0},{3,1},{4,6},{5,7},{6,4},{7,5},{8,10},{9,11},{10,... | collective-permute-start | bytes 245768 | tf_op jit(solution)/shard_map/ppermute | solution.py:535
  28.3 1.8 %collective-permute-start.15 = (f32[20,8,128]{2,1,0:T(8,128)S(1)}, f32[20,8,128]{2,1,0:T(8,128)S(1)}, u32[]{:S(2)}, u32[]{:S(2)}) collective-permute-start(f32[20,8,128]{2,1,0:T(8,128)S(1)} %group_total.2.refs_8_), channel_id=1, source_target_pairs={{0,8},{1,9},{2,10},{3,11},{4,12},{5,13},{6,14},{7,15},{8,0},{9,1},... | collective-permute-start | bytes 245768 | tf_op jit(solution)/shard_map/ppermute | solution.py:535
  30.3 1.1 %collective-permute-start.14 = (f32[20,8,128]{2,1,0:T(8,128)S(1)}, f32[20,8,128]{2,1,0:T(8,128)S(1)}, u32[]{:S(2)}, u32[]{:S(2)}) collective-permute-start(f32[20,8,128]{2,1,0:T(8,128)S(1)} %group_total.2.refs_8_), channel_id=1, source_target_pairs={{0,12},{1,13},{2,14},{3,15},{4,8},{5,9},{6,10},{7,11},{8,4},{9,5},... | collective-permute-start | bytes 245768 | tf_op jit(solution)/shard_map/ppermute | solution.py:535
  33.0 2.2 %collective-permute-start.18 = (f32[20,8,128]{2,1,0:T(8,128)S(1)}, f32[20,8,128]{2,1,0:T(8,128)S(1)}, u32[]{:S(2)}, u32[]{:S(2)}) collective-permute-start(f32[20,8,128]{2,1,0:T(8,128)S(1)} %group_total.3.refs_12_), channel_id=1, source_target_pairs={{0,8},{1,9},{2,10},{3,11},{4,12},{5,13},{6,14},{7,15},{8,0},{9,1},... | collective-permute-start | bytes 245768 | tf_op jit(solution)/shard_map/ppermute | solution.py:535
  36.7 2.4 %collective-permute-done.18.refs_15_ = f32[20,8,128]{2,1,0:T(8,128)S(1)} collective-permute-done((f32[20,8,128]{2,1,0:T(8,128)S(1)}, f32[20,8,128]{2,1,0:T(8,128)S(1)}, u32[]{:S(2)}, u32[]{:S(2)}) %collective-permute-start.18) | collective-permute-done | bytes 81952 | tf_op jit(solution)/shard_map/ppermute | solution.py:535
  39.2 1.7 %collective-permute-done.17.refs_14_ = f32[20,8,128]{2,1,0:T(8,128)S(1)} collective-permute-done((f32[20,8,128]{2,1,0:T(8,128)S(1)}, f32[20,8,128]{2,1,0:T(8,128)S(1)}, u32[]{:S(2)}, u32[]{:S(2)}) %collective-permute-start.17) | collective-permute-done | bytes 81952 | tf_op jit(solution)/shard_map/ppermute | solution.py:535
  41.8 1.2 %collective-permute-done.19.got_a = f32[24,128]{1,0:T(8,128)S(1)} collective-permute-done((f32[24,128]{1,0:T(8,128)S(1)}, f32[24,128]{1,0:T(8,128)S(1)}, u32[]{:S(2)}, u32[]{:S(2)}) %collective-permute-start.19) | collective-permute-done | bytes 12320 | tf_op jit(solution)/shard_map/ppermute | solution.py:540
  43.0 5.4 %collective-permute-start.21 = (f32[24,128]{1,0:T(8,128)S(1)}, f32[24,128]{1,0:T(8,128)S(1)}, u32[]{:S(2)}, u32[]{:S(2)}) collective-permute-start(f32[24,128]{1,0:T(8,128)S(1)} %select_add_fusion.1.sent_b), channel_id=1, source_target_pairs={{0,112},{16,32},{32,16},{48,64},{64,48},{80,96},{96,80},{112,0},{1... | collective-permute-start | bytes 36872 | tf_op jit(solution)/shard_map/ppermute | solution.py:545
  49.6 3.9 %collective-permute-done.22.got_c = f32[8,128]{1,0:T(8,128)S(1)} collective-permute-done((f32[8,128]{1,0:T(8,128)S(1)}, f32[8,128]{1,0:T(8,128)S(1)}, u32[]{:S(2)}, u32[]{:S(2)}) %collective-permute-start.22) | collective-permute-done | bytes 4128 | tf_op jit(solution)/shard_map/ppermute | solution.py:546
  54.0 3.5 %collective-permute-start.25 = (f32[4,16,128]{2,1,0:T(8,128)S(1)}, f32[4,16,128]{2,1,0:T(8,128)S(1)}, u32[]{:S(2)}, u32[]{:S(2)}) collective-permute-start(f32[4,16,128]{2,1,0:T(8,128)S(1)} %get-tuple-element.62.refs_8_.refs_16_), channel_id=1, source_target_pairs={{0,2},{1,3},{2,0},{3,1},{4,6},{5,7},{6,4},{7,5},{8,10},{9,11},{10,... | collective-permute-start | bytes 98312 | tf_op jit(solution)/shard_map/ppermute | solution.py:535
  58.2 1.3 %collective-permute-done.25.refs_11_.refs_19_ = f32[4,16,128]{2,1,0:T(8,128)S(1)} collective-permute-done((f32[4,16,128]{2,1,0:T(8,128)S(1)}, f32[4,16,128]{2,1,0:T(8,128)S(1)}, u32[]{:S(2)}, u32[]{:S(2)}) %collective-permute-start.25) | collective-permute-done | bytes 32800 | tf_op jit(solution)/shard_map/ppermute | solution.py:535
  59.5 3.1 %collective-permute-done.24.refs_10_.refs_18_ = f32[4,16,128]{2,1,0:T(8,128)S(1)} collective-permute-done((f32[4,16,128]{2,1,0:T(8,128)S(1)}, f32[4,16,128]{2,1,0:T(8,128)S(1)}, u32[]{:S(2)}, u32[]{:S(2)}) %collective-permute-start.24) | collective-permute-done | bytes 32800 | tf_op jit(solution)/shard_map/ppermute | solution.py:535
  62.8 1.5 %collective-permute-start.28 = (f32[4,16,128]{2,1,0:T(8,128)S(1)}, f32[4,16,128]{2,1,0:T(8,128)S(1)}, u32[]{:S(2)}, u32[]{:S(2)}) collective-permute-start(f32[4,16,128]{2,1,0:T(8,128)S(1)} %group_total_again.1.refs_20_), channel_id=1, source_target_pairs={{0,8},{1,9},{2,10},{3,11},{4,12},{5,13},{6,14},{7,15},{8,0},{9,1},... | collective-permute-start | bytes 98312 | tf_op jit(solution)/shard_map/ppermute | solution.py:535
  66.3 2.1 %collective-permute-done.28.refs_23_ = f32[4,16,128]{2,1,0:T(8,128)S(1)} collective-permute-done((f32[4,16,128]{2,1,0:T(8,128)S(1)}, f32[4,16,128]{2,1,0:T(8,128)S(1)}, u32[]{:S(2)}, u32[]{:S(2)}) %collective-permute-start.28) | collective-permute-done | bytes 32800 | tf_op jit(solution)/shard_map/ppermute | solution.py:535
  70.4 1.2 %collective-permute-done.29.got_a = f32[24,128]{1,0:T(8,128)S(1)} collective-permute-done((f32[24,128]{1,0:T(8,128)S(1)}, f32[24,128]{1,0:T(8,128)S(1)}, u32[]{:S(2)}, u32[]{:S(2)}) %collective-permute-start.29) | collective-permute-done | bytes 12320 | tf_op jit(solution)/shard_map/ppermute | solution.py:540
  71.6 1.2 %collective-permute-start.31 = (f32[24,128]{1,0:T(8,128)S(1)}, f32[24,128]{1,0:T(8,128)S(1)}, u32[]{:S(2)}, u32[]{:S(2)}) collective-permute-start(f32[24,128]{1,0:T(8,128)S(1)} %select_add_fusion.sent_b), channel_id=1, source_target_pairs={{0,112},{16,32},{32,16},{48,64},{64,48},{80,96},{96,80},{112,0},{1... | collective-permute-start | bytes 36872 | tf_op jit(solution)/shard_map/ppermute | solution.py:545
  73.8 2.3 %collective-permute-start.30 = (f32[8,128]{1,0:T(8,128)S(1)}, f32[8,128]{1,0:T(8,128)S(1)}, u32[]{:S(2)}, u32[]{:S(2)}) collective-permute-start(f32[8,128]{1,0:T(8,128)S(1)} %slice_add_fusion), channel_id=1, source_target_pairs={{0,96},{16,48},{32,0},{48,80},{64,32},{80,112},{96,64},{112,16},{1... | collective-permute-start | bytes 12296 | tf_op jit(solution)/shard_map/ppermute | solution.py:544
  76.1 1.9 %collective-permute-done.32.got_c = f32[8,128]{1,0:T(8,128)S(1)} collective-permute-done((f32[8,128]{1,0:T(8,128)S(1)}, f32[8,128]{1,0:T(8,128)S(1)}, u32[]{:S(2)}, u32[]{:S(2)}) %collective-permute-start.32) | collective-permute-done | bytes 4128 | tf_op jit(solution)/shard_map/ppermute | solution.py:546
  79.6 2.0 %collective-permute-start.36 = (f32[8,128]{1,0:T(8,128)S(1)}, f32[8,128]{1,0:T(8,128)S(1)}, u32[]{:S(2)}, u32[]{:S(2)}) collective-permute-start(f32[8,128]{1,0:T(8,128)S(1)} %add.53), channel_id=1, source_target_pairs={{0,64},{16,80},{32,96},{48,112},{64,0},{80,16},{96,32},{112,48},{1... | collective-permute-start | bytes 12296 | tf_op jit(solution)/shard_map/ppermute | solution.py:552
  81.7 1.2 %collective-permute-start.35 = (f32[8,128]{1,0:T(8,128)S(1)}, f32[8,128]{1,0:T(8,128)S(1)}, u32[]{:S(2)}, u32[]{:S(2)}) collective-permute-start(f32[8,128]{1,0:T(8,128)S(1)} %add.53), channel_id=1, source_target_pairs={{0,96},{16,112},{32,0},{48,16},{64,32},{80,48},{96,64},{112,80},{1... | collective-permute-start | bytes 12296 | tf_op jit(solution)/shard_map/ppermute | solution.py:552
  83.7 1.1 %collective-permute-done.36 = f32[8,128]{1,0:T(8,128)S(1)} collective-permute-done((f32[8,128]{1,0:T(8,128)S(1)}, f32[8,128]{1,0:T(8,128)S(1)}, u32[]{:S(2)}, u32[]{:S(2)}) %collective-permute-start.36) | collective-permute-done | bytes 4128 | tf_op jit(solution)/shard_map/ppermute | solution.py:552
  85.3 2.4 %collective-permute-done.34 = f32[8,128]{1,0:T(8,128)S(1)} collective-permute-done((f32[8,128]{1,0:T(8,128)S(1)}, f32[8,128]{1,0:T(8,128)S(1)}, u32[]{:S(2)}, u32[]{:S(2)}) %collective-permute-start.34) | collective-permute-done | bytes 4128 | tf_op jit(solution)/shard_map/ppermute | solution.py:552
  87.7 12.6 %all_to_all.5.got = f32[16,8,128]{2,1,0:T(8,128)S(1)} all-to-all(f32[16,8,128]{2,1,0:T(8,128)S(1)} %broadcast_in_dim.40), channel_id=1, replica_groups=mesh['gx'=8,'gy'=16] {'gy'}, dimensions={0} | all-to-all | bytes 131072 | tf_op jit(solution)/shard_map/all_to_all | solution.py:555
  (85 shorter events, 21.1 us)
Async XLA Ops:
  2.2 7.4 %collective-permute-start.2 = (f32[40,128]{1,0:T(8,128)}, f32[40,128]{1,0:T(8,128)S(1)}, u32[]{:S(2)}, u32[]{:S(2)}) collective-permute-start(f32[40,128]{1,0:T(8,128)} %get-tuple-element.45.refs_0_), channel_id=1, source_target_pairs={{0,2},{1,3},{2,0},{3,1},{4,6},{5,7},{6,4},{7,5},{8,10},{9,11},{10,... | collective-permute-start | bytes 61448 | tf_op jit(solution)/shard_map/ppermute | solution.py:535
  6.2 5.2 %collective-permute-start.1 = (f32[40,128]{1,0:T(8,128)}, f32[40,128]{1,0:T(8,128)S(1)}, u32[]{:S(2)}, u32[]{:S(2)}) collective-permute-start(f32[40,128]{1,0:T(8,128)} %get-tuple-element.45.refs_0_), channel_id=1, source_target_pairs={{0,3},{1,2},{2,1},{3,0},{4,7},{5,6},{6,5},{7,4},{8,11},{9,10},{10,... | collective-permute-start | bytes 61448 | tf_op jit(solution)/shard_map/ppermute | solution.py:535
  6.9 4.5 %collective-permute-start = (f32[40,128]{1,0:T(8,128)}, f32[40,128]{1,0:T(8,128)S(1)}, u32[]{:S(2)}, u32[]{:S(2)}) collective-permute-start(f32[40,128]{1,0:T(8,128)} %get-tuple-element.45.refs_0_), channel_id=1, source_target_pairs={{0,1},{1,0},{2,3},{3,2},{4,5},{5,4},{6,7},{7,6},{8,9},{9,8},{10,11... | collective-permute-start | bytes 61448 | tf_op jit(solution)/shard_map/ppermute | solution.py:535
  11.5 5.7 %collective-permute-start.6 = (f32[40,128]{1,0:T(8,128)S(1)}, f32[40,128]{1,0:T(8,128)S(1)}, u32[]{:S(2)}, u32[]{:S(2)}) collective-permute-start(f32[40,128]{1,0:T(8,128)S(1)} %select_select_fusion.refs_4_), channel_id=1, source_target_pairs={{0,8},{1,9},{2,10},{3,11},{4,12},{5,13},{6,14},{7,15},{8,0},{9,1},... | collective-permute-start | bytes 61448 | tf_op jit(solution)/shard_map/ppermute | solution.py:535
  14.8 5.0 %collective-permute-start.5 = (f32[40,128]{1,0:T(8,128)S(1)}, f32[40,128]{1,0:T(8,128)S(1)}, u32[]{:S(2)}, u32[]{:S(2)}) collective-permute-start(f32[40,128]{1,0:T(8,128)S(1)} %select_select_fusion.refs_4_), channel_id=1, source_target_pairs={{0,12},{1,13},{2,14},{3,15},{4,8},{5,9},{6,10},{7,11},{8,4},{9,5},... | collective-permute-start | bytes 61448 | tf_op jit(solution)/shard_map/ppermute | solution.py:535
  15.9 3.9 %collective-permute-start.4 = (f32[40,128]{1,0:T(8,128)S(1)}, f32[40,128]{1,0:T(8,128)S(1)}, u32[]{:S(2)}, u32[]{:S(2)}) collective-permute-start(f32[40,128]{1,0:T(8,128)S(1)} %select_select_fusion.refs_4_), channel_id=1, source_target_pairs={{0,4},{1,5},{2,6},{3,7},{4,0},{5,1},{6,2},{7,3},{8,12},{9,13},{10,... | collective-permute-start | bytes 61448 | tf_op jit(solution)/shard_map/ppermute | solution.py:535
  20.2 7.6 %collective-permute-start.9 = (f32[20,8,128]{2,1,0:T(8,128)S(1)}, f32[20,8,128]{2,1,0:T(8,128)S(1)}, u32[]{:S(2)}, u32[]{:S(2)}) collective-permute-start(f32[20,8,128]{2,1,0:T(8,128)S(1)} %get-tuple-element.49.own.refs_0_), channel_id=1, source_target_pairs={{0,2},{1,3},{2,0},{3,1},{4,6},{5,7},{6,4},{7,5},{8,10},{9,11},{10,... | collective-permute-start | bytes 245768 | tf_op jit(solution)/shard_map/ppermute | solution.py:535
  22.2 6.0 %collective-permute-start.8 = (f32[20,8,128]{2,1,0:T(8,128)S(1)}, f32[20,8,128]{2,1,0:T(8,128)S(1)}, u32[]{:S(2)}, u32[]{:S(2)}) collective-permute-start(f32[20,8,128]{2,1,0:T(8,128)S(1)} %get-tuple-element.49.own.refs_0_), channel_id=1, source_target_pairs={{0,3},{1,2},{2,1},{3,0},{4,7},{5,6},{6,5},{7,4},{8,11},{9,10},{10,... | collective-permute-start | bytes 245768 | tf_op jit(solution)/shard_map/ppermute | solution.py:535
  22.8 5.3 %collective-permute-start.7 = (f32[20,8,128]{2,1,0:T(8,128)S(1)}, f32[20,8,128]{2,1,0:T(8,128)S(1)}, u32[]{:S(2)}, u32[]{:S(2)}) collective-permute-start(f32[20,8,128]{2,1,0:T(8,128)S(1)} %get-tuple-element.49.own.refs_0_), channel_id=1, source_target_pairs={{0,1},{1,0},{2,3},{3,2},{4,5},{5,4},{6,7},{7,6},{8,9},{9,8},{10,11... | collective-permute-start | bytes 245768 | tf_op jit(solution)/shard_map/ppermute | solution.py:535
  24.0 7.3 %collective-permute-start.12 = (f32[20,8,128]{2,1,0:T(8,128)S(1)}, f32[20,8,128]{2,1,0:T(8,128)S(1)}, u32[]{:S(2)}, u32[]{:S(2)}) collective-permute-start(f32[20,8,128]{2,1,0:T(8,128)S(1)} %get-tuple-element.50.own.refs_4_), channel_id=1, source_target_pairs={{0,2},{1,3},{2,0},{3,1},{4,6},{5,7},{6,4},{7,5},{8,10},{9,11},{10,... | collective-permute-start | bytes 245768 | tf_op jit(solution)/shard_map/ppermute | solution.py:535
  27.1 5.7 %collective-permute-start.11 = (f32[20,8,128]{2,1,0:T(8,128)S(1)}, f32[20,8,128]{2,1,0:T(8,128)S(1)}, u32[]{:S(2)}, u32[]{:S(2)}) collective-permute-start(f32[20,8,128]{2,1,0:T(8,128)S(1)} %get-tuple-element.50.own.refs_4_), channel_id=1, source_target_pairs={{0,3},{1,2},{2,1},{3,0},{4,7},{5,6},{6,5},{7,4},{8,11},{9,10},{10,... | collective-permute-start | bytes 245768 | tf_op jit(solution)/shard_map/ppermute | solution.py:535
  27.8 5.1 %collective-permute-start.10 = (f32[20,8,128]{2,1,0:T(8,128)S(1)}, f32[20,8,128]{2,1,0:T(8,128)S(1)}, u32[]{:S(2)}, u32[]{:S(2)}) collective-permute-start(f32[20,8,128]{2,1,0:T(8,128)S(1)} %get-tuple-element.50.own.refs_4_), channel_id=1, source_target_pairs={{0,1},{1,0},{2,3},{3,2},{4,5},{5,4},{6,7},{7,6},{8,9},{9,8},{10,11... | collective-permute-start | bytes 245768 | tf_op jit(solution)/shard_map/ppermute | solution.py:535
  28.3 8.0 %collective-permute-start.15 = (f32[20,8,128]{2,1,0:T(8,128)S(1)}, f32[20,8,128]{2,1,0:T(8,128)S(1)}, u32[]{:S(2)}, u32[]{:S(2)}) collective-permute-start(f32[20,8,128]{2,1,0:T(8,128)S(1)} %group_total.2.refs_8_), channel_id=1, source_target_pairs={{0,8},{1,9},{2,10},{3,11},{4,12},{5,13},{6,14},{7,15},{8,0},{9,1},... | collective-permute-start | bytes 245768 | tf_op jit(solution)/shard_map/ppermute | solution.py:535
  30.3 6.5 %collective-permute-start.14 = (f32[20,8,128]{2,1,0:T(8,128)S(1)}, f32[20,8,128]{2,1,0:T(8,128)S(1)}, u32[]{:S(2)}, u32[]{:S(2)}) collective-permute-start(f32[20,8,128]{2,1,0:T(8,128)S(1)} %group_total.2.refs_8_), channel_id=1, source_target_pairs={{0,12},{1,13},{2,14},{3,15},{4,8},{5,9},{6,10},{7,11},{8,4},{9,5},... | collective-permute-start | bytes 245768 | tf_op jit(solution)/shard_map/ppermute | solution.py:535
  31.3 5.4 %collective-permute-start.13 = (f32[20,8,128]{2,1,0:T(8,128)S(1)}, f32[20,8,128]{2,1,0:T(8,128)S(1)}, u32[]{:S(2)}, u32[]{:S(2)}) collective-permute-start(f32[20,8,128]{2,1,0:T(8,128)S(1)} %group_total.2.refs_8_), channel_id=1, source_target_pairs={{0,4},{1,5},{2,6},{3,7},{4,0},{5,1},{6,2},{7,3},{8,12},{9,13},{10,... | collective-permute-start | bytes 245768 | tf_op jit(solution)/shard_map/ppermute | solution.py:535
  33.0 6.2 %collective-permute-start.18 = (f32[20,8,128]{2,1,0:T(8,128)S(1)}, f32[20,8,128]{2,1,0:T(8,128)S(1)}, u32[]{:S(2)}, u32[]{:S(2)}) collective-permute-start(f32[20,8,128]{2,1,0:T(8,128)S(1)} %group_total.3.refs_12_), channel_id=1, source_target_pairs={{0,8},{1,9},{2,10},{3,11},{4,12},{5,13},{6,14},{7,15},{8,0},{9,1},... | collective-permute-start | bytes 245768 | tf_op jit(solution)/shard_map/ppermute | solution.py:535
  35.2 5.7 %collective-permute-start.17 = (f32[20,8,128]{2,1,0:T(8,128)S(1)}, f32[20,8,128]{2,1,0:T(8,128)S(1)}, u32[]{:S(2)}, u32[]{:S(2)}) collective-permute-start(f32[20,8,128]{2,1,0:T(8,128)S(1)} %group_total.3.refs_12_), channel_id=1, source_target_pairs={{0,12},{1,13},{2,14},{3,15},{4,8},{5,9},{6,10},{7,11},{8,4},{9,5},... | collective-permute-start | bytes 245768 | tf_op jit(solution)/shard_map/ppermute | solution.py:535
  36.3 4.6 %collective-permute-start.16 = (f32[20,8,128]{2,1,0:T(8,128)S(1)}, f32[20,8,128]{2,1,0:T(8,128)S(1)}, u32[]{:S(2)}, u32[]{:S(2)}) collective-permute-start(f32[20,8,128]{2,1,0:T(8,128)S(1)} %group_total.3.refs_12_), channel_id=1, source_target_pairs={{0,4},{1,5},{2,6},{3,7},{4,0},{5,1},{6,2},{7,3},{8,12},{9,13},{10,... | collective-permute-start | bytes 245768 | tf_op jit(solution)/shard_map/ppermute | solution.py:535
  43.0 10.6 %collective-permute-start.21 = (f32[24,128]{1,0:T(8,128)S(1)}, f32[24,128]{1,0:T(8,128)S(1)}, u32[]{:S(2)}, u32[]{:S(2)}) collective-permute-start(f32[24,128]{1,0:T(8,128)S(1)} %select_add_fusion.1.sent_b), channel_id=1, source_target_pairs={{0,112},{16,32},{32,16},{48,64},{64,48},{80,96},{96,80},{112,0},{1... | collective-permute-start | bytes 36872 | tf_op jit(solution)/shard_map/ppermute | solution.py:545
  48.4 5.1 %collective-permute-start.22 = (f32[8,128]{1,0:T(8,128)S(1)}, f32[8,128]{1,0:T(8,128)S(1)}, u32[]{:S(2)}, u32[]{:S(2)}) collective-permute-start(f32[8,128]{1,0:T(8,128)S(1)} %slice_add_fusion.1), channel_id=1, source_target_pairs={{0,64},{16,80},{32,96},{48,112},{64,0},{80,16},{96,32},{112,48},{1... | collective-permute-start | bytes 12296 | tf_op jit(solution)/shard_map/ppermute | solution.py:546
  48.7 4.9 %collective-permute-start.20 = (f32[8,128]{1,0:T(8,128)S(1)}, f32[8,128]{1,0:T(8,128)S(1)}, u32[]{:S(2)}, u32[]{:S(2)}) collective-permute-start(f32[8,128]{1,0:T(8,128)S(1)} %slice_add_fusion.1), channel_id=1, source_target_pairs={{0,96},{16,48},{32,0},{48,80},{64,32},{80,112},{96,64},{112,16},{1... | collective-permute-start | bytes 12296 | tf_op jit(solution)/shard_map/ppermute | solution.py:544
  54.0 5.5 %collective-permute-start.25 = (f32[4,16,128]{2,1,0:T(8,128)S(1)}, f32[4,16,128]{2,1,0:T(8,128)S(1)}, u32[]{:S(2)}, u32[]{:S(2)}) collective-permute-start(f32[4,16,128]{2,1,0:T(8,128)S(1)} %get-tuple-element.62.refs_8_.refs_16_), channel_id=1, source_target_pairs={{0,2},{1,3},{2,0},{3,1},{4,6},{5,7},{6,4},{7,5},{8,10},{9,11},{10,... | collective-permute-start | bytes 98312 | tf_op jit(solution)/shard_map/ppermute | solution.py:535
  57.5 5.1 %collective-permute-start.24 = (f32[4,16,128]{2,1,0:T(8,128)S(1)}, f32[4,16,128]{2,1,0:T(8,128)S(1)}, u32[]{:S(2)}, u32[]{:S(2)}) collective-permute-start(f32[4,16,128]{2,1,0:T(8,128)S(1)} %get-tuple-element.62.refs_8_.refs_16_), channel_id=1, source_target_pairs={{0,3},{1,2},{2,1},{3,0},{4,7},{5,6},{6,5},{7,4},{8,11},{9,10},{10,... | collective-permute-start | bytes 98312 | tf_op jit(solution)/shard_map/ppermute | solution.py:535
  58.2 4.4 %collective-permute-start.23 = (f32[4,16,128]{2,1,0:T(8,128)S(1)}, f32[4,16,128]{2,1,0:T(8,128)S(1)}, u32[]{:S(2)}, u32[]{:S(2)}) collective-permute-start(f32[4,16,128]{2,1,0:T(8,128)S(1)} %get-tuple-element.62.refs_8_.refs_16_), channel_id=1, source_target_pairs={{0,1},{1,0},{2,3},{3,2},{4,5},{5,4},{6,7},{7,6},{8,9},{9,8},{10,11... | collective-permute-start | bytes 98312 | tf_op jit(solution)/shard_map/ppermute | solution.py:535
  62.8 5.6 %collective-permute-start.28 = (f32[4,16,128]{2,1,0:T(8,128)S(1)}, f32[4,16,128]{2,1,0:T(8,128)S(1)}, u32[]{:S(2)}, u32[]{:S(2)}) collective-permute-start(f32[4,16,128]{2,1,0:T(8,128)S(1)} %group_total_again.1.refs_20_), channel_id=1, source_target_pairs={{0,8},{1,9},{2,10},{3,11},{4,12},{5,13},{6,14},{7,15},{8,0},{9,1},... | collective-permute-start | bytes 98312 | tf_op jit(solution)/shard_map/ppermute | solution.py:535
  64.3 5.1 %collective-permute-start.27 = (f32[4,16,128]{2,1,0:T(8,128)S(1)}, f32[4,16,128]{2,1,0:T(8,128)S(1)}, u32[]{:S(2)}, u32[]{:S(2)}) collective-permute-start(f32[4,16,128]{2,1,0:T(8,128)S(1)} %group_total_again.1.refs_20_), channel_id=1, source_target_pairs={{0,12},{1,13},{2,14},{3,15},{4,8},{5,9},{6,10},{7,11},{8,4},{9,5},... | collective-permute-start | bytes 98312 | tf_op jit(solution)/shard_map/ppermute | solution.py:535
  65.3 4.1 %collective-permute-start.26 = (f32[4,16,128]{2,1,0:T(8,128)S(1)}, f32[4,16,128]{2,1,0:T(8,128)S(1)}, u32[]{:S(2)}, u32[]{:S(2)}) collective-permute-start(f32[4,16,128]{2,1,0:T(8,128)S(1)} %group_total_again.1.refs_20_), channel_id=1, source_target_pairs={{0,4},{1,5},{2,6},{3,7},{4,0},{5,1},{6,2},{7,3},{8,12},{9,13},{10,... | collective-permute-start | bytes 98312 | tf_op jit(solution)/shard_map/ppermute | solution.py:535
  71.6 6.3 %collective-permute-start.31 = (f32[24,128]{1,0:T(8,128)S(1)}, f32[24,128]{1,0:T(8,128)S(1)}, u32[]{:S(2)}, u32[]{:S(2)}) collective-permute-start(f32[24,128]{1,0:T(8,128)S(1)} %select_add_fusion.sent_b), channel_id=1, source_target_pairs={{0,112},{16,32},{32,16},{48,64},{64,48},{80,96},{96,80},{112,0},{1... | collective-permute-start | bytes 36872 | tf_op jit(solution)/shard_map/ppermute | solution.py:545
  72.9 5.1 %collective-permute-start.32 = (f32[8,128]{1,0:T(8,128)S(1)}, f32[8,128]{1,0:T(8,128)S(1)}, u32[]{:S(2)}, u32[]{:S(2)}) collective-permute-start(f32[8,128]{1,0:T(8,128)S(1)} %slice_add_fusion), channel_id=1, source_target_pairs={{0,64},{16,80},{32,96},{48,112},{64,0},{80,16},{96,32},{112,48},{1... | collective-permute-start | bytes 12296 | tf_op jit(solution)/shard_map/ppermute | solution.py:546
  73.8 4.2 %collective-permute-start.30 = (f32[8,128]{1,0:T(8,128)S(1)}, f32[8,128]{1,0:T(8,128)S(1)}, u32[]{:S(2)}, u32[]{:S(2)}) collective-permute-start(f32[8,128]{1,0:T(8,128)S(1)} %slice_add_fusion), channel_id=1, source_target_pairs={{0,96},{16,48},{32,0},{48,80},{64,32},{80,112},{96,64},{112,16},{1... | collective-permute-start | bytes 12296 | tf_op jit(solution)/shard_map/ppermute | solution.py:544
  79.6 5.1 %collective-permute-start.36 = (f32[8,128]{1,0:T(8,128)S(1)}, f32[8,128]{1,0:T(8,128)S(1)}, u32[]{:S(2)}, u32[]{:S(2)}) collective-permute-start(f32[8,128]{1,0:T(8,128)S(1)} %add.53), channel_id=1, source_target_pairs={{0,64},{16,80},{32,96},{48,112},{64,0},{80,16},{96,32},{112,48},{1... | collective-permute-start | bytes 12296 | tf_op jit(solution)/shard_map/ppermute | solution.py:552
  82.9 4.8 %collective-permute-start.34 = (f32[8,128]{1,0:T(8,128)S(1)}, f32[8,128]{1,0:T(8,128)S(1)}, u32[]{:S(2)}, u32[]{:S(2)}) collective-permute-start(f32[8,128]{1,0:T(8,128)S(1)} %add.53), channel_id=1, source_target_pairs={{0,32},{16,48},{32,64},{48,80},{64,96},{80,112},{96,0},{112,16},{1... | collective-permute-start | bytes 12296 | tf_op jit(solution)/shard_map/ppermute | solution.py:552
  (10 other events, 23.9 us)

commit v6 on v5

--- a/solution.py
+++ b/solution.py
@@ -14,7 +14,7 @@
 PLANE = (CX, NZ)
 N_GX, N_GY = 8, 16
 W_ALL = 128
-PARTNERS = (0, 1, 3, 2)
+PARTNERS = (0, 2, 1, 3)
 PREPARE_VMEM = 54400
 EDGES_VMEM = 55296
 SLOTS_ALL = 256
@@ -345,34 +345,91 @@
     return [out[3 * i : 3 * i + 1] + out[3 * i + 1 : 3 * i + 2] + out[3 * i + 2 : 3 * i + 3] for i in range(n)]
 
 
+def make_inner_kernel(whole):
+    def kernel(*refs):
+        halves = (refs[0:4], refs[4:8])
+        vecs, rest = (None, refs[8:]) if whole else (refs[8:12], refs[12:])
+        if whole:
+            sinv, tau_r, rhs, left, right, base, from_left, from_right, mat_s, vec_s = rest
+        else:
+            sinv, tau_r, rhs, left, right, base, mat_s, vec_s = rest
+        z = position()[1] % 4
+        if whole:
+            gather_both(z, halves, mat_s, vec_s)
+        else:
+            gather_matrices(z, halves, mat_s)
+            gather_vectors(z, vecs, vec_s)
+        segs = [load_segment(mat_s.at[m], vec_s.at[m], 0) for m in range(4)]
+        pair = join(segs[0], segs[1])
+        store_segment(left, choose(z == 1, segs[0], choose(z == 2, pair, join(pair, segs[2]))), True)
+        pair = join(segs[2], segs[3])
+        store_segment(right, choose(z == 2, segs[3], choose(z == 1, pair, join(segs[1], pair))), True)
+
+        def tau(j):
+            return pair_at(tau_r, j)
+
+        def sv(j):
+            return block_at(sinv, j)
+
+        y = sweep_forward(sv, tau, [pair_at(rhs, j) for j in range(CY)])
+        u = None
+        for j in range(CY - 1, -1, -1):
+            v = y[j] if u is None else tuple(y[j][c] + tau(j + 1)[c] * u[c] for c in range(2))
+            u = mv(sv(j), v)
+            for c in range(2):
+                base[c, j] = u[c]
+        if not whole:
+            return
+        zero = jnp.zeros(PLANE, F32)
+        units = [(tau(0)[0], zero, zero, tau(0)[1])]
+        for j in range(1, CY):
+            units.append(rows_by(tau(j), mm(sv(j - 1), units[-1])))
+        ul = ur = None
+        for j in range(CY - 1, -1, -1):
+            if ul is None:
+                ul = mm(sv(j), units[j])
+                ur = columns_by(sv(j), tau(CY))
+            else:
+                ul = mm(sv(j), madd(units[j], rows_by(tau(j + 1), ul)))
+                ur = mm(sv(j), rows_by(tau(j + 1), ur))
+            for i in range(4):
+                from_left[i, j] = ul[i]
+                from_right[i, j] = ur[i]
+
+    return kernel
+
+
 def make_solve_kernel(whole):
     def kernel(*refs):
-        inner, outer = (refs[0:4], refs[4:8]), (refs[8:12], refs[12:16])
-        rest = refs[16:] if whole else refs[24:]
-        sinv, tau_r, rhs, cells, wells, weights = rest[:6]
-        p_out, ends, msg_a, msg_b = rest[6:10]
-        mat_i, vec_i, mat_o, vec_o, edge = rest[10:]
+        own_m, outer = refs[0:2], (refs[2:6], refs[6:10])
+        own_v, outer_v, rest = (None, None, refs[10:]) if whole else (refs[10], refs[11:15], refs[15:])
+        left, right, base, from_left, from_right, cells, wells, weights = rest[:8]
+        p_out, ends, msg_a, msg_b = rest[8:12]
+        mat_o, vec_o, mat_i, vec_i, edge = rest[12:]
         gx, gy = position()
         z_at, y_at = gy % 4, gy // 4
+        for half, ref in enumerate(own_m):
+            mat_i[:, 8 * half : 8 * half + 8, :] = ref[0:16]
+            if whole:
+                vec_i[:, 8 * half : 8 * half + 8, :] = ref[16:20]
         if whole:
-            gather_both(z_at, inner, mat_i, vec_i)
             gather_both(y_at, outer, mat_o, vec_o)
         else:
-            gather_matrices(z_at, inner, mat_i)
+            vec_i[...] = own_v[...]
             gather_matrices(y_at, outer, mat_o)
-            gather_vectors(z_at, refs[16:20], vec_i)
-            gather_vectors(y_at, refs[20:24], vec_o)
+            gather_vectors(y_at, outer_v, vec_o)
         zero = jnp.zeros(PLANE, F32)
         before = ((zero,) * 4, (zero,) * 2)
         after = ((zero,) * 4, (zero,) * 2)
-        for mat_s, vec_s, here in ((mat_o, vec_o, y_at), (mat_i, vec_i, z_at)):
-            for m in range(3):
-                seg = load_segment(mat_s.at[m], vec_s.at[m], 0)
-                before = choose(m < here, join_before(before, seg), before)
-                m = 3 - m
-                seg = load_segment(mat_s.at[m], vec_s.at[m], 0)
-                after = choose(m > here, join_after(seg, after), after)
-        own = load_segment(mat_i.at[z_at], vec_i.at[z_at], 0)
+        for m in range(3):
+            seg = load_segment(mat_o.at[m], vec_o.at[m], 0)
+            before = choose(m < y_at, join_before(before, seg), before)
+            m = 3 - m
+            seg = load_segment(mat_o.at[m], vec_o.at[m], 0)
+            after = choose(m > y_at, join_after(seg, after), after)
+        before = choose(z_at > 0, join_before(before, load_segment(left, left, 16)), before)
+        after = choose(z_at < 3, join_after(load_segment(right, right, 16), after), after)
+        own = load_segment(mat_i, vec_i, 0)
         ff, fl, lf, ll, gf, gl = own
         up_m, up_v = join_before(before, own)
         last = mv(inv2(one_minus(mm(up_m, after[0]))), madd(up_v, mv(up_m, after[1])))
@@ -384,18 +441,8 @@
             ends[c] = behind[c]
             ends[2 + c] = beyond[c]
 
-        def tau(j):
-            return pair_at(tau_r, j)
-
-        def sv(j):
-            return block_at(sinv, j)
-
-        r = [pair_at(rhs, j) for j in range(CY)]
-        r[0] = tuple(r[0][c] + tau(0)[c] * behind[c] for c in range(2))
-        y = sweep_forward(sv, tau, r)
-        u = beyond
-        for j in range(CY - 1, -1, -1):
-            u = mv(sv(j), tuple(y[j][c] + tau(j + 1)[c] * u[c] for c in range(2)))
+        for j in range(CY):
+            u = madd(pair_at(base, j), madd(mv(block_at(from_left, j), behind), mv(block_at(from_right, j), beyond)))
             for c in range(2):
                 p_out[c, j] = u[c]
                 edge[0, c * CY + j : c * CY + j + 1, :] = u[c][0:1, :]
@@ -420,7 +467,7 @@
 
 def apply_operator(got, cells, wells, weights):
     gx = position()[0]
-    got_a, sent_b, got_d, got_b, got_c = got
+    got_a, sent_b, got_c, got_b, got_d = got
     tail = sent_b[16:24, :] + got_b[16:24, :] + got_c[...] + got_d[...]
     rates = tail[0:1] / jnp.maximum(tail[1:2], 1.0)
     at_row, at_layer, at_well = slot_tables(cells, wells)
@@ -453,8 +500,8 @@
     return out
 
 
-def first_image_kernel(got_a, sent_b, got_d, got_b, got_c, p, ends, dmat, tau_r, sinv, binv, rhs, tx, ty, tz, lx_in, ly_in, cells, wells, weights, q_out, e_out, vec_out, dots):
-    well_add, after, before = apply_operator((got_a, sent_b, got_d, got_b, got_c), cells, wells, weights)
+def first_image_kernel(got_a, sent_b, got_c, got_b, got_d, p, ends, dmat, tau_r, sinv, binv, rhs, tx, ty, tz, lx_in, ly_in, cells, wells, weights, q_out, e_out, vec_out, dots):
+    well_add, after, before = apply_operator((got_a, sent_b, got_c, got_b, got_d), cells, wells, weights)
     eq = jnp.zeros(PLANE, F32)
     qq = jnp.zeros(PLANE, F32)
     e = []
@@ -484,8 +531,8 @@
         vec_out[2 + c] = last[c]
 
 
-def second_image_kernel(got_a, sent_b, got_d, got_b, got_c, p, ends, dmat, tx, ty, tz, lx_in, ly_in, cells, wells, weights, q_in, e_in, dots_in, s_out, dots):
-    well_add, after, before = apply_operator((got_a, sent_b, got_d, got_b, got_c), cells, wells, weights)
+def second_image_kernel(got_a, sent_b, got_c, got_b, got_d, p, ends, dmat, tx, ty, tz, lx_in, ly_in, cells, wells, weights, q_in, e_in, dots_in, s_out, dots):
+    well_add, after, before = apply_operator((got_a, sent_b, got_c, got_b, got_d), cells, wells, weights)
     sq = jnp.zeros(PLANE, F32)
     ss = jnp.zeros(PLANE, F32)
     es = jnp.zeros(PLANE, F32)
@@ -544,12 +591,12 @@
     got_d = lax.ppermute(tail, "gx", [(i, (i + 2 if i % 2 else i - 2) % N_GX) for i in range(N_GX)])
     got_b = lax.ppermute(sent_b, "gx", [(i, (i + 1 if i % 2 else i - 1) % N_GX) for i in range(N_GX)])
     got_c = lax.ppermute(tail, "gx", [(i, i ^ 4) for i in range(N_GX)])
-    return got_a, sent_b, got_d, got_b, got_c
+    return got_a, sent_b, got_c, got_b, got_d
 
 
 def sum_everywhere(x):
     x = x + lax.ppermute(x, "gx", [(i, i ^ 1) for i in range(N_GX)])
-    others = [lax.ppermute(x, "gx", [(i, (i + 2 * k) % N_GX) for i in range(N_GX)]) for k in (1, 3, 2)]
+    others = [lax.ppermute(x, "gx", [(i, (i + 2 * k) % N_GX) for i in range(N_GX)]) for k in PARTNERS[1:]]
     x = x + others[0] + others[1] + others[2]
     x = jnp.broadcast_to(x[None], (N_GY,) + x.shape)
     return lax.all_to_all(x, "gy", split_axis=0, concat_axis=0, tiled=True)
@@ -577,7 +624,6 @@
     )
     edges = swapped(edge, 1)
     lx = lax.ppermute(sx, "gx", [(i, i + 1) for i in range(N_GX - 1)])
-    *edges, lx = lax.optimization_barrier((*edges, lx))
     relayed = swapped(relay(*edges), 4)
     slots = perf_cell.shape[3]
     live = jnp.arange(slots, dtype=jnp.int32)[None, :] < perf_count.reshape(N_GX, 1)
@@ -599,10 +645,15 @@
         outer.append(swapped(group, 4))
     inner = inner[0] + inner[1]
     outer = outer[0] + outer[1]
-    solve_scratch = order + order + [(2, 16, NZ)]
+    solve_scratch = order + [(16, CX, NZ), (4, CX, NZ), (2, 16, NZ)]
+    joined = (20, CX, NZ)
+    left, right, base, from_left, from_right = call(
+        make_inner_kernel(True), "inner_first", (joined, joined, field, block, block), order, *inner, sinv, tau, rhs,
+    )
+    owns = (own_a, own_b)
     p, ends, msg_a, msg_b = call(
         make_solve_kernel(True), "solve_first", (field, vec, message, message), solve_scratch,
-        *inner, *outer, sinv, tau, rhs, *perfs,
+        *owns, *outer, left, right, base, from_left, from_right, *perfs,
     )
     got = exchange_rows(msg_a, msg_b)
     q, e, own_v, dots = call(
@@ -612,9 +663,12 @@
     inner_v = swapped(own_v, 1)
     (group_v,) = call(total_again_kernel, "group_total_again", (vec,), order, *inner, *inner_v)
     outer_v = swapped(group_v, 4)
+    left, right, base = call(
+        make_inner_kernel(False), "inner_second", (joined, joined, field), order, *inner, *inner_v, sinv, tau, e,
+    )
     w, ends, msg_a, msg_b = call(
         make_solve_kernel(False), "solve_second", (field, vec, message, message), solve_scratch,
-        *inner, *outer, *inner_v, *outer_v, sinv, tau, e, *perfs,
+        *owns, *outer, own_v, *outer_v, left, right, base, from_left, from_right, *perfs,
     )
     got = exchange_rows(msg_a, msg_b)
     s, dots = call(

time: 101 us -> 101 us (level)
  blocking collectives: 12.6 us -> 10.6 us
    ppermute x24, waiting for transfers between devices: 17.3 us -> 19.8 us  [swapped(): lax.ppermute(block, 'gy', [(i, i ^ k * stride) for i in range(N_GY)])]
    ppermute x2, starting transfers between devices: 6.66 us -> 4.45 us  [exchange_rows(): lax.ppermute(sent_b, 'gx', [(i, (i + 1 if i % 2 else i - 1) % N_GX) for i...]
    all_to_all x1, blocking collectives: 12.6 us -> 10.6 us  [sum_everywhere(): return lax.all_to_all(x, 'gy', split_axis=0, concat_axis=0, tiled=True)]
    ppermute x2, waiting for transfers between devices: 5.77 us -> 4.12 us  [exchange_rows(): got_c = lax.ppermute(tail, 'gx', [(i, i ^ 4) for i in range(N_GX)])]
    ppermute x2, starting transfers between devices: 1.17 us -> 2.82 us  [exchange_rows(): got_c = lax.ppermute(tail, 'gx', [(i, i ^ 4) for i in range(N_GX)])]
    ppermute x3, waiting for transfers between devices: 4.02 us -> 2.96 us  [sum_everywhere(): lax.ppermute(x, 'gx', [(i, (i + 2 * k) % N_GX) for i in range(N_GX)])]
    pallas_call x11 -> x13, Pallas kernels: 7.24 us -> 7.64 us  [call(): pl.pallas_call(kernel, name=name, out_shape=tuple(outs), in_specs=specs o...]
  transfers between devices with their start and end apart: 37 -> 37, of which waited for: 19 -> 23; matrix products, arithmetic and copies ran while one was open for 1% -> 1% of each run, Pallas kernels for 2% -> 2%
where the time goes in v6:
time: 101 us
  starting transfers between devices  49.1 us (49%)
  waiting for transfers between devices  30.9 us (31%)
  blocking collectives  10.6 us (10%)
  Pallas kernels  7.64 us (8%)
  local copies, waits for them, and re-layouts  1.03 us (1%)
    ppermute x24, starting transfers between devices, swapped(): lax.ppermute(block, 'gy', [(i, i ^ k * stride) for i in range(N_GY)])  32.2 us
    ppermute x24, waiting for transfers between devices, swapped(): lax.ppermute(block, 'gy', [(i, i ^ k * stride) for i in range(N_GY)])  19.8 us
    all_to_all x1, blocking collectives, sum_everywhere(): return lax.all_to_all(x, 'gy', split_axis=0, concat_axis=0, tiled=True)  10.6 us
    pallas_call x13, Pallas kernels, call(): pl.pallas_call(kernel, name=name, out_shape=tuple(outs), in_specs=specs o...  7.64 us
    ppermute x3, starting transfers between devices, sum_everywhere(): lax.ppermute(x, 'gx', [(i, (i + 2 * k) % N_GX) for i in range(N_GX)])  5 us
    ppermute x2, starting transfers between devices, exchange_rows(): lax.ppermute(sent_b, 'gx', [(i, (i + 1 if i % 2 else i - 1) % N_GX) for i...  4.45 us
    ppermute x2, waiting for transfers between devices, exchange_rows(): got_c = lax.ppermute(tail, 'gx', [(i, i ^ 4) for i in range(N_GX)])  4.12 us
    ppermute x2, starting transfers between devices, exchange_rows(): lax.ppermute(tail, 'gx', [(i, (i + 2 if i % 2 else i - 2) % N_GX) for i i...  3.28 us
  transfers between devices with their start and end apart: 37, of which 23 were waited for; matrix products, arithmetic and copies ran while one was open for 1% of the time, Pallas kernels for 2%

profile of v6, /device:TPU:0, one launch (start us, length us, event | category | flops | bytes accessed | tf_op | source)
XLA Modules:
  0.0 100.5 jit_solution(11779278262053175665)
XLA Ops:
  0.6 1.6 %edges.1 = (f32[2,8,128]{2,1,0:T(8,128)}, f32[40,128]{1,0:T(8,128)}) custom-call(f32[2,128,128]{2,1,0:T(8,128)} %bitcast.14, f32[2,128,128]{2,1,0:T(8,128)} %bitcast.16, s32[1,128]{1,0:T(1,128)} %brk_h.1), custom_call_target="tpu_custom_call" | custom-call | tf_op jit(solution)/shard_map/edges/pallas_call | solution.py:570
  2.2 4.0 %collective-permute-start.1 = (f32[40,128]{1,0:T(8,128)}, f32[40,128]{1,0:T(8,128)S(1)}, u32[]{:S(2)}, u32[]{:S(2)}) collective-permute-start(f32[40,128]{1,0:T(8,128)} %get-tuple-element.46.refs_0_), channel_id=1, source_target_pairs={{0,2},{1,3},{2,0},{3,1},{4,6},{5,7},{6,4},{7,5},{8,10},{9,11},{10,... | collective-permute-start | bytes 61448 | tf_op jit(solution)/shard_map/ppermute | solution.py:582
  8.2 2.0 %collective-permute-done.2.refs_2_ = f32[40,128]{1,0:T(8,128)S(1)} collective-permute-done((f32[40,128]{1,0:T(8,128)}, f32[40,128]{1,0:T(8,128)S(1)}, u32[]{:S(2)}, u32[]{:S(2)}) %collective-permute-start.2) | collective-permute-done | bytes 20512 | tf_op jit(solution)/shard_map/ppermute | solution.py:582
  10.2 2.2 %collective-permute-done.3.refs_3_ = f32[40,128]{1,0:T(8,128)S(1)} collective-permute-done((f32[40,128]{1,0:T(8,128)}, f32[40,128]{1,0:T(8,128)S(1)}, u32[]{:S(2)}, u32[]{:S(2)}) %collective-permute-start.3) | collective-permute-done | bytes 20512 | tf_op jit(solution)/shard_map/ppermute | solution.py:582
  12.6 3.3 %collective-permute-start.4 = (f32[40,128]{1,0:T(8,128)S(1)}, f32[40,128]{1,0:T(8,128)S(1)}, u32[]{:S(2)}, u32[]{:S(2)}) collective-permute-start(f32[40,128]{1,0:T(8,128)S(1)} %select_select_fusion.refs_4_), channel_id=1, source_target_pairs={{0,8},{1,9},{2,10},{3,11},{4,12},{5,13},{6,14},{7,15},{8,0},{9,1},... | collective-permute-start | bytes 61448 | tf_op jit(solution)/shard_map/ppermute | solution.py:582
  16.9 1.3 %collective-permute-start = (f32[2,8,128]{2,1,0:T(8,128)S(1)}, f32[2,8,128]{2,1,0:T(8,128)S(1)}, u32[]{:S(2)}, u32[]{:S(2)}) collective-permute-start(f32[2,8,128]{2,1,0:T(8,128)S(1)} %copy-done.4), channel_id=1, source_target_pairs={{0,16},{16,32},{32,48},{48,64},{64,80},{80,96},{96,112},{1,17},{17... | collective-permute-start | bytes 24584 | tf_op jit(solution)/shard_map/ppermute | solution.py:626
  18.2 1.4 %prepare.1 = (f32[2,8,16,128]{3,2,1,0:T(8,128)S(1)}, f32[2,8,16,128]{3,2,1,0:T(8,128)S(1)}, f32[2,8,16,128]{3,2,1,0:T(8,128)S(1)}, f32[2,8,16,128]{3,2,1,0:T(8,1...) custom-call(f32[2,128,128]{2,1,0:T(8,128)} %bitcast.19, f32[4,128,128]{2,1,0:T(8,128)} %bitcast.18, ...), custom_call_target="tpu_custom_call" | custom-call | tf_op jit(solution)/shard_map/prepare/pallas_call | solution.py:570
  19.6 1.9 %collective-permute-done.6.refs_7_ = f32[40,128]{1,0:T(8,128)S(1)} collective-permute-done((f32[40,128]{1,0:T(8,128)S(1)}, f32[40,128]{1,0:T(8,128)S(1)}, u32[]{:S(2)}, u32[]{:S(2)}) %collective-permute-start.6) | collective-permute-done | bytes 20512 | tf_op jit(solution)/shard_map/ppermute | solution.py:582
  22.9 3.2 %collective-permute-start.15 = (f32[20,8,128]{2,1,0:T(8,128)S(1)}, f32[20,8,128]{2,1,0:T(8,128)S(1)}, u32[]{:S(2)}, u32[]{:S(2)}) collective-permute-start(f32[20,8,128]{2,1,0:T(8,128)S(1)} %get-tuple-element.48.own.refs_4_.refs_1_), channel_id=1, source_target_pairs={{0,3},{1,2},{2,1},{3,0},{4,7},{5,6},{6,5},{7,4},{8,11},{9,10},{10,... | collective-permute-start | bytes 245768 | tf_op jit(solution)/shard_map/ppermute | solution.py:582
  27.2 1.5 %collective-permute-done.13.m1.refs_5_ = f32[20,8,128]{2,1,0:T(8,128)S(1)} collective-permute-done((f32[20,8,128]{2,1,0:T(8,128)S(1)}, f32[20,8,128]{2,1,0:T(8,128)S(1)}, u32[]{:S(2)}, u32[]{:S(2)}) %collective-permute-start.13) | collective-permute-done | bytes 81952 | tf_op jit(solution)/shard_map/ppermute | solution.py:582
  28.8 1.7 %collective-permute-start.9 = (f32[20,8,128]{2,1,0:T(8,128)S(1)}, f32[20,8,128]{2,1,0:T(8,128)S(1)}, u32[]{:S(2)}, u32[]{:S(2)}) collective-permute-start(f32[20,8,128]{2,1,0:T(8,128)S(1)} %get-tuple-element.47.own.refs_0_), channel_id=1, source_target_pairs={{0,3},{1,2},{2,1},{3,0},{4,7},{5,6},{6,5},{7,4},{8,11},{9,10},{10,... | collective-permute-start | bytes 245768 | tf_op jit(solution)/shard_map/ppermute | solution.py:582
  30.6 1.2 %collective-permute-start.16 = (f32[20,8,128]{2,1,0:T(8,128)S(1)}, f32[20,8,128]{2,1,0:T(8,128)S(1)}, u32[]{:S(2)}, u32[]{:S(2)}) collective-permute-start(f32[20,8,128]{2,1,0:T(8,128)S(1)} %group_total.3.refs_6_), channel_id=1, source_target_pairs={{0,8},{1,9},{2,10},{3,11},{4,12},{5,13},{6,14},{7,15},{8,0},{9,1},... | collective-permute-start | bytes 245768 | tf_op jit(solution)/shard_map/ppermute | solution.py:582
  32.7 2.1 %collective-permute-start.18 = (f32[20,8,128]{2,1,0:T(8,128)S(1)}, f32[20,8,128]{2,1,0:T(8,128)S(1)}, u32[]{:S(2)}, u32[]{:S(2)}) collective-permute-start(f32[20,8,128]{2,1,0:T(8,128)S(1)} %group_total.3.refs_6_), channel_id=1, source_target_pairs={{0,12},{1,13},{2,14},{3,15},{4,8},{5,9},{6,10},{7,11},{8,4},{9,5},... | collective-permute-start | bytes 245768 | tf_op jit(solution)/shard_map/ppermute | solution.py:582
  34.9 1.2 %collective-permute-start.10 = (f32[20,8,128]{2,1,0:T(8,128)S(1)}, f32[20,8,128]{2,1,0:T(8,128)S(1)}, u32[]{:S(2)}, u32[]{:S(2)}) collective-permute-start(f32[20,8,128]{2,1,0:T(8,128)S(1)} %group_total.2.refs_2_), channel_id=1, source_target_pairs={{0,8},{1,9},{2,10},{3,11},{4,12},{5,13},{6,14},{7,15},{8,0},{9,1},... | collective-permute-start | bytes 245768 | tf_op jit(solution)/shard_map/ppermute | solution.py:582
  37.4 1.6 %collective-permute-start.12 = (f32[20,8,128]{2,1,0:T(8,128)S(1)}, f32[20,8,128]{2,1,0:T(8,128)S(1)}, u32[]{:S(2)}, u32[]{:S(2)}) collective-permute-start(f32[20,8,128]{2,1,0:T(8,128)S(1)} %group_total.2.refs_2_), channel_id=1, source_target_pairs={{0,12},{1,13},{2,14},{3,15},{4,8},{5,9},{6,10},{7,11},{8,4},{9,5},... | collective-permute-start | bytes 245768 | tf_op jit(solution)/shard_map/ppermute | solution.py:582
  41.5 1.6 %collective-permute-done.12.refs_5_ = f32[20,8,128]{2,1,0:T(8,128)S(1)} collective-permute-done((f32[20,8,128]{2,1,0:T(8,128)S(1)}, f32[20,8,128]{2,1,0:T(8,128)S(1)}, u32[]{:S(2)}, u32[]{:S(2)}) %collective-permute-start.12) | collective-permute-done | bytes 81952 | tf_op jit(solution)/shard_map/ppermute | solution.py:582
  45.0 4.2 %collective-permute-start.21 = (f32[24,128]{1,0:T(8,128)S(1)}, f32[24,128]{1,0:T(8,128)S(1)}, u32[]{:S(2)}, u32[]{:S(2)}) collective-permute-start(f32[24,128]{1,0:T(8,128)S(1)} %select_add_fusion.1.sent_b), channel_id=1, source_target_pairs={{0,112},{16,32},{32,16},{48,64},{64,48},{80,96},{96,80},{112,0},{1... | collective-permute-start | bytes 36872 | tf_op jit(solution)/shard_map/ppermute | solution.py:592
  50.9 3.4 %collective-permute-done.20.got_c = f32[8,128]{1,0:T(8,128)S(1)} collective-permute-done((f32[8,128]{1,0:T(8,128)S(1)}, f32[8,128]{1,0:T(8,128)S(1)}, u32[]{:S(2)}, u32[]{:S(2)}) %collective-permute-start.20) | collective-permute-done | bytes 4128 | tf_op jit(solution)/shard_map/ppermute | solution.py:593
  55.8 2.9 %collective-permute-start.24 = (f32[4,16,128]{2,1,0:T(8,128)S(1)}, f32[4,16,128]{2,1,0:T(8,128)S(1)}, u32[]{:S(2)}, u32[]{:S(2)}) collective-permute-start(f32[4,16,128]{2,1,0:T(8,128)S(1)} %get-tuple-element.65.refs_8_.refs_10_), channel_id=1, source_target_pairs={{0,1},{1,0},{2,3},{3,2},{4,5},{5,4},{6,7},{7,6},{8,9},{9,8},{10,11... | collective-permute-start | bytes 98312 | tf_op jit(solution)/shard_map/ppermute | solution.py:582
  58.9 1.6 %collective-permute-done.23.refs_9_ = f32[4,16,128]{2,1,0:T(8,128)S(1)} collective-permute-done((f32[4,16,128]{2,1,0:T(8,128)S(1)}, f32[4,16,128]{2,1,0:T(8,128)S(1)}, u32[]{:S(2)}, u32[]{:S(2)}) %collective-permute-start.23) | collective-permute-done | bytes 32800 | tf_op jit(solution)/shard_map/ppermute | solution.py:582
  60.9 2.9 %collective-permute-done.25.refs_11_ = f32[4,16,128]{2,1,0:T(8,128)S(1)} collective-permute-done((f32[4,16,128]{2,1,0:T(8,128)S(1)}, f32[4,16,128]{2,1,0:T(8,128)S(1)}, u32[]{:S(2)}, u32[]{:S(2)}) %collective-permute-start.25) | collective-permute-done | bytes 32800 | tf_op jit(solution)/shard_map/ppermute | solution.py:582
  64.6 1.7 %collective-permute-start.27 = (f32[4,16,128]{2,1,0:T(8,128)S(1)}, f32[4,16,128]{2,1,0:T(8,128)S(1)}, u32[]{:S(2)}, u32[]{:S(2)}) collective-permute-start(f32[4,16,128]{2,1,0:T(8,128)S(1)} %group_total_again.1.refs_11_), channel_id=1, source_target_pairs={{0,4},{1,5},{2,6},{3,7},{4,0},{5,1},{6,2},{7,3},{8,12},{9,13},{10,... | collective-permute-start | bytes 98312 | tf_op jit(solution)/shard_map/ppermute | solution.py:582
  66.3 1.8 %collective-permute-start.28 = (f32[4,16,128]{2,1,0:T(8,128)S(1)}, f32[4,16,128]{2,1,0:T(8,128)S(1)}, u32[]{:S(2)}, u32[]{:S(2)}) collective-permute-start(f32[4,16,128]{2,1,0:T(8,128)S(1)} %group_total_again.1.refs_11_), channel_id=1, source_target_pairs={{0,12},{1,13},{2,14},{3,15},{4,8},{5,9},{6,10},{7,11},{8,4},{9,5},... | collective-permute-start | bytes 98312 | tf_op jit(solution)/shard_map/ppermute | solution.py:582
  69.4 2.0 %collective-permute-done.28.refs_14_ = f32[4,16,128]{2,1,0:T(8,128)S(1)} collective-permute-done((f32[4,16,128]{2,1,0:T(8,128)S(1)}, f32[4,16,128]{2,1,0:T(8,128)S(1)}, u32[]{:S(2)}, u32[]{:S(2)}) %collective-permute-start.28) | collective-permute-done | bytes 32800 | tf_op jit(solution)/shard_map/ppermute | solution.py:582
  72.2 1.2 %collective-permute-done.29.got_a = f32[24,128]{1,0:T(8,128)S(1)} collective-permute-done((f32[24,128]{1,0:T(8,128)S(1)}, f32[24,128]{1,0:T(8,128)S(1)}, u32[]{:S(2)}, u32[]{:S(2)}) %collective-permute-start.29) | collective-permute-done | bytes 12320 | tf_op jit(solution)/shard_map/ppermute | solution.py:587
  73.7 2.0 %collective-permute-start.30 = (f32[8,128]{1,0:T(8,128)S(1)}, f32[8,128]{1,0:T(8,128)S(1)}, u32[]{:S(2)}, u32[]{:S(2)}) collective-permute-start(f32[8,128]{1,0:T(8,128)S(1)} %slice_add_fusion), channel_id=1, source_target_pairs={{0,64},{16,80},{32,96},{48,112},{64,0},{80,16},{96,32},{112,48},{1... | collective-permute-start | bytes 12296 | tf_op jit(solution)/shard_map/ppermute | solution.py:593
  75.7 2.3 %collective-permute-start.32 = (f32[8,128]{1,0:T(8,128)S(1)}, f32[8,128]{1,0:T(8,128)S(1)}, u32[]{:S(2)}, u32[]{:S(2)}) collective-permute-start(f32[8,128]{1,0:T(8,128)S(1)} %slice_add_fusion), channel_id=1, source_target_pairs={{0,96},{16,48},{32,0},{48,80},{64,32},{80,112},{96,64},{112,16},{1... | collective-permute-start | bytes 12296 | tf_op jit(solution)/shard_map/ppermute | solution.py:591
  81.1 1.8 %collective-permute-start.34 = (f32[8,128]{1,0:T(8,128)S(1)}, f32[8,128]{1,0:T(8,128)S(1)}, u32[]{:S(2)}, u32[]{:S(2)}) collective-permute-start(f32[8,128]{1,0:T(8,128)S(1)} %add.53), channel_id=1, source_target_pairs={{0,64},{16,80},{32,96},{48,112},{64,0},{80,16},{96,32},{112,48},{1... | collective-permute-start | bytes 12296 | tf_op jit(solution)/shard_map/ppermute | solution.py:599
  82.8 2.6 %collective-permute-start.35 = (f32[8,128]{1,0:T(8,128)S(1)}, f32[8,128]{1,0:T(8,128)S(1)}, u32[]{:S(2)}, u32[]{:S(2)}) collective-permute-start(f32[8,128]{1,0:T(8,128)S(1)} %add.53), channel_id=1, source_target_pairs={{0,32},{16,48},{32,64},{48,80},{64,96},{80,112},{96,0},{112,16},{1... | collective-permute-start | bytes 12296 | tf_op jit(solution)/shard_map/ppermute | solution.py:599
  86.2 1.5 %collective-permute-done.35 = f32[8,128]{1,0:T(8,128)S(1)} collective-permute-done((f32[8,128]{1,0:T(8,128)S(1)}, f32[8,128]{1,0:T(8,128)S(1)}, u32[]{:S(2)}, u32[]{:S(2)}) %collective-permute-start.35) | collective-permute-done | bytes 4128 | tf_op jit(solution)/shard_map/ppermute | solution.py:599
  87.6 1.4 %collective-permute-done.36 = f32[8,128]{1,0:T(8,128)S(1)} collective-permute-done((f32[8,128]{1,0:T(8,128)S(1)}, f32[8,128]{1,0:T(8,128)S(1)}, u32[]{:S(2)}, u32[]{:S(2)}) %collective-permute-start.36) | collective-permute-done | bytes 4128 | tf_op jit(solution)/shard_map/ppermute | solution.py:599
  89.0 10.6 %all_to_all.5.got = f32[16,8,128]{2,1,0:T(8,128)S(1)} all-to-all(f32[16,8,128]{2,1,0:T(8,128)S(1)} %broadcast_in_dim.40), channel_id=1, replica_groups=mesh['gx'=8,'gy'=16] {'gy'}, dimensions={0} | all-to-all | bytes 131072 | tf_op jit(solution)/shard_map/all_to_all | solution.py:602
  (89 shorter events, 24.2 us)
Async XLA Ops:
  2.2 6.0 %collective-permute-start.1 = (f32[40,128]{1,0:T(8,128)}, f32[40,128]{1,0:T(8,128)S(1)}, u32[]{:S(2)}, u32[]{:S(2)}) collective-permute-start(f32[40,128]{1,0:T(8,128)} %get-tuple-element.46.refs_0_), channel_id=1, source_target_pairs={{0,2},{1,3},{2,0},{3,1},{4,6},{5,7},{6,4},{7,5},{8,10},{9,11},{10,... | collective-permute-start | bytes 61448 | tf_op jit(solution)/shard_map/ppermute | solution.py:582
  6.2 4.0 %collective-permute-start.2 = (f32[40,128]{1,0:T(8,128)}, f32[40,128]{1,0:T(8,128)S(1)}, u32[]{:S(2)}, u32[]{:S(2)}) collective-permute-start(f32[40,128]{1,0:T(8,128)} %get-tuple-element.46.refs_0_), channel_id=1, source_target_pairs={{0,1},{1,0},{2,3},{3,2},{4,5},{5,4},{6,7},{7,6},{8,9},{9,8},{10,11... | collective-permute-start | bytes 61448 | tf_op jit(solution)/shard_map/ppermute | solution.py:582
  7.3 5.2 %collective-permute-start.3 = (f32[40,128]{1,0:T(8,128)}, f32[40,128]{1,0:T(8,128)S(1)}, u32[]{:S(2)}, u32[]{:S(2)}) collective-permute-start(f32[40,128]{1,0:T(8,128)} %get-tuple-element.46.refs_0_), channel_id=1, source_target_pairs={{0,3},{1,2},{2,1},{3,0},{4,7},{5,6},{6,5},{7,4},{8,11},{9,10},{10,... | collective-permute-start | bytes 61448 | tf_op jit(solution)/shard_map/ppermute | solution.py:582
  12.6 7.0 %collective-permute-start.4 = (f32[40,128]{1,0:T(8,128)S(1)}, f32[40,128]{1,0:T(8,128)S(1)}, u32[]{:S(2)}, u32[]{:S(2)}) collective-permute-start(f32[40,128]{1,0:T(8,128)S(1)} %select_select_fusion.refs_4_), channel_id=1, source_target_pairs={{0,8},{1,9},{2,10},{3,11},{4,12},{5,13},{6,14},{7,15},{8,0},{9,1},... | collective-permute-start | bytes 61448 | tf_op jit(solution)/shard_map/ppermute | solution.py:582
  15.8 3.8 %collective-permute-start.5 = (f32[40,128]{1,0:T(8,128)S(1)}, f32[40,128]{1,0:T(8,128)S(1)}, u32[]{:S(2)}, u32[]{:S(2)}) collective-permute-start(f32[40,128]{1,0:T(8,128)S(1)} %select_select_fusion.refs_4_), channel_id=1, source_target_pairs={{0,4},{1,5},{2,6},{3,7},{4,0},{5,1},{6,2},{7,3},{8,12},{9,13},{10,... | collective-permute-start | bytes 61448 | tf_op jit(solution)/shard_map/ppermute | solution.py:582
  16.5 5.0 %collective-permute-start.6 = (f32[40,128]{1,0:T(8,128)S(1)}, f32[40,128]{1,0:T(8,128)S(1)}, u32[]{:S(2)}, u32[]{:S(2)}) collective-permute-start(f32[40,128]{1,0:T(8,128)S(1)} %select_select_fusion.refs_4_), channel_id=1, source_target_pairs={{0,12},{1,13},{2,14},{3,15},{4,8},{5,9},{6,10},{7,11},{8,4},{9,5},... | collective-permute-start | bytes 61448 | tf_op jit(solution)/shard_map/ppermute | solution.py:582
  21.9 6.9 %collective-permute-start.13 = (f32[20,8,128]{2,1,0:T(8,128)S(1)}, f32[20,8,128]{2,1,0:T(8,128)S(1)}, u32[]{:S(2)}, u32[]{:S(2)}) collective-permute-start(f32[20,8,128]{2,1,0:T(8,128)S(1)} %get-tuple-element.48.own.refs_4_.refs_1_), channel_id=1, source_target_pairs={{0,2},{1,3},{2,0},{3,1},{4,6},{5,7},{6,4},{7,5},{8,10},{9,11},{10,... | collective-permute-start | bytes 245768 | tf_op jit(solution)/shard_map/ppermute | solution.py:582
  22.0 8.5 %collective-permute-start.14 = (f32[20,8,128]{2,1,0:T(8,128)S(1)}, f32[20,8,128]{2,1,0:T(8,128)S(1)}, u32[]{:S(2)}, u32[]{:S(2)}) collective-permute-start(f32[20,8,128]{2,1,0:T(8,128)S(1)} %get-tuple-element.48.own.refs_4_.refs_1_), channel_id=1, source_target_pairs={{0,1},{1,0},{2,3},{3,2},{4,5},{5,4},{6,7},{7,6},{8,9},{9,8},{10,11... | collective-permute-start | bytes 245768 | tf_op jit(solution)/shard_map/ppermute | solution.py:582
  22.9 7.6 %collective-permute-start.15 = (f32[20,8,128]{2,1,0:T(8,128)S(1)}, f32[20,8,128]{2,1,0:T(8,128)S(1)}, u32[]{:S(2)}, u32[]{:S(2)}) collective-permute-start(f32[20,8,128]{2,1,0:T(8,128)S(1)} %get-tuple-element.48.own.refs_4_.refs_1_), channel_id=1, source_target_pairs={{0,3},{1,2},{2,1},{3,0},{4,7},{5,6},{6,5},{7,4},{8,11},{9,10},{10,... | collective-permute-start | bytes 245768 | tf_op jit(solution)/shard_map/ppermute | solution.py:582
  26.3 6.4 %collective-permute-start.7 = (f32[20,8,128]{2,1,0:T(8,128)S(1)}, f32[20,8,128]{2,1,0:T(8,128)S(1)}, u32[]{:S(2)}, u32[]{:S(2)}) collective-permute-start(f32[20,8,128]{2,1,0:T(8,128)S(1)} %get-tuple-element.47.own.refs_0_), channel_id=1, source_target_pairs={{0,2},{1,3},{2,0},{3,1},{4,6},{5,7},{6,4},{7,5},{8,10},{9,11},{10,... | collective-permute-start | bytes 245768 | tf_op jit(solution)/shard_map/ppermute | solution.py:582
  26.4 8.3 %collective-permute-start.8 = (f32[20,8,128]{2,1,0:T(8,128)S(1)}, f32[20,8,128]{2,1,0:T(8,128)S(1)}, u32[]{:S(2)}, u32[]{:S(2)}) collective-permute-start(f32[20,8,128]{2,1,0:T(8,128)S(1)} %get-tuple-element.47.own.refs_0_), channel_id=1, source_target_pairs={{0,1},{1,0},{2,3},{3,2},{4,5},{5,4},{6,7},{7,6},{8,9},{9,8},{10,11... | collective-permute-start | bytes 245768 | tf_op jit(solution)/shard_map/ppermute | solution.py:582
  28.8 6.0 %collective-permute-start.9 = (f32[20,8,128]{2,1,0:T(8,128)S(1)}, f32[20,8,128]{2,1,0:T(8,128)S(1)}, u32[]{:S(2)}, u32[]{:S(2)}) collective-permute-start(f32[20,8,128]{2,1,0:T(8,128)S(1)} %get-tuple-element.47.own.refs_0_), channel_id=1, source_target_pairs={{0,3},{1,2},{2,1},{3,0},{4,7},{5,6},{6,5},{7,4},{8,11},{9,10},{10,... | collective-permute-start | bytes 245768 | tf_op jit(solution)/shard_map/ppermute | solution.py:582
  30.6 6.9 %collective-permute-start.16 = (f32[20,8,128]{2,1,0:T(8,128)S(1)}, f32[20,8,128]{2,1,0:T(8,128)S(1)}, u32[]{:S(2)}, u32[]{:S(2)}) collective-permute-start(f32[20,8,128]{2,1,0:T(8,128)S(1)} %group_total.3.refs_6_), channel_id=1, source_target_pairs={{0,8},{1,9},{2,10},{3,11},{4,12},{5,13},{6,14},{7,15},{8,0},{9,1},... | collective-permute-start | bytes 245768 | tf_op jit(solution)/shard_map/ppermute | solution.py:582
  31.8 8.6 %collective-permute-start.17 = (f32[20,8,128]{2,1,0:T(8,128)S(1)}, f32[20,8,128]{2,1,0:T(8,128)S(1)}, u32[]{:S(2)}, u32[]{:S(2)}) collective-permute-start(f32[20,8,128]{2,1,0:T(8,128)S(1)} %group_total.3.refs_6_), channel_id=1, source_target_pairs={{0,4},{1,5},{2,6},{3,7},{4,0},{5,1},{6,2},{7,3},{8,12},{9,13},{10,... | collective-permute-start | bytes 245768 | tf_op jit(solution)/shard_map/ppermute | solution.py:582
  32.7 7.7 %collective-permute-start.18 = (f32[20,8,128]{2,1,0:T(8,128)S(1)}, f32[20,8,128]{2,1,0:T(8,128)S(1)}, u32[]{:S(2)}, u32[]{:S(2)}) collective-permute-start(f32[20,8,128]{2,1,0:T(8,128)S(1)} %group_total.3.refs_6_), channel_id=1, source_target_pairs={{0,12},{1,13},{2,14},{3,15},{4,8},{5,9},{6,10},{7,11},{8,4},{9,5},... | collective-permute-start | bytes 245768 | tf_op jit(solution)/shard_map/ppermute | solution.py:582
  34.9 6.6 %collective-permute-start.10 = (f32[20,8,128]{2,1,0:T(8,128)S(1)}, f32[20,8,128]{2,1,0:T(8,128)S(1)}, u32[]{:S(2)}, u32[]{:S(2)}) collective-permute-start(f32[20,8,128]{2,1,0:T(8,128)S(1)} %group_total.2.refs_2_), channel_id=1, source_target_pairs={{0,8},{1,9},{2,10},{3,11},{4,12},{5,13},{6,14},{7,15},{8,0},{9,1},... | collective-permute-start | bytes 245768 | tf_op jit(solution)/shard_map/ppermute | solution.py:582
  36.1 5.4 %collective-permute-start.11 = (f32[20,8,128]{2,1,0:T(8,128)S(1)}, f32[20,8,128]{2,1,0:T(8,128)S(1)}, u32[]{:S(2)}, u32[]{:S(2)}) collective-permute-start(f32[20,8,128]{2,1,0:T(8,128)S(1)} %group_total.2.refs_2_), channel_id=1, source_target_pairs={{0,4},{1,5},{2,6},{3,7},{4,0},{5,1},{6,2},{7,3},{8,12},{9,13},{10,... | collective-permute-start | bytes 245768 | tf_op jit(solution)/shard_map/ppermute | solution.py:582
  37.4 5.7 %collective-permute-start.12 = (f32[20,8,128]{2,1,0:T(8,128)S(1)}, f32[20,8,128]{2,1,0:T(8,128)S(1)}, u32[]{:S(2)}, u32[]{:S(2)}) collective-permute-start(f32[20,8,128]{2,1,0:T(8,128)S(1)} %group_total.2.refs_2_), channel_id=1, source_target_pairs={{0,12},{1,13},{2,14},{3,15},{4,8},{5,9},{6,10},{7,11},{8,4},{9,5},... | collective-permute-start | bytes 245768 | tf_op jit(solution)/shard_map/ppermute | solution.py:582
  45.0 9.3 %collective-permute-start.21 = (f32[24,128]{1,0:T(8,128)S(1)}, f32[24,128]{1,0:T(8,128)S(1)}, u32[]{:S(2)}, u32[]{:S(2)}) collective-permute-start(f32[24,128]{1,0:T(8,128)S(1)} %select_add_fusion.1.sent_b), channel_id=1, source_target_pairs={{0,112},{16,32},{32,16},{48,64},{64,48},{80,96},{96,80},{112,0},{1... | collective-permute-start | bytes 36872 | tf_op jit(solution)/shard_map/ppermute | solution.py:592
  49.2 5.1 %collective-permute-start.20 = (f32[8,128]{1,0:T(8,128)S(1)}, f32[8,128]{1,0:T(8,128)S(1)}, u32[]{:S(2)}, u32[]{:S(2)}) collective-permute-start(f32[8,128]{1,0:T(8,128)S(1)} %slice_add_fusion.1), channel_id=1, source_target_pairs={{0,64},{16,80},{32,96},{48,112},{64,0},{80,16},{96,32},{112,48},{1... | collective-permute-start | bytes 12296 | tf_op jit(solution)/shard_map/ppermute | solution.py:593
  50.0 4.3 %collective-permute-start.22 = (f32[8,128]{1,0:T(8,128)S(1)}, f32[8,128]{1,0:T(8,128)S(1)}, u32[]{:S(2)}, u32[]{:S(2)}) collective-permute-start(f32[8,128]{1,0:T(8,128)S(1)} %slice_add_fusion.1), channel_id=1, source_target_pairs={{0,96},{16,48},{32,0},{48,80},{64,32},{80,112},{96,64},{112,16},{1... | collective-permute-start | bytes 12296 | tf_op jit(solution)/shard_map/ppermute | solution.py:591
  54.8 5.7 %collective-permute-start.23 = (f32[4,16,128]{2,1,0:T(8,128)S(1)}, f32[4,16,128]{2,1,0:T(8,128)S(1)}, u32[]{:S(2)}, u32[]{:S(2)}) collective-permute-start(f32[4,16,128]{2,1,0:T(8,128)S(1)} %get-tuple-element.65.refs_8_.refs_10_), channel_id=1, source_target_pairs={{0,2},{1,3},{2,0},{3,1},{4,6},{5,7},{6,4},{7,5},{8,10},{9,11},{10,... | collective-permute-start | bytes 98312 | tf_op jit(solution)/shard_map/ppermute | solution.py:582
  55.8 5.1 %collective-permute-start.24 = (f32[4,16,128]{2,1,0:T(8,128)S(1)}, f32[4,16,128]{2,1,0:T(8,128)S(1)}, u32[]{:S(2)}, u32[]{:S(2)}) collective-permute-start(f32[4,16,128]{2,1,0:T(8,128)S(1)} %get-tuple-element.65.refs_8_.refs_10_), channel_id=1, source_target_pairs={{0,1},{1,0},{2,3},{3,2},{4,5},{5,4},{6,7},{7,6},{8,9},{9,8},{10,11... | collective-permute-start | bytes 98312 | tf_op jit(solution)/shard_map/ppermute | solution.py:582
  58.7 5.1 %collective-permute-start.25 = (f32[4,16,128]{2,1,0:T(8,128)S(1)}, f32[4,16,128]{2,1,0:T(8,128)S(1)}, u32[]{:S(2)}, u32[]{:S(2)}) collective-permute-start(f32[4,16,128]{2,1,0:T(8,128)S(1)} %get-tuple-element.65.refs_8_.refs_10_), channel_id=1, source_target_pairs={{0,3},{1,2},{2,1},{3,0},{4,7},{5,6},{6,5},{7,4},{8,11},{9,10},{10,... | collective-permute-start | bytes 98312 | tf_op jit(solution)/shard_map/ppermute | solution.py:582
  63.9 5.5 %collective-permute-start.26 = (f32[4,16,128]{2,1,0:T(8,128)S(1)}, f32[4,16,128]{2,1,0:T(8,128)S(1)}, u32[]{:S(2)}, u32[]{:S(2)}) collective-permute-start(f32[4,16,128]{2,1,0:T(8,128)S(1)} %group_total_again.1.refs_11_), channel_id=1, source_target_pairs={{0,8},{1,9},{2,10},{3,11},{4,12},{5,13},{6,14},{7,15},{8,0},{9,1},... | collective-permute-start | bytes 98312 | tf_op jit(solution)/shard_map/ppermute | solution.py:582
  64.6 4.8 %collective-permute-start.27 = (f32[4,16,128]{2,1,0:T(8,128)S(1)}, f32[4,16,128]{2,1,0:T(8,128)S(1)}, u32[]{:S(2)}, u32[]{:S(2)}) collective-permute-start(f32[4,16,128]{2,1,0:T(8,128)S(1)} %group_total_again.1.refs_11_), channel_id=1, source_target_pairs={{0,4},{1,5},{2,6},{3,7},{4,0},{5,1},{6,2},{7,3},{8,12},{9,13},{10,... | collective-permute-start | bytes 98312 | tf_op jit(solution)/shard_map/ppermute | solution.py:582
  66.3 5.1 %collective-permute-start.28 = (f32[4,16,128]{2,1,0:T(8,128)S(1)}, f32[4,16,128]{2,1,0:T(8,128)S(1)}, u32[]{:S(2)}, u32[]{:S(2)}) collective-permute-start(f32[4,16,128]{2,1,0:T(8,128)S(1)} %group_total_again.1.refs_11_), channel_id=1, source_target_pairs={{0,12},{1,13},{2,14},{3,15},{4,8},{5,9},{6,10},{7,11},{8,4},{9,5},... | collective-permute-start | bytes 98312 | tf_op jit(solution)/shard_map/ppermute | solution.py:582
  73.4 6.0 %collective-permute-start.31 = (f32[24,128]{1,0:T(8,128)S(1)}, f32[24,128]{1,0:T(8,128)S(1)}, u32[]{:S(2)}, u32[]{:S(2)}) collective-permute-start(f32[24,128]{1,0:T(8,128)S(1)} %select_add_fusion.sent_b), channel_id=1, source_target_pairs={{0,112},{16,32},{32,16},{48,64},{64,48},{80,96},{96,80},{112,0},{1... | collective-permute-start | bytes 36872 | tf_op jit(solution)/shard_map/ppermute | solution.py:592
  73.7 5.1 %collective-permute-start.30 = (f32[8,128]{1,0:T(8,128)S(1)}, f32[8,128]{1,0:T(8,128)S(1)}, u32[]{:S(2)}, u32[]{:S(2)}) collective-permute-start(f32[8,128]{1,0:T(8,128)S(1)} %slice_add_fusion), channel_id=1, source_target_pairs={{0,64},{16,80},{32,96},{48,112},{64,0},{80,16},{96,32},{112,48},{1... | collective-permute-start | bytes 12296 | tf_op jit(solution)/shard_map/ppermute | solution.py:593
  75.7 3.7 %collective-permute-start.32 = (f32[8,128]{1,0:T(8,128)S(1)}, f32[8,128]{1,0:T(8,128)S(1)}, u32[]{:S(2)}, u32[]{:S(2)}) collective-permute-start(f32[8,128]{1,0:T(8,128)S(1)} %slice_add_fusion), channel_id=1, source_target_pairs={{0,96},{16,48},{32,0},{48,80},{64,32},{80,112},{96,64},{112,16},{1... | collective-permute-start | bytes 12296 | tf_op jit(solution)/shard_map/ppermute | solution.py:591
  81.1 5.1 %collective-permute-start.34 = (f32[8,128]{1,0:T(8,128)S(1)}, f32[8,128]{1,0:T(8,128)S(1)}, u32[]{:S(2)}, u32[]{:S(2)}) collective-permute-start(f32[8,128]{1,0:T(8,128)S(1)} %add.53), channel_id=1, source_target_pairs={{0,64},{16,80},{32,96},{48,112},{64,0},{80,16},{96,32},{112,48},{1... | collective-permute-start | bytes 12296 | tf_op jit(solution)/shard_map/ppermute | solution.py:599
  82.8 4.8 %collective-permute-start.35 = (f32[8,128]{1,0:T(8,128)S(1)}, f32[8,128]{1,0:T(8,128)S(1)}, u32[]{:S(2)}, u32[]{:S(2)}) collective-permute-start(f32[8,128]{1,0:T(8,128)S(1)} %add.53), channel_id=1, source_target_pairs={{0,32},{16,48},{32,64},{48,80},{64,96},{80,112},{96,0},{112,16},{1... | collective-permute-start | bytes 12296 | tf_op jit(solution)/shard_map/ppermute | solution.py:599
  (11 other events, 29.9 us)

commit v7 on v6

--- a/solution.py
+++ b/solution.py
@@ -544,15 +544,19 @@
             ss = ss + s * s
             es = es + s * e_in[c, j]
     sums = [jnp.sum(x, axis=0, keepdims=True) for x in (dots_in[0], dots_in[1], sq, ss, es)]
-    dots[...] = jnp.concatenate(sums + [jnp.zeros((3, NZ), F32)], axis=0)
+    lane = lax.broadcasted_iota(jnp.int32, (1, NZ), 1)
+    row = jnp.zeros((1, NZ), F32)
+    for i, x in enumerate(sums):
+        row = jnp.where(lane == i, jnp.sum(x, axis=1, keepdims=True), row)
+    dots[...] = row
 
 
 def finish_kernel(got, p, w, q, e, s, x_out, r_out):
-    total = got[0]
-    for d in range(1, N_GY):
-        total = total + got[d]
-    total = jnp.broadcast_to(jnp.sum(total, axis=1, keepdims=True), (8, NZ))
-    eq, qq, sq, ss, es = (total[i : i + 1] for i in range(5))
+    total = jnp.sum(got[...], axis=0, keepdims=True)
+    lane = lax.broadcasted_iota(jnp.int32, (1, NZ), 1)
+    eq, qq, sq, ss, es = (
+        jnp.broadcast_to(jnp.sum(jnp.where(lane == i, total, 0.0), axis=1, keepdims=True), (1, NZ)) for i in range(5)
+    )
     rest = -eq / qq
     g = sq / qq
     k = (es - g * eq) / (ss - g * sq)
@@ -598,7 +602,7 @@
     x = x + lax.ppermute(x, "gx", [(i, i ^ 1) for i in range(N_GX)])
     others = [lax.ppermute(x, "gx", [(i, (i + 2 * k) % N_GX) for i in range(N_GX)]) for k in PARTNERS[1:]]
     x = x + others[0] + others[1] + others[2]
-    x = jnp.broadcast_to(x[None], (N_GY,) + x.shape)
+    x = jnp.broadcast_to(x, (N_GY, NZ))
     return lax.all_to_all(x, "gy", split_axis=0, concat_axis=0, tiled=True)
 
 
@@ -624,6 +628,7 @@
     )
     edges = swapped(edge, 1)
     lx = lax.ppermute(sx, "gx", [(i, i + 1) for i in range(N_GX - 1)])
+    *edges, rhs, tx, ty, tz, diag, cross = lax.optimization_barrier((*edges, rhs, tx, ty, tz, diag, cross))
     relayed = swapped(relay(*edges), 4)
     slots = perf_cell.shape[3]
     live = jnp.arange(slots, dtype=jnp.int32)[None, :] < perf_count.reshape(N_GX, 1)
@@ -672,7 +677,7 @@
     )
     got = exchange_rows(msg_a, msg_b)
     s, dots = call(
-        second_image_kernel, "second_image", (field, (8, NZ)), [],
+        second_image_kernel, "second_image", (field, (1, NZ)), [],
         *got, w, ends, dmat, tx, ty, tz, lx, ly, *perfs, q, e, dots,
     )
     dots = sum_everywhere(dots)

time: 101 us -> 101 us (level)
  transfers between devices with their start and end apart: 37 -> 37, of which waited for: 23 -> 22; matrix products, arithmetic and copies ran while one was open for 1% -> 1% of each run, Pallas kernels for 2% -> 2%
where the time goes in v7:
time: 101 us; the launch traced here: 100 us
  starting transfers between devices  49.4 us (49%)
  waiting for transfers between devices  30.5 us (30%)
  blocking collectives  10.5 us (10%)
  Pallas kernels  7.68 us (8%)
  local copies, waits for them, and re-layouts  1.04 us (1%)
    ppermute x24, starting transfers between devices, swapped(): lax.ppermute(block, 'gy', [(i, i ^ k * stride) for i in range(N_GY)])  32.1 us
    ppermute x24, waiting for transfers between devices, swapped(): lax.ppermute(block, 'gy', [(i, i ^ k * stride) for i in range(N_GY)])  19 us
    all_to_all x1, blocking collectives, sum_everywhere(): return lax.all_to_all(x, 'gy', split_axis=0, concat_axis=0, tiled=True)  10.5 us
    pallas_call x13, Pallas kernels, call(): pl.pallas_call(kernel, name=name, out_shape=tuple(outs), in_specs=specs o...  7.68 us
    ppermute x2, starting transfers between devices, exchange_rows(): lax.ppermute(sent_b, 'gx', [(i, (i + 1 if i % 2 else i - 1) % N_GX) for i...  5.31 us
    ppermute x3, starting transfers between devices, sum_everywhere(): lax.ppermute(x, 'gx', [(i, (i + 2 * k) % N_GX) for i in range(N_GX)])  5.26 us
    ppermute x2, waiting for transfers between devices, exchange_rows(): got_c = lax.ppermute(tail, 'gx', [(i, i ^ 4) for i in range(N_GX)])  4.81 us
    ppermute x2, starting transfers between devices, exchange_rows(): lax.ppermute(tail, 'gx', [(i, (i + 2 if i % 2 else i - 2) % N_GX) for i i...  3.28 us
  transfers between devices with their start and end apart: 37, of which 22 were waited for; matrix products, arithmetic and copies ran while one was open for 1% of the time, Pallas kernels for 2%

profile of v7, /device:TPU:0, one launch (start us, length us, event | category | flops | bytes accessed | tf_op | source)
XLA Modules:
  0.0 100.3 jit_solution(8552934258151534538)
XLA Ops:
  0.6 1.6 %edges.1 = (f32[2,8,128]{2,1,0:T(8,128)}, f32[40,128]{1,0:T(8,128)}) custom-call(f32[2,128,128]{2,1,0:T(8,128)} %bitcast.18, f32[2,128,128]{2,1,0:T(8,128)} %bitcast.20, s32[1,128]{1,0:T(1,128)} %brk_h.1), custom_call_target="tpu_custom_call" | custom-call | tf_op jit(solution)/shard_map/edges/pallas_call | solution.py:574
  2.2 4.0 %collective-permute-start = (f32[40,128]{1,0:T(8,128)}, f32[40,128]{1,0:T(8,128)S(1)}, u32[]{:S(2)}, u32[]{:S(2)}) collective-permute-start(f32[40,128]{1,0:T(8,128)} %get-tuple-element.63.refs_0_), channel_id=1, source_target_pairs={{0,2},{1,3},{2,0},{3,1},{4,6},{5,7},{6,4},{7,5},{8,10},{9,11},{10,... | collective-permute-start | bytes 61448 | tf_op jit(solution)/shard_map/ppermute | solution.py:586
  7.3 1.4 %prepare.1 = (f32[2,8,16,128]{3,2,1,0:T(8,128)S(1)}, f32[2,8,16,128]{3,2,1,0:T(8,128)S(1)}, f32[2,8,16,128]{3,2,1,0:T(8,128)S(1)}, f32[2,8,16,128]{3,2,1,0:T(8,1...) custom-call(f32[2,128,128]{2,1,0:T(8,128)} %bitcast.23, f32[4,128,128]{2,1,0:T(8,128)} %bitcast.22, ...), custom_call_target="tpu_custom_call" | custom-call | tf_op jit(solution)/shard_map/prepare/pallas_call | solution.py:574
  8.7 1.5 %collective-permute-done.1.refs_2_ = f32[40,128]{1,0:T(8,128)S(1)} collective-permute-done((f32[40,128]{1,0:T(8,128)}, f32[40,128]{1,0:T(8,128)S(1)}, u32[]{:S(2)}, u32[]{:S(2)}) %collective-permute-start.1) | collective-permute-done | bytes 20512 | tf_op jit(solution)/shard_map/ppermute | solution.py:586
  10.2 2.2 %collective-permute-done.2.refs_3_ = f32[40,128]{1,0:T(8,128)S(1)} collective-permute-done((f32[40,128]{1,0:T(8,128)}, f32[40,128]{1,0:T(8,128)S(1)}, u32[]{:S(2)}, u32[]{:S(2)}) %collective-permute-start.2) | collective-permute-done | bytes 20512 | tf_op jit(solution)/shard_map/ppermute | solution.py:586
  12.6 3.3 %collective-permute-start.4 = (f32[40,128]{1,0:T(8,128)S(1)}, f32[40,128]{1,0:T(8,128)S(1)}, u32[]{:S(2)}, u32[]{:S(2)}) collective-permute-start(f32[40,128]{1,0:T(8,128)S(1)} %select_select_fusion.refs_4_), channel_id=1, source_target_pairs={{0,8},{1,9},{2,10},{3,11},{4,12},{5,13},{6,14},{7,15},{8,0},{9,1},... | collective-permute-start | bytes 61448 | tf_op jit(solution)/shard_map/ppermute | solution.py:586
  16.9 1.3 %collective-permute-start.3 = (f32[2,8,128]{2,1,0:T(8,128)S(1)}, f32[2,8,128]{2,1,0:T(8,128)S(1)}, u32[]{:S(2)}, u32[]{:S(2)}) collective-permute-start(f32[2,8,128]{2,1,0:T(8,128)S(1)} %copy-done.4), channel_id=1, source_target_pairs={{0,16},{16,32},{32,48},{48,64},{64,80},{80,96},{96,112},{1,17},{17... | collective-permute-start | bytes 24584 | tf_op jit(solution)/shard_map/ppermute | solution.py:630
  19.6 1.9 %collective-permute-done.6.refs_7_ = f32[40,128]{1,0:T(8,128)S(1)} collective-permute-done((f32[40,128]{1,0:T(8,128)S(1)}, f32[40,128]{1,0:T(8,128)S(1)}, u32[]{:S(2)}, u32[]{:S(2)}) %collective-permute-start.6) | collective-permute-done | bytes 20512 | tf_op jit(solution)/shard_map/ppermute | solution.py:586
  22.9 3.2 %collective-permute-start.15 = (f32[20,8,128]{2,1,0:T(8,128)S(1)}, f32[20,8,128]{2,1,0:T(8,128)S(1)}, u32[]{:S(2)}, u32[]{:S(2)}) collective-permute-start(f32[20,8,128]{2,1,0:T(8,128)S(1)} %get-tuple-element.68.own.refs_4_.refs_1_), channel_id=1, source_target_pairs={{0,3},{1,2},{2,1},{3,0},{4,7},{5,6},{6,5},{7,4},{8,11},{9,10},{10,... | collective-permute-start | bytes 245768 | tf_op jit(solution)/shard_map/ppermute | solution.py:586
  27.2 1.2 %collective-permute-done.13.m1.refs_5_ = f32[20,8,128]{2,1,0:T(8,128)S(1)} collective-permute-done((f32[20,8,128]{2,1,0:T(8,128)S(1)}, f32[20,8,128]{2,1,0:T(8,128)S(1)}, u32[]{:S(2)}, u32[]{:S(2)}) %collective-permute-start.13) | collective-permute-done | bytes 81952 | tf_op jit(solution)/shard_map/ppermute | solution.py:586
  28.4 2.0 %collective-permute-start.9 = (f32[20,8,128]{2,1,0:T(8,128)S(1)}, f32[20,8,128]{2,1,0:T(8,128)S(1)}, u32[]{:S(2)}, u32[]{:S(2)}) collective-permute-start(f32[20,8,128]{2,1,0:T(8,128)S(1)} %get-tuple-element.67.own.refs_0_), channel_id=1, source_target_pairs={{0,3},{1,2},{2,1},{3,0},{4,7},{5,6},{6,5},{7,4},{8,11},{9,10},{10,... | collective-permute-start | bytes 245768 | tf_op jit(solution)/shard_map/ppermute | solution.py:586
  32.3 2.5 %collective-permute-start.18 = (f32[20,8,128]{2,1,0:T(8,128)S(1)}, f32[20,8,128]{2,1,0:T(8,128)S(1)}, u32[]{:S(2)}, u32[]{:S(2)}) collective-permute-start(f32[20,8,128]{2,1,0:T(8,128)S(1)} %group_total.3.refs_6_), channel_id=1, source_target_pairs={{0,12},{1,13},{2,14},{3,15},{4,8},{5,9},{6,10},{7,11},{8,4},{9,5},... | collective-permute-start | bytes 245768 | tf_op jit(solution)/shard_map/ppermute | solution.py:586
  37.3 1.8 %collective-permute-start.12 = (f32[20,8,128]{2,1,0:T(8,128)S(1)}, f32[20,8,128]{2,1,0:T(8,128)S(1)}, u32[]{:S(2)}, u32[]{:S(2)}) collective-permute-start(f32[20,8,128]{2,1,0:T(8,128)S(1)} %group_total.2.refs_2_), channel_id=1, source_target_pairs={{0,12},{1,13},{2,14},{3,15},{4,8},{5,9},{6,10},{7,11},{8,4},{9,5},... | collective-permute-start | bytes 245768 | tf_op jit(solution)/shard_map/ppermute | solution.py:586
  41.0 2.0 %collective-permute-done.12.refs_5_ = f32[20,8,128]{2,1,0:T(8,128)S(1)} collective-permute-done((f32[20,8,128]{2,1,0:T(8,128)S(1)}, f32[20,8,128]{2,1,0:T(8,128)S(1)}, u32[]{:S(2)}, u32[]{:S(2)}) %collective-permute-start.12) | collective-permute-done | bytes 81952 | tf_op jit(solution)/shard_map/ppermute | solution.py:586
  43.6 1.2 %collective-permute-done.19.got_a = f32[24,128]{1,0:T(8,128)S(1)} collective-permute-done((f32[24,128]{1,0:T(8,128)S(1)}, f32[24,128]{1,0:T(8,128)S(1)}, u32[]{:S(2)}, u32[]{:S(2)}) %collective-permute-start.19) | collective-permute-done | bytes 12320 | tf_op jit(solution)/shard_map/ppermute | solution.py:591
  44.9 4.3 %collective-permute-start.21 = (f32[24,128]{1,0:T(8,128)S(1)}, f32[24,128]{1,0:T(8,128)S(1)}, u32[]{:S(2)}, u32[]{:S(2)}) collective-permute-start(f32[24,128]{1,0:T(8,128)S(1)} %select_add_fusion.1.sent_b), channel_id=1, source_target_pairs={{0,112},{16,32},{32,16},{48,64},{64,48},{80,96},{96,80},{112,0},{1... | collective-permute-start | bytes 36872 | tf_op jit(solution)/shard_map/ppermute | solution.py:596
  50.9 3.4 %collective-permute-done.20.got_c = f32[8,128]{1,0:T(8,128)S(1)} collective-permute-done((f32[8,128]{1,0:T(8,128)S(1)}, f32[8,128]{1,0:T(8,128)S(1)}, u32[]{:S(2)}, u32[]{:S(2)}) %collective-permute-start.20) | collective-permute-done | bytes 4128 | tf_op jit(solution)/shard_map/ppermute | solution.py:597
  55.8 2.9 %collective-permute-start.24 = (f32[4,16,128]{2,1,0:T(8,128)S(1)}, f32[4,16,128]{2,1,0:T(8,128)S(1)}, u32[]{:S(2)}, u32[]{:S(2)}) collective-permute-start(f32[4,16,128]{2,1,0:T(8,128)S(1)} %get-tuple-element.85.refs_8_.refs_10_), channel_id=1, source_target_pairs={{0,1},{1,0},{2,3},{3,2},{4,5},{5,4},{6,7},{7,6},{8,9},{9,8},{10,11... | collective-permute-start | bytes 98312 | tf_op jit(solution)/shard_map/ppermute | solution.py:586
  58.9 1.6 %collective-permute-done.23.refs_9_ = f32[4,16,128]{2,1,0:T(8,128)S(1)} collective-permute-done((f32[4,16,128]{2,1,0:T(8,128)S(1)}, f32[4,16,128]{2,1,0:T(8,128)S(1)}, u32[]{:S(2)}, u32[]{:S(2)}) %collective-permute-start.23) | collective-permute-done | bytes 32800 | tf_op jit(solution)/shard_map/ppermute | solution.py:586
  60.9 2.9 %collective-permute-done.25.refs_11_ = f32[4,16,128]{2,1,0:T(8,128)S(1)} collective-permute-done((f32[4,16,128]{2,1,0:T(8,128)S(1)}, f32[4,16,128]{2,1,0:T(8,128)S(1)}, u32[]{:S(2)}, u32[]{:S(2)}) %collective-permute-start.25) | collective-permute-done | bytes 32800 | tf_op jit(solution)/shard_map/ppermute | solution.py:586
  64.6 1.7 %collective-permute-start.27 = (f32[4,16,128]{2,1,0:T(8,128)S(1)}, f32[4,16,128]{2,1,0:T(8,128)S(1)}, u32[]{:S(2)}, u32[]{:S(2)}) collective-permute-start(f32[4,16,128]{2,1,0:T(8,128)S(1)} %group_total_again.1.refs_11_), channel_id=1, source_target_pairs={{0,4},{1,5},{2,6},{3,7},{4,0},{5,1},{6,2},{7,3},{8,12},{9,13},{10,... | collective-permute-start | bytes 98312 | tf_op jit(solution)/shard_map/ppermute | solution.py:586
  66.3 1.8 %collective-permute-start.28 = (f32[4,16,128]{2,1,0:T(8,128)S(1)}, f32[4,16,128]{2,1,0:T(8,128)S(1)}, u32[]{:S(2)}, u32[]{:S(2)}) collective-permute-start(f32[4,16,128]{2,1,0:T(8,128)S(1)} %group_total_again.1.refs_11_), channel_id=1, source_target_pairs={{0,12},{1,13},{2,14},{3,15},{4,8},{5,9},{6,10},{7,11},{8,4},{9,5},... | collective-permute-start | bytes 98312 | tf_op jit(solution)/shard_map/ppermute | solution.py:586
  69.4 2.0 %collective-permute-done.28.refs_14_ = f32[4,16,128]{2,1,0:T(8,128)S(1)} collective-permute-done((f32[4,16,128]{2,1,0:T(8,128)S(1)}, f32[4,16,128]{2,1,0:T(8,128)S(1)}, u32[]{:S(2)}, u32[]{:S(2)}) %collective-permute-start.28) | collective-permute-done | bytes 32800 | tf_op jit(solution)/shard_map/ppermute | solution.py:586
  72.2 1.2 %collective-permute-done.29.got_a = f32[24,128]{1,0:T(8,128)S(1)} collective-permute-done((f32[24,128]{1,0:T(8,128)S(1)}, f32[24,128]{1,0:T(8,128)S(1)}, u32[]{:S(2)}, u32[]{:S(2)}) %collective-permute-start.29) | collective-permute-done | bytes 12320 | tf_op jit(solution)/shard_map/ppermute | solution.py:591
  74.4 1.3 %collective-permute-start.30 = (f32[8,128]{1,0:T(8,128)S(1)}, f32[8,128]{1,0:T(8,128)S(1)}, u32[]{:S(2)}, u32[]{:S(2)}) collective-permute-start(f32[8,128]{1,0:T(8,128)S(1)} %slice_add_fusion), channel_id=1, source_target_pairs={{0,64},{16,80},{32,96},{48,112},{64,0},{80,16},{96,32},{112,48},{1... | collective-permute-start | bytes 12296 | tf_op jit(solution)/shard_map/ppermute | solution.py:597
  75.7 2.3 %collective-permute-start.32 = (f32[8,128]{1,0:T(8,128)S(1)}, f32[8,128]{1,0:T(8,128)S(1)}, u32[]{:S(2)}, u32[]{:S(2)}) collective-permute-start(f32[8,128]{1,0:T(8,128)S(1)} %slice_add_fusion), channel_id=1, source_target_pairs={{0,96},{16,48},{32,0},{48,80},{64,32},{80,112},{96,64},{112,16},{1... | collective-permute-start | bytes 12296 | tf_op jit(solution)/shard_map/ppermute | solution.py:595
  78.1 1.4 %collective-permute-done.30.got_c = f32[8,128]{1,0:T(8,128)S(1)} collective-permute-done((f32[8,128]{1,0:T(8,128)S(1)}, f32[8,128]{1,0:T(8,128)S(1)}, u32[]{:S(2)}, u32[]{:S(2)}) %collective-permute-start.30) | collective-permute-done | bytes 4128 | tf_op jit(solution)/shard_map/ppermute | solution.py:597
  81.2 2.0 %collective-permute-start.34 = (f32[1,128]{1,0:T(1,128)S(1)}, f32[1,128]{1,0:T(1,128)S(1)}, u32[]{:S(2)}, u32[]{:S(2)}) collective-permute-start(f32[1,128]{1,0:T(1,128)S(1)} %add.55), channel_id=1, source_target_pairs={{0,64},{16,80},{32,96},{48,112},{64,0},{80,16},{96,32},{112,48},{1... | collective-permute-start | bytes 1544 | tf_op jit(solution)/shard_map/ppermute | solution.py:603
  83.2 2.2 %collective-permute-start.35 = (f32[1,128]{1,0:T(1,128)S(1)}, f32[1,128]{1,0:T(1,128)S(1)}, u32[]{:S(2)}, u32[]{:S(2)}) collective-permute-start(f32[1,128]{1,0:T(1,128)S(1)} %add.55), channel_id=1, source_target_pairs={{0,32},{16,48},{32,64},{48,80},{64,96},{80,112},{96,0},{112,16},{1... | collective-permute-start | bytes 1544 | tf_op jit(solution)/shard_map/ppermute | solution.py:603
  85.4 1.0 %collective-permute-start.36 = (f32[1,128]{1,0:T(1,128)S(1)}, f32[1,128]{1,0:T(1,128)S(1)}, u32[]{:S(2)}, u32[]{:S(2)}) collective-permute-start(f32[1,128]{1,0:T(1,128)S(1)} %add.55), channel_id=1, source_target_pairs={{0,96},{16,112},{32,0},{48,16},{64,32},{80,48},{96,64},{112,80},{1... | collective-permute-start | bytes 1544 | tf_op jit(solution)/shard_map/ppermute | solution.py:603
  86.4 1.5 %collective-permute-done.35 = f32[1,128]{1,0:T(1,128)S(1)} collective-permute-done((f32[1,128]{1,0:T(1,128)S(1)}, f32[1,128]{1,0:T(1,128)S(1)}, u32[]{:S(2)}, u32[]{:S(2)}) %collective-permute-start.35) | collective-permute-done | bytes 544 | tf_op jit(solution)/shard_map/ppermute | solution.py:603
  88.9 10.5 %all_to_all.8 = f32[16,1,128]{2,1,0:T(1,128)S(1)} all-to-all(f32[16,1,128]{2,1,0:T(1,128)S(1)} %broadcast_in_dim.39), channel_id=1, replica_groups=mesh['gx'=8,'gy'=16] {'gy'}, dimensions={0} | all-to-all | bytes 16384 | tf_op jit(solution)/shard_map/all_to_all | solution.py:606
  (89 shorter events, 24.4 us)
Async XLA Ops:
  2.2 6.5 %collective-permute-start = (f32[40,128]{1,0:T(8,128)}, f32[40,128]{1,0:T(8,128)S(1)}, u32[]{:S(2)}, u32[]{:S(2)}) collective-permute-start(f32[40,128]{1,0:T(8,128)} %get-tuple-element.63.refs_0_), channel_id=1, source_target_pairs={{0,2},{1,3},{2,0},{3,1},{4,6},{5,7},{6,4},{7,5},{8,10},{9,11},{10,... | collective-permute-start | bytes 61448 | tf_op jit(solution)/shard_map/ppermute | solution.py:586
  6.2 4.0 %collective-permute-start.1 = (f32[40,128]{1,0:T(8,128)}, f32[40,128]{1,0:T(8,128)S(1)}, u32[]{:S(2)}, u32[]{:S(2)}) collective-permute-start(f32[40,128]{1,0:T(8,128)} %get-tuple-element.63.refs_0_), channel_id=1, source_target_pairs={{0,1},{1,0},{2,3},{3,2},{4,5},{5,4},{6,7},{7,6},{8,9},{9,8},{10,11... | collective-permute-start | bytes 61448 | tf_op jit(solution)/shard_map/ppermute | solution.py:586
  7.3 5.2 %collective-permute-start.2 = (f32[40,128]{1,0:T(8,128)}, f32[40,128]{1,0:T(8,128)S(1)}, u32[]{:S(2)}, u32[]{:S(2)}) collective-permute-start(f32[40,128]{1,0:T(8,128)} %get-tuple-element.63.refs_0_), channel_id=1, source_target_pairs={{0,3},{1,2},{2,1},{3,0},{4,7},{5,6},{6,5},{7,4},{8,11},{9,10},{10,... | collective-permute-start | bytes 61448 | tf_op jit(solution)/shard_map/ppermute | solution.py:586
  12.6 6.4 %collective-permute-start.4 = (f32[40,128]{1,0:T(8,128)S(1)}, f32[40,128]{1,0:T(8,128)S(1)}, u32[]{:S(2)}, u32[]{:S(2)}) collective-permute-start(f32[40,128]{1,0:T(8,128)S(1)} %select_select_fusion.refs_4_), channel_id=1, source_target_pairs={{0,8},{1,9},{2,10},{3,11},{4,12},{5,13},{6,14},{7,15},{8,0},{9,1},... | collective-permute-start | bytes 61448 | tf_op jit(solution)/shard_map/ppermute | solution.py:586
  15.8 3.8 %collective-permute-start.5 = (f32[40,128]{1,0:T(8,128)S(1)}, f32[40,128]{1,0:T(8,128)S(1)}, u32[]{:S(2)}, u32[]{:S(2)}) collective-permute-start(f32[40,128]{1,0:T(8,128)S(1)} %select_select_fusion.refs_4_), channel_id=1, source_target_pairs={{0,4},{1,5},{2,6},{3,7},{4,0},{5,1},{6,2},{7,3},{8,12},{9,13},{10,... | collective-permute-start | bytes 61448 | tf_op jit(solution)/shard_map/ppermute | solution.py:586
  16.5 5.0 %collective-permute-start.6 = (f32[40,128]{1,0:T(8,128)S(1)}, f32[40,128]{1,0:T(8,128)S(1)}, u32[]{:S(2)}, u32[]{:S(2)}) collective-permute-start(f32[40,128]{1,0:T(8,128)S(1)} %select_select_fusion.refs_4_), channel_id=1, source_target_pairs={{0,12},{1,13},{2,14},{3,15},{4,8},{5,9},{6,10},{7,11},{8,4},{9,5},... | collective-permute-start | bytes 61448 | tf_op jit(solution)/shard_map/ppermute | solution.py:586
  21.9 6.6 %collective-permute-start.13 = (f32[20,8,128]{2,1,0:T(8,128)S(1)}, f32[20,8,128]{2,1,0:T(8,128)S(1)}, u32[]{:S(2)}, u32[]{:S(2)}) collective-permute-start(f32[20,8,128]{2,1,0:T(8,128)S(1)} %get-tuple-element.68.own.refs_4_.refs_1_), channel_id=1, source_target_pairs={{0,2},{1,3},{2,0},{3,1},{4,6},{5,7},{6,4},{7,5},{8,10},{9,11},{10,... | collective-permute-start | bytes 245768 | tf_op jit(solution)/shard_map/ppermute | solution.py:586
  22.0 8.4 %collective-permute-start.14 = (f32[20,8,128]{2,1,0:T(8,128)S(1)}, f32[20,8,128]{2,1,0:T(8,128)S(1)}, u32[]{:S(2)}, u32[]{:S(2)}) collective-permute-start(f32[20,8,128]{2,1,0:T(8,128)S(1)} %get-tuple-element.68.own.refs_4_.refs_1_), channel_id=1, source_target_pairs={{0,1},{1,0},{2,3},{3,2},{4,5},{5,4},{6,7},{7,6},{8,9},{9,8},{10,11... | collective-permute-start | bytes 245768 | tf_op jit(solution)/shard_map/ppermute | solution.py:586
  22.9 7.6 %collective-permute-start.15 = (f32[20,8,128]{2,1,0:T(8,128)S(1)}, f32[20,8,128]{2,1,0:T(8,128)S(1)}, u32[]{:S(2)}, u32[]{:S(2)}) collective-permute-start(f32[20,8,128]{2,1,0:T(8,128)S(1)} %get-tuple-element.68.own.refs_4_.refs_1_), channel_id=1, source_target_pairs={{0,3},{1,2},{2,1},{3,0},{4,7},{5,6},{6,5},{7,4},{8,11},{9,10},{10,... | collective-permute-start | bytes 245768 | tf_op jit(solution)/shard_map/ppermute | solution.py:586
  26.3 6.0 %collective-permute-start.7 = (f32[20,8,128]{2,1,0:T(8,128)S(1)}, f32[20,8,128]{2,1,0:T(8,128)S(1)}, u32[]{:S(2)}, u32[]{:S(2)}) collective-permute-start(f32[20,8,128]{2,1,0:T(8,128)S(1)} %get-tuple-element.67.own.refs_0_), channel_id=1, source_target_pairs={{0,2},{1,3},{2,0},{3,1},{4,6},{5,7},{6,4},{7,5},{8,10},{9,11},{10,... | collective-permute-start | bytes 245768 | tf_op jit(solution)/shard_map/ppermute | solution.py:586
  26.4 8.3 %collective-permute-start.8 = (f32[20,8,128]{2,1,0:T(8,128)S(1)}, f32[20,8,128]{2,1,0:T(8,128)S(1)}, u32[]{:S(2)}, u32[]{:S(2)}) collective-permute-start(f32[20,8,128]{2,1,0:T(8,128)S(1)} %get-tuple-element.67.own.refs_0_), channel_id=1, source_target_pairs={{0,1},{1,0},{2,3},{3,2},{4,5},{5,4},{6,7},{7,6},{8,9},{9,8},{10,11... | collective-permute-start | bytes 245768 | tf_op jit(solution)/shard_map/ppermute | solution.py:586
  28.4 6.3 %collective-permute-start.9 = (f32[20,8,128]{2,1,0:T(8,128)S(1)}, f32[20,8,128]{2,1,0:T(8,128)S(1)}, u32[]{:S(2)}, u32[]{:S(2)}) collective-permute-start(f32[20,8,128]{2,1,0:T(8,128)S(1)} %get-tuple-element.67.own.refs_0_), channel_id=1, source_target_pairs={{0,3},{1,2},{2,1},{3,0},{4,7},{5,6},{6,5},{7,4},{8,11},{9,10},{10,... | collective-permute-start | bytes 245768 | tf_op jit(solution)/shard_map/ppermute | solution.py:586
  30.6 6.7 %collective-permute-start.16 = (f32[20,8,128]{2,1,0:T(8,128)S(1)}, f32[20,8,128]{2,1,0:T(8,128)S(1)}, u32[]{:S(2)}, u32[]{:S(2)}) collective-permute-start(f32[20,8,128]{2,1,0:T(8,128)S(1)} %group_total.3.refs_6_), channel_id=1, source_target_pairs={{0,8},{1,9},{2,10},{3,11},{4,12},{5,13},{6,14},{7,15},{8,0},{9,1},... | collective-permute-start | bytes 245768 | tf_op jit(solution)/shard_map/ppermute | solution.py:586
  31.3 9.1 %collective-permute-start.17 = (f32[20,8,128]{2,1,0:T(8,128)S(1)}, f32[20,8,128]{2,1,0:T(8,128)S(1)}, u32[]{:S(2)}, u32[]{:S(2)}) collective-permute-start(f32[20,8,128]{2,1,0:T(8,128)S(1)} %group_total.3.refs_6_), channel_id=1, source_target_pairs={{0,4},{1,5},{2,6},{3,7},{4,0},{5,1},{6,2},{7,3},{8,12},{9,13},{10,... | collective-permute-start | bytes 245768 | tf_op jit(solution)/shard_map/ppermute | solution.py:586
  32.3 8.1 %collective-permute-start.18 = (f32[20,8,128]{2,1,0:T(8,128)S(1)}, f32[20,8,128]{2,1,0:T(8,128)S(1)}, u32[]{:S(2)}, u32[]{:S(2)}) collective-permute-start(f32[20,8,128]{2,1,0:T(8,128)S(1)} %group_total.3.refs_6_), channel_id=1, source_target_pairs={{0,12},{1,13},{2,14},{3,15},{4,8},{5,9},{6,10},{7,11},{8,4},{9,5},... | collective-permute-start | bytes 245768 | tf_op jit(solution)/shard_map/ppermute | solution.py:586
  34.9 6.1 %collective-permute-start.10 = (f32[20,8,128]{2,1,0:T(8,128)S(1)}, f32[20,8,128]{2,1,0:T(8,128)S(1)}, u32[]{:S(2)}, u32[]{:S(2)}) collective-permute-start(f32[20,8,128]{2,1,0:T(8,128)S(1)} %group_total.2.refs_2_), channel_id=1, source_target_pairs={{0,8},{1,9},{2,10},{3,11},{4,12},{5,13},{6,14},{7,15},{8,0},{9,1},... | collective-permute-start | bytes 245768 | tf_op jit(solution)/shard_map/ppermute | solution.py:586
  35.6 5.4 %collective-permute-start.11 = (f32[20,8,128]{2,1,0:T(8,128)S(1)}, f32[20,8,128]{2,1,0:T(8,128)S(1)}, u32[]{:S(2)}, u32[]{:S(2)}) collective-permute-start(f32[20,8,128]{2,1,0:T(8,128)S(1)} %group_total.2.refs_2_), channel_id=1, source_target_pairs={{0,4},{1,5},{2,6},{3,7},{4,0},{5,1},{6,2},{7,3},{8,12},{9,13},{10,... | collective-permute-start | bytes 245768 | tf_op jit(solution)/shard_map/ppermute | solution.py:586
  37.3 5.7 %collective-permute-start.12 = (f32[20,8,128]{2,1,0:T(8,128)S(1)}, f32[20,8,128]{2,1,0:T(8,128)S(1)}, u32[]{:S(2)}, u32[]{:S(2)}) collective-permute-start(f32[20,8,128]{2,1,0:T(8,128)S(1)} %group_total.2.refs_2_), channel_id=1, source_target_pairs={{0,12},{1,13},{2,14},{3,15},{4,8},{5,9},{6,10},{7,11},{8,4},{9,5},... | collective-permute-start | bytes 245768 | tf_op jit(solution)/shard_map/ppermute | solution.py:586
  44.9 9.4 %collective-permute-start.21 = (f32[24,128]{1,0:T(8,128)S(1)}, f32[24,128]{1,0:T(8,128)S(1)}, u32[]{:S(2)}, u32[]{:S(2)}) collective-permute-start(f32[24,128]{1,0:T(8,128)S(1)} %select_add_fusion.1.sent_b), channel_id=1, source_target_pairs={{0,112},{16,32},{32,16},{48,64},{64,48},{80,96},{96,80},{112,0},{1... | collective-permute-start | bytes 36872 | tf_op jit(solution)/shard_map/ppermute | solution.py:596
  49.2 5.1 %collective-permute-start.20 = (f32[8,128]{1,0:T(8,128)S(1)}, f32[8,128]{1,0:T(8,128)S(1)}, u32[]{:S(2)}, u32[]{:S(2)}) collective-permute-start(f32[8,128]{1,0:T(8,128)S(1)} %slice_add_fusion.1), channel_id=1, source_target_pairs={{0,64},{16,80},{32,96},{48,112},{64,0},{80,16},{96,32},{112,48},{1... | collective-permute-start | bytes 12296 | tf_op jit(solution)/shard_map/ppermute | solution.py:597
  50.0 4.3 %collective-permute-start.22 = (f32[8,128]{1,0:T(8,128)S(1)}, f32[8,128]{1,0:T(8,128)S(1)}, u32[]{:S(2)}, u32[]{:S(2)}) collective-permute-start(f32[8,128]{1,0:T(8,128)S(1)} %slice_add_fusion.1), channel_id=1, source_target_pairs={{0,96},{16,48},{32,0},{48,80},{64,32},{80,112},{96,64},{112,16},{1... | collective-permute-start | bytes 12296 | tf_op jit(solution)/shard_map/ppermute | solution.py:595
  54.8 5.7 %collective-permute-start.23 = (f32[4,16,128]{2,1,0:T(8,128)S(1)}, f32[4,16,128]{2,1,0:T(8,128)S(1)}, u32[]{:S(2)}, u32[]{:S(2)}) collective-permute-start(f32[4,16,128]{2,1,0:T(8,128)S(1)} %get-tuple-element.85.refs_8_.refs_10_), channel_id=1, source_target_pairs={{0,2},{1,3},{2,0},{3,1},{4,6},{5,7},{6,4},{7,5},{8,10},{9,11},{10,... | collective-permute-start | bytes 98312 | tf_op jit(solution)/shard_map/ppermute | solution.py:586
  55.8 5.1 %collective-permute-start.24 = (f32[4,16,128]{2,1,0:T(8,128)S(1)}, f32[4,16,128]{2,1,0:T(8,128)S(1)}, u32[]{:S(2)}, u32[]{:S(2)}) collective-permute-start(f32[4,16,128]{2,1,0:T(8,128)S(1)} %get-tuple-element.85.refs_8_.refs_10_), channel_id=1, source_target_pairs={{0,1},{1,0},{2,3},{3,2},{4,5},{5,4},{6,7},{7,6},{8,9},{9,8},{10,11... | collective-permute-start | bytes 98312 | tf_op jit(solution)/shard_map/ppermute | solution.py:586
  58.7 5.1 %collective-permute-start.25 = (f32[4,16,128]{2,1,0:T(8,128)S(1)}, f32[4,16,128]{2,1,0:T(8,128)S(1)}, u32[]{:S(2)}, u32[]{:S(2)}) collective-permute-start(f32[4,16,128]{2,1,0:T(8,128)S(1)} %get-tuple-element.85.refs_8_.refs_10_), channel_id=1, source_target_pairs={{0,3},{1,2},{2,1},{3,0},{4,7},{5,6},{6,5},{7,4},{8,11},{9,10},{10,... | collective-permute-start | bytes 98312 | tf_op jit(solution)/shard_map/ppermute | solution.py:586
  63.9 5.5 %collective-permute-start.26 = (f32[4,16,128]{2,1,0:T(8,128)S(1)}, f32[4,16,128]{2,1,0:T(8,128)S(1)}, u32[]{:S(2)}, u32[]{:S(2)}) collective-permute-start(f32[4,16,128]{2,1,0:T(8,128)S(1)} %group_total_again.1.refs_11_), channel_id=1, source_target_pairs={{0,8},{1,9},{2,10},{3,11},{4,12},{5,13},{6,14},{7,15},{8,0},{9,1},... | collective-permute-start | bytes 98312 | tf_op jit(solution)/shard_map/ppermute | solution.py:586
  64.6 4.8 %collective-permute-start.27 = (f32[4,16,128]{2,1,0:T(8,128)S(1)}, f32[4,16,128]{2,1,0:T(8,128)S(1)}, u32[]{:S(2)}, u32[]{:S(2)}) collective-permute-start(f32[4,16,128]{2,1,0:T(8,128)S(1)} %group_total_again.1.refs_11_), channel_id=1, source_target_pairs={{0,4},{1,5},{2,6},{3,7},{4,0},{5,1},{6,2},{7,3},{8,12},{9,13},{10,... | collective-permute-start | bytes 98312 | tf_op jit(solution)/shard_map/ppermute | solution.py:586
  66.3 5.1 %collective-permute-start.28 = (f32[4,16,128]{2,1,0:T(8,128)S(1)}, f32[4,16,128]{2,1,0:T(8,128)S(1)}, u32[]{:S(2)}, u32[]{:S(2)}) collective-permute-start(f32[4,16,128]{2,1,0:T(8,128)S(1)} %group_total_again.1.refs_11_), channel_id=1, source_target_pairs={{0,12},{1,13},{2,14},{3,15},{4,8},{5,9},{6,10},{7,11},{8,4},{9,5},... | collective-permute-start | bytes 98312 | tf_op jit(solution)/shard_map/ppermute | solution.py:586
  73.4 6.1 %collective-permute-start.31 = (f32[24,128]{1,0:T(8,128)S(1)}, f32[24,128]{1,0:T(8,128)S(1)}, u32[]{:S(2)}, u32[]{:S(2)}) collective-permute-start(f32[24,128]{1,0:T(8,128)S(1)} %select_add_fusion.sent_b), channel_id=1, source_target_pairs={{0,112},{16,32},{32,16},{48,64},{64,48},{80,96},{96,80},{112,0},{1... | collective-permute-start | bytes 36872 | tf_op jit(solution)/shard_map/ppermute | solution.py:596
  74.4 5.1 %collective-permute-start.30 = (f32[8,128]{1,0:T(8,128)S(1)}, f32[8,128]{1,0:T(8,128)S(1)}, u32[]{:S(2)}, u32[]{:S(2)}) collective-permute-start(f32[8,128]{1,0:T(8,128)S(1)} %slice_add_fusion), channel_id=1, source_target_pairs={{0,64},{16,80},{32,96},{48,112},{64,0},{80,16},{96,32},{112,48},{1... | collective-permute-start | bytes 12296 | tf_op jit(solution)/shard_map/ppermute | solution.py:597
  75.7 3.8 %collective-permute-start.32 = (f32[8,128]{1,0:T(8,128)S(1)}, f32[8,128]{1,0:T(8,128)S(1)}, u32[]{:S(2)}, u32[]{:S(2)}) collective-permute-start(f32[8,128]{1,0:T(8,128)S(1)} %slice_add_fusion), channel_id=1, source_target_pairs={{0,96},{16,48},{32,0},{48,80},{64,32},{80,112},{96,64},{112,16},{1... | collective-permute-start | bytes 12296 | tf_op jit(solution)/shard_map/ppermute | solution.py:595
  81.2 5.3 %collective-permute-start.34 = (f32[1,128]{1,0:T(1,128)S(1)}, f32[1,128]{1,0:T(1,128)S(1)}, u32[]{:S(2)}, u32[]{:S(2)}) collective-permute-start(f32[1,128]{1,0:T(1,128)S(1)} %add.55), channel_id=1, source_target_pairs={{0,64},{16,80},{32,96},{48,112},{64,0},{80,16},{96,32},{112,48},{1... | collective-permute-start | bytes 1544 | tf_op jit(solution)/shard_map/ppermute | solution.py:603
  83.2 4.8 %collective-permute-start.35 = (f32[1,128]{1,0:T(1,128)S(1)}, f32[1,128]{1,0:T(1,128)S(1)}, u32[]{:S(2)}, u32[]{:S(2)}) collective-permute-start(f32[1,128]{1,0:T(1,128)S(1)} %add.55), channel_id=1, source_target_pairs={{0,32},{16,48},{32,64},{48,80},{64,96},{80,112},{96,0},{112,16},{1... | collective-permute-start | bytes 1544 | tf_op jit(solution)/shard_map/ppermute | solution.py:603
  (11 other events, 29.0 us)

commit v8 on v7

--- a/solution.py
+++ b/solution.py
@@ -14,7 +14,7 @@
 PLANE = (CX, NZ)
 N_GX, N_GY = 8, 16
 W_ALL = 128
-PARTNERS = (0, 2, 1, 3)
+PARTNERS = (0, 1, 2, 3)
 PREPARE_VMEM = 54400
 EDGES_VMEM = 55296
 SLOTS_ALL = 256
@@ -628,7 +628,7 @@
     )
     edges = swapped(edge, 1)
     lx = lax.ppermute(sx, "gx", [(i, i + 1) for i in range(N_GX - 1)])
-    *edges, rhs, tx, ty, tz, diag, cross = lax.optimization_barrier((*edges, rhs, tx, ty, tz, diag, cross))
+    *edges, lx = lax.optimization_barrier((*edges, lx))
     relayed = swapped(relay(*edges), 4)
     slots = perf_cell.shape[3]
     live = jnp.arange(slots, dtype=jnp.int32)[None, :] < perf_count.reshape(N_GX, 1)

time: 101 us -> 104 us (1.030)
  starting transfers between devices: 49.4 us -> 55.6 us
  waiting for transfers between devices: 30.5 us -> 28.5 us
    ppermute x24, starting transfers between devices: 32.1 us -> 39 us  [swapped(): lax.ppermute(block, 'gy', [(i, i ^ k * stride) for i in range(N_GY)])]
    ppermute x24, waiting for transfers between devices: 19 us -> 15.5 us  [swapped(): lax.ppermute(block, 'gy', [(i, i ^ k * stride) for i in range(N_GY)])]
  transfers between devices with their start and end apart: 37 -> 37, of which waited for: 22 -> 17; matrix products, arithmetic and copies ran while one was open for 1% -> 1% of each run, Pallas kernels for 2% -> 2%
where the time goes in v8:
time: 104 us
  starting transfers between devices  55.6 us (53%)
  waiting for transfers between devices  28.5 us (27%)
  blocking collectives  10.1 us (10%)
  Pallas kernels  7.67 us (7%)
    ppermute x24, starting transfers between devices, swapped(): lax.ppermute(block, 'gy', [(i, i ^ k * stride) for i in range(N_GY)])  39 us
    ppermute x24, waiting for transfers between devices, swapped(): lax.ppermute(block, 'gy', [(i, i ^ k * stride) for i in range(N_GY)])  15.5 us
    all_to_all x1, blocking collectives, sum_everywhere(): return lax.all_to_all(x, 'gy', split_axis=0, concat_axis=0, tiled=True)  10.1 us
    pallas_call x13, Pallas kernels, call(): pl.pallas_call(kernel, name=name, out_shape=tuple(outs), in_specs=specs o...  7.67 us
    ppermute x2, starting transfers between devices, exchange_rows(): lax.ppermute(sent_b, 'gx', [(i, (i + 1 if i % 2 else i - 1) % N_GX) for i...  5.64 us
    ppermute x2, waiting for transfers between devices, exchange_rows(): got_c = lax.ppermute(tail, 'gx', [(i, i ^ 4) for i in range(N_GX)])  5.34 us
    ppermute x3, starting transfers between devices, sum_everywhere(): lax.ppermute(x, 'gx', [(i, (i + 2 * k) % N_GX) for i in range(N_GX)])  4.65 us
    ppermute x3, waiting for transfers between devices, sum_everywhere(): lax.ppermute(x, 'gx', [(i, (i + 2 * k) % N_GX) for i in range(N_GX)])  3.31 us
  transfers between devices with their start and end apart: 37, of which 17 were waited for; matrix products, arithmetic and copies ran while one was open for 1% of the time, Pallas kernels for 2%

profile of v8, /device:TPU:0, one launch (start us, length us, event | category | flops | bytes accessed | tf_op | source)
XLA Modules:
  0.0 104.2 jit_solution(14462577272601685001)
XLA Ops:
  0.6 1.6 %edges.1 = (f32[2,8,128]{2,1,0:T(8,128)}, f32[40,128]{1,0:T(8,128)}) custom-call(f32[2,128,128]{2,1,0:T(8,128)} %bitcast.18, f32[2,128,128]{2,1,0:T(8,128)} %bitcast.20, s32[1,128]{1,0:T(1,128)} %brk_h.1), custom_call_target="tpu_custom_call" | custom-call | tf_op jit(solution)/shard_map/edges/pallas_call | solution.py:574
  2.2 2.1 %collective-permute-start = (f32[40,128]{1,0:T(8,128)}, f32[40,128]{1,0:T(8,128)S(1)}, u32[]{:S(2)}, u32[]{:S(2)}) collective-permute-start(f32[40,128]{1,0:T(8,128)} %get-tuple-element.53.refs_0_), channel_id=1, source_target_pairs={{0,1},{1,0},{2,3},{3,2},{4,5},{5,4},{6,7},{7,6},{8,9},{9,8},{10,11... | collective-permute-start | bytes 61448 | tf_op jit(solution)/shard_map/ppermute | solution.py:586
  4.3 3.6 %collective-permute-start.1 = (f32[40,128]{1,0:T(8,128)}, f32[40,128]{1,0:T(8,128)S(1)}, u32[]{:S(2)}, u32[]{:S(2)}) collective-permute-start(f32[40,128]{1,0:T(8,128)} %get-tuple-element.53.refs_0_), channel_id=1, source_target_pairs={{0,2},{1,3},{2,0},{3,1},{4,6},{5,7},{6,4},{7,5},{8,10},{9,11},{10,... | collective-permute-start | bytes 61448 | tf_op jit(solution)/shard_map/ppermute | solution.py:586
  7.9 1.3 %collective-permute-start.3 = (f32[2,8,128]{2,1,0:T(8,128)}, f32[2,8,128]{2,1,0:T(8,128)S(1)}, u32[]{:S(2)}, u32[]{:S(2)}) collective-permute-start(f32[2,8,128]{2,1,0:T(8,128)} %get-tuple-element.51), channel_id=1, source_target_pairs={{0,16},{16,32},{32,48},{48,64},{64,80},{80,96},{96,112},{1,17},{17... | collective-permute-start | bytes 24584 | tf_op jit(solution)/shard_map/ppermute | solution.py:630
  10.2 2.9 %collective-permute-done.2.refs_3_ = f32[40,128]{1,0:T(8,128)S(1)} collective-permute-done((f32[40,128]{1,0:T(8,128)}, f32[40,128]{1,0:T(8,128)S(1)}, u32[]{:S(2)}, u32[]{:S(2)}) %collective-permute-start.2) | collective-permute-done | bytes 20512 | tf_op jit(solution)/shard_map/ppermute | solution.py:586
  13.2 1.7 %collective-permute-start.4 = (f32[40,128]{1,0:T(8,128)S(1)}, f32[40,128]{1,0:T(8,128)S(1)}, u32[]{:S(2)}, u32[]{:S(2)}) collective-permute-start(f32[40,128]{1,0:T(8,128)S(1)} %select_select_fusion.refs_4_), channel_id=1, source_target_pairs={{0,4},{1,5},{2,6},{3,7},{4,0},{5,1},{6,2},{7,3},{8,12},{9,13},{10,... | collective-permute-start | bytes 61448 | tf_op jit(solution)/shard_map/ppermute | solution.py:586
  14.8 2.9 %collective-permute-start.5 = (f32[40,128]{1,0:T(8,128)S(1)}, f32[40,128]{1,0:T(8,128)S(1)}, u32[]{:S(2)}, u32[]{:S(2)}) collective-permute-start(f32[40,128]{1,0:T(8,128)S(1)} %select_select_fusion.refs_4_), channel_id=1, source_target_pairs={{0,8},{1,9},{2,10},{3,11},{4,12},{5,13},{6,14},{7,15},{8,0},{9,1},... | collective-permute-start | bytes 61448 | tf_op jit(solution)/shard_map/ppermute | solution.py:586
  17.9 1.4 %prepare.1 = (f32[2,8,16,128]{3,2,1,0:T(8,128)S(1)}, f32[2,8,16,128]{3,2,1,0:T(8,128)S(1)}, f32[2,8,16,128]{3,2,1,0:T(8,128)S(1)}, f32[2,8,16,128]{3,2,1,0:T(8,1...) custom-call(f32[2,128,128]{2,1,0:T(8,128)} %bitcast.23, f32[4,128,128]{2,1,0:T(8,128)} %bitcast.22, ...), custom_call_target="tpu_custom_call" | custom-call | tf_op jit(solution)/shard_map/prepare/pallas_call | solution.py:574
  20.1 2.6 %collective-permute-done.6.refs_7_ = f32[40,128]{1,0:T(8,128)S(1)} collective-permute-done((f32[40,128]{1,0:T(8,128)S(1)}, f32[40,128]{1,0:T(8,128)S(1)}, u32[]{:S(2)}, u32[]{:S(2)}) %collective-permute-start.6) | collective-permute-done | bytes 20512 | tf_op jit(solution)/shard_map/ppermute | solution.py:586
  23.2 1.8 %collective-permute-start.14 = (f32[20,8,128]{2,1,0:T(8,128)S(1)}, f32[20,8,128]{2,1,0:T(8,128)S(1)}, u32[]{:S(2)}, u32[]{:S(2)}) collective-permute-start(f32[20,8,128]{2,1,0:T(8,128)S(1)} %get-tuple-element.58.own.refs_4_.refs_1_), channel_id=1, source_target_pairs={{0,2},{1,3},{2,0},{3,1},{4,6},{5,7},{6,4},{7,5},{8,10},{9,11},{10,... | collective-permute-start | bytes 245768 | tf_op jit(solution)/shard_map/ppermute | solution.py:586
  25.0 2.9 %collective-permute-start.15 = (f32[20,8,128]{2,1,0:T(8,128)S(1)}, f32[20,8,128]{2,1,0:T(8,128)S(1)}, u32[]{:S(2)}, u32[]{:S(2)}) collective-permute-start(f32[20,8,128]{2,1,0:T(8,128)S(1)} %get-tuple-element.58.own.refs_4_.refs_1_), channel_id=1, source_target_pairs={{0,3},{1,2},{2,1},{3,0},{4,7},{5,6},{6,5},{7,4},{8,11},{9,10},{10,... | collective-permute-start | bytes 245768 | tf_op jit(solution)/shard_map/ppermute | solution.py:586
  28.2 1.8 %collective-permute-start.8 = (f32[20,8,128]{2,1,0:T(8,128)S(1)}, f32[20,8,128]{2,1,0:T(8,128)S(1)}, u32[]{:S(2)}, u32[]{:S(2)}) collective-permute-start(f32[20,8,128]{2,1,0:T(8,128)S(1)} %get-tuple-element.57.own.refs_0_), channel_id=1, source_target_pairs={{0,2},{1,3},{2,0},{3,1},{4,6},{5,7},{6,4},{7,5},{8,10},{9,11},{10,... | collective-permute-start | bytes 245768 | tf_op jit(solution)/shard_map/ppermute | solution.py:586
  30.0 2.9 %collective-permute-start.9 = (f32[20,8,128]{2,1,0:T(8,128)S(1)}, f32[20,8,128]{2,1,0:T(8,128)S(1)}, u32[]{:S(2)}, u32[]{:S(2)}) collective-permute-start(f32[20,8,128]{2,1,0:T(8,128)S(1)} %get-tuple-element.57.own.refs_0_), channel_id=1, source_target_pairs={{0,3},{1,2},{2,1},{3,0},{4,7},{5,6},{6,5},{7,4},{8,11},{9,10},{10,... | collective-permute-start | bytes 245768 | tf_op jit(solution)/shard_map/ppermute | solution.py:586
  33.1 1.7 %collective-permute-start.17 = (f32[20,8,128]{2,1,0:T(8,128)S(1)}, f32[20,8,128]{2,1,0:T(8,128)S(1)}, u32[]{:S(2)}, u32[]{:S(2)}) collective-permute-start(f32[20,8,128]{2,1,0:T(8,128)S(1)} %group_total.3.refs_6_), channel_id=1, source_target_pairs={{0,8},{1,9},{2,10},{3,11},{4,12},{5,13},{6,14},{7,15},{8,0},{9,1},... | collective-permute-start | bytes 245768 | tf_op jit(solution)/shard_map/ppermute | solution.py:586
  34.7 3.0 %collective-permute-start.18 = (f32[20,8,128]{2,1,0:T(8,128)S(1)}, f32[20,8,128]{2,1,0:T(8,128)S(1)}, u32[]{:S(2)}, u32[]{:S(2)}) collective-permute-start(f32[20,8,128]{2,1,0:T(8,128)S(1)} %group_total.3.refs_6_), channel_id=1, source_target_pairs={{0,12},{1,13},{2,14},{3,15},{4,8},{5,9},{6,10},{7,11},{8,4},{9,5},... | collective-permute-start | bytes 245768 | tf_op jit(solution)/shard_map/ppermute | solution.py:586
  38.0 1.7 %collective-permute-start.11 = (f32[20,8,128]{2,1,0:T(8,128)S(1)}, f32[20,8,128]{2,1,0:T(8,128)S(1)}, u32[]{:S(2)}, u32[]{:S(2)}) collective-permute-start(f32[20,8,128]{2,1,0:T(8,128)S(1)} %group_total.2.refs_2_), channel_id=1, source_target_pairs={{0,8},{1,9},{2,10},{3,11},{4,12},{5,13},{6,14},{7,15},{8,0},{9,1},... | collective-permute-start | bytes 245768 | tf_op jit(solution)/shard_map/ppermute | solution.py:586
  39.7 3.0 %collective-permute-start.12 = (f32[20,8,128]{2,1,0:T(8,128)S(1)}, f32[20,8,128]{2,1,0:T(8,128)S(1)}, u32[]{:S(2)}, u32[]{:S(2)}) collective-permute-start(f32[20,8,128]{2,1,0:T(8,128)S(1)} %group_total.2.refs_2_), channel_id=1, source_target_pairs={{0,12},{1,13},{2,14},{3,15},{4,8},{5,9},{6,10},{7,11},{8,4},{9,5},... | collective-permute-start | bytes 245768 | tf_op jit(solution)/shard_map/ppermute | solution.py:586
  44.0 1.3 %collective-permute-done.12.refs_5_ = f32[20,8,128]{2,1,0:T(8,128)S(1)} collective-permute-done((f32[20,8,128]{2,1,0:T(8,128)S(1)}, f32[20,8,128]{2,1,0:T(8,128)S(1)}, u32[]{:S(2)}, u32[]{:S(2)}) %collective-permute-start.12) | collective-permute-done | bytes 81952 | tf_op jit(solution)/shard_map/ppermute | solution.py:586
  47.3 4.2 %collective-permute-start.21 = (f32[24,128]{1,0:T(8,128)S(1)}, f32[24,128]{1,0:T(8,128)S(1)}, u32[]{:S(2)}, u32[]{:S(2)}) collective-permute-start(f32[24,128]{1,0:T(8,128)S(1)} %select_add_fusion.1.sent_b), channel_id=1, source_target_pairs={{0,112},{16,32},{32,16},{48,64},{64,48},{80,96},{96,80},{112,0},{1... | collective-permute-start | bytes 36872 | tf_op jit(solution)/shard_map/ppermute | solution.py:596
  53.1 3.5 %collective-permute-done.20.got_c = f32[8,128]{1,0:T(8,128)S(1)} collective-permute-done((f32[8,128]{1,0:T(8,128)S(1)}, f32[8,128]{1,0:T(8,128)S(1)}, u32[]{:S(2)}, u32[]{:S(2)}) %collective-permute-start.20) | collective-permute-done | bytes 4128 | tf_op jit(solution)/shard_map/ppermute | solution.py:597
  57.2 3.0 %collective-permute-start.24 = (f32[4,16,128]{2,1,0:T(8,128)S(1)}, f32[4,16,128]{2,1,0:T(8,128)S(1)}, u32[]{:S(2)}, u32[]{:S(2)}) collective-permute-start(f32[4,16,128]{2,1,0:T(8,128)S(1)} %get-tuple-element.75.refs_8_.refs_10_), channel_id=1, source_target_pairs={{0,2},{1,3},{2,0},{3,1},{4,6},{5,7},{6,4},{7,5},{8,10},{9,11},{10,... | collective-permute-start | bytes 98312 | tf_op jit(solution)/shard_map/ppermute | solution.py:586
  60.2 1.7 %collective-permute-start.25 = (f32[4,16,128]{2,1,0:T(8,128)S(1)}, f32[4,16,128]{2,1,0:T(8,128)S(1)}, u32[]{:S(2)}, u32[]{:S(2)}) collective-permute-start(f32[4,16,128]{2,1,0:T(8,128)S(1)} %get-tuple-element.75.refs_8_.refs_10_), channel_id=1, source_target_pairs={{0,3},{1,2},{2,1},{3,0},{4,7},{5,6},{6,5},{7,4},{8,11},{9,10},{10,... | collective-permute-start | bytes 98312 | tf_op jit(solution)/shard_map/ppermute | solution.py:586
  62.7 2.6 %collective-permute-done.25.refs_11_ = f32[4,16,128]{2,1,0:T(8,128)S(1)} collective-permute-done((f32[4,16,128]{2,1,0:T(8,128)S(1)}, f32[4,16,128]{2,1,0:T(8,128)S(1)}, u32[]{:S(2)}, u32[]{:S(2)}) %collective-permute-start.25) | collective-permute-done | bytes 32800 | tf_op jit(solution)/shard_map/ppermute | solution.py:586
  66.1 3.8 %collective-permute-start.27 = (f32[4,16,128]{2,1,0:T(8,128)S(1)}, f32[4,16,128]{2,1,0:T(8,128)S(1)}, u32[]{:S(2)}, u32[]{:S(2)}) collective-permute-start(f32[4,16,128]{2,1,0:T(8,128)S(1)} %group_total_again.1.refs_11_), channel_id=1, source_target_pairs={{0,8},{1,9},{2,10},{3,11},{4,12},{5,13},{6,14},{7,15},{8,0},{9,1},... | collective-permute-start | bytes 98312 | tf_op jit(solution)/shard_map/ppermute | solution.py:586
  70.6 1.7 %collective-permute-done.27.refs_13_ = f32[4,16,128]{2,1,0:T(8,128)S(1)} collective-permute-done((f32[4,16,128]{2,1,0:T(8,128)S(1)}, f32[4,16,128]{2,1,0:T(8,128)S(1)}, u32[]{:S(2)}, u32[]{:S(2)}) %collective-permute-start.27) | collective-permute-done | bytes 32800 | tf_op jit(solution)/shard_map/ppermute | solution.py:586
  72.3 2.8 %collective-permute-done.28.refs_14_ = f32[4,16,128]{2,1,0:T(8,128)S(1)} collective-permute-done((f32[4,16,128]{2,1,0:T(8,128)S(1)}, f32[4,16,128]{2,1,0:T(8,128)S(1)}, u32[]{:S(2)}, u32[]{:S(2)}) %collective-permute-start.28) | collective-permute-done | bytes 32800 | tf_op jit(solution)/shard_map/ppermute | solution.py:586
  77.1 1.4 %collective-permute-start.31 = (f32[24,128]{1,0:T(8,128)S(1)}, f32[24,128]{1,0:T(8,128)S(1)}, u32[]{:S(2)}, u32[]{:S(2)}) collective-permute-start(f32[24,128]{1,0:T(8,128)S(1)} %select_add_fusion.sent_b), channel_id=1, source_target_pairs={{0,112},{16,32},{32,16},{48,64},{64,48},{80,96},{96,80},{112,0},{1... | collective-permute-start | bytes 36872 | tf_op jit(solution)/shard_map/ppermute | solution.py:596
  79.4 2.3 %collective-permute-start.32 = (f32[8,128]{1,0:T(8,128)S(1)}, f32[8,128]{1,0:T(8,128)S(1)}, u32[]{:S(2)}, u32[]{:S(2)}) collective-permute-start(f32[8,128]{1,0:T(8,128)S(1)} %slice_add_fusion), channel_id=1, source_target_pairs={{0,96},{16,48},{32,0},{48,80},{64,32},{80,112},{96,64},{112,16},{1... | collective-permute-start | bytes 12296 | tf_op jit(solution)/shard_map/ppermute | solution.py:595
  81.7 1.9 %collective-permute-done.30.got_c = f32[8,128]{1,0:T(8,128)S(1)} collective-permute-done((f32[8,128]{1,0:T(8,128)S(1)}, f32[8,128]{1,0:T(8,128)S(1)}, u32[]{:S(2)}, u32[]{:S(2)}) %collective-permute-start.30) | collective-permute-done | bytes 4128 | tf_op jit(solution)/shard_map/ppermute | solution.py:597
  85.8 3.8 %collective-permute-start.35 = (f32[1,128]{1,0:T(1,128)S(1)}, f32[1,128]{1,0:T(1,128)S(1)}, u32[]{:S(2)}, u32[]{:S(2)}) collective-permute-start(f32[1,128]{1,0:T(1,128)S(1)} %add.55), channel_id=1, source_target_pairs={{0,64},{16,80},{32,96},{48,112},{64,0},{80,16},{96,32},{112,48},{1... | collective-permute-start | bytes 1544 | tf_op jit(solution)/shard_map/ppermute | solution.py:603
  91.2 2.0 %collective-permute-done.36 = f32[1,128]{1,0:T(1,128)S(1)} collective-permute-done((f32[1,128]{1,0:T(1,128)S(1)}, f32[1,128]{1,0:T(1,128)S(1)}, u32[]{:S(2)}, u32[]{:S(2)}) %collective-permute-start.36) | collective-permute-done | bytes 544 | tf_op jit(solution)/shard_map/ppermute | solution.py:603
  93.2 10.1 %all_to_all.8 = f32[16,1,128]{2,1,0:T(1,128)S(1)} all-to-all(f32[16,1,128]{2,1,0:T(1,128)S(1)} %broadcast_in_dim.39), channel_id=1, replica_groups=mesh['gx'=8,'gy'=16] {'gy'}, dimensions={0} | all-to-all | bytes 16384 | tf_op jit(solution)/shard_map/all_to_all | solution.py:606
  (87 shorter events, 18.4 us)
Async XLA Ops:
  2.2 8.0 %collective-permute-start = (f32[40,128]{1,0:T(8,128)}, f32[40,128]{1,0:T(8,128)S(1)}, u32[]{:S(2)}, u32[]{:S(2)}) collective-permute-start(f32[40,128]{1,0:T(8,128)} %get-tuple-element.53.refs_0_), channel_id=1, source_target_pairs={{0,1},{1,0},{2,3},{3,2},{4,5},{5,4},{6,7},{7,6},{8,9},{9,8},{10,11... | collective-permute-start | bytes 61448 | tf_op jit(solution)/shard_map/ppermute | solution.py:586
  4.3 5.9 %collective-permute-start.1 = (f32[40,128]{1,0:T(8,128)}, f32[40,128]{1,0:T(8,128)S(1)}, u32[]{:S(2)}, u32[]{:S(2)}) collective-permute-start(f32[40,128]{1,0:T(8,128)} %get-tuple-element.53.refs_0_), channel_id=1, source_target_pairs={{0,2},{1,3},{2,0},{3,1},{4,6},{5,7},{6,4},{7,5},{8,10},{9,11},{10,... | collective-permute-start | bytes 61448 | tf_op jit(solution)/shard_map/ppermute | solution.py:586
  7.9 5.2 %collective-permute-start.2 = (f32[40,128]{1,0:T(8,128)}, f32[40,128]{1,0:T(8,128)S(1)}, u32[]{:S(2)}, u32[]{:S(2)}) collective-permute-start(f32[40,128]{1,0:T(8,128)} %get-tuple-element.53.refs_0_), channel_id=1, source_target_pairs={{0,3},{1,2},{2,1},{3,0},{4,7},{5,6},{6,5},{7,4},{8,11},{9,10},{10,... | collective-permute-start | bytes 61448 | tf_op jit(solution)/shard_map/ppermute | solution.py:586
  13.2 6.2 %collective-permute-start.4 = (f32[40,128]{1,0:T(8,128)S(1)}, f32[40,128]{1,0:T(8,128)S(1)}, u32[]{:S(2)}, u32[]{:S(2)}) collective-permute-start(f32[40,128]{1,0:T(8,128)S(1)} %select_select_fusion.refs_4_), channel_id=1, source_target_pairs={{0,4},{1,5},{2,6},{3,7},{4,0},{5,1},{6,2},{7,3},{8,12},{9,13},{10,... | collective-permute-start | bytes 61448 | tf_op jit(solution)/shard_map/ppermute | solution.py:586
  14.8 5.3 %collective-permute-start.5 = (f32[40,128]{1,0:T(8,128)S(1)}, f32[40,128]{1,0:T(8,128)S(1)}, u32[]{:S(2)}, u32[]{:S(2)}) collective-permute-start(f32[40,128]{1,0:T(8,128)S(1)} %select_select_fusion.refs_4_), channel_id=1, source_target_pairs={{0,8},{1,9},{2,10},{3,11},{4,12},{5,13},{6,14},{7,15},{8,0},{9,1},... | collective-permute-start | bytes 61448 | tf_op jit(solution)/shard_map/ppermute | solution.py:586
  17.7 5.0 %collective-permute-start.6 = (f32[40,128]{1,0:T(8,128)S(1)}, f32[40,128]{1,0:T(8,128)S(1)}, u32[]{:S(2)}, u32[]{:S(2)}) collective-permute-start(f32[40,128]{1,0:T(8,128)S(1)} %select_select_fusion.refs_4_), channel_id=1, source_target_pairs={{0,12},{1,13},{2,14},{3,15},{4,8},{5,9},{6,10},{7,11},{8,4},{9,5},... | collective-permute-start | bytes 61448 | tf_op jit(solution)/shard_map/ppermute | solution.py:586
  23.1 6.9 %collective-permute-start.13 = (f32[20,8,128]{2,1,0:T(8,128)S(1)}, f32[20,8,128]{2,1,0:T(8,128)S(1)}, u32[]{:S(2)}, u32[]{:S(2)}) collective-permute-start(f32[20,8,128]{2,1,0:T(8,128)S(1)} %get-tuple-element.58.own.refs_4_.refs_1_), channel_id=1, source_target_pairs={{0,1},{1,0},{2,3},{3,2},{4,5},{5,4},{6,7},{7,6},{8,9},{9,8},{10,11... | collective-permute-start | bytes 245768 | tf_op jit(solution)/shard_map/ppermute | solution.py:586
  23.2 9.7 %collective-permute-start.14 = (f32[20,8,128]{2,1,0:T(8,128)S(1)}, f32[20,8,128]{2,1,0:T(8,128)S(1)}, u32[]{:S(2)}, u32[]{:S(2)}) collective-permute-start(f32[20,8,128]{2,1,0:T(8,128)S(1)} %get-tuple-element.58.own.refs_4_.refs_1_), channel_id=1, source_target_pairs={{0,2},{1,3},{2,0},{3,1},{4,6},{5,7},{6,4},{7,5},{8,10},{9,11},{10,... | collective-permute-start | bytes 245768 | tf_op jit(solution)/shard_map/ppermute | solution.py:586
  25.0 7.8 %collective-permute-start.15 = (f32[20,8,128]{2,1,0:T(8,128)S(1)}, f32[20,8,128]{2,1,0:T(8,128)S(1)}, u32[]{:S(2)}, u32[]{:S(2)}) collective-permute-start(f32[20,8,128]{2,1,0:T(8,128)S(1)} %get-tuple-element.58.own.refs_4_.refs_1_), channel_id=1, source_target_pairs={{0,3},{1,2},{2,1},{3,0},{4,7},{5,6},{6,5},{7,4},{8,11},{9,10},{10,... | collective-permute-start | bytes 245768 | tf_op jit(solution)/shard_map/ppermute | solution.py:586
  28.1 6.6 %collective-permute-start.7 = (f32[20,8,128]{2,1,0:T(8,128)S(1)}, f32[20,8,128]{2,1,0:T(8,128)S(1)}, u32[]{:S(2)}, u32[]{:S(2)}) collective-permute-start(f32[20,8,128]{2,1,0:T(8,128)S(1)} %get-tuple-element.57.own.refs_0_), channel_id=1, source_target_pairs={{0,1},{1,0},{2,3},{3,2},{4,5},{5,4},{6,7},{7,6},{8,9},{9,8},{10,11... | collective-permute-start | bytes 245768 | tf_op jit(solution)/shard_map/ppermute | solution.py:586
  28.2 9.6 %collective-permute-start.8 = (f32[20,8,128]{2,1,0:T(8,128)S(1)}, f32[20,8,128]{2,1,0:T(8,128)S(1)}, u32[]{:S(2)}, u32[]{:S(2)}) collective-permute-start(f32[20,8,128]{2,1,0:T(8,128)S(1)} %get-tuple-element.57.own.refs_0_), channel_id=1, source_target_pairs={{0,2},{1,3},{2,0},{3,1},{4,6},{5,7},{6,4},{7,5},{8,10},{9,11},{10,... | collective-permute-start | bytes 245768 | tf_op jit(solution)/shard_map/ppermute | solution.py:586
  30.0 7.8 %collective-permute-start.9 = (f32[20,8,128]{2,1,0:T(8,128)S(1)}, f32[20,8,128]{2,1,0:T(8,128)S(1)}, u32[]{:S(2)}, u32[]{:S(2)}) collective-permute-start(f32[20,8,128]{2,1,0:T(8,128)S(1)} %get-tuple-element.57.own.refs_0_), channel_id=1, source_target_pairs={{0,3},{1,2},{2,1},{3,0},{4,7},{5,6},{6,5},{7,4},{8,11},{9,10},{10,... | collective-permute-start | bytes 245768 | tf_op jit(solution)/shard_map/ppermute | solution.py:586
  33.0 6.7 %collective-permute-start.16 = (f32[20,8,128]{2,1,0:T(8,128)S(1)}, f32[20,8,128]{2,1,0:T(8,128)S(1)}, u32[]{:S(2)}, u32[]{:S(2)}) collective-permute-start(f32[20,8,128]{2,1,0:T(8,128)S(1)} %group_total.3.refs_6_), channel_id=1, source_target_pairs={{0,4},{1,5},{2,6},{3,7},{4,0},{5,1},{6,2},{7,3},{8,12},{9,13},{10,... | collective-permute-start | bytes 245768 | tf_op jit(solution)/shard_map/ppermute | solution.py:586
  33.1 10.9 %collective-permute-start.17 = (f32[20,8,128]{2,1,0:T(8,128)S(1)}, f32[20,8,128]{2,1,0:T(8,128)S(1)}, u32[]{:S(2)}, u32[]{:S(2)}) collective-permute-start(f32[20,8,128]{2,1,0:T(8,128)S(1)} %group_total.3.refs_6_), channel_id=1, source_target_pairs={{0,8},{1,9},{2,10},{3,11},{4,12},{5,13},{6,14},{7,15},{8,0},{9,1},... | collective-permute-start | bytes 245768 | tf_op jit(solution)/shard_map/ppermute | solution.py:586
  34.7 9.3 %collective-permute-start.18 = (f32[20,8,128]{2,1,0:T(8,128)S(1)}, f32[20,8,128]{2,1,0:T(8,128)S(1)}, u32[]{:S(2)}, u32[]{:S(2)}) collective-permute-start(f32[20,8,128]{2,1,0:T(8,128)S(1)} %group_total.3.refs_6_), channel_id=1, source_target_pairs={{0,12},{1,13},{2,14},{3,15},{4,8},{5,9},{6,10},{7,11},{8,4},{9,5},... | collective-permute-start | bytes 245768 | tf_op jit(solution)/shard_map/ppermute | solution.py:586
  37.9 6.1 %collective-permute-start.10 = (f32[20,8,128]{2,1,0:T(8,128)S(1)}, f32[20,8,128]{2,1,0:T(8,128)S(1)}, u32[]{:S(2)}, u32[]{:S(2)}) collective-permute-start(f32[20,8,128]{2,1,0:T(8,128)S(1)} %group_total.2.refs_2_), channel_id=1, source_target_pairs={{0,4},{1,5},{2,6},{3,7},{4,0},{5,1},{6,2},{7,3},{8,12},{9,13},{10,... | collective-permute-start | bytes 245768 | tf_op jit(solution)/shard_map/ppermute | solution.py:586
  38.0 6.0 %collective-permute-start.11 = (f32[20,8,128]{2,1,0:T(8,128)S(1)}, f32[20,8,128]{2,1,0:T(8,128)S(1)}, u32[]{:S(2)}, u32[]{:S(2)}) collective-permute-start(f32[20,8,128]{2,1,0:T(8,128)S(1)} %group_total.2.refs_2_), channel_id=1, source_target_pairs={{0,8},{1,9},{2,10},{3,11},{4,12},{5,13},{6,14},{7,15},{8,0},{9,1},... | collective-permute-start | bytes 245768 | tf_op jit(solution)/shard_map/ppermute | solution.py:586
  39.7 5.7 %collective-permute-start.12 = (f32[20,8,128]{2,1,0:T(8,128)S(1)}, f32[20,8,128]{2,1,0:T(8,128)S(1)}, u32[]{:S(2)}, u32[]{:S(2)}) collective-permute-start(f32[20,8,128]{2,1,0:T(8,128)S(1)} %group_total.2.refs_2_), channel_id=1, source_target_pairs={{0,12},{1,13},{2,14},{3,15},{4,8},{5,9},{6,10},{7,11},{8,4},{9,5},... | collective-permute-start | bytes 245768 | tf_op jit(solution)/shard_map/ppermute | solution.py:586
  47.3 9.4 %collective-permute-start.21 = (f32[24,128]{1,0:T(8,128)S(1)}, f32[24,128]{1,0:T(8,128)S(1)}, u32[]{:S(2)}, u32[]{:S(2)}) collective-permute-start(f32[24,128]{1,0:T(8,128)S(1)} %select_add_fusion.1.sent_b), channel_id=1, source_target_pairs={{0,112},{16,32},{32,16},{48,64},{64,48},{80,96},{96,80},{112,0},{1... | collective-permute-start | bytes 36872 | tf_op jit(solution)/shard_map/ppermute | solution.py:596
  51.5 5.1 %collective-permute-start.20 = (f32[8,128]{1,0:T(8,128)S(1)}, f32[8,128]{1,0:T(8,128)S(1)}, u32[]{:S(2)}, u32[]{:S(2)}) collective-permute-start(f32[8,128]{1,0:T(8,128)S(1)} %slice_add_fusion.1), channel_id=1, source_target_pairs={{0,64},{16,80},{32,96},{48,112},{64,0},{80,16},{96,32},{112,48},{1... | collective-permute-start | bytes 12296 | tf_op jit(solution)/shard_map/ppermute | solution.py:597
  52.2 4.4 %collective-permute-start.22 = (f32[8,128]{1,0:T(8,128)S(1)}, f32[8,128]{1,0:T(8,128)S(1)}, u32[]{:S(2)}, u32[]{:S(2)}) collective-permute-start(f32[8,128]{1,0:T(8,128)S(1)} %slice_add_fusion.1), channel_id=1, source_target_pairs={{0,96},{16,48},{32,0},{48,80},{64,32},{80,112},{96,64},{112,16},{1... | collective-permute-start | bytes 12296 | tf_op jit(solution)/shard_map/ppermute | solution.py:595
  57.1 4.8 %collective-permute-start.23 = (f32[4,16,128]{2,1,0:T(8,128)S(1)}, f32[4,16,128]{2,1,0:T(8,128)S(1)}, u32[]{:S(2)}, u32[]{:S(2)}) collective-permute-start(f32[4,16,128]{2,1,0:T(8,128)S(1)} %get-tuple-element.75.refs_8_.refs_10_), channel_id=1, source_target_pairs={{0,1},{1,0},{2,3},{3,2},{4,5},{5,4},{6,7},{7,6},{8,9},{9,8},{10,11... | collective-permute-start | bytes 98312 | tf_op jit(solution)/shard_map/ppermute | solution.py:586
  57.2 5.5 %collective-permute-start.24 = (f32[4,16,128]{2,1,0:T(8,128)S(1)}, f32[4,16,128]{2,1,0:T(8,128)S(1)}, u32[]{:S(2)}, u32[]{:S(2)}) collective-permute-start(f32[4,16,128]{2,1,0:T(8,128)S(1)} %get-tuple-element.75.refs_8_.refs_10_), channel_id=1, source_target_pairs={{0,2},{1,3},{2,0},{3,1},{4,6},{5,7},{6,4},{7,5},{8,10},{9,11},{10,... | collective-permute-start | bytes 98312 | tf_op jit(solution)/shard_map/ppermute | solution.py:586
  60.2 5.1 %collective-permute-start.25 = (f32[4,16,128]{2,1,0:T(8,128)S(1)}, f32[4,16,128]{2,1,0:T(8,128)S(1)}, u32[]{:S(2)}, u32[]{:S(2)}) collective-permute-start(f32[4,16,128]{2,1,0:T(8,128)S(1)} %get-tuple-element.75.refs_8_.refs_10_), channel_id=1, source_target_pairs={{0,3},{1,2},{2,1},{3,0},{4,7},{5,6},{6,5},{7,4},{8,11},{9,10},{10,... | collective-permute-start | bytes 98312 | tf_op jit(solution)/shard_map/ppermute | solution.py:586
  65.4 5.2 %collective-permute-start.26 = (f32[4,16,128]{2,1,0:T(8,128)S(1)}, f32[4,16,128]{2,1,0:T(8,128)S(1)}, u32[]{:S(2)}, u32[]{:S(2)}) collective-permute-start(f32[4,16,128]{2,1,0:T(8,128)S(1)} %group_total_again.1.refs_11_), channel_id=1, source_target_pairs={{0,4},{1,5},{2,6},{3,7},{4,0},{5,1},{6,2},{7,3},{8,12},{9,13},{10,... | collective-permute-start | bytes 98312 | tf_op jit(solution)/shard_map/ppermute | solution.py:586
  66.1 6.2 %collective-permute-start.27 = (f32[4,16,128]{2,1,0:T(8,128)S(1)}, f32[4,16,128]{2,1,0:T(8,128)S(1)}, u32[]{:S(2)}, u32[]{:S(2)}) collective-permute-start(f32[4,16,128]{2,1,0:T(8,128)S(1)} %group_total_again.1.refs_11_), channel_id=1, source_target_pairs={{0,8},{1,9},{2,10},{3,11},{4,12},{5,13},{6,14},{7,15},{8,0},{9,1},... | collective-permute-start | bytes 98312 | tf_op jit(solution)/shard_map/ppermute | solution.py:586
  70.0 5.1 %collective-permute-start.28 = (f32[4,16,128]{2,1,0:T(8,128)S(1)}, f32[4,16,128]{2,1,0:T(8,128)S(1)}, u32[]{:S(2)}, u32[]{:S(2)}) collective-permute-start(f32[4,16,128]{2,1,0:T(8,128)S(1)} %group_total_again.1.refs_11_), channel_id=1, source_target_pairs={{0,12},{1,13},{2,14},{3,15},{4,8},{5,9},{6,10},{7,11},{8,4},{9,5},... | collective-permute-start | bytes 98312 | tf_op jit(solution)/shard_map/ppermute | solution.py:586
  77.1 6.5 %collective-permute-start.31 = (f32[24,128]{1,0:T(8,128)S(1)}, f32[24,128]{1,0:T(8,128)S(1)}, u32[]{:S(2)}, u32[]{:S(2)}) collective-permute-start(f32[24,128]{1,0:T(8,128)S(1)} %select_add_fusion.sent_b), channel_id=1, source_target_pairs={{0,112},{16,32},{32,16},{48,64},{64,48},{80,96},{96,80},{112,0},{1... | collective-permute-start | bytes 36872 | tf_op jit(solution)/shard_map/ppermute | solution.py:596
  78.5 5.1 %collective-permute-start.30 = (f32[8,128]{1,0:T(8,128)S(1)}, f32[8,128]{1,0:T(8,128)S(1)}, u32[]{:S(2)}, u32[]{:S(2)}) collective-permute-start(f32[8,128]{1,0:T(8,128)S(1)} %slice_add_fusion), channel_id=1, source_target_pairs={{0,64},{16,80},{32,96},{48,112},{64,0},{80,16},{96,32},{112,48},{1... | collective-permute-start | bytes 12296 | tf_op jit(solution)/shard_map/ppermute | solution.py:597
  79.4 4.2 %collective-permute-start.32 = (f32[8,128]{1,0:T(8,128)S(1)}, f32[8,128]{1,0:T(8,128)S(1)}, u32[]{:S(2)}, u32[]{:S(2)}) collective-permute-start(f32[8,128]{1,0:T(8,128)S(1)} %slice_add_fusion), channel_id=1, source_target_pairs={{0,96},{16,48},{32,0},{48,80},{64,32},{80,112},{96,64},{112,16},{1... | collective-permute-start | bytes 12296 | tf_op jit(solution)/shard_map/ppermute | solution.py:595
  85.2 4.8 %collective-permute-start.34 = (f32[1,128]{1,0:T(1,128)S(1)}, f32[1,128]{1,0:T(1,128)S(1)}, u32[]{:S(2)}, u32[]{:S(2)}) collective-permute-start(f32[1,128]{1,0:T(1,128)S(1)} %add.55), channel_id=1, source_target_pairs={{0,32},{16,48},{32,64},{48,80},{64,96},{80,112},{96,0},{112,16},{1... | collective-permute-start | bytes 1544 | tf_op jit(solution)/shard_map/ppermute | solution.py:603
  85.8 5.4 %collective-permute-start.35 = (f32[1,128]{1,0:T(1,128)S(1)}, f32[1,128]{1,0:T(1,128)S(1)}, u32[]{:S(2)}, u32[]{:S(2)}) collective-permute-start(f32[1,128]{1,0:T(1,128)S(1)} %add.55), channel_id=1, source_target_pairs={{0,64},{16,80},{32,96},{48,112},{64,0},{80,16},{96,32},{112,48},{1... | collective-permute-start | bytes 1544 | tf_op jit(solution)/shard_map/ppermute | solution.py:603
  (10 other events, 24.8 us)

commit v9 on v8

--- a/solution.py
+++ b/solution.py
@@ -14,7 +14,7 @@
 PLANE = (CX, NZ)
 N_GX, N_GY = 8, 16
 W_ALL = 128
-PARTNERS = (0, 1, 2, 3)
+PARTNERS = (0, 3, 2, 1)
 PREPARE_VMEM = 54400
 EDGES_VMEM = 55296
 SLOTS_ALL = 256

time: 104 us -> 99.5 us (0.957)
  starting transfers between devices: 55.6 us -> 49.7 us
  blocking collectives: 10.1 us -> 12.2 us
  waiting for transfers between devices: 28.5 us -> 27.4 us
    ppermute x24, starting transfers between devices: 39 us -> 33.8 us  [swapped(): lax.ppermute(block, 'gy', [(i, i ^ k * stride) for i in range(N_GY)])]
    ppermute x24, waiting for transfers between devices: 15.5 us -> 13.3 us  [swapped(): lax.ppermute(block, 'gy', [(i, i ^ k * stride) for i in range(N_GY)])]
    all_to_all x1, blocking collectives: 10.1 us -> 12.2 us  [sum_everywhere(): return lax.all_to_all(x, 'gy', split_axis=0, concat_axis=0, tiled=True)]
    ppermute x3, starting transfers between devices: 4.65 us -> 3.44 us  [sum_everywhere(): lax.ppermute(x, 'gx', [(i, (i + 2 * k) % N_GX) for i in range(N_GX)])]
  transfers between devices with their start and end apart: 37 -> 37, of which waited for: 17 -> 18; matrix products, arithmetic and copies ran while one was open for 1% -> 1% of each run, Pallas kernels for 2% -> 2%
where the time goes in v9:
time: 99.5 us; the launch traced here: 99.2 us
  starting transfers between devices  49.7 us (50%)
  waiting for transfers between devices  27.4 us (28%)
  blocking collectives  12.2 us (12%)
  Pallas kernels  7.69 us (8%)
  local copies, waits for them, and re-layouts  1.03 us (1%)
    ppermute x24, starting transfers between devices, swapped(): lax.ppermute(block, 'gy', [(i, i ^ k * stride) for i in range(N_GY)])  33.8 us
    ppermute x24, waiting for transfers between devices, swapped(): lax.ppermute(block, 'gy', [(i, i ^ k * stride) for i in range(N_GY)])  13.3 us
    all_to_all x1, blocking collectives, sum_everywhere(): return lax.all_to_all(x, 'gy', split_axis=0, concat_axis=0, tiled=True)  12.2 us
    pallas_call x13, Pallas kernels, call(): pl.pallas_call(kernel, name=name, out_shape=tuple(outs), in_specs=specs o...  7.69 us
    ppermute x2, starting transfers between devices, exchange_rows(): lax.ppermute(sent_b, 'gx', [(i, (i + 1 if i % 2 else i - 1) % N_GX) for i...  6.52 us
    ppermute x2, waiting for transfers between devices, exchange_rows(): got_c = lax.ppermute(tail, 'gx', [(i, i ^ 4) for i in range(N_GX)])  5.74 us
    ppermute x3, waiting for transfers between devices, sum_everywhere(): lax.ppermute(x, 'gx', [(i, (i + 2 * k) % N_GX) for i in range(N_GX)])  4.1 us
    ppermute x3, starting transfers between devices, sum_everywhere(): lax.ppermute(x, 'gx', [(i, (i + 2 * k) % N_GX) for i in range(N_GX)])  3.44 us
  transfers between devices with their start and end apart: 37, of which 18 were waited for; matrix products, arithmetic and copies ran while one was open for 1% of the time, Pallas kernels for 2%

profile of v9, /device:TPU:0, one launch (start us, length us, event | category | flops | bytes accessed | tf_op | source)
XLA Modules:
  0.0 99.2 jit_solution(4764501231468555882)
XLA Ops:
  0.6 1.6 %edges.1 = (f32[2,8,128]{2,1,0:T(8,128)}, f32[40,128]{1,0:T(8,128)}) custom-call(f32[2,128,128]{2,1,0:T(8,128)} %bitcast.18, f32[2,128,128]{2,1,0:T(8,128)} %bitcast.20, s32[1,128]{1,0:T(1,128)} %brk_h.1), custom_call_target="tpu_custom_call" | custom-call | tf_op jit(solution)/shard_map/edges/pallas_call | solution.py:574
  2.2 4.2 %collective-permute-start = (f32[40,128]{1,0:T(8,128)}, f32[40,128]{1,0:T(8,128)S(1)}, u32[]{:S(2)}, u32[]{:S(2)}) collective-permute-start(f32[40,128]{1,0:T(8,128)} %get-tuple-element.53.refs_0_), channel_id=1, source_target_pairs={{0,3},{1,2},{2,1},{3,0},{4,7},{5,6},{6,5},{7,4},{8,11},{9,10},{10,... | collective-permute-start | bytes 61448 | tf_op jit(solution)/shard_map/ppermute | solution.py:586
  7.3 1.3 %collective-permute-start.3 = (f32[2,8,128]{2,1,0:T(8,128)}, f32[2,8,128]{2,1,0:T(8,128)S(1)}, u32[]{:S(2)}, u32[]{:S(2)}) collective-permute-start(f32[2,8,128]{2,1,0:T(8,128)} %get-tuple-element.51), channel_id=1, source_target_pairs={{0,16},{16,32},{32,48},{48,64},{64,80},{80,96},{96,112},{1,17},{17... | collective-permute-start | bytes 24584 | tf_op jit(solution)/shard_map/ppermute | solution.py:630
  9.7 2.2 %collective-permute-done.1.refs_2_ = f32[40,128]{1,0:T(8,128)S(1)} collective-permute-done((f32[40,128]{1,0:T(8,128)}, f32[40,128]{1,0:T(8,128)S(1)}, u32[]{:S(2)}, u32[]{:S(2)}) %collective-permute-start.1) | collective-permute-done | bytes 20512 | tf_op jit(solution)/shard_map/ppermute | solution.py:586
  12.0 3.1 %collective-permute-start.4 = (f32[40,128]{1,0:T(8,128)S(1)}, f32[40,128]{1,0:T(8,128)S(1)}, u32[]{:S(2)}, u32[]{:S(2)}) collective-permute-start(f32[40,128]{1,0:T(8,128)S(1)} %select_select_fusion.refs_4_), channel_id=1, source_target_pairs={{0,12},{1,13},{2,14},{3,15},{4,8},{5,9},{6,10},{7,11},{8,4},{9,5},... | collective-permute-start | bytes 61448 | tf_op jit(solution)/shard_map/ppermute | solution.py:586
  16.2 1.4 %prepare.1 = (f32[2,8,16,128]{3,2,1,0:T(8,128)S(1)}, f32[2,8,16,128]{3,2,1,0:T(8,128)S(1)}, f32[2,8,16,128]{3,2,1,0:T(8,128)S(1)}, f32[2,8,16,128]{3,2,1,0:T(8,1...) custom-call(f32[2,128,128]{2,1,0:T(8,128)} %bitcast.23, f32[4,128,128]{2,1,0:T(8,128)} %bitcast.22, ...), custom_call_target="tpu_custom_call" | custom-call | tf_op jit(solution)/shard_map/prepare/pallas_call | solution.py:574
  17.6 2.8 %collective-permute-done.5.refs_6_ = f32[40,128]{1,0:T(8,128)S(1)} collective-permute-done((f32[40,128]{1,0:T(8,128)S(1)}, f32[40,128]{1,0:T(8,128)S(1)}, u32[]{:S(2)}, u32[]{:S(2)}) %collective-permute-start.5) | collective-permute-done | bytes 20512 | tf_op jit(solution)/shard_map/ppermute | solution.py:586
  21.8 1.2 %collective-permute-start.14 = (f32[20,8,128]{2,1,0:T(8,128)S(1)}, f32[20,8,128]{2,1,0:T(8,128)S(1)}, u32[]{:S(2)}, u32[]{:S(2)}) collective-permute-start(f32[20,8,128]{2,1,0:T(8,128)S(1)} %get-tuple-element.58.own.refs_4_.refs_1_), channel_id=1, source_target_pairs={{0,2},{1,3},{2,0},{3,1},{4,6},{5,7},{6,4},{7,5},{8,10},{9,11},{10,... | collective-permute-start | bytes 245768 | tf_op jit(solution)/shard_map/ppermute | solution.py:586
  23.0 1.9 %collective-permute-start.15 = (f32[20,8,128]{2,1,0:T(8,128)S(1)}, f32[20,8,128]{2,1,0:T(8,128)S(1)}, u32[]{:S(2)}, u32[]{:S(2)}) collective-permute-start(f32[20,8,128]{2,1,0:T(8,128)S(1)} %get-tuple-element.58.own.refs_4_.refs_1_), channel_id=1, source_target_pairs={{0,1},{1,0},{2,3},{3,2},{4,5},{5,4},{6,7},{7,6},{8,9},{9,8},{10,11... | collective-permute-start | bytes 245768 | tf_op jit(solution)/shard_map/ppermute | solution.py:586
  26.2 1.2 %collective-permute-start.8 = (f32[20,8,128]{2,1,0:T(8,128)S(1)}, f32[20,8,128]{2,1,0:T(8,128)S(1)}, u32[]{:S(2)}, u32[]{:S(2)}) collective-permute-start(f32[20,8,128]{2,1,0:T(8,128)S(1)} %get-tuple-element.57.own.refs_0_), channel_id=1, source_target_pairs={{0,2},{1,3},{2,0},{3,1},{4,6},{5,7},{6,4},{7,5},{8,10},{9,11},{10,... | collective-permute-start | bytes 245768 | tf_op jit(solution)/shard_map/ppermute | solution.py:586
  27.4 1.9 %collective-permute-start.9 = (f32[20,8,128]{2,1,0:T(8,128)S(1)}, f32[20,8,128]{2,1,0:T(8,128)S(1)}, u32[]{:S(2)}, u32[]{:S(2)}) collective-permute-start(f32[20,8,128]{2,1,0:T(8,128)S(1)} %get-tuple-element.57.own.refs_0_), channel_id=1, source_target_pairs={{0,1},{1,0},{2,3},{3,2},{4,5},{5,4},{6,7},{7,6},{8,9},{9,8},{10,11... | collective-permute-start | bytes 245768 | tf_op jit(solution)/shard_map/ppermute | solution.py:586
  29.4 1.4 %collective-permute-start.16 = (f32[20,8,128]{2,1,0:T(8,128)S(1)}, f32[20,8,128]{2,1,0:T(8,128)S(1)}, u32[]{:S(2)}, u32[]{:S(2)}) collective-permute-start(f32[20,8,128]{2,1,0:T(8,128)S(1)} %group_total.3.refs_6_), channel_id=1, source_target_pairs={{0,12},{1,13},{2,14},{3,15},{4,8},{5,9},{6,10},{7,11},{8,4},{9,5},... | collective-permute-start | bytes 245768 | tf_op jit(solution)/shard_map/ppermute | solution.py:586
  32.2 1.4 %collective-permute-start.18 = (f32[20,8,128]{2,1,0:T(8,128)S(1)}, f32[20,8,128]{2,1,0:T(8,128)S(1)}, u32[]{:S(2)}, u32[]{:S(2)}) collective-permute-start(f32[20,8,128]{2,1,0:T(8,128)S(1)} %group_total.3.refs_6_), channel_id=1, source_target_pairs={{0,4},{1,5},{2,6},{3,7},{4,0},{5,1},{6,2},{7,3},{8,12},{9,13},{10,... | collective-permute-start | bytes 245768 | tf_op jit(solution)/shard_map/ppermute | solution.py:586
  33.8 1.4 %collective-permute-start.10 = (f32[20,8,128]{2,1,0:T(8,128)S(1)}, f32[20,8,128]{2,1,0:T(8,128)S(1)}, u32[]{:S(2)}, u32[]{:S(2)}) collective-permute-start(f32[20,8,128]{2,1,0:T(8,128)S(1)} %group_total.2.refs_2_), channel_id=1, source_target_pairs={{0,12},{1,13},{2,14},{3,15},{4,8},{5,9},{6,10},{7,11},{8,4},{9,5},... | collective-permute-start | bytes 245768 | tf_op jit(solution)/shard_map/ppermute | solution.py:586
  35.1 1.4 %collective-permute-start.11 = (f32[20,8,128]{2,1,0:T(8,128)S(1)}, f32[20,8,128]{2,1,0:T(8,128)S(1)}, u32[]{:S(2)}, u32[]{:S(2)}) collective-permute-start(f32[20,8,128]{2,1,0:T(8,128)S(1)} %group_total.2.refs_2_), channel_id=1, source_target_pairs={{0,8},{1,9},{2,10},{3,11},{4,12},{5,13},{6,14},{7,15},{8,0},{9,1},... | collective-permute-start | bytes 245768 | tf_op jit(solution)/shard_map/ppermute | solution.py:586
  36.5 1.4 %collective-permute-start.12 = (f32[20,8,128]{2,1,0:T(8,128)S(1)}, f32[20,8,128]{2,1,0:T(8,128)S(1)}, u32[]{:S(2)}, u32[]{:S(2)}) collective-permute-start(f32[20,8,128]{2,1,0:T(8,128)S(1)} %group_total.2.refs_2_), channel_id=1, source_target_pairs={{0,4},{1,5},{2,6},{3,7},{4,0},{5,1},{6,2},{7,3},{8,12},{9,13},{10,... | collective-permute-start | bytes 245768 | tf_op jit(solution)/shard_map/ppermute | solution.py:586
  39.5 1.6 %collective-permute-done.11.refs_4_ = f32[20,8,128]{2,1,0:T(8,128)S(1)} collective-permute-done((f32[20,8,128]{2,1,0:T(8,128)S(1)}, f32[20,8,128]{2,1,0:T(8,128)S(1)}, u32[]{:S(2)}, u32[]{:S(2)}) %collective-permute-start.11) | collective-permute-done | bytes 81952 | tf_op jit(solution)/shard_map/ppermute | solution.py:586
  43.2 4.7 %collective-permute-start.21 = (f32[24,128]{1,0:T(8,128)S(1)}, f32[24,128]{1,0:T(8,128)S(1)}, u32[]{:S(2)}, u32[]{:S(2)}) collective-permute-start(f32[24,128]{1,0:T(8,128)S(1)} %select_add_fusion.1.sent_b), channel_id=1, source_target_pairs={{0,112},{16,32},{32,16},{48,64},{64,48},{80,96},{96,80},{112,0},{1... | collective-permute-start | bytes 36872 | tf_op jit(solution)/shard_map/ppermute | solution.py:596
  49.5 3.4 %collective-permute-done.20.got_c = f32[8,128]{1,0:T(8,128)S(1)} collective-permute-done((f32[8,128]{1,0:T(8,128)S(1)}, f32[8,128]{1,0:T(8,128)S(1)}, u32[]{:S(2)}, u32[]{:S(2)}) %collective-permute-start.20) | collective-permute-done | bytes 4128 | tf_op jit(solution)/shard_map/ppermute | solution.py:597
  53.4 1.7 %collective-permute-start.23 = (f32[4,16,128]{2,1,0:T(8,128)S(1)}, f32[4,16,128]{2,1,0:T(8,128)S(1)}, u32[]{:S(2)}, u32[]{:S(2)}) collective-permute-start(f32[4,16,128]{2,1,0:T(8,128)S(1)} %get-tuple-element.75.refs_8_.refs_10_), channel_id=1, source_target_pairs={{0,3},{1,2},{2,1},{3,0},{4,7},{5,6},{6,5},{7,4},{8,11},{9,10},{10,... | collective-permute-start | bytes 98312 | tf_op jit(solution)/shard_map/ppermute | solution.py:586
  55.8 1.8 %collective-permute-start.25 = (f32[4,16,128]{2,1,0:T(8,128)S(1)}, f32[4,16,128]{2,1,0:T(8,128)S(1)}, u32[]{:S(2)}, u32[]{:S(2)}) collective-permute-start(f32[4,16,128]{2,1,0:T(8,128)S(1)} %get-tuple-element.75.refs_8_.refs_10_), channel_id=1, source_target_pairs={{0,1},{1,0},{2,3},{3,2},{4,5},{5,4},{6,7},{7,6},{8,9},{9,8},{10,11... | collective-permute-start | bytes 98312 | tf_op jit(solution)/shard_map/ppermute | solution.py:586
  58.6 2.0 %collective-permute-done.24.refs_10_ = f32[4,16,128]{2,1,0:T(8,128)S(1)} collective-permute-done((f32[4,16,128]{2,1,0:T(8,128)S(1)}, f32[4,16,128]{2,1,0:T(8,128)S(1)}, u32[]{:S(2)}, u32[]{:S(2)}) %collective-permute-start.24) | collective-permute-done | bytes 32800 | tf_op jit(solution)/shard_map/ppermute | solution.py:586
  60.8 1.9 %collective-permute-start.26 = (f32[4,16,128]{2,1,0:T(8,128)S(1)}, f32[4,16,128]{2,1,0:T(8,128)S(1)}, u32[]{:S(2)}, u32[]{:S(2)}) collective-permute-start(f32[4,16,128]{2,1,0:T(8,128)S(1)} %group_total_again.1.refs_11_), channel_id=1, source_target_pairs={{0,12},{1,13},{2,14},{3,15},{4,8},{5,9},{6,10},{7,11},{8,4},{9,5},... | collective-permute-start | bytes 98312 | tf_op jit(solution)/shard_map/ppermute | solution.py:586
  62.7 1.4 %collective-permute-start.27 = (f32[4,16,128]{2,1,0:T(8,128)S(1)}, f32[4,16,128]{2,1,0:T(8,128)S(1)}, u32[]{:S(2)}, u32[]{:S(2)}) collective-permute-start(f32[4,16,128]{2,1,0:T(8,128)S(1)} %group_total_again.1.refs_11_), channel_id=1, source_target_pairs={{0,8},{1,9},{2,10},{3,11},{4,12},{5,13},{6,14},{7,15},{8,0},{9,1},... | collective-permute-start | bytes 98312 | tf_op jit(solution)/shard_map/ppermute | solution.py:586
  66.0 2.1 %collective-permute-done.27.refs_13_ = f32[4,16,128]{2,1,0:T(8,128)S(1)} collective-permute-done((f32[4,16,128]{2,1,0:T(8,128)S(1)}, f32[4,16,128]{2,1,0:T(8,128)S(1)}, u32[]{:S(2)}, u32[]{:S(2)}) %collective-permute-start.27) | collective-permute-done | bytes 32800 | tf_op jit(solution)/shard_map/ppermute | solution.py:586
  68.8 1.2 %collective-permute-done.29.got_a = f32[24,128]{1,0:T(8,128)S(1)} collective-permute-done((f32[24,128]{1,0:T(8,128)S(1)}, f32[24,128]{1,0:T(8,128)S(1)}, u32[]{:S(2)}, u32[]{:S(2)}) %collective-permute-start.29) | collective-permute-done | bytes 12320 | tf_op jit(solution)/shard_map/ppermute | solution.py:591
  70.0 1.9 %collective-permute-start.31 = (f32[24,128]{1,0:T(8,128)S(1)}, f32[24,128]{1,0:T(8,128)S(1)}, u32[]{:S(2)}, u32[]{:S(2)}) collective-permute-start(f32[24,128]{1,0:T(8,128)S(1)} %select_add_fusion.sent_b), channel_id=1, source_target_pairs={{0,112},{16,32},{32,16},{48,64},{64,48},{80,96},{96,80},{112,0},{1... | collective-permute-start | bytes 36872 | tf_op jit(solution)/shard_map/ppermute | solution.py:596
  72.7 2.0 %collective-permute-start.32 = (f32[8,128]{1,0:T(8,128)S(1)}, f32[8,128]{1,0:T(8,128)S(1)}, u32[]{:S(2)}, u32[]{:S(2)}) collective-permute-start(f32[8,128]{1,0:T(8,128)S(1)} %slice_add_fusion), channel_id=1, source_target_pairs={{0,96},{16,48},{32,0},{48,80},{64,32},{80,112},{96,64},{112,16},{1... | collective-permute-start | bytes 12296 | tf_op jit(solution)/shard_map/ppermute | solution.py:595
  74.7 2.3 %collective-permute-done.30.got_c = f32[8,128]{1,0:T(8,128)S(1)} collective-permute-done((f32[8,128]{1,0:T(8,128)S(1)}, f32[8,128]{1,0:T(8,128)S(1)}, u32[]{:S(2)}, u32[]{:S(2)}) %collective-permute-start.30) | collective-permute-done | bytes 4128 | tf_op jit(solution)/shard_map/ppermute | solution.py:597
  78.7 2.5 %collective-permute-start.34 = (f32[1,128]{1,0:T(1,128)S(1)}, f32[1,128]{1,0:T(1,128)S(1)}, u32[]{:S(2)}, u32[]{:S(2)}) collective-permute-start(f32[1,128]{1,0:T(1,128)S(1)} %add.55), channel_id=1, source_target_pairs={{0,96},{16,112},{32,0},{48,16},{64,32},{80,48},{96,64},{112,80},{1... | collective-permute-start | bytes 1544 | tf_op jit(solution)/shard_map/ppermute | solution.py:603
  82.5 3.7 %collective-permute-done.35 = f32[1,128]{1,0:T(1,128)S(1)} collective-permute-done((f32[1,128]{1,0:T(1,128)S(1)}, f32[1,128]{1,0:T(1,128)S(1)}, u32[]{:S(2)}, u32[]{:S(2)}) %collective-permute-start.35) | collective-permute-done | bytes 544 | tf_op jit(solution)/shard_map/ppermute | solution.py:603
  86.2 12.2 %all_to_all.8 = f32[16,1,128]{2,1,0:T(1,128)S(1)} all-to-all(f32[16,1,128]{2,1,0:T(1,128)S(1)} %broadcast_in_dim.39), channel_id=1, replica_groups=mesh['gx'=8,'gy'=16] {'gy'}, dimensions={0} | all-to-all | bytes 16384 | tf_op jit(solution)/shard_map/all_to_all | solution.py:606
  (87 shorter events, 22.2 us)
Async XLA Ops:
  2.2 7.5 %collective-permute-start = (f32[40,128]{1,0:T(8,128)}, f32[40,128]{1,0:T(8,128)S(1)}, u32[]{:S(2)}, u32[]{:S(2)}) collective-permute-start(f32[40,128]{1,0:T(8,128)} %get-tuple-element.53.refs_0_), channel_id=1, source_target_pairs={{0,3},{1,2},{2,1},{3,0},{4,7},{5,6},{6,5},{7,4},{8,11},{9,10},{10,... | collective-permute-start | bytes 61448 | tf_op jit(solution)/shard_map/ppermute | solution.py:586
  6.4 5.5 %collective-permute-start.1 = (f32[40,128]{1,0:T(8,128)}, f32[40,128]{1,0:T(8,128)S(1)}, u32[]{:S(2)}, u32[]{:S(2)}) collective-permute-start(f32[40,128]{1,0:T(8,128)} %get-tuple-element.53.refs_0_), channel_id=1, source_target_pairs={{0,2},{1,3},{2,0},{3,1},{4,6},{5,7},{6,4},{7,5},{8,10},{9,11},{10,... | collective-permute-start | bytes 61448 | tf_op jit(solution)/shard_map/ppermute | solution.py:586
  6.4 5.5 %collective-permute-start.2 = (f32[40,128]{1,0:T(8,128)}, f32[40,128]{1,0:T(8,128)S(1)}, u32[]{:S(2)}, u32[]{:S(2)}) collective-permute-start(f32[40,128]{1,0:T(8,128)} %get-tuple-element.53.refs_0_), channel_id=1, source_target_pairs={{0,1},{1,0},{2,3},{3,2},{4,5},{5,4},{6,7},{7,6},{8,9},{9,8},{10,11... | collective-permute-start | bytes 61448 | tf_op jit(solution)/shard_map/ppermute | solution.py:586
  12.0 5.6 %collective-permute-start.4 = (f32[40,128]{1,0:T(8,128)S(1)}, f32[40,128]{1,0:T(8,128)S(1)}, u32[]{:S(2)}, u32[]{:S(2)}) collective-permute-start(f32[40,128]{1,0:T(8,128)S(1)} %select_select_fusion.refs_4_), channel_id=1, source_target_pairs={{0,12},{1,13},{2,14},{3,15},{4,8},{5,9},{6,10},{7,11},{8,4},{9,5},... | collective-permute-start | bytes 61448 | tf_op jit(solution)/shard_map/ppermute | solution.py:586
  15.1 5.3 %collective-permute-start.5 = (f32[40,128]{1,0:T(8,128)S(1)}, f32[40,128]{1,0:T(8,128)S(1)}, u32[]{:S(2)}, u32[]{:S(2)}) collective-permute-start(f32[40,128]{1,0:T(8,128)S(1)} %select_select_fusion.refs_4_), channel_id=1, source_target_pairs={{0,8},{1,9},{2,10},{3,11},{4,12},{5,13},{6,14},{7,15},{8,0},{9,1},... | collective-permute-start | bytes 61448 | tf_op jit(solution)/shard_map/ppermute | solution.py:586
  15.7 4.7 %collective-permute-start.6 = (f32[40,128]{1,0:T(8,128)S(1)}, f32[40,128]{1,0:T(8,128)S(1)}, u32[]{:S(2)}, u32[]{:S(2)}) collective-permute-start(f32[40,128]{1,0:T(8,128)S(1)} %select_select_fusion.refs_4_), channel_id=1, source_target_pairs={{0,4},{1,5},{2,6},{3,7},{4,0},{5,1},{6,2},{7,3},{8,12},{9,13},{10,... | collective-permute-start | bytes 61448 | tf_op jit(solution)/shard_map/ppermute | solution.py:586
  20.8 6.6 %collective-permute-start.13 = (f32[20,8,128]{2,1,0:T(8,128)S(1)}, f32[20,8,128]{2,1,0:T(8,128)S(1)}, u32[]{:S(2)}, u32[]{:S(2)}) collective-permute-start(f32[20,8,128]{2,1,0:T(8,128)S(1)} %get-tuple-element.58.own.refs_4_.refs_1_), channel_id=1, source_target_pairs={{0,3},{1,2},{2,1},{3,0},{4,7},{5,6},{6,5},{7,4},{8,11},{9,10},{10,... | collective-permute-start | bytes 245768 | tf_op jit(solution)/shard_map/ppermute | solution.py:586
  21.8 7.5 %collective-permute-start.14 = (f32[20,8,128]{2,1,0:T(8,128)S(1)}, f32[20,8,128]{2,1,0:T(8,128)S(1)}, u32[]{:S(2)}, u32[]{:S(2)}) collective-permute-start(f32[20,8,128]{2,1,0:T(8,128)S(1)} %get-tuple-element.58.own.refs_4_.refs_1_), channel_id=1, source_target_pairs={{0,2},{1,3},{2,0},{3,1},{4,6},{5,7},{6,4},{7,5},{8,10},{9,11},{10,... | collective-permute-start | bytes 245768 | tf_op jit(solution)/shard_map/ppermute | solution.py:586
  23.0 6.3 %collective-permute-start.15 = (f32[20,8,128]{2,1,0:T(8,128)S(1)}, f32[20,8,128]{2,1,0:T(8,128)S(1)}, u32[]{:S(2)}, u32[]{:S(2)}) collective-permute-start(f32[20,8,128]{2,1,0:T(8,128)S(1)} %get-tuple-element.58.own.refs_4_.refs_1_), channel_id=1, source_target_pairs={{0,1},{1,0},{2,3},{3,2},{4,5},{5,4},{6,7},{7,6},{8,9},{9,8},{10,11... | collective-permute-start | bytes 245768 | tf_op jit(solution)/shard_map/ppermute | solution.py:586
  25.2 7.0 %collective-permute-start.7 = (f32[20,8,128]{2,1,0:T(8,128)S(1)}, f32[20,8,128]{2,1,0:T(8,128)S(1)}, u32[]{:S(2)}, u32[]{:S(2)}) collective-permute-start(f32[20,8,128]{2,1,0:T(8,128)S(1)} %get-tuple-element.57.own.refs_0_), channel_id=1, source_target_pairs={{0,3},{1,2},{2,1},{3,0},{4,7},{5,6},{6,5},{7,4},{8,11},{9,10},{10,... | collective-permute-start | bytes 245768 | tf_op jit(solution)/shard_map/ppermute | solution.py:586
  26.2 7.5 %collective-permute-start.8 = (f32[20,8,128]{2,1,0:T(8,128)S(1)}, f32[20,8,128]{2,1,0:T(8,128)S(1)}, u32[]{:S(2)}, u32[]{:S(2)}) collective-permute-start(f32[20,8,128]{2,1,0:T(8,128)S(1)} %get-tuple-element.57.own.refs_0_), channel_id=1, source_target_pairs={{0,2},{1,3},{2,0},{3,1},{4,6},{5,7},{6,4},{7,5},{8,10},{9,11},{10,... | collective-permute-start | bytes 245768 | tf_op jit(solution)/shard_map/ppermute | solution.py:586
  27.4 6.2 %collective-permute-start.9 = (f32[20,8,128]{2,1,0:T(8,128)S(1)}, f32[20,8,128]{2,1,0:T(8,128)S(1)}, u32[]{:S(2)}, u32[]{:S(2)}) collective-permute-start(f32[20,8,128]{2,1,0:T(8,128)S(1)} %get-tuple-element.57.own.refs_0_), channel_id=1, source_target_pairs={{0,1},{1,0},{2,3},{3,2},{4,5},{5,4},{6,7},{7,6},{8,9},{9,8},{10,11... | collective-permute-start | bytes 245768 | tf_op jit(solution)/shard_map/ppermute | solution.py:586
  29.4 7.1 %collective-permute-start.16 = (f32[20,8,128]{2,1,0:T(8,128)S(1)}, f32[20,8,128]{2,1,0:T(8,128)S(1)}, u32[]{:S(2)}, u32[]{:S(2)}) collective-permute-start(f32[20,8,128]{2,1,0:T(8,128)S(1)} %group_total.3.refs_6_), channel_id=1, source_target_pairs={{0,12},{1,13},{2,14},{3,15},{4,8},{5,9},{6,10},{7,11},{8,4},{9,5},... | collective-permute-start | bytes 245768 | tf_op jit(solution)/shard_map/ppermute | solution.py:586
  30.8 8.4 %collective-permute-start.17 = (f32[20,8,128]{2,1,0:T(8,128)S(1)}, f32[20,8,128]{2,1,0:T(8,128)S(1)}, u32[]{:S(2)}, u32[]{:S(2)}) collective-permute-start(f32[20,8,128]{2,1,0:T(8,128)S(1)} %group_total.3.refs_6_), channel_id=1, source_target_pairs={{0,8},{1,9},{2,10},{3,11},{4,12},{5,13},{6,14},{7,15},{8,0},{9,1},... | collective-permute-start | bytes 245768 | tf_op jit(solution)/shard_map/ppermute | solution.py:586
  32.2 7.1 %collective-permute-start.18 = (f32[20,8,128]{2,1,0:T(8,128)S(1)}, f32[20,8,128]{2,1,0:T(8,128)S(1)}, u32[]{:S(2)}, u32[]{:S(2)}) collective-permute-start(f32[20,8,128]{2,1,0:T(8,128)S(1)} %group_total.3.refs_6_), channel_id=1, source_target_pairs={{0,4},{1,5},{2,6},{3,7},{4,0},{5,1},{6,2},{7,3},{8,12},{9,13},{10,... | collective-permute-start | bytes 245768 | tf_op jit(solution)/shard_map/ppermute | solution.py:586
  33.8 5.7 %collective-permute-start.10 = (f32[20,8,128]{2,1,0:T(8,128)S(1)}, f32[20,8,128]{2,1,0:T(8,128)S(1)}, u32[]{:S(2)}, u32[]{:S(2)}) collective-permute-start(f32[20,8,128]{2,1,0:T(8,128)S(1)} %group_total.2.refs_2_), channel_id=1, source_target_pairs={{0,12},{1,13},{2,14},{3,15},{4,8},{5,9},{6,10},{7,11},{8,4},{9,5},... | collective-permute-start | bytes 245768 | tf_op jit(solution)/shard_map/ppermute | solution.py:586
  35.1 5.9 %collective-permute-start.11 = (f32[20,8,128]{2,1,0:T(8,128)S(1)}, f32[20,8,128]{2,1,0:T(8,128)S(1)}, u32[]{:S(2)}, u32[]{:S(2)}) collective-permute-start(f32[20,8,128]{2,1,0:T(8,128)S(1)} %group_total.2.refs_2_), channel_id=1, source_target_pairs={{0,8},{1,9},{2,10},{3,11},{4,12},{5,13},{6,14},{7,15},{8,0},{9,1},... | collective-permute-start | bytes 245768 | tf_op jit(solution)/shard_map/ppermute | solution.py:586
  36.5 4.7 %collective-permute-start.12 = (f32[20,8,128]{2,1,0:T(8,128)S(1)}, f32[20,8,128]{2,1,0:T(8,128)S(1)}, u32[]{:S(2)}, u32[]{:S(2)}) collective-permute-start(f32[20,8,128]{2,1,0:T(8,128)S(1)} %group_total.2.refs_2_), channel_id=1, source_target_pairs={{0,4},{1,5},{2,6},{3,7},{4,0},{5,1},{6,2},{7,3},{8,12},{9,13},{10,... | collective-permute-start | bytes 245768 | tf_op jit(solution)/shard_map/ppermute | solution.py:586
  43.2 9.8 %collective-permute-start.21 = (f32[24,128]{1,0:T(8,128)S(1)}, f32[24,128]{1,0:T(8,128)S(1)}, u32[]{:S(2)}, u32[]{:S(2)}) collective-permute-start(f32[24,128]{1,0:T(8,128)S(1)} %select_add_fusion.1.sent_b), channel_id=1, source_target_pairs={{0,112},{16,32},{32,16},{48,64},{64,48},{80,96},{96,80},{112,0},{1... | collective-permute-start | bytes 36872 | tf_op jit(solution)/shard_map/ppermute | solution.py:596
  47.8 5.1 %collective-permute-start.20 = (f32[8,128]{1,0:T(8,128)S(1)}, f32[8,128]{1,0:T(8,128)S(1)}, u32[]{:S(2)}, u32[]{:S(2)}) collective-permute-start(f32[8,128]{1,0:T(8,128)S(1)} %slice_add_fusion.1), channel_id=1, source_target_pairs={{0,64},{16,80},{32,96},{48,112},{64,0},{80,16},{96,32},{112,48},{1... | collective-permute-start | bytes 12296 | tf_op jit(solution)/shard_map/ppermute | solution.py:597
  48.6 4.4 %collective-permute-start.22 = (f32[8,128]{1,0:T(8,128)S(1)}, f32[8,128]{1,0:T(8,128)S(1)}, u32[]{:S(2)}, u32[]{:S(2)}) collective-permute-start(f32[8,128]{1,0:T(8,128)S(1)} %slice_add_fusion.1), channel_id=1, source_target_pairs={{0,96},{16,48},{32,0},{48,80},{64,32},{80,112},{96,64},{112,16},{1... | collective-permute-start | bytes 12296 | tf_op jit(solution)/shard_map/ppermute | solution.py:595
  53.4 5.2 %collective-permute-start.23 = (f32[4,16,128]{2,1,0:T(8,128)S(1)}, f32[4,16,128]{2,1,0:T(8,128)S(1)}, u32[]{:S(2)}, u32[]{:S(2)}) collective-permute-start(f32[4,16,128]{2,1,0:T(8,128)S(1)} %get-tuple-element.75.refs_8_.refs_10_), channel_id=1, source_target_pairs={{0,3},{1,2},{2,1},{3,0},{4,7},{5,6},{6,5},{7,4},{8,11},{9,10},{10,... | collective-permute-start | bytes 98312 | tf_op jit(solution)/shard_map/ppermute | solution.py:586
  55.1 5.5 %collective-permute-start.24 = (f32[4,16,128]{2,1,0:T(8,128)S(1)}, f32[4,16,128]{2,1,0:T(8,128)S(1)}, u32[]{:S(2)}, u32[]{:S(2)}) collective-permute-start(f32[4,16,128]{2,1,0:T(8,128)S(1)} %get-tuple-element.75.refs_8_.refs_10_), channel_id=1, source_target_pairs={{0,2},{1,3},{2,0},{3,1},{4,6},{5,7},{6,4},{7,5},{8,10},{9,11},{10,... | collective-permute-start | bytes 98312 | tf_op jit(solution)/shard_map/ppermute | solution.py:586
  55.8 4.8 %collective-permute-start.25 = (f32[4,16,128]{2,1,0:T(8,128)S(1)}, f32[4,16,128]{2,1,0:T(8,128)S(1)}, u32[]{:S(2)}, u32[]{:S(2)}) collective-permute-start(f32[4,16,128]{2,1,0:T(8,128)S(1)} %get-tuple-element.75.refs_8_.refs_10_), channel_id=1, source_target_pairs={{0,1},{1,0},{2,3},{3,2},{4,5},{5,4},{6,7},{7,6},{8,9},{9,8},{10,11... | collective-permute-start | bytes 98312 | tf_op jit(solution)/shard_map/ppermute | solution.py:586
  60.8 5.2 %collective-permute-start.26 = (f32[4,16,128]{2,1,0:T(8,128)S(1)}, f32[4,16,128]{2,1,0:T(8,128)S(1)}, u32[]{:S(2)}, u32[]{:S(2)}) collective-permute-start(f32[4,16,128]{2,1,0:T(8,128)S(1)} %group_total_again.1.refs_11_), channel_id=1, source_target_pairs={{0,12},{1,13},{2,14},{3,15},{4,8},{5,9},{6,10},{7,11},{8,4},{9,5},... | collective-permute-start | bytes 98312 | tf_op jit(solution)/shard_map/ppermute | solution.py:586
  62.7 5.4 %collective-permute-start.27 = (f32[4,16,128]{2,1,0:T(8,128)S(1)}, f32[4,16,128]{2,1,0:T(8,128)S(1)}, u32[]{:S(2)}, u32[]{:S(2)}) collective-permute-start(f32[4,16,128]{2,1,0:T(8,128)S(1)} %group_total_again.1.refs_11_), channel_id=1, source_target_pairs={{0,8},{1,9},{2,10},{3,11},{4,12},{5,13},{6,14},{7,15},{8,0},{9,1},... | collective-permute-start | bytes 98312 | tf_op jit(solution)/shard_map/ppermute | solution.py:586
  64.1 4.0 %collective-permute-start.28 = (f32[4,16,128]{2,1,0:T(8,128)S(1)}, f32[4,16,128]{2,1,0:T(8,128)S(1)}, u32[]{:S(2)}, u32[]{:S(2)}) collective-permute-start(f32[4,16,128]{2,1,0:T(8,128)S(1)} %group_total_again.1.refs_11_), channel_id=1, source_target_pairs={{0,4},{1,5},{2,6},{3,7},{4,0},{5,1},{6,2},{7,3},{8,12},{9,13},{10,... | collective-permute-start | bytes 98312 | tf_op jit(solution)/shard_map/ppermute | solution.py:586
  70.0 7.0 %collective-permute-start.31 = (f32[24,128]{1,0:T(8,128)S(1)}, f32[24,128]{1,0:T(8,128)S(1)}, u32[]{:S(2)}, u32[]{:S(2)}) collective-permute-start(f32[24,128]{1,0:T(8,128)S(1)} %select_add_fusion.sent_b), channel_id=1, source_target_pairs={{0,112},{16,32},{32,16},{48,64},{64,48},{80,96},{96,80},{112,0},{1... | collective-permute-start | bytes 36872 | tf_op jit(solution)/shard_map/ppermute | solution.py:596
  71.9 5.1 %collective-permute-start.30 = (f32[8,128]{1,0:T(8,128)S(1)}, f32[8,128]{1,0:T(8,128)S(1)}, u32[]{:S(2)}, u32[]{:S(2)}) collective-permute-start(f32[8,128]{1,0:T(8,128)S(1)} %slice_add_fusion), channel_id=1, source_target_pairs={{0,64},{16,80},{32,96},{48,112},{64,0},{80,16},{96,32},{112,48},{1... | collective-permute-start | bytes 12296 | tf_op jit(solution)/shard_map/ppermute | solution.py:597
  72.7 4.3 %collective-permute-start.32 = (f32[8,128]{1,0:T(8,128)S(1)}, f32[8,128]{1,0:T(8,128)S(1)}, u32[]{:S(2)}, u32[]{:S(2)}) collective-permute-start(f32[8,128]{1,0:T(8,128)S(1)} %slice_add_fusion), channel_id=1, source_target_pairs={{0,96},{16,48},{32,0},{48,80},{64,32},{80,112},{96,64},{112,16},{1... | collective-permute-start | bytes 12296 | tf_op jit(solution)/shard_map/ppermute | solution.py:595
  81.2 5.0 %collective-permute-start.35 = (f32[1,128]{1,0:T(1,128)S(1)}, f32[1,128]{1,0:T(1,128)S(1)}, u32[]{:S(2)}, u32[]{:S(2)}) collective-permute-start(f32[1,128]{1,0:T(1,128)S(1)} %add.55), channel_id=1, source_target_pairs={{0,64},{16,80},{32,96},{48,112},{64,0},{80,16},{96,32},{112,48},{1... | collective-permute-start | bytes 1544 | tf_op jit(solution)/shard_map/ppermute | solution.py:603
  81.2 5.0 %collective-permute-start.36 = (f32[1,128]{1,0:T(1,128)S(1)}, f32[1,128]{1,0:T(1,128)S(1)}, u32[]{:S(2)}, u32[]{:S(2)}) collective-permute-start(f32[1,128]{1,0:T(1,128)S(1)} %add.55), channel_id=1, source_target_pairs={{0,32},{16,48},{32,64},{48,80},{64,96},{80,112},{96,0},{112,16},{1... | collective-permute-start | bytes 1544 | tf_op jit(solution)/shard_map/ppermute | solution.py:603
  (10 other events, 23.2 us)

commit v10 on v9

--- a/solution.py
+++ b/solution.py
@@ -602,8 +602,10 @@
     x = x + lax.ppermute(x, "gx", [(i, i ^ 1) for i in range(N_GX)])
     others = [lax.ppermute(x, "gx", [(i, (i + 2 * k) % N_GX) for i in range(N_GX)]) for k in PARTNERS[1:]]
     x = x + others[0] + others[1] + others[2]
-    x = jnp.broadcast_to(x, (N_GY, NZ))
-    return lax.all_to_all(x, "gy", split_axis=0, concat_axis=0, tiled=True)
+    for stride in (1, 4):
+        x, *others = swapped(x, stride)
+        x = x + others[0] + others[1] + others[2]
+    return x
 
 
 def body(right_side, accumulation, trans_x, trans_y, trans_z, perf_cell, perf_well, perf_weight, perf_count, breaks):

time: 99.5 us -> 101 us (1.015)
  blocking collectives: 12.2 us -> 0 us
  starting transfers between devices: 49.7 us -> 58 us
  waiting for transfers between devices: 27.4 us -> 32.4 us
    all_to_all x1 -> x0, blocking collectives: 12.2 us -> none  [sum_everywhere(): return lax.all_to_all(x, 'gy', split_axis=0, concat_axis=0, tiled=True)]
    ppermute x24 -> x30, starting transfers between devices: 33.8 us -> 42.2 us  [swapped(): lax.ppermute(block, 'gy', [(i, i ^ k * stride) for i in range(N_GY)])]
    ppermute x24 -> x30, waiting for transfers between devices: 13.3 us -> 18.2 us  [swapped(): lax.ppermute(block, 'gy', [(i, i ^ k * stride) for i in range(N_GY)])]
  transfers between devices with their start and end apart: 37 -> 43, of which waited for: 18 -> 22; matrix products, arithmetic and copies ran while one was open for 1% -> 1% of each run, Pallas kernels for 2% -> 2%
where the time goes in v10:
time: 101 us; the launch traced here: 100 us
  starting transfers between devices  58 us (57%)
  waiting for transfers between devices  32.4 us (32%)
  Pallas kernels  7.68 us (8%)
  local copies, waits for them, and re-layouts  1.02 us (1%)
    ppermute x30, starting transfers between devices, swapped(): lax.ppermute(block, 'gy', [(i, i ^ k * stride) for i in range(N_GY)])  42.2 us
    ppermute x30, waiting for transfers between devices, swapped(): lax.ppermute(block, 'gy', [(i, i ^ k * stride) for i in range(N_GY)])  18.2 us
    pallas_call x13, Pallas kernels, call(): pl.pallas_call(kernel, name=name, out_shape=tuple(outs), in_specs=specs o...  7.68 us
    ppermute x2, starting transfers between devices, exchange_rows(): lax.ppermute(sent_b, 'gx', [(i, (i + 1 if i % 2 else i - 1) % N_GX) for i...  6.52 us
    ppermute x2, waiting for transfers between devices, exchange_rows(): got_c = lax.ppermute(tail, 'gx', [(i, i ^ 4) for i in range(N_GX)])  5.74 us
    ppermute x3, waiting for transfers between devices, sum_everywhere(): lax.ppermute(x, 'gx', [(i, (i + 2 * k) % N_GX) for i in range(N_GX)])  4.1 us
    ppermute x3, starting transfers between devices, sum_everywhere(): lax.ppermute(x, 'gx', [(i, (i + 2 * k) % N_GX) for i in range(N_GX)])  3.44 us
    ppermute x2, starting transfers between devices, exchange_rows(): lax.ppermute(tail, 'gx', [(i, (i + 2 if i % 2 else i - 2) % N_GX) for i i...  2.92 us
  transfers between devices with their start and end apart: 43, of which 22 were waited for; matrix products, arithmetic and copies ran while one was open for 1% of the time, Pallas kernels for 2%

profile of v10, /device:TPU:0, one launch (start us, length us, event | category | flops | bytes accessed | tf_op | source)
XLA Modules:
  0.0 100.4 jit_solution(444136204416282640)
XLA Ops:
  0.6 1.6 %edges.1 = (f32[2,8,128]{2,1,0:T(8,128)}, f32[40,128]{1,0:T(8,128)}) custom-call(f32[2,128,128]{2,1,0:T(8,128)} %bitcast.14, f32[2,128,128]{2,1,0:T(8,128)} %bitcast.16, s32[1,128]{1,0:T(1,128)} %brk_h.1), custom_call_target="tpu_custom_call" | custom-call | tf_op jit(solution)/shard_map/edges/pallas_call | solution.py:574
  2.2 4.2 %collective-permute-start = (f32[40,128]{1,0:T(8,128)}, f32[40,128]{1,0:T(8,128)S(1)}, u32[]{:S(2)}, u32[]{:S(2)}) collective-permute-start(f32[40,128]{1,0:T(8,128)} %get-tuple-element.53.refs_0_), channel_id=1, source_target_pairs={{0,3},{1,2},{2,1},{3,0},{4,7},{5,6},{6,5},{7,4},{8,11},{9,10},{10,... | collective-permute-start | bytes 61448 | tf_op jit(solution)/shard_map/ppermute | solution.py:586
  9.7 2.2 %collective-permute-done.1.refs_2_ = f32[40,128]{1,0:T(8,128)S(1)} collective-permute-done((f32[40,128]{1,0:T(8,128)}, f32[40,128]{1,0:T(8,128)S(1)}, u32[]{:S(2)}, u32[]{:S(2)}) %collective-permute-start.1) | collective-permute-done | bytes 20512 | tf_op jit(solution)/shard_map/ppermute | solution.py:586
  12.0 3.1 %collective-permute-start.4 = (f32[40,128]{1,0:T(8,128)S(1)}, f32[40,128]{1,0:T(8,128)S(1)}, u32[]{:S(2)}, u32[]{:S(2)}) collective-permute-start(f32[40,128]{1,0:T(8,128)S(1)} %select_select_fusion.refs_4_), channel_id=1, source_target_pairs={{0,12},{1,13},{2,14},{3,15},{4,8},{5,9},{6,10},{7,11},{8,4},{9,5},... | collective-permute-start | bytes 61448 | tf_op jit(solution)/shard_map/ppermute | solution.py:586
  16.2 1.4 %prepare.1 = (f32[2,8,16,128]{3,2,1,0:T(8,128)S(1)}, f32[2,8,16,128]{3,2,1,0:T(8,128)S(1)}, f32[2,8,16,128]{3,2,1,0:T(8,128)S(1)}, f32[2,8,16,128]{3,2,1,0:T(8,1...) custom-call(f32[2,128,128]{2,1,0:T(8,128)} %bitcast.19, f32[4,128,128]{2,1,0:T(8,128)} %bitcast.18, ...), custom_call_target="tpu_custom_call" | custom-call | tf_op jit(solution)/shard_map/prepare/pallas_call | solution.py:574
  17.6 2.8 %collective-permute-done.5.refs_6_ = f32[40,128]{1,0:T(8,128)S(1)} collective-permute-done((f32[40,128]{1,0:T(8,128)S(1)}, f32[40,128]{1,0:T(8,128)S(1)}, u32[]{:S(2)}, u32[]{:S(2)}) %collective-permute-start.5) | collective-permute-done | bytes 20512 | tf_op jit(solution)/shard_map/ppermute | solution.py:586
  23.0 1.9 %collective-permute-start.15 = (f32[20,8,128]{2,1,0:T(8,128)S(1)}, f32[20,8,128]{2,1,0:T(8,128)S(1)}, u32[]{:S(2)}, u32[]{:S(2)}) collective-permute-start(f32[20,8,128]{2,1,0:T(8,128)S(1)} %get-tuple-element.58.own.refs_4_.refs_1_), channel_id=1, source_target_pairs={{0,1},{1,0},{2,3},{3,2},{4,5},{5,4},{6,7},{7,6},{8,9},{9,8},{10,11... | collective-permute-start | bytes 245768 | tf_op jit(solution)/shard_map/ppermute | solution.py:586
  27.4 1.9 %collective-permute-start.9 = (f32[20,8,128]{2,1,0:T(8,128)S(1)}, f32[20,8,128]{2,1,0:T(8,128)S(1)}, u32[]{:S(2)}, u32[]{:S(2)}) collective-permute-start(f32[20,8,128]{2,1,0:T(8,128)S(1)} %get-tuple-element.57.own.refs_0_), channel_id=1, source_target_pairs={{0,1},{1,0},{2,3},{3,2},{4,5},{5,4},{6,7},{7,6},{8,9},{9,8},{10,11... | collective-permute-start | bytes 245768 | tf_op jit(solution)/shard_map/ppermute | solution.py:586
  29.4 1.4 %collective-permute-start.16 = (f32[20,8,128]{2,1,0:T(8,128)S(1)}, f32[20,8,128]{2,1,0:T(8,128)S(1)}, u32[]{:S(2)}, u32[]{:S(2)}) collective-permute-start(f32[20,8,128]{2,1,0:T(8,128)S(1)} %group_total.3.refs_6_), channel_id=1, source_target_pairs={{0,12},{1,13},{2,14},{3,15},{4,8},{5,9},{6,10},{7,11},{8,4},{9,5},... | collective-permute-start | bytes 245768 | tf_op jit(solution)/shard_map/ppermute | solution.py:586
  32.2 1.4 %collective-permute-start.18 = (f32[20,8,128]{2,1,0:T(8,128)S(1)}, f32[20,8,128]{2,1,0:T(8,128)S(1)}, u32[]{:S(2)}, u32[]{:S(2)}) collective-permute-start(f32[20,8,128]{2,1,0:T(8,128)S(1)} %group_total.3.refs_6_), channel_id=1, source_target_pairs={{0,4},{1,5},{2,6},{3,7},{4,0},{5,1},{6,2},{7,3},{8,12},{9,13},{10,... | collective-permute-start | bytes 245768 | tf_op jit(solution)/shard_map/ppermute | solution.py:586
  33.8 1.4 %collective-permute-start.10 = (f32[20,8,128]{2,1,0:T(8,128)S(1)}, f32[20,8,128]{2,1,0:T(8,128)S(1)}, u32[]{:S(2)}, u32[]{:S(2)}) collective-permute-start(f32[20,8,128]{2,1,0:T(8,128)S(1)} %group_total.2.refs_2_), channel_id=1, source_target_pairs={{0,12},{1,13},{2,14},{3,15},{4,8},{5,9},{6,10},{7,11},{8,4},{9,5},... | collective-permute-start | bytes 245768 | tf_op jit(solution)/shard_map/ppermute | solution.py:586
  35.1 1.4 %collective-permute-start.11 = (f32[20,8,128]{2,1,0:T(8,128)S(1)}, f32[20,8,128]{2,1,0:T(8,128)S(1)}, u32[]{:S(2)}, u32[]{:S(2)}) collective-permute-start(f32[20,8,128]{2,1,0:T(8,128)S(1)} %group_total.2.refs_2_), channel_id=1, source_target_pairs={{0,8},{1,9},{2,10},{3,11},{4,12},{5,13},{6,14},{7,15},{8,0},{9,1},... | collective-permute-start | bytes 245768 | tf_op jit(solution)/shard_map/ppermute | solution.py:586
  36.5 1.4 %collective-permute-start.12 = (f32[20,8,128]{2,1,0:T(8,128)S(1)}, f32[20,8,128]{2,1,0:T(8,128)S(1)}, u32[]{:S(2)}, u32[]{:S(2)}) collective-permute-start(f32[20,8,128]{2,1,0:T(8,128)S(1)} %group_total.2.refs_2_), channel_id=1, source_target_pairs={{0,4},{1,5},{2,6},{3,7},{4,0},{5,1},{6,2},{7,3},{8,12},{9,13},{10,... | collective-permute-start | bytes 245768 | tf_op jit(solution)/shard_map/ppermute | solution.py:586
  39.5 1.6 %collective-permute-done.11.refs_4_ = f32[20,8,128]{2,1,0:T(8,128)S(1)} collective-permute-done((f32[20,8,128]{2,1,0:T(8,128)S(1)}, f32[20,8,128]{2,1,0:T(8,128)S(1)}, u32[]{:S(2)}, u32[]{:S(2)}) %collective-permute-start.11) | collective-permute-done | bytes 81952 | tf_op jit(solution)/shard_map/ppermute | solution.py:586
  43.2 4.7 %collective-permute-start.21 = (f32[24,128]{1,0:T(8,128)S(1)}, f32[24,128]{1,0:T(8,128)S(1)}, u32[]{:S(2)}, u32[]{:S(2)}) collective-permute-start(f32[24,128]{1,0:T(8,128)S(1)} %select_add_fusion.1.sent_b), channel_id=1, source_target_pairs={{0,112},{16,32},{32,16},{48,64},{64,48},{80,96},{96,80},{112,0},{1... | collective-permute-start | bytes 36872 | tf_op jit(solution)/shard_map/ppermute | solution.py:596
  49.5 3.4 %collective-permute-done.20.got_c = f32[8,128]{1,0:T(8,128)S(1)} collective-permute-done((f32[8,128]{1,0:T(8,128)S(1)}, f32[8,128]{1,0:T(8,128)S(1)}, u32[]{:S(2)}, u32[]{:S(2)}) %collective-permute-start.20) | collective-permute-done | bytes 4128 | tf_op jit(solution)/shard_map/ppermute | solution.py:597
  53.4 1.7 %collective-permute-start.23 = (f32[4,16,128]{2,1,0:T(8,128)S(1)}, f32[4,16,128]{2,1,0:T(8,128)S(1)}, u32[]{:S(2)}, u32[]{:S(2)}) collective-permute-start(f32[4,16,128]{2,1,0:T(8,128)S(1)} %get-tuple-element.75.refs_8_.refs_10_), channel_id=1, source_target_pairs={{0,3},{1,2},{2,1},{3,0},{4,7},{5,6},{6,5},{7,4},{8,11},{9,10},{10,... | collective-permute-start | bytes 98312 | tf_op jit(solution)/shard_map/ppermute | solution.py:586
  55.8 1.8 %collective-permute-start.25 = (f32[4,16,128]{2,1,0:T(8,128)S(1)}, f32[4,16,128]{2,1,0:T(8,128)S(1)}, u32[]{:S(2)}, u32[]{:S(2)}) collective-permute-start(f32[4,16,128]{2,1,0:T(8,128)S(1)} %get-tuple-element.75.refs_8_.refs_10_), channel_id=1, source_target_pairs={{0,1},{1,0},{2,3},{3,2},{4,5},{5,4},{6,7},{7,6},{8,9},{9,8},{10,11... | collective-permute-start | bytes 98312 | tf_op jit(solution)/shard_map/ppermute | solution.py:586
  58.6 2.0 %collective-permute-done.24.refs_10_ = f32[4,16,128]{2,1,0:T(8,128)S(1)} collective-permute-done((f32[4,16,128]{2,1,0:T(8,128)S(1)}, f32[4,16,128]{2,1,0:T(8,128)S(1)}, u32[]{:S(2)}, u32[]{:S(2)}) %collective-permute-start.24) | collective-permute-done | bytes 32800 | tf_op jit(solution)/shard_map/ppermute | solution.py:586
  60.8 1.9 %collective-permute-start.26 = (f32[4,16,128]{2,1,0:T(8,128)S(1)}, f32[4,16,128]{2,1,0:T(8,128)S(1)}, u32[]{:S(2)}, u32[]{:S(2)}) collective-permute-start(f32[4,16,128]{2,1,0:T(8,128)S(1)} %group_total_again.1.refs_11_), channel_id=1, source_target_pairs={{0,12},{1,13},{2,14},{3,15},{4,8},{5,9},{6,10},{7,11},{8,4},{9,5},... | collective-permute-start | bytes 98312 | tf_op jit(solution)/shard_map/ppermute | solution.py:586
  62.7 1.4 %collective-permute-start.27 = (f32[4,16,128]{2,1,0:T(8,128)S(1)}, f32[4,16,128]{2,1,0:T(8,128)S(1)}, u32[]{:S(2)}, u32[]{:S(2)}) collective-permute-start(f32[4,16,128]{2,1,0:T(8,128)S(1)} %group_total_again.1.refs_11_), channel_id=1, source_target_pairs={{0,8},{1,9},{2,10},{3,11},{4,12},{5,13},{6,14},{7,15},{8,0},{9,1},... | collective-permute-start | bytes 98312 | tf_op jit(solution)/shard_map/ppermute | solution.py:586
  66.0 2.1 %collective-permute-done.27.refs_13_ = f32[4,16,128]{2,1,0:T(8,128)S(1)} collective-permute-done((f32[4,16,128]{2,1,0:T(8,128)S(1)}, f32[4,16,128]{2,1,0:T(8,128)S(1)}, u32[]{:S(2)}, u32[]{:S(2)}) %collective-permute-start.27) | collective-permute-done | bytes 32800 | tf_op jit(solution)/shard_map/ppermute | solution.py:586
  70.0 1.9 %collective-permute-start.31 = (f32[24,128]{1,0:T(8,128)S(1)}, f32[24,128]{1,0:T(8,128)S(1)}, u32[]{:S(2)}, u32[]{:S(2)}) collective-permute-start(f32[24,128]{1,0:T(8,128)S(1)} %select_add_fusion.sent_b), channel_id=1, source_target_pairs={{0,112},{16,32},{32,16},{48,64},{64,48},{80,96},{96,80},{112,0},{1... | collective-permute-start | bytes 36872 | tf_op jit(solution)/shard_map/ppermute | solution.py:596
  72.7 2.0 %collective-permute-start.32 = (f32[8,128]{1,0:T(8,128)S(1)}, f32[8,128]{1,0:T(8,128)S(1)}, u32[]{:S(2)}, u32[]{:S(2)}) collective-permute-start(f32[8,128]{1,0:T(8,128)S(1)} %slice_add_fusion), channel_id=1, source_target_pairs={{0,96},{16,48},{32,0},{48,80},{64,32},{80,112},{96,64},{112,16},{1... | collective-permute-start | bytes 12296 | tf_op jit(solution)/shard_map/ppermute | solution.py:595
  74.7 2.3 %collective-permute-done.30.got_c = f32[8,128]{1,0:T(8,128)S(1)} collective-permute-done((f32[8,128]{1,0:T(8,128)S(1)}, f32[8,128]{1,0:T(8,128)S(1)}, u32[]{:S(2)}, u32[]{:S(2)}) %collective-permute-start.30) | collective-permute-done | bytes 4128 | tf_op jit(solution)/shard_map/ppermute | solution.py:597
  78.7 2.5 %collective-permute-start.34 = (f32[1,128]{1,0:T(1,128)S(1)}, f32[1,128]{1,0:T(1,128)S(1)}, u32[]{:S(2)}, u32[]{:S(2)}) collective-permute-start(f32[1,128]{1,0:T(1,128)S(1)} %add.71), channel_id=1, source_target_pairs={{0,96},{16,112},{32,0},{48,16},{64,32},{80,48},{96,64},{112,80},{1... | collective-permute-start | bytes 1544 | tf_op jit(solution)/shard_map/ppermute | solution.py:603
  82.5 3.7 %collective-permute-done.35 = f32[1,128]{1,0:T(1,128)S(1)} collective-permute-done((f32[1,128]{1,0:T(1,128)S(1)}, f32[1,128]{1,0:T(1,128)S(1)}, u32[]{:S(2)}, u32[]{:S(2)}) %collective-permute-start.35) | collective-permute-done | bytes 544 | tf_op jit(solution)/shard_map/ppermute | solution.py:603
  86.2 1.7 %collective-permute-start.37 = (f32[1,128]{1,0:T(1,128)S(1)}, f32[1,128]{1,0:T(1,128)S(1)}, u32[]{:S(2)}, u32[]{:S(2)}) collective-permute-start(f32[1,128]{1,0:T(1,128)S(1)} %add_add_fusion.2), channel_id=1, source_target_pairs={{0,3},{1,2},{2,1},{3,0},{4,7},{5,6},{6,5},{7,4},{8,11},{9,10},{10,... | collective-permute-start | bytes 1544 | tf_op jit(solution)/shard_map/ppermute | solution.py:586
  91.0 1.9 %collective-permute-done.38 = f32[1,128]{1,0:T(1,128)S(1)} collective-permute-done((f32[1,128]{1,0:T(1,128)S(1)}, f32[1,128]{1,0:T(1,128)S(1)}, u32[]{:S(2)}, u32[]{:S(2)}) %collective-permute-start.38) | collective-permute-done | bytes 544 | tf_op jit(solution)/shard_map/ppermute | solution.py:586
  93.0 1.5 %collective-permute-start.40 = (f32[1,128]{1,0:T(1,128)S(1)}, f32[1,128]{1,0:T(1,128)S(1)}, u32[]{:S(2)}, u32[]{:S(2)}) collective-permute-start(f32[1,128]{1,0:T(1,128)S(1)} %add_add_fusion.1), channel_id=1, source_target_pairs={{0,12},{1,13},{2,14},{3,15},{4,8},{5,9},{6,10},{7,11},{8,4},{9,5},... | collective-permute-start | bytes 1544 | tf_op jit(solution)/shard_map/ppermute | solution.py:586
  94.5 1.4 %collective-permute-start.41 = (f32[1,128]{1,0:T(1,128)S(1)}, f32[1,128]{1,0:T(1,128)S(1)}, u32[]{:S(2)}, u32[]{:S(2)}) collective-permute-start(f32[1,128]{1,0:T(1,128)S(1)} %add_add_fusion.1), channel_id=1, source_target_pairs={{0,8},{1,9},{2,10},{3,11},{4,12},{5,13},{6,14},{7,15},{8,0},{9,1},... | collective-permute-start | bytes 1544 | tf_op jit(solution)/shard_map/ppermute | solution.py:586
  97.8 1.7 %collective-permute-done.41 = f32[1,128]{1,0:T(1,128)S(1)} collective-permute-done((f32[1,128]{1,0:T(1,128)S(1)}, f32[1,128]{1,0:T(1,128)S(1)}, u32[]{:S(2)}, u32[]{:S(2)}) %collective-permute-start.41) | collective-permute-done | bytes 544 | tf_op jit(solution)/shard_map/ppermute | solution.py:586
  (99 shorter events, 32.2 us)
Async XLA Ops:
  2.2 7.5 %collective-permute-start = (f32[40,128]{1,0:T(8,128)}, f32[40,128]{1,0:T(8,128)S(1)}, u32[]{:S(2)}, u32[]{:S(2)}) collective-permute-start(f32[40,128]{1,0:T(8,128)} %get-tuple-element.53.refs_0_), channel_id=1, source_target_pairs={{0,3},{1,2},{2,1},{3,0},{4,7},{5,6},{6,5},{7,4},{8,11},{9,10},{10,... | collective-permute-start | bytes 61448 | tf_op jit(solution)/shard_map/ppermute | solution.py:586
  6.4 5.5 %collective-permute-start.1 = (f32[40,128]{1,0:T(8,128)}, f32[40,128]{1,0:T(8,128)S(1)}, u32[]{:S(2)}, u32[]{:S(2)}) collective-permute-start(f32[40,128]{1,0:T(8,128)} %get-tuple-element.53.refs_0_), channel_id=1, source_target_pairs={{0,2},{1,3},{2,0},{3,1},{4,6},{5,7},{6,4},{7,5},{8,10},{9,11},{10,... | collective-permute-start | bytes 61448 | tf_op jit(solution)/shard_map/ppermute | solution.py:586
  6.4 5.5 %collective-permute-start.2 = (f32[40,128]{1,0:T(8,128)}, f32[40,128]{1,0:T(8,128)S(1)}, u32[]{:S(2)}, u32[]{:S(2)}) collective-permute-start(f32[40,128]{1,0:T(8,128)} %get-tuple-element.53.refs_0_), channel_id=1, source_target_pairs={{0,1},{1,0},{2,3},{3,2},{4,5},{5,4},{6,7},{7,6},{8,9},{9,8},{10,11... | collective-permute-start | bytes 61448 | tf_op jit(solution)/shard_map/ppermute | solution.py:586
  12.0 5.6 %collective-permute-start.4 = (f32[40,128]{1,0:T(8,128)S(1)}, f32[40,128]{1,0:T(8,128)S(1)}, u32[]{:S(2)}, u32[]{:S(2)}) collective-permute-start(f32[40,128]{1,0:T(8,128)S(1)} %select_select_fusion.refs_4_), channel_id=1, source_target_pairs={{0,12},{1,13},{2,14},{3,15},{4,8},{5,9},{6,10},{7,11},{8,4},{9,5},... | collective-permute-start | bytes 61448 | tf_op jit(solution)/shard_map/ppermute | solution.py:586
  15.1 5.3 %collective-permute-start.5 = (f32[40,128]{1,0:T(8,128)S(1)}, f32[40,128]{1,0:T(8,128)S(1)}, u32[]{:S(2)}, u32[]{:S(2)}) collective-permute-start(f32[40,128]{1,0:T(8,128)S(1)} %select_select_fusion.refs_4_), channel_id=1, source_target_pairs={{0,8},{1,9},{2,10},{3,11},{4,12},{5,13},{6,14},{7,15},{8,0},{9,1},... | collective-permute-start | bytes 61448 | tf_op jit(solution)/shard_map/ppermute | solution.py:586
  20.8 6.6 %collective-permute-start.13 = (f32[20,8,128]{2,1,0:T(8,128)S(1)}, f32[20,8,128]{2,1,0:T(8,128)S(1)}, u32[]{:S(2)}, u32[]{:S(2)}) collective-permute-start(f32[20,8,128]{2,1,0:T(8,128)S(1)} %get-tuple-element.58.own.refs_4_.refs_1_), channel_id=1, source_target_pairs={{0,3},{1,2},{2,1},{3,0},{4,7},{5,6},{6,5},{7,4},{8,11},{9,10},{10,... | collective-permute-start | bytes 245768 | tf_op jit(solution)/shard_map/ppermute | solution.py:586
  21.8 7.5 %collective-permute-start.14 = (f32[20,8,128]{2,1,0:T(8,128)S(1)}, f32[20,8,128]{2,1,0:T(8,128)S(1)}, u32[]{:S(2)}, u32[]{:S(2)}) collective-permute-start(f32[20,8,128]{2,1,0:T(8,128)S(1)} %get-tuple-element.58.own.refs_4_.refs_1_), channel_id=1, source_target_pairs={{0,2},{1,3},{2,0},{3,1},{4,6},{5,7},{6,4},{7,5},{8,10},{9,11},{10,... | collective-permute-start | bytes 245768 | tf_op jit(solution)/shard_map/ppermute | solution.py:586
  23.0 6.3 %collective-permute-start.15 = (f32[20,8,128]{2,1,0:T(8,128)S(1)}, f32[20,8,128]{2,1,0:T(8,128)S(1)}, u32[]{:S(2)}, u32[]{:S(2)}) collective-permute-start(f32[20,8,128]{2,1,0:T(8,128)S(1)} %get-tuple-element.58.own.refs_4_.refs_1_), channel_id=1, source_target_pairs={{0,1},{1,0},{2,3},{3,2},{4,5},{5,4},{6,7},{7,6},{8,9},{9,8},{10,11... | collective-permute-start | bytes 245768 | tf_op jit(solution)/shard_map/ppermute | solution.py:586
  25.2 7.0 %collective-permute-start.7 = (f32[20,8,128]{2,1,0:T(8,128)S(1)}, f32[20,8,128]{2,1,0:T(8,128)S(1)}, u32[]{:S(2)}, u32[]{:S(2)}) collective-permute-start(f32[20,8,128]{2,1,0:T(8,128)S(1)} %get-tuple-element.57.own.refs_0_), channel_id=1, source_target_pairs={{0,3},{1,2},{2,1},{3,0},{4,7},{5,6},{6,5},{7,4},{8,11},{9,10},{10,... | collective-permute-start | bytes 245768 | tf_op jit(solution)/shard_map/ppermute | solution.py:586
  26.2 7.5 %collective-permute-start.8 = (f32[20,8,128]{2,1,0:T(8,128)S(1)}, f32[20,8,128]{2,1,0:T(8,128)S(1)}, u32[]{:S(2)}, u32[]{:S(2)}) collective-permute-start(f32[20,8,128]{2,1,0:T(8,128)S(1)} %get-tuple-element.57.own.refs_0_), channel_id=1, source_target_pairs={{0,2},{1,3},{2,0},{3,1},{4,6},{5,7},{6,4},{7,5},{8,10},{9,11},{10,... | collective-permute-start | bytes 245768 | tf_op jit(solution)/shard_map/ppermute | solution.py:586
  27.4 6.2 %collective-permute-start.9 = (f32[20,8,128]{2,1,0:T(8,128)S(1)}, f32[20,8,128]{2,1,0:T(8,128)S(1)}, u32[]{:S(2)}, u32[]{:S(2)}) collective-permute-start(f32[20,8,128]{2,1,0:T(8,128)S(1)} %get-tuple-element.57.own.refs_0_), channel_id=1, source_target_pairs={{0,1},{1,0},{2,3},{3,2},{4,5},{5,4},{6,7},{7,6},{8,9},{9,8},{10,11... | collective-permute-start | bytes 245768 | tf_op jit(solution)/shard_map/ppermute | solution.py:586
  29.4 7.1 %collective-permute-start.16 = (f32[20,8,128]{2,1,0:T(8,128)S(1)}, f32[20,8,128]{2,1,0:T(8,128)S(1)}, u32[]{:S(2)}, u32[]{:S(2)}) collective-permute-start(f32[20,8,128]{2,1,0:T(8,128)S(1)} %group_total.3.refs_6_), channel_id=1, source_target_pairs={{0,12},{1,13},{2,14},{3,15},{4,8},{5,9},{6,10},{7,11},{8,4},{9,5},... | collective-permute-start | bytes 245768 | tf_op jit(solution)/shard_map/ppermute | solution.py:586
  30.8 8.4 %collective-permute-start.17 = (f32[20,8,128]{2,1,0:T(8,128)S(1)}, f32[20,8,128]{2,1,0:T(8,128)S(1)}, u32[]{:S(2)}, u32[]{:S(2)}) collective-permute-start(f32[20,8,128]{2,1,0:T(8,128)S(1)} %group_total.3.refs_6_), channel_id=1, source_target_pairs={{0,8},{1,9},{2,10},{3,11},{4,12},{5,13},{6,14},{7,15},{8,0},{9,1},... | collective-permute-start | bytes 245768 | tf_op jit(solution)/shard_map/ppermute | solution.py:586
  32.2 7.1 %collective-permute-start.18 = (f32[20,8,128]{2,1,0:T(8,128)S(1)}, f32[20,8,128]{2,1,0:T(8,128)S(1)}, u32[]{:S(2)}, u32[]{:S(2)}) collective-permute-start(f32[20,8,128]{2,1,0:T(8,128)S(1)} %group_total.3.refs_6_), channel_id=1, source_target_pairs={{0,4},{1,5},{2,6},{3,7},{4,0},{5,1},{6,2},{7,3},{8,12},{9,13},{10,... | collective-permute-start | bytes 245768 | tf_op jit(solution)/shard_map/ppermute | solution.py:586
  33.8 5.7 %collective-permute-start.10 = (f32[20,8,128]{2,1,0:T(8,128)S(1)}, f32[20,8,128]{2,1,0:T(8,128)S(1)}, u32[]{:S(2)}, u32[]{:S(2)}) collective-permute-start(f32[20,8,128]{2,1,0:T(8,128)S(1)} %group_total.2.refs_2_), channel_id=1, source_target_pairs={{0,12},{1,13},{2,14},{3,15},{4,8},{5,9},{6,10},{7,11},{8,4},{9,5},... | collective-permute-start | bytes 245768 | tf_op jit(solution)/shard_map/ppermute | solution.py:586
  35.1 5.9 %collective-permute-start.11 = (f32[20,8,128]{2,1,0:T(8,128)S(1)}, f32[20,8,128]{2,1,0:T(8,128)S(1)}, u32[]{:S(2)}, u32[]{:S(2)}) collective-permute-start(f32[20,8,128]{2,1,0:T(8,128)S(1)} %group_total.2.refs_2_), channel_id=1, source_target_pairs={{0,8},{1,9},{2,10},{3,11},{4,12},{5,13},{6,14},{7,15},{8,0},{9,1},... | collective-permute-start | bytes 245768 | tf_op jit(solution)/shard_map/ppermute | solution.py:586
  36.5 4.7 %collective-permute-start.12 = (f32[20,8,128]{2,1,0:T(8,128)S(1)}, f32[20,8,128]{2,1,0:T(8,128)S(1)}, u32[]{:S(2)}, u32[]{:S(2)}) collective-permute-start(f32[20,8,128]{2,1,0:T(8,128)S(1)} %group_total.2.refs_2_), channel_id=1, source_target_pairs={{0,4},{1,5},{2,6},{3,7},{4,0},{5,1},{6,2},{7,3},{8,12},{9,13},{10,... | collective-permute-start | bytes 245768 | tf_op jit(solution)/shard_map/ppermute | solution.py:586
  43.2 9.8 %collective-permute-start.21 = (f32[24,128]{1,0:T(8,128)S(1)}, f32[24,128]{1,0:T(8,128)S(1)}, u32[]{:S(2)}, u32[]{:S(2)}) collective-permute-start(f32[24,128]{1,0:T(8,128)S(1)} %select_add_fusion.1.sent_b), channel_id=1, source_target_pairs={{0,112},{16,32},{32,16},{48,64},{64,48},{80,96},{96,80},{112,0},{1... | collective-permute-start | bytes 36872 | tf_op jit(solution)/shard_map/ppermute | solution.py:596
  47.8 5.1 %collective-permute-start.20 = (f32[8,128]{1,0:T(8,128)S(1)}, f32[8,128]{1,0:T(8,128)S(1)}, u32[]{:S(2)}, u32[]{:S(2)}) collective-permute-start(f32[8,128]{1,0:T(8,128)S(1)} %slice_add_fusion.1), channel_id=1, source_target_pairs={{0,64},{16,80},{32,96},{48,112},{64,0},{80,16},{96,32},{112,48},{1... | collective-permute-start | bytes 12296 | tf_op jit(solution)/shard_map/ppermute | solution.py:597
  53.4 5.2 %collective-permute-start.23 = (f32[4,16,128]{2,1,0:T(8,128)S(1)}, f32[4,16,128]{2,1,0:T(8,128)S(1)}, u32[]{:S(2)}, u32[]{:S(2)}) collective-permute-start(f32[4,16,128]{2,1,0:T(8,128)S(1)} %get-tuple-element.75.refs_8_.refs_10_), channel_id=1, source_target_pairs={{0,3},{1,2},{2,1},{3,0},{4,7},{5,6},{6,5},{7,4},{8,11},{9,10},{10,... | collective-permute-start | bytes 98312 | tf_op jit(solution)/shard_map/ppermute | solution.py:586
  55.1 5.5 %collective-permute-start.24 = (f32[4,16,128]{2,1,0:T(8,128)S(1)}, f32[4,16,128]{2,1,0:T(8,128)S(1)}, u32[]{:S(2)}, u32[]{:S(2)}) collective-permute-start(f32[4,16,128]{2,1,0:T(8,128)S(1)} %get-tuple-element.75.refs_8_.refs_10_), channel_id=1, source_target_pairs={{0,2},{1,3},{2,0},{3,1},{4,6},{5,7},{6,4},{7,5},{8,10},{9,11},{10,... | collective-permute-start | bytes 98312 | tf_op jit(solution)/shard_map/ppermute | solution.py:586
  55.8 4.8 %collective-permute-start.25 = (f32[4,16,128]{2,1,0:T(8,128)S(1)}, f32[4,16,128]{2,1,0:T(8,128)S(1)}, u32[]{:S(2)}, u32[]{:S(2)}) collective-permute-start(f32[4,16,128]{2,1,0:T(8,128)S(1)} %get-tuple-element.75.refs_8_.refs_10_), channel_id=1, source_target_pairs={{0,1},{1,0},{2,3},{3,2},{4,5},{5,4},{6,7},{7,6},{8,9},{9,8},{10,11... | collective-permute-start | bytes 98312 | tf_op jit(solution)/shard_map/ppermute | solution.py:586
  60.8 5.2 %collective-permute-start.26 = (f32[4,16,128]{2,1,0:T(8,128)S(1)}, f32[4,16,128]{2,1,0:T(8,128)S(1)}, u32[]{:S(2)}, u32[]{:S(2)}) collective-permute-start(f32[4,16,128]{2,1,0:T(8,128)S(1)} %group_total_again.1.refs_11_), channel_id=1, source_target_pairs={{0,12},{1,13},{2,14},{3,15},{4,8},{5,9},{6,10},{7,11},{8,4},{9,5},... | collective-permute-start | bytes 98312 | tf_op jit(solution)/shard_map/ppermute | solution.py:586
  62.7 5.4 %collective-permute-start.27 = (f32[4,16,128]{2,1,0:T(8,128)S(1)}, f32[4,16,128]{2,1,0:T(8,128)S(1)}, u32[]{:S(2)}, u32[]{:S(2)}) collective-permute-start(f32[4,16,128]{2,1,0:T(8,128)S(1)} %group_total_again.1.refs_11_), channel_id=1, source_target_pairs={{0,8},{1,9},{2,10},{3,11},{4,12},{5,13},{6,14},{7,15},{8,0},{9,1},... | collective-permute-start | bytes 98312 | tf_op jit(solution)/shard_map/ppermute | solution.py:586
  70.0 7.0 %collective-permute-start.31 = (f32[24,128]{1,0:T(8,128)S(1)}, f32[24,128]{1,0:T(8,128)S(1)}, u32[]{:S(2)}, u32[]{:S(2)}) collective-permute-start(f32[24,128]{1,0:T(8,128)S(1)} %select_add_fusion.sent_b), channel_id=1, source_target_pairs={{0,112},{16,32},{32,16},{48,64},{64,48},{80,96},{96,80},{112,0},{1... | collective-permute-start | bytes 36872 | tf_op jit(solution)/shard_map/ppermute | solution.py:596
  71.9 5.1 %collective-permute-start.30 = (f32[8,128]{1,0:T(8,128)S(1)}, f32[8,128]{1,0:T(8,128)S(1)}, u32[]{:S(2)}, u32[]{:S(2)}) collective-permute-start(f32[8,128]{1,0:T(8,128)S(1)} %slice_add_fusion), channel_id=1, source_target_pairs={{0,64},{16,80},{32,96},{48,112},{64,0},{80,16},{96,32},{112,48},{1... | collective-permute-start | bytes 12296 | tf_op jit(solution)/shard_map/ppermute | solution.py:597
  81.2 5.0 %collective-permute-start.35 = (f32[1,128]{1,0:T(1,128)S(1)}, f32[1,128]{1,0:T(1,128)S(1)}, u32[]{:S(2)}, u32[]{:S(2)}) collective-permute-start(f32[1,128]{1,0:T(1,128)S(1)} %add.71), channel_id=1, source_target_pairs={{0,64},{16,80},{32,96},{48,112},{64,0},{80,16},{96,32},{112,48},{1... | collective-permute-start | bytes 1544 | tf_op jit(solution)/shard_map/ppermute | solution.py:603
  81.2 5.0 %collective-permute-start.36 = (f32[1,128]{1,0:T(1,128)S(1)}, f32[1,128]{1,0:T(1,128)S(1)}, u32[]{:S(2)}, u32[]{:S(2)}) collective-permute-start(f32[1,128]{1,0:T(1,128)S(1)} %add.71), channel_id=1, source_target_pairs={{0,32},{16,48},{32,64},{48,80},{64,96},{80,112},{96,0},{112,16},{1... | collective-permute-start | bytes 1544 | tf_op jit(solution)/shard_map/ppermute | solution.py:603
  86.2 4.8 %collective-permute-start.37 = (f32[1,128]{1,0:T(1,128)S(1)}, f32[1,128]{1,0:T(1,128)S(1)}, u32[]{:S(2)}, u32[]{:S(2)}) collective-permute-start(f32[1,128]{1,0:T(1,128)S(1)} %add_add_fusion.2), channel_id=1, source_target_pairs={{0,3},{1,2},{2,1},{3,0},{4,7},{5,6},{6,5},{7,4},{8,11},{9,10},{10,... | collective-permute-start | bytes 1544 | tf_op jit(solution)/shard_map/ppermute | solution.py:586
  87.9 5.0 %collective-permute-start.38 = (f32[1,128]{1,0:T(1,128)S(1)}, f32[1,128]{1,0:T(1,128)S(1)}, u32[]{:S(2)}, u32[]{:S(2)}) collective-permute-start(f32[1,128]{1,0:T(1,128)S(1)} %add_add_fusion.2), channel_id=1, source_target_pairs={{0,2},{1,3},{2,0},{3,1},{4,6},{5,7},{6,4},{7,5},{8,10},{9,11},{10,... | collective-permute-start | bytes 1544 | tf_op jit(solution)/shard_map/ppermute | solution.py:586
  93.0 4.8 %collective-permute-start.40 = (f32[1,128]{1,0:T(1,128)S(1)}, f32[1,128]{1,0:T(1,128)S(1)}, u32[]{:S(2)}, u32[]{:S(2)}) collective-permute-start(f32[1,128]{1,0:T(1,128)S(1)} %add_add_fusion.1), channel_id=1, source_target_pairs={{0,12},{1,13},{2,14},{3,15},{4,8},{5,9},{6,10},{7,11},{8,4},{9,5},... | collective-permute-start | bytes 1544 | tf_op jit(solution)/shard_map/ppermute | solution.py:586
  94.5 5.0 %collective-permute-start.41 = (f32[1,128]{1,0:T(1,128)S(1)}, f32[1,128]{1,0:T(1,128)S(1)}, u32[]{:S(2)}, u32[]{:S(2)}) collective-permute-start(f32[1,128]{1,0:T(1,128)S(1)} %add_add_fusion.1), channel_id=1, source_target_pairs={{0,8},{1,9},{2,10},{3,11},{4,12},{5,13},{6,14},{7,15},{8,0},{9,1},... | collective-permute-start | bytes 1544 | tf_op jit(solution)/shard_map/ppermute | solution.py:586
  (16 other events, 47.9 us)

commit v11 on v9

--- a/solution.py
+++ b/solution.py
@@ -587,20 +587,24 @@
     return [block] + others
 
 
+def chips(step):
+    return [(i, (i + step if i % 2 else i - step) % N_GX) for i in range(N_GX)]
+
+
 def exchange_rows(msg_a, msg_b):
     got_a = lax.ppermute(msg_a, "gx", [(i, i ^ 1) for i in range(N_GX)])
     below = lax.broadcasted_iota(jnp.int32, msg_b.shape, 0) >= 16
     tail = msg_b[16:] + got_a[16:]
     sent_b = msg_b + jnp.where(below, got_a, 0.0)
-    got_d = lax.ppermute(tail, "gx", [(i, (i + 2 if i % 2 else i - 2) % N_GX) for i in range(N_GX)])
-    got_b = lax.ppermute(sent_b, "gx", [(i, (i + 1 if i % 2 else i - 1) % N_GX) for i in range(N_GX)])
-    got_c = lax.ppermute(tail, "gx", [(i, i ^ 4) for i in range(N_GX)])
+    got_d = lax.ppermute(tail, "gx", chips(-3))
+    got_b = lax.ppermute(sent_b, "gx", chips(1))
+    got_c = lax.ppermute(tail, "gx", chips(4))
     return got_a, sent_b, got_c, got_b, got_d
 
 
 def sum_everywhere(x):
     x = x + lax.ppermute(x, "gx", [(i, i ^ 1) for i in range(N_GX)])
-    others = [lax.ppermute(x, "gx", [(i, (i + 2 * k) % N_GX) for i in range(N_GX)]) for k in PARTNERS[1:]]
+    others = [lax.ppermute(x, "gx", chips(step)) for step in (-3, 4, 1)]
     x = x + others[0] + others[1] + others[2]
     x = jnp.broadcast_to(x, (N_GY, NZ))
     return lax.all_to_all(x, "gy", split_axis=0, concat_axis=0, tiled=True)

time: 99.5 us -> 99.1 us (level)
    ppermute x9, starting transfers between devices: 14.4 us -> 13.1 us  [the longest x2 5.8 us: exchange_rows(): got_b = lax.ppermute(sent_b, 'gx', chips(1))]
where the time goes in v11:
time: 99.1 us; the launch traced here: 98.9 us
  starting transfers between devices  48.9 us (49%)
  waiting for transfers between devices  27.9 us (28%)
  blocking collectives  12.1 us (12%)
  Pallas kernels  7.68 us (8%)
  local copies, waits for them, and re-layouts  1.03 us (1%)
    ppermute x24, starting transfers between devices, swapped(): lax.ppermute(block, 'gy', [(i, i ^ k * stride) for i in range(N_GY)])  33.9 us
    ppermute x24, waiting for transfers between devices, swapped(): lax.ppermute(block, 'gy', [(i, i ^ k * stride) for i in range(N_GY)])  13.3 us
    all_to_all x1, blocking collectives, sum_everywhere(): return lax.all_to_all(x, 'gy', split_axis=0, concat_axis=0, tiled=True)  12.1 us
    pallas_call x13, Pallas kernels, call(): pl.pallas_call(kernel, name=name, out_shape=tuple(outs), in_specs=specs o...  7.68 us
    ppermute x2, waiting for transfers between devices, exchange_rows(): got_c = lax.ppermute(tail, 'gx', chips(4))  7.07 us
    ppermute x2, starting transfers between devices, exchange_rows(): got_b = lax.ppermute(sent_b, 'gx', chips(1))  5.8 us
    ppermute x3, starting transfers between devices, sum_everywhere(): others = [lax.ppermute(x, 'gx', chips(step)) for step in (-3, 4, 1)]  4.14 us
    ppermute x3, waiting for transfers between devices, sum_everywhere(): others = [lax.ppermute(x, 'gx', chips(step)) for step in (-3, 4, 1)]  3.42 us
  transfers between devices with their start and end apart: 37, of which 18 were waited for; matrix products, arithmetic and copies ran while one was open for 1% of the time, Pallas kernels for 2%

profile of v11, /device:TPU:0, one launch (start us, length us, event | category | flops | bytes accessed | tf_op | source)
XLA Modules:
  0.0 98.9 jit_solution(11681461657640522952)
XLA Ops:
  0.6 1.6 %edges.1 = (f32[2,8,128]{2,1,0:T(8,128)}, f32[40,128]{1,0:T(8,128)}) custom-call(f32[2,128,128]{2,1,0:T(8,128)} %bitcast.18, f32[2,128,128]{2,1,0:T(8,128)} %bitcast.20, s32[1,128]{1,0:T(1,128)} %brk_h.1), custom_call_target="tpu_custom_call" | custom-call | tf_op jit(solution)/shard_map/edges/pallas_call | solution.py:574
  2.2 4.2 %collective-permute-start = (f32[40,128]{1,0:T(8,128)}, f32[40,128]{1,0:T(8,128)S(1)}, u32[]{:S(2)}, u32[]{:S(2)}) collective-permute-start(f32[40,128]{1,0:T(8,128)} %get-tuple-element.53.refs_0_), channel_id=1, source_target_pairs={{0,3},{1,2},{2,1},{3,0},{4,7},{5,6},{6,5},{7,4},{8,11},{9,10},{10,... | collective-permute-start | bytes 61448 | tf_op jit(solution)/shard_map/ppermute | solution.py:586
  7.3 1.3 %collective-permute-start.3 = (f32[2,8,128]{2,1,0:T(8,128)}, f32[2,8,128]{2,1,0:T(8,128)S(1)}, u32[]{:S(2)}, u32[]{:S(2)}) collective-permute-start(f32[2,8,128]{2,1,0:T(8,128)} %get-tuple-element.51), channel_id=1, source_target_pairs={{0,16},{16,32},{32,48},{48,64},{64,80},{80,96},{96,112},{1,17},{17... | collective-permute-start | bytes 24584 | tf_op jit(solution)/shard_map/ppermute | solution.py:634
  9.7 2.2 %collective-permute-done.1.refs_2_ = f32[40,128]{1,0:T(8,128)S(1)} collective-permute-done((f32[40,128]{1,0:T(8,128)}, f32[40,128]{1,0:T(8,128)S(1)}, u32[]{:S(2)}, u32[]{:S(2)}) %collective-permute-start.1) | collective-permute-done | bytes 20512 | tf_op jit(solution)/shard_map/ppermute | solution.py:586
  12.0 3.1 %collective-permute-start.4 = (f32[40,128]{1,0:T(8,128)S(1)}, f32[40,128]{1,0:T(8,128)S(1)}, u32[]{:S(2)}, u32[]{:S(2)}) collective-permute-start(f32[40,128]{1,0:T(8,128)S(1)} %select_select_fusion.refs_4_), channel_id=1, source_target_pairs={{0,12},{1,13},{2,14},{3,15},{4,8},{5,9},{6,10},{7,11},{8,4},{9,5},... | collective-permute-start | bytes 61448 | tf_op jit(solution)/shard_map/ppermute | solution.py:586
  16.2 1.4 %prepare.1 = (f32[2,8,16,128]{3,2,1,0:T(8,128)S(1)}, f32[2,8,16,128]{3,2,1,0:T(8,128)S(1)}, f32[2,8,16,128]{3,2,1,0:T(8,128)S(1)}, f32[2,8,16,128]{3,2,1,0:T(8,1...) custom-call(f32[2,128,128]{2,1,0:T(8,128)} %bitcast.23, f32[4,128,128]{2,1,0:T(8,128)} %bitcast.22, ...), custom_call_target="tpu_custom_call" | custom-call | tf_op jit(solution)/shard_map/prepare/pallas_call | solution.py:574
  17.6 2.8 %collective-permute-done.5.refs_6_ = f32[40,128]{1,0:T(8,128)S(1)} collective-permute-done((f32[40,128]{1,0:T(8,128)S(1)}, f32[40,128]{1,0:T(8,128)S(1)}, u32[]{:S(2)}, u32[]{:S(2)}) %collective-permute-start.5) | collective-permute-done | bytes 20512 | tf_op jit(solution)/shard_map/ppermute | solution.py:586
  21.8 1.2 %collective-permute-start.14 = (f32[20,8,128]{2,1,0:T(8,128)S(1)}, f32[20,8,128]{2,1,0:T(8,128)S(1)}, u32[]{:S(2)}, u32[]{:S(2)}) collective-permute-start(f32[20,8,128]{2,1,0:T(8,128)S(1)} %get-tuple-element.58.own.refs_4_.refs_1_), channel_id=1, source_target_pairs={{0,2},{1,3},{2,0},{3,1},{4,6},{5,7},{6,4},{7,5},{8,10},{9,11},{10,... | collective-permute-start | bytes 245768 | tf_op jit(solution)/shard_map/ppermute | solution.py:586
  23.0 1.9 %collective-permute-start.15 = (f32[20,8,128]{2,1,0:T(8,128)S(1)}, f32[20,8,128]{2,1,0:T(8,128)S(1)}, u32[]{:S(2)}, u32[]{:S(2)}) collective-permute-start(f32[20,8,128]{2,1,0:T(8,128)S(1)} %get-tuple-element.58.own.refs_4_.refs_1_), channel_id=1, source_target_pairs={{0,1},{1,0},{2,3},{3,2},{4,5},{5,4},{6,7},{7,6},{8,9},{9,8},{10,11... | collective-permute-start | bytes 245768 | tf_op jit(solution)/shard_map/ppermute | solution.py:586
  26.2 1.2 %collective-permute-start.8 = (f32[20,8,128]{2,1,0:T(8,128)S(1)}, f32[20,8,128]{2,1,0:T(8,128)S(1)}, u32[]{:S(2)}, u32[]{:S(2)}) collective-permute-start(f32[20,8,128]{2,1,0:T(8,128)S(1)} %get-tuple-element.57.own.refs_0_), channel_id=1, source_target_pairs={{0,2},{1,3},{2,0},{3,1},{4,6},{5,7},{6,4},{7,5},{8,10},{9,11},{10,... | collective-permute-start | bytes 245768 | tf_op jit(solution)/shard_map/ppermute | solution.py:586
  27.4 1.9 %collective-permute-start.9 = (f32[20,8,128]{2,1,0:T(8,128)S(1)}, f32[20,8,128]{2,1,0:T(8,128)S(1)}, u32[]{:S(2)}, u32[]{:S(2)}) collective-permute-start(f32[20,8,128]{2,1,0:T(8,128)S(1)} %get-tuple-element.57.own.refs_0_), channel_id=1, source_target_pairs={{0,1},{1,0},{2,3},{3,2},{4,5},{5,4},{6,7},{7,6},{8,9},{9,8},{10,11... | collective-permute-start | bytes 245768 | tf_op jit(solution)/shard_map/ppermute | solution.py:586
  29.4 1.4 %collective-permute-start.16 = (f32[20,8,128]{2,1,0:T(8,128)S(1)}, f32[20,8,128]{2,1,0:T(8,128)S(1)}, u32[]{:S(2)}, u32[]{:S(2)}) collective-permute-start(f32[20,8,128]{2,1,0:T(8,128)S(1)} %group_total.3.refs_6_), channel_id=1, source_target_pairs={{0,12},{1,13},{2,14},{3,15},{4,8},{5,9},{6,10},{7,11},{8,4},{9,5},... | collective-permute-start | bytes 245768 | tf_op jit(solution)/shard_map/ppermute | solution.py:586
  32.2 1.4 %collective-permute-start.18 = (f32[20,8,128]{2,1,0:T(8,128)S(1)}, f32[20,8,128]{2,1,0:T(8,128)S(1)}, u32[]{:S(2)}, u32[]{:S(2)}) collective-permute-start(f32[20,8,128]{2,1,0:T(8,128)S(1)} %group_total.3.refs_6_), channel_id=1, source_target_pairs={{0,4},{1,5},{2,6},{3,7},{4,0},{5,1},{6,2},{7,3},{8,12},{9,13},{10,... | collective-permute-start | bytes 245768 | tf_op jit(solution)/shard_map/ppermute | solution.py:586
  33.8 1.4 %collective-permute-start.10 = (f32[20,8,128]{2,1,0:T(8,128)S(1)}, f32[20,8,128]{2,1,0:T(8,128)S(1)}, u32[]{:S(2)}, u32[]{:S(2)}) collective-permute-start(f32[20,8,128]{2,1,0:T(8,128)S(1)} %group_total.2.refs_2_), channel_id=1, source_target_pairs={{0,12},{1,13},{2,14},{3,15},{4,8},{5,9},{6,10},{7,11},{8,4},{9,5},... | collective-permute-start | bytes 245768 | tf_op jit(solution)/shard_map/ppermute | solution.py:586
  35.1 1.4 %collective-permute-start.11 = (f32[20,8,128]{2,1,0:T(8,128)S(1)}, f32[20,8,128]{2,1,0:T(8,128)S(1)}, u32[]{:S(2)}, u32[]{:S(2)}) collective-permute-start(f32[20,8,128]{2,1,0:T(8,128)S(1)} %group_total.2.refs_2_), channel_id=1, source_target_pairs={{0,8},{1,9},{2,10},{3,11},{4,12},{5,13},{6,14},{7,15},{8,0},{9,1},... | collective-permute-start | bytes 245768 | tf_op jit(solution)/shard_map/ppermute | solution.py:586
  36.5 1.4 %collective-permute-start.12 = (f32[20,8,128]{2,1,0:T(8,128)S(1)}, f32[20,8,128]{2,1,0:T(8,128)S(1)}, u32[]{:S(2)}, u32[]{:S(2)}) collective-permute-start(f32[20,8,128]{2,1,0:T(8,128)S(1)} %group_total.2.refs_2_), channel_id=1, source_target_pairs={{0,4},{1,5},{2,6},{3,7},{4,0},{5,1},{6,2},{7,3},{8,12},{9,13},{10,... | collective-permute-start | bytes 245768 | tf_op jit(solution)/shard_map/ppermute | solution.py:586
  39.5 1.6 %collective-permute-done.11.refs_4_ = f32[20,8,128]{2,1,0:T(8,128)S(1)} collective-permute-done((f32[20,8,128]{2,1,0:T(8,128)S(1)}, f32[20,8,128]{2,1,0:T(8,128)S(1)}, u32[]{:S(2)}, u32[]{:S(2)}) %collective-permute-start.11) | collective-permute-done | bytes 81952 | tf_op jit(solution)/shard_map/ppermute | solution.py:586
  41.9 1.2 %collective-permute-done.19.got_a = f32[24,128]{1,0:T(8,128)S(1)} collective-permute-done((f32[24,128]{1,0:T(8,128)S(1)}, f32[24,128]{1,0:T(8,128)S(1)}, u32[]{:S(2)}, u32[]{:S(2)}) %collective-permute-start.19) | collective-permute-done | bytes 12320 | tf_op jit(solution)/shard_map/ppermute | solution.py:595
  43.2 4.7 %collective-permute-start.21 = (f32[24,128]{1,0:T(8,128)S(1)}, f32[24,128]{1,0:T(8,128)S(1)}, u32[]{:S(2)}, u32[]{:S(2)}) collective-permute-start(f32[24,128]{1,0:T(8,128)S(1)} %select_add_fusion.1.sent_b), channel_id=1, source_target_pairs={{0,112},{16,32},{32,16},{48,64},{64,48},{80,96},{96,80},{112,0},{1... | collective-permute-start | bytes 36872 | tf_op jit(solution)/shard_map/ppermute | solution.py:600
  48.6 4.4 %collective-permute-done.20.got_c = f32[8,128]{1,0:T(8,128)S(1)} collective-permute-done((f32[8,128]{1,0:T(8,128)S(1)}, f32[8,128]{1,0:T(8,128)S(1)}, u32[]{:S(2)}, u32[]{:S(2)}) %collective-permute-start.20) | collective-permute-done | bytes 4128 | tf_op jit(solution)/shard_map/ppermute | solution.py:601
  53.4 1.7 %collective-permute-start.23 = (f32[4,16,128]{2,1,0:T(8,128)S(1)}, f32[4,16,128]{2,1,0:T(8,128)S(1)}, u32[]{:S(2)}, u32[]{:S(2)}) collective-permute-start(f32[4,16,128]{2,1,0:T(8,128)S(1)} %get-tuple-element.75.refs_8_.refs_10_), channel_id=1, source_target_pairs={{0,3},{1,2},{2,1},{3,0},{4,7},{5,6},{6,5},{7,4},{8,11},{9,10},{10,... | collective-permute-start | bytes 98312 | tf_op jit(solution)/shard_map/ppermute | solution.py:586
  55.8 1.8 %collective-permute-start.25 = (f32[4,16,128]{2,1,0:T(8,128)S(1)}, f32[4,16,128]{2,1,0:T(8,128)S(1)}, u32[]{:S(2)}, u32[]{:S(2)}) collective-permute-start(f32[4,16,128]{2,1,0:T(8,128)S(1)} %get-tuple-element.75.refs_8_.refs_10_), channel_id=1, source_target_pairs={{0,1},{1,0},{2,3},{3,2},{4,5},{5,4},{6,7},{7,6},{8,9},{9,8},{10,11... | collective-permute-start | bytes 98312 | tf_op jit(solution)/shard_map/ppermute | solution.py:586
  58.7 2.0 %collective-permute-done.24.refs_10_ = f32[4,16,128]{2,1,0:T(8,128)S(1)} collective-permute-done((f32[4,16,128]{2,1,0:T(8,128)S(1)}, f32[4,16,128]{2,1,0:T(8,128)S(1)}, u32[]{:S(2)}, u32[]{:S(2)}) %collective-permute-start.24) | collective-permute-done | bytes 32800 | tf_op jit(solution)/shard_map/ppermute | solution.py:586
  60.9 1.9 %collective-permute-start.26 = (f32[4,16,128]{2,1,0:T(8,128)S(1)}, f32[4,16,128]{2,1,0:T(8,128)S(1)}, u32[]{:S(2)}, u32[]{:S(2)}) collective-permute-start(f32[4,16,128]{2,1,0:T(8,128)S(1)} %group_total_again.1.refs_11_), channel_id=1, source_target_pairs={{0,12},{1,13},{2,14},{3,15},{4,8},{5,9},{6,10},{7,11},{8,4},{9,5},... | collective-permute-start | bytes 98312 | tf_op jit(solution)/shard_map/ppermute | solution.py:586
  62.7 1.4 %collective-permute-start.27 = (f32[4,16,128]{2,1,0:T(8,128)S(1)}, f32[4,16,128]{2,1,0:T(8,128)S(1)}, u32[]{:S(2)}, u32[]{:S(2)}) collective-permute-start(f32[4,16,128]{2,1,0:T(8,128)S(1)} %group_total_again.1.refs_11_), channel_id=1, source_target_pairs={{0,8},{1,9},{2,10},{3,11},{4,12},{5,13},{6,14},{7,15},{8,0},{9,1},... | collective-permute-start | bytes 98312 | tf_op jit(solution)/shard_map/ppermute | solution.py:586
  66.4 1.8 %collective-permute-done.27.refs_13_ = f32[4,16,128]{2,1,0:T(8,128)S(1)} collective-permute-done((f32[4,16,128]{2,1,0:T(8,128)S(1)}, f32[4,16,128]{2,1,0:T(8,128)S(1)}, u32[]{:S(2)}, u32[]{:S(2)}) %collective-permute-start.27) | collective-permute-done | bytes 32800 | tf_op jit(solution)/shard_map/ppermute | solution.py:586
  68.8 1.2 %collective-permute-done.29.got_a = f32[24,128]{1,0:T(8,128)S(1)} collective-permute-done((f32[24,128]{1,0:T(8,128)S(1)}, f32[24,128]{1,0:T(8,128)S(1)}, u32[]{:S(2)}, u32[]{:S(2)}) %collective-permute-start.29) | collective-permute-done | bytes 12320 | tf_op jit(solution)/shard_map/ppermute | solution.py:595
  72.0 1.6 %collective-permute-start.32 = (f32[8,128]{1,0:T(8,128)S(1)}, f32[8,128]{1,0:T(8,128)S(1)}, u32[]{:S(2)}, u32[]{:S(2)}) collective-permute-start(f32[8,128]{1,0:T(8,128)S(1)} %slice_add_fusion), channel_id=1, source_target_pairs={{0,48},{16,96},{32,80},{48,0},{64,112},{80,32},{96,16},{112,64},{1... | collective-permute-start | bytes 12296 | tf_op jit(solution)/shard_map/ppermute | solution.py:599
  73.7 2.7 %collective-permute-done.30.got_c = f32[8,128]{1,0:T(8,128)S(1)} collective-permute-done((f32[8,128]{1,0:T(8,128)S(1)}, f32[8,128]{1,0:T(8,128)S(1)}, u32[]{:S(2)}, u32[]{:S(2)}) %collective-permute-start.30) | collective-permute-done | bytes 4128 | tf_op jit(solution)/shard_map/ppermute | solution.py:601
  78.5 3.3 %collective-permute-start.35 = (f32[1,128]{1,0:T(1,128)S(1)}, f32[1,128]{1,0:T(1,128)S(1)}, u32[]{:S(2)}, u32[]{:S(2)}) collective-permute-start(f32[1,128]{1,0:T(1,128)S(1)} %add.55), channel_id=1, source_target_pairs={{0,64},{16,80},{32,96},{48,112},{64,0},{80,16},{96,32},{112,48},{1... | collective-permute-start | bytes 1544 | tf_op jit(solution)/shard_map/ppermute | solution.py:607
  83.5 2.4 %collective-permute-done.36 = f32[1,128]{1,0:T(1,128)S(1)} collective-permute-done((f32[1,128]{1,0:T(1,128)S(1)}, f32[1,128]{1,0:T(1,128)S(1)}, u32[]{:S(2)}, u32[]{:S(2)}) %collective-permute-start.36) | collective-permute-done | bytes 544 | tf_op jit(solution)/shard_map/ppermute | solution.py:607
  85.9 12.1 %all_to_all.8 = f32[16,1,128]{2,1,0:T(1,128)S(1)} all-to-all(f32[16,1,128]{2,1,0:T(1,128)S(1)} %broadcast_in_dim.39), channel_id=1, replica_groups=mesh['gx'=8,'gy'=16] {'gy'}, dimensions={0} | all-to-all | bytes 16384 | tf_op jit(solution)/shard_map/all_to_all | solution.py:610
  (87 shorter events, 22.5 us)
Async XLA Ops:
  2.2 7.5 %collective-permute-start = (f32[40,128]{1,0:T(8,128)}, f32[40,128]{1,0:T(8,128)S(1)}, u32[]{:S(2)}, u32[]{:S(2)}) collective-permute-start(f32[40,128]{1,0:T(8,128)} %get-tuple-element.53.refs_0_), channel_id=1, source_target_pairs={{0,3},{1,2},{2,1},{3,0},{4,7},{5,6},{6,5},{7,4},{8,11},{9,10},{10,... | collective-permute-start | bytes 61448 | tf_op jit(solution)/shard_map/ppermute | solution.py:586
  6.4 5.5 %collective-permute-start.1 = (f32[40,128]{1,0:T(8,128)}, f32[40,128]{1,0:T(8,128)S(1)}, u32[]{:S(2)}, u32[]{:S(2)}) collective-permute-start(f32[40,128]{1,0:T(8,128)} %get-tuple-element.53.refs_0_), channel_id=1, source_target_pairs={{0,2},{1,3},{2,0},{3,1},{4,6},{5,7},{6,4},{7,5},{8,10},{9,11},{10,... | collective-permute-start | bytes 61448 | tf_op jit(solution)/shard_map/ppermute | solution.py:586
  6.4 5.5 %collective-permute-start.2 = (f32[40,128]{1,0:T(8,128)}, f32[40,128]{1,0:T(8,128)S(1)}, u32[]{:S(2)}, u32[]{:S(2)}) collective-permute-start(f32[40,128]{1,0:T(8,128)} %get-tuple-element.53.refs_0_), channel_id=1, source_target_pairs={{0,1},{1,0},{2,3},{3,2},{4,5},{5,4},{6,7},{7,6},{8,9},{9,8},{10,11... | collective-permute-start | bytes 61448 | tf_op jit(solution)/shard_map/ppermute | solution.py:586
  12.0 5.6 %collective-permute-start.4 = (f32[40,128]{1,0:T(8,128)S(1)}, f32[40,128]{1,0:T(8,128)S(1)}, u32[]{:S(2)}, u32[]{:S(2)}) collective-permute-start(f32[40,128]{1,0:T(8,128)S(1)} %select_select_fusion.refs_4_), channel_id=1, source_target_pairs={{0,12},{1,13},{2,14},{3,15},{4,8},{5,9},{6,10},{7,11},{8,4},{9,5},... | collective-permute-start | bytes 61448 | tf_op jit(solution)/shard_map/ppermute | solution.py:586
  15.1 5.3 %collective-permute-start.5 = (f32[40,128]{1,0:T(8,128)S(1)}, f32[40,128]{1,0:T(8,128)S(1)}, u32[]{:S(2)}, u32[]{:S(2)}) collective-permute-start(f32[40,128]{1,0:T(8,128)S(1)} %select_select_fusion.refs_4_), channel_id=1, source_target_pairs={{0,8},{1,9},{2,10},{3,11},{4,12},{5,13},{6,14},{7,15},{8,0},{9,1},... | collective-permute-start | bytes 61448 | tf_op jit(solution)/shard_map/ppermute | solution.py:586
  15.7 4.7 %collective-permute-start.6 = (f32[40,128]{1,0:T(8,128)S(1)}, f32[40,128]{1,0:T(8,128)S(1)}, u32[]{:S(2)}, u32[]{:S(2)}) collective-permute-start(f32[40,128]{1,0:T(8,128)S(1)} %select_select_fusion.refs_4_), channel_id=1, source_target_pairs={{0,4},{1,5},{2,6},{3,7},{4,0},{5,1},{6,2},{7,3},{8,12},{9,13},{10,... | collective-permute-start | bytes 61448 | tf_op jit(solution)/shard_map/ppermute | solution.py:586
  20.8 6.6 %collective-permute-start.13 = (f32[20,8,128]{2,1,0:T(8,128)S(1)}, f32[20,8,128]{2,1,0:T(8,128)S(1)}, u32[]{:S(2)}, u32[]{:S(2)}) collective-permute-start(f32[20,8,128]{2,1,0:T(8,128)S(1)} %get-tuple-element.58.own.refs_4_.refs_1_), channel_id=1, source_target_pairs={{0,3},{1,2},{2,1},{3,0},{4,7},{5,6},{6,5},{7,4},{8,11},{9,10},{10,... | collective-permute-start | bytes 245768 | tf_op jit(solution)/shard_map/ppermute | solution.py:586
  21.8 7.5 %collective-permute-start.14 = (f32[20,8,128]{2,1,0:T(8,128)S(1)}, f32[20,8,128]{2,1,0:T(8,128)S(1)}, u32[]{:S(2)}, u32[]{:S(2)}) collective-permute-start(f32[20,8,128]{2,1,0:T(8,128)S(1)} %get-tuple-element.58.own.refs_4_.refs_1_), channel_id=1, source_target_pairs={{0,2},{1,3},{2,0},{3,1},{4,6},{5,7},{6,4},{7,5},{8,10},{9,11},{10,... | collective-permute-start | bytes 245768 | tf_op jit(solution)/shard_map/ppermute | solution.py:586
  23.0 6.3 %collective-permute-start.15 = (f32[20,8,128]{2,1,0:T(8,128)S(1)}, f32[20,8,128]{2,1,0:T(8,128)S(1)}, u32[]{:S(2)}, u32[]{:S(2)}) collective-permute-start(f32[20,8,128]{2,1,0:T(8,128)S(1)} %get-tuple-element.58.own.refs_4_.refs_1_), channel_id=1, source_target_pairs={{0,1},{1,0},{2,3},{3,2},{4,5},{5,4},{6,7},{7,6},{8,9},{9,8},{10,11... | collective-permute-start | bytes 245768 | tf_op jit(solution)/shard_map/ppermute | solution.py:586
  25.2 7.0 %collective-permute-start.7 = (f32[20,8,128]{2,1,0:T(8,128)S(1)}, f32[20,8,128]{2,1,0:T(8,128)S(1)}, u32[]{:S(2)}, u32[]{:S(2)}) collective-permute-start(f32[20,8,128]{2,1,0:T(8,128)S(1)} %get-tuple-element.57.own.refs_0_), channel_id=1, source_target_pairs={{0,3},{1,2},{2,1},{3,0},{4,7},{5,6},{6,5},{7,4},{8,11},{9,10},{10,... | collective-permute-start | bytes 245768 | tf_op jit(solution)/shard_map/ppermute | solution.py:586
  26.2 7.5 %collective-permute-start.8 = (f32[20,8,128]{2,1,0:T(8,128)S(1)}, f32[20,8,128]{2,1,0:T(8,128)S(1)}, u32[]{:S(2)}, u32[]{:S(2)}) collective-permute-start(f32[20,8,128]{2,1,0:T(8,128)S(1)} %get-tuple-element.57.own.refs_0_), channel_id=1, source_target_pairs={{0,2},{1,3},{2,0},{3,1},{4,6},{5,7},{6,4},{7,5},{8,10},{9,11},{10,... | collective-permute-start | bytes 245768 | tf_op jit(solution)/shard_map/ppermute | solution.py:586
  27.4 6.2 %collective-permute-start.9 = (f32[20,8,128]{2,1,0:T(8,128)S(1)}, f32[20,8,128]{2,1,0:T(8,128)S(1)}, u32[]{:S(2)}, u32[]{:S(2)}) collective-permute-start(f32[20,8,128]{2,1,0:T(8,128)S(1)} %get-tuple-element.57.own.refs_0_), channel_id=1, source_target_pairs={{0,1},{1,0},{2,3},{3,2},{4,5},{5,4},{6,7},{7,6},{8,9},{9,8},{10,11... | collective-permute-start | bytes 245768 | tf_op jit(solution)/shard_map/ppermute | solution.py:586
  29.4 7.1 %collective-permute-start.16 = (f32[20,8,128]{2,1,0:T(8,128)S(1)}, f32[20,8,128]{2,1,0:T(8,128)S(1)}, u32[]{:S(2)}, u32[]{:S(2)}) collective-permute-start(f32[20,8,128]{2,1,0:T(8,128)S(1)} %group_total.3.refs_6_), channel_id=1, source_target_pairs={{0,12},{1,13},{2,14},{3,15},{4,8},{5,9},{6,10},{7,11},{8,4},{9,5},... | collective-permute-start | bytes 245768 | tf_op jit(solution)/shard_map/ppermute | solution.py:586
  30.8 8.4 %collective-permute-start.17 = (f32[20,8,128]{2,1,0:T(8,128)S(1)}, f32[20,8,128]{2,1,0:T(8,128)S(1)}, u32[]{:S(2)}, u32[]{:S(2)}) collective-permute-start(f32[20,8,128]{2,1,0:T(8,128)S(1)} %group_total.3.refs_6_), channel_id=1, source_target_pairs={{0,8},{1,9},{2,10},{3,11},{4,12},{5,13},{6,14},{7,15},{8,0},{9,1},... | collective-permute-start | bytes 245768 | tf_op jit(solution)/shard_map/ppermute | solution.py:586
  32.2 7.1 %collective-permute-start.18 = (f32[20,8,128]{2,1,0:T(8,128)S(1)}, f32[20,8,128]{2,1,0:T(8,128)S(1)}, u32[]{:S(2)}, u32[]{:S(2)}) collective-permute-start(f32[20,8,128]{2,1,0:T(8,128)S(1)} %group_total.3.refs_6_), channel_id=1, source_target_pairs={{0,4},{1,5},{2,6},{3,7},{4,0},{5,1},{6,2},{7,3},{8,12},{9,13},{10,... | collective-permute-start | bytes 245768 | tf_op jit(solution)/shard_map/ppermute | solution.py:586
  33.8 5.7 %collective-permute-start.10 = (f32[20,8,128]{2,1,0:T(8,128)S(1)}, f32[20,8,128]{2,1,0:T(8,128)S(1)}, u32[]{:S(2)}, u32[]{:S(2)}) collective-permute-start(f32[20,8,128]{2,1,0:T(8,128)S(1)} %group_total.2.refs_2_), channel_id=1, source_target_pairs={{0,12},{1,13},{2,14},{3,15},{4,8},{5,9},{6,10},{7,11},{8,4},{9,5},... | collective-permute-start | bytes 245768 | tf_op jit(solution)/shard_map/ppermute | solution.py:586
  35.1 5.9 %collective-permute-start.11 = (f32[20,8,128]{2,1,0:T(8,128)S(1)}, f32[20,8,128]{2,1,0:T(8,128)S(1)}, u32[]{:S(2)}, u32[]{:S(2)}) collective-permute-start(f32[20,8,128]{2,1,0:T(8,128)S(1)} %group_total.2.refs_2_), channel_id=1, source_target_pairs={{0,8},{1,9},{2,10},{3,11},{4,12},{5,13},{6,14},{7,15},{8,0},{9,1},... | collective-permute-start | bytes 245768 | tf_op jit(solution)/shard_map/ppermute | solution.py:586
  36.5 4.7 %collective-permute-start.12 = (f32[20,8,128]{2,1,0:T(8,128)S(1)}, f32[20,8,128]{2,1,0:T(8,128)S(1)}, u32[]{:S(2)}, u32[]{:S(2)}) collective-permute-start(f32[20,8,128]{2,1,0:T(8,128)S(1)} %group_total.2.refs_2_), channel_id=1, source_target_pairs={{0,4},{1,5},{2,6},{3,7},{4,0},{5,1},{6,2},{7,3},{8,12},{9,13},{10,... | collective-permute-start | bytes 245768 | tf_op jit(solution)/shard_map/ppermute | solution.py:586
  43.2 9.8 %collective-permute-start.21 = (f32[24,128]{1,0:T(8,128)S(1)}, f32[24,128]{1,0:T(8,128)S(1)}, u32[]{:S(2)}, u32[]{:S(2)}) collective-permute-start(f32[24,128]{1,0:T(8,128)S(1)} %select_add_fusion.1.sent_b), channel_id=1, source_target_pairs={{0,112},{16,32},{32,16},{48,64},{64,48},{80,96},{96,80},{112,0},{1... | collective-permute-start | bytes 36872 | tf_op jit(solution)/shard_map/ppermute | solution.py:600
  47.8 5.1 %collective-permute-start.20 = (f32[8,128]{1,0:T(8,128)S(1)}, f32[8,128]{1,0:T(8,128)S(1)}, u32[]{:S(2)}, u32[]{:S(2)}) collective-permute-start(f32[8,128]{1,0:T(8,128)S(1)} %slice_add_fusion.1), channel_id=1, source_target_pairs={{0,64},{16,80},{32,96},{48,112},{64,0},{80,16},{96,32},{112,48},{1... | collective-permute-start | bytes 12296 | tf_op jit(solution)/shard_map/ppermute | solution.py:601
  48.6 4.4 %collective-permute-start.22 = (f32[8,128]{1,0:T(8,128)S(1)}, f32[8,128]{1,0:T(8,128)S(1)}, u32[]{:S(2)}, u32[]{:S(2)}) collective-permute-start(f32[8,128]{1,0:T(8,128)S(1)} %slice_add_fusion.1), channel_id=1, source_target_pairs={{0,48},{16,96},{32,80},{48,0},{64,112},{80,32},{96,16},{112,64},{1... | collective-permute-start | bytes 12296 | tf_op jit(solution)/shard_map/ppermute | solution.py:599
  53.4 5.2 %collective-permute-start.23 = (f32[4,16,128]{2,1,0:T(8,128)S(1)}, f32[4,16,128]{2,1,0:T(8,128)S(1)}, u32[]{:S(2)}, u32[]{:S(2)}) collective-permute-start(f32[4,16,128]{2,1,0:T(8,128)S(1)} %get-tuple-element.75.refs_8_.refs_10_), channel_id=1, source_target_pairs={{0,3},{1,2},{2,1},{3,0},{4,7},{5,6},{6,5},{7,4},{8,11},{9,10},{10,... | collective-permute-start | bytes 98312 | tf_op jit(solution)/shard_map/ppermute | solution.py:586
  55.2 5.5 %collective-permute-start.24 = (f32[4,16,128]{2,1,0:T(8,128)S(1)}, f32[4,16,128]{2,1,0:T(8,128)S(1)}, u32[]{:S(2)}, u32[]{:S(2)}) collective-permute-start(f32[4,16,128]{2,1,0:T(8,128)S(1)} %get-tuple-element.75.refs_8_.refs_10_), channel_id=1, source_target_pairs={{0,2},{1,3},{2,0},{3,1},{4,6},{5,7},{6,4},{7,5},{8,10},{9,11},{10,... | collective-permute-start | bytes 98312 | tf_op jit(solution)/shard_map/ppermute | solution.py:586
  55.8 4.9 %collective-permute-start.25 = (f32[4,16,128]{2,1,0:T(8,128)S(1)}, f32[4,16,128]{2,1,0:T(8,128)S(1)}, u32[]{:S(2)}, u32[]{:S(2)}) collective-permute-start(f32[4,16,128]{2,1,0:T(8,128)S(1)} %get-tuple-element.75.refs_8_.refs_10_), channel_id=1, source_target_pairs={{0,1},{1,0},{2,3},{3,2},{4,5},{5,4},{6,7},{7,6},{8,9},{9,8},{10,11... | collective-permute-start | bytes 98312 | tf_op jit(solution)/shard_map/ppermute | solution.py:586
  60.9 5.5 %collective-permute-start.26 = (f32[4,16,128]{2,1,0:T(8,128)S(1)}, f32[4,16,128]{2,1,0:T(8,128)S(1)}, u32[]{:S(2)}, u32[]{:S(2)}) collective-permute-start(f32[4,16,128]{2,1,0:T(8,128)S(1)} %group_total_again.1.refs_11_), channel_id=1, source_target_pairs={{0,12},{1,13},{2,14},{3,15},{4,8},{5,9},{6,10},{7,11},{8,4},{9,5},... | collective-permute-start | bytes 98312 | tf_op jit(solution)/shard_map/ppermute | solution.py:586
  62.7 5.4 %collective-permute-start.27 = (f32[4,16,128]{2,1,0:T(8,128)S(1)}, f32[4,16,128]{2,1,0:T(8,128)S(1)}, u32[]{:S(2)}, u32[]{:S(2)}) collective-permute-start(f32[4,16,128]{2,1,0:T(8,128)S(1)} %group_total_again.1.refs_11_), channel_id=1, source_target_pairs={{0,8},{1,9},{2,10},{3,11},{4,12},{5,13},{6,14},{7,15},{8,0},{9,1},... | collective-permute-start | bytes 98312 | tf_op jit(solution)/shard_map/ppermute | solution.py:586
  70.1 6.3 %collective-permute-start.31 = (f32[24,128]{1,0:T(8,128)S(1)}, f32[24,128]{1,0:T(8,128)S(1)}, u32[]{:S(2)}, u32[]{:S(2)}) collective-permute-start(f32[24,128]{1,0:T(8,128)S(1)} %select_add_fusion.sent_b), channel_id=1, source_target_pairs={{0,112},{16,32},{32,16},{48,64},{64,48},{80,96},{96,80},{112,0},{1... | collective-permute-start | bytes 36872 | tf_op jit(solution)/shard_map/ppermute | solution.py:600
  71.2 5.1 %collective-permute-start.30 = (f32[8,128]{1,0:T(8,128)S(1)}, f32[8,128]{1,0:T(8,128)S(1)}, u32[]{:S(2)}, u32[]{:S(2)}) collective-permute-start(f32[8,128]{1,0:T(8,128)S(1)} %slice_add_fusion), channel_id=1, source_target_pairs={{0,64},{16,80},{32,96},{48,112},{64,0},{80,16},{96,32},{112,48},{1... | collective-permute-start | bytes 12296 | tf_op jit(solution)/shard_map/ppermute | solution.py:601
  72.0 4.3 %collective-permute-start.32 = (f32[8,128]{1,0:T(8,128)S(1)}, f32[8,128]{1,0:T(8,128)S(1)}, u32[]{:S(2)}, u32[]{:S(2)}) collective-permute-start(f32[8,128]{1,0:T(8,128)S(1)} %slice_add_fusion), channel_id=1, source_target_pairs={{0,48},{16,96},{32,80},{48,0},{64,112},{80,32},{96,16},{112,64},{1... | collective-permute-start | bytes 12296 | tf_op jit(solution)/shard_map/ppermute | solution.py:599
  78.3 4.1 %collective-permute-start.34 = (f32[1,128]{1,0:T(1,128)S(1)}, f32[1,128]{1,0:T(1,128)S(1)}, u32[]{:S(2)}, u32[]{:S(2)}) collective-permute-start(f32[1,128]{1,0:T(1,128)S(1)} %add.55), channel_id=1, source_target_pairs={{0,48},{16,96},{32,80},{48,0},{64,112},{80,32},{96,16},{112,64},{1... | collective-permute-start | bytes 1544 | tf_op jit(solution)/shard_map/ppermute | solution.py:607
  78.5 5.0 %collective-permute-start.35 = (f32[1,128]{1,0:T(1,128)S(1)}, f32[1,128]{1,0:T(1,128)S(1)}, u32[]{:S(2)}, u32[]{:S(2)}) collective-permute-start(f32[1,128]{1,0:T(1,128)S(1)} %add.55), channel_id=1, source_target_pairs={{0,64},{16,80},{32,96},{48,112},{64,0},{80,16},{96,32},{112,48},{1... | collective-permute-start | bytes 1544 | tf_op jit(solution)/shard_map/ppermute | solution.py:607
  81.7 4.2 %collective-permute-start.36 = (f32[1,128]{1,0:T(1,128)S(1)}, f32[1,128]{1,0:T(1,128)S(1)}, u32[]{:S(2)}, u32[]{:S(2)}) collective-permute-start(f32[1,128]{1,0:T(1,128)S(1)} %add.55), channel_id=1, source_target_pairs={{0,112},{16,32},{32,16},{48,64},{64,48},{80,96},{96,80},{112,0},{1... | collective-permute-start | bytes 1544 | tf_op jit(solution)/shard_map/ppermute | solution.py:607
  (10 other events, 23.7 us)
